TPU v7x, 32 devices: a whole 2x2x4 slice. The times are simulated.
32 devices in a mesh: rows: 8 (over z, x), cols: 4 (over y, core).
Axes of the slice: x: 2, y: 2, z: 4, core: 2. Of those that a mesh axis runs over, the one named last changes fastest.
Arguments:
- x_img: bfloat16 [8, 1024, 1536], P('rows', None, 'cols'), may hold values from -6 to 6
- x_txt: bfloat16 [8, 154, 1536], P('rows', None, 'cols'), may hold values from -6 to 6
- cond: float32 [8, 1536], P(None, 'rows'), may hold values from -6 to 6
- back_img: bfloat16 [8, 1024, 1536], P('rows', None, 'cols'), may hold values from -6 to 6
- back_txt: bfloat16 [8, 154, 1536], P('rows', None, 'cols'), may hold values from -6 to 6
- w_mod: float32 [1536, 2, 6, 1536], P('rows', None, None, 'cols'), may hold values from -0.15625 to 0.15625
- w_qkv: float32 [1536, 2, 3, 1536], P('rows', None, None, 'cols'), may hold values from -1 to 1
- w_proj: float32 [1536, 2, 1536], P('rows', None, 'cols'), may hold values from -0.4375 to 0.4375
- w_up: float32 [1536, 2, 4, 1536], P('rows', None, None, 'cols'), may hold values from -0.15625 to 0.15625
- w_down: float32 [1536, 2, 4, 1536], P('rows', None, None, 'cols'), may hold values from -0.078125 to 0.078125
- biases: float32 [2, 14, 1536], P(None, None, 'cols'), may hold values from -0.3 to 0.3
- moments_mod: float32 [2, 1536, 2, 6, 1536], P(None, 'rows', None, None, 'cols'), may hold values from -8192 to 8192, as said below
- moments_qkv: float32 [2, 1536, 2, 3, 1536], P(None, 'rows', None, None, 'cols'), may hold values from -8192 to 8192, as said below
- moments_proj: float32 [2, 1536, 2, 1536], P(None, 'rows', None, 'cols'), may hold values from -8192 to 8192, as said below
- moments_up: float32 [2, 1536, 2, 4, 1536], P(None, 'rows', None, None, 'cols'), may hold values from -8192 to 8192, as said below
- moments_down: float32 [2, 1536, 2, 4, 1536], P(None, 'rows', None, None, 'cols'), may hold values from -8192 to 8192, as said below
- moments_bias: float32 [2, 2, 14, 1536], P(None, None, None, 'cols'), may hold values from -8192 to 8192, as said below
Outputs:
- out_img: bfloat16 [8, 1024, 1536], P('rows', None, 'cols')
- out_txt: bfloat16 [8, 154, 1536], P('rows', None, 'cols')
- grad_img: float32 [8, 1024, 1536], P('rows', None, 'cols')
- grad_txt: float32 [8, 154, 1536], P('rows', None, 'cols')
- grad_cond: float32 [8, 1536], P(None, 'rows')
- grad_mod: float32 [1536, 2, 6, 1536], P('rows', None, None, 'cols')
- grad_qkv: float32 [1536, 2, 3, 1536], P('rows', None, None, 'cols')
- grad_proj: float32 [1536, 2, 1536], P('rows', None, 'cols')
- grad_up: float32 [1536, 2, 4, 1536], P('rows', None, None, 'cols')
- grad_down: float32 [1536, 2, 4, 1536], P('rows', None, None, 'cols')
- grad_bias: float32 [2, 14, 1536], P(None, None, 'cols')
- next_mod: float32 [1536, 2, 6, 1536], P('rows', None, None, 'cols')
- next_qkv: float32 [1536, 2, 3, 1536], P('rows', None, None, 'cols')
- next_proj: float32 [1536, 2, 1536], P('rows', None, 'cols')
- next_up: float32 [1536, 2, 4, 1536], P('rows', None, None, 'cols')
- next_down: float32 [1536, 2, 4, 1536], P('rows', None, None, 'cols')
- next_bias: float32 [2, 14, 1536], P(None, None, 'cols')
- next_first_mod: float32 [1536, 2, 6, 1536], P('rows', None, None, 'cols')
- next_second_mod: float32 [1536, 2, 6, 1536], P('rows', None, None, 'cols')
- next_moments_qkv: float32 [2, 1536, 2, 3, 1536], P(None, 'rows', None, None, 'cols')
- next_moments_proj: float32 [2, 1536, 2, 1536], P(None, 'rows', None, 'cols')
- next_moments_up: float32 [2, 1536, 2, 4, 1536], P(None, 'rows', None, None, 'cols')
- next_moments_down: float32 [2, 1536, 2, 4, 1536], P(None, 'rows', None, None, 'cols')
- next_first_bias: float32 [2, 14, 1536], P(None, None, 'cols')
- next_second_bias: float32 [2, 14, 1536], P(None, None, 'cols')
Inputs may be any that keep to these rules, and one draw needn't show every extreme that they name: `moments_mod`: entries at index 1 of the first dimension are positive. `moments_qkv`: entries at index 1 of the first dimension are positive. `moments_proj`: entries at index 1 of the first dimension are positive. `moments_up`: entries at index 1 of the first dimension are positive. `moments_down`: entries at index 1 of the first dimension are positive. `moments_bias`: entries at index 1 of the first dimension are positive.
All inputs are finite; a program needn't handle non-finite values.
Results may differ from a plain program's by a relative error of at most 0.012.
Values may be sent and summed in bfloat16 or wider, within the bound.
No kernel may reach another device: no remote copies, remote signals or barrier semaphores. Data moves between devices by JAX's collectives and lax.ppermute only.
A program may use at most 384 MiB of HBM per device.

v0:
```python
import jax
import jax.numpy as jnp
from jax import lax
from jax.sharding import PartitionSpec as P

D = 1536
HEAD_FEATURES = 64
IMAGE_TOKENS = 1024
TXT = 154
STEP = 2


BETA_ONE = 0.9
BETA_TWO = 0.95
LEARN_RATE = 0.02
DECAY_RATE = 0.1
ADAM_EPS = 1e-08
NORM_EPS = 1e-06
GELU_COEF = 0.7978845608028654
GELU_CUBE = 0.044715


def narrow(values):
    return values.astype(jnp.bfloat16)


def gelu_value(inputs):
    return (
        0.5 * inputs * (1.0 + jnp.tanh(GELU_COEF * (inputs + GELU_CUBE * inputs * inputs * inputs)))
    )


def gelu_slope(inputs):
    tangent = jnp.tanh(GELU_COEF * (inputs + GELU_CUBE * inputs * inputs * inputs))
    return 0.5 * (1.0 + tangent) + 0.5 * inputs * (1.0 - tangent * tangent) * GELU_COEF * (
        1.0 + 3.0 * GELU_CUBE * inputs * inputs
    )


def column_total(parts):
    return lax.psum(parts, "cols")


def normalize(values):
    totals = column_total((jnp.sum(values, axis=2), jnp.sum(values * values, axis=2)))
    center = totals[0][:, :, None] / D
    inverse = lax.rsqrt(totals[1][:, :, None] / D - center * center + NORM_EPS)
    return ((values - center) * inverse, inverse)


def normalize_back(grad_unit, unit_rows, inverse):
    totals = column_total((jnp.sum(grad_unit, axis=2), jnp.sum(grad_unit * unit_rows, axis=2)))
    return inverse * (
        grad_unit - totals[0][:, :, None] / D - unit_rows * (totals[1][:, :, None] / D)
    )


def per_token(table):
    seq_count, width = (table.shape[0], table.shape[2])
    return jnp.concatenate(
        [
            jnp.broadcast_to(table[:, 0:1], (seq_count, IMAGE_TOKENS, width)),
            jnp.broadcast_to(table[:, 1:2], (seq_count, TXT, width)),
        ],
        axis=1,
    )


def stream_bias(table):
    trailing = table.shape[1:]
    return jnp.concatenate(
        [
            jnp.broadcast_to(table[0][None, None], (1, IMAGE_TOKENS) + trailing),
            jnp.broadcast_to(table[1][None, None], (1, TXT) + trailing),
        ],
        axis=1,
    )


def stream_sums(values):
    return jnp.stack(
        [jnp.sum(values[:, :IMAGE_TOKENS], axis=1), jnp.sum(values[:, IMAGE_TOKENS:], axis=1)],
        axis=1,
    )


def gather_width(values):
    return lax.all_gather(values, "cols", axis=2, tiled=True)


def scatter_width(partial_value):
    return lax.psum_scatter(partial_value, "cols", scatter_dimension=2, tiled=True)


def apply_rows(activations_complete, weight_portion):
    image_part = jnp.einsum(
        "xbq,qgu->xbgu",
        activations_complete[:, :IMAGE_TOKENS],
        weight_portion[:, 0],
        preferred_element_type=jnp.float32,
    )
    text_part = jnp.einsum(
        "xbq,qgu->xbgu",
        activations_complete[:, IMAGE_TOKENS:],
        weight_portion[:, 1],
        preferred_element_type=jnp.float32,
    )
    return jnp.concatenate([image_part, text_part], axis=1)


def contract_rows(weight, activations_complete):
    return apply_rows(activations_complete, weight)


def emit_rows(acts_local, weight_portion):
    image_part = jnp.einsum(
        "slkc,jkc->slj",
        acts_local[:, :IMAGE_TOKENS],
        weight_portion[:, 0],
        preferred_element_type=jnp.float32,
    )
    text_part = jnp.einsum(
        "slkc,jkc->slj",
        acts_local[:, IMAGE_TOKENS:],
        weight_portion[:, 1],
        preferred_element_type=jnp.float32,
    )
    return jnp.concatenate([image_part, text_part], axis=1)


def expand_rows(weight, acts_local):
    partial_value = emit_rows(acts_local, weight)
    return scatter_width(partial_value)


def grad_terms(outer_full, inner_local):
    image_part = jnp.einsum(
        "slj,slkc->jkc",
        outer_full[:, :IMAGE_TOKENS],
        inner_local[:, :IMAGE_TOKENS],
        preferred_element_type=jnp.float32,
    )
    text_part = jnp.einsum(
        "slj,slkc->jkc",
        outer_full[:, IMAGE_TOKENS:],
        inner_local[:, IMAGE_TOKENS:],
        preferred_element_type=jnp.float32,
    )
    return jnp.stack([image_part, text_part], axis=1)


def weight_grad(outer_full, inner_local):
    return grad_terms(outer_full, inner_local)


def pair_slice(values, offset):
    seq_count, length = (values.shape[0], values.shape[1])
    return lax.dynamic_slice_in_dim(values, offset, 2 * HEAD_FEATURES, 2).reshape(
        seq_count, length, 2, HEAD_FEATURES
    )


def pair_scores(query_part, key_part):
    return jnp.einsum(
        "sqhe,skhe->shqk", query_part, key_part, preferred_element_type=jnp.float32
    ) * HEAD_FEATURES ** (-0.5)


def attention(triple):
    seq_count, length, width = (triple.shape[0], triple.shape[1], triple.shape[3])
    queries, keys_all, values_all = (triple[:, :, 0], triple[:, :, 1], triple[:, :, 2])

    def pair_step(pair_index, state):
        mixture, log_totals = state
        offset = pair_index * 2 * HEAD_FEATURES
        query_part = pair_slice(queries, offset)
        key_part = pair_slice(keys_all, offset)
        value_part = pair_slice(values_all, offset)
        scores = pair_scores(query_part, key_part)
        highest = jnp.max(scores, axis=3, keepdims=True)
        log_total = highest + jnp.log(jnp.sum(jnp.exp(scores - highest), axis=3, keepdims=True))
        soft_weights = narrow(jnp.exp(scores - log_total))
        head_out = jnp.einsum(
            "shqk,skhe->sqhe", soft_weights, value_part, preferred_element_type=jnp.float32
        )
        mixture = lax.dynamic_update_slice_in_dim(
            mixture, narrow(head_out.reshape(seq_count, length, 2 * HEAD_FEATURES)), offset, 2
        )
        log_totals = lax.dynamic_update_index_in_dim(log_totals, log_total, pair_index, 0)
        return (mixture, log_totals)

    pairs = width // (2 * HEAD_FEATURES)
    initial = (
        jnp.zeros((seq_count, length, width), jnp.bfloat16),
        jnp.zeros((pairs, seq_count, 2, length, 1), jnp.float32),
    )
    return lax.fori_loop(0, pairs, pair_step, initial)


def attention_back(triple, log_totals, grad_mix):
    seq_count, length, width = (triple.shape[0], triple.shape[1], triple.shape[3])
    queries, keys_all, values_all = (triple[:, :, 0], triple[:, :, 1], triple[:, :, 2])
    scale_factor = HEAD_FEATURES ** (-0.5)

    def pair_step(pair_index, state):
        grad_queries, grad_keys, value_gradients = state
        offset = pair_index * 2 * HEAD_FEATURES
        query_part = pair_slice(queries, offset)
        key_part = pair_slice(keys_all, offset)
        value_part = pair_slice(values_all, offset)
        grad_part = pair_slice(grad_mix, offset)
        scores = pair_scores(query_part, key_part)
        soft_full = jnp.exp(
            scores - lax.dynamic_index_in_dim(log_totals, pair_index, 0, keepdims=False)
        )
        soft_round = narrow(soft_full)
        grad_value = jnp.einsum(
            "shqk,sqhe->skhe", soft_round, grad_part, preferred_element_type=jnp.float32
        )
        grad_soft = jnp.einsum(
            "sqhe,skhe->shqk", grad_part, value_part, preferred_element_type=jnp.float32
        )
        delta_row = jnp.sum(soft_full * grad_soft, axis=3, keepdims=True)
        score_round = narrow(soft_full * (grad_soft - delta_row))
        grad_query = (
            jnp.einsum("shqk,skhe->sqhe", score_round, key_part, preferred_element_type=jnp.float32)
            * scale_factor
        )
        grad_key = (
            jnp.einsum(
                "shqk,sqhe->skhe", score_round, query_part, preferred_element_type=jnp.float32
            )
            * scale_factor
        )
        flat_shape = (seq_count, length, 2 * HEAD_FEATURES)
        grad_queries = lax.dynamic_update_slice_in_dim(
            grad_queries, grad_query.reshape(flat_shape), offset, 2
        )
        grad_keys = lax.dynamic_update_slice_in_dim(
            grad_keys, grad_key.reshape(flat_shape), offset, 2
        )
        value_gradients = lax.dynamic_update_slice_in_dim(
            value_gradients, grad_value.reshape(flat_shape), offset, 2
        )
        return (grad_queries, grad_keys, value_gradients)

    zeros_block = jnp.zeros((seq_count, length, width), jnp.float32)
    return lax.fori_loop(
        0, width // (2 * HEAD_FEATURES), pair_step, (zeros_block, zeros_block, zeros_block)
    )


def adam_step(param, moments, gradient):
    first_moment = BETA_ONE * moments[0] + (1.0 - BETA_ONE) * gradient
    second_moment = BETA_TWO * moments[1] + (1.0 - BETA_TWO) * gradient * gradient
    update = (
        first_moment
        / (1.0 - BETA_ONE**STEP)
        / (jnp.sqrt(second_moment / (1.0 - BETA_TWO**STEP)) + ADAM_EPS)
    )
    return (param - LEARN_RATE * (update + DECAY_RATE * param), first_moment, second_moment)


def shards(
    x_img,
    x_txt,
    cond,
    back_img,
    back_txt,
    w_mod,
    w_qkv,
    w_proj,
    w_up,
    w_down,
    biases,
    moments_mod,
    moments_qkv,
    moments_proj,
    moments_up,
    moments_down,
    moments_bias,
):
    silu_cond = narrow(jax.nn.silu(cond))
    mod_round = narrow(w_mod)
    modulation = (
        lax.psum_scatter(
            jnp.einsum("bd,dsic->bsic", silu_cond, mod_round, preferred_element_type=jnp.float32),
            "rows",
            scatter_dimension=0,
            tiled=True,
        )
        + biases[None, :, 0:6]
    )
    shift_one, scale_one, gate_one, shift_two, scale_two, gate_two = [
        per_token(modulation[:, :, slot_index]) for slot_index in range(6)
    ]
    local_weights = (narrow(w_qkv), narrow(w_proj)[:, :, None, :], narrow(w_up), narrow(w_down))
    weights_used = (
        lax.all_gather(local_weights[0], "rows", axis=0, tiled=True),
        lax.all_gather(local_weights[1], "rows", axis=0, tiled=True),
        lax.all_gather(local_weights[2], "rows", axis=0, tiled=True),
        lax.all_gather(local_weights[3], "rows", axis=0, tiled=True),
    )
    triple_weight, project_weight, raise_weight, lower_weight = weights_used
    source = jnp.concatenate([x_img, x_txt], axis=1).astype(jnp.float32)
    unit_one, inverse_one = normalize(source)
    normed_one = gather_width(narrow(unit_one * (1.0 + scale_one) + shift_one))
    triple_bias = jnp.stack([biases[:, 6], jnp.zeros_like(biases[:, 6]), biases[:, 7]], axis=1)
    triple = narrow(contract_rows(triple_weight, normed_one) + stream_bias(triple_bias))
    attended, log_totals = attention(triple)
    attended_items = attended[:, :, None, :]
    projected = expand_rows(project_weight, attended_items) + stream_bias(biases[:, 8])
    residual = source + gate_one * projected
    unit_two, inverse_two = normalize(residual)
    normed_two = gather_width(narrow(unit_two * (1.0 + scale_two) + shift_two))
    hidden_pre = contract_rows(raise_weight, normed_two) + stream_bias(biases[:, 9:13])
    hidden_act = narrow(gelu_value(hidden_pre))
    lowered = expand_rows(lower_weight, hidden_act) + stream_bias(biases[:, 13])
    output = narrow(residual + gate_two * lowered)
    cotangent = jnp.concatenate([back_img, back_txt], axis=1).astype(jnp.float32)
    grad_lowered = gate_two * cotangent
    lowered_full = gather_width(narrow(grad_lowered))
    grad_down = weight_grad(lowered_full, hidden_act)
    grad_hidden = contract_rows(lower_weight, lowered_full) * gelu_slope(hidden_pre)
    hidden_round = narrow(grad_hidden)
    grad_up = weight_grad(normed_two, hidden_round)
    grad_normed_two = expand_rows(raise_weight, hidden_round)
    grad_residual = cotangent + normalize_back(
        grad_normed_two * (1.0 + scale_two), unit_two, inverse_two
    )
    grad_projected = gate_one * grad_residual
    projected_full = gather_width(narrow(grad_projected))
    grad_proj = weight_grad(projected_full, attended_items)
    grad_attended = narrow(contract_rows(project_weight, projected_full)[:, :, 0])
    grad_query, grad_key, grad_value = attention_back(triple, log_totals, grad_attended)
    triple_round = narrow(jnp.stack([grad_query, grad_key, grad_value], axis=2))
    grad_qkv = weight_grad(normed_one, triple_round)
    gradient_first_normalized = expand_rows(triple_weight, triple_round)
    grad_source = grad_residual + normalize_back(
        gradient_first_normalized * (1.0 + scale_one), unit_one, inverse_one
    )
    table = jnp.stack(
        [
            stream_sums(gradient_first_normalized),
            stream_sums(gradient_first_normalized * unit_one),
            stream_sums(grad_residual * projected),
            stream_sums(grad_normed_two),
            stream_sums(grad_normed_two * unit_two),
            stream_sums(cotangent * lowered),
        ],
        axis=2,
    )
    bias_part = jnp.concatenate(
        [
            jnp.sum(stream_sums(grad_query), axis=0)[:, None],
            jnp.sum(stream_sums(grad_value), axis=0)[:, None],
            jnp.sum(stream_sums(grad_projected), axis=0)[:, None],
            jnp.sum(stream_sums(grad_hidden), axis=0),
            jnp.sum(stream_sums(grad_lowered), axis=0)[:, None],
        ],
        axis=1,
    )
    table_all, bias_all = (
        lax.all_gather(table, "rows", axis=0, tiled=True),
        lax.all_gather(bias_part[None], "rows", axis=0, tiled=True),
    )
    table_round = narrow(table_all)
    grad_mod = jnp.einsum(
        "bd,bsic->dsic", silu_cond, table_round, preferred_element_type=jnp.float32
    )
    grad_bias = jnp.concatenate([jnp.sum(table_all, axis=0), jnp.sum(bias_all, axis=0)], axis=1)
    grad_silu = column_total(
        jnp.einsum("bsic,dsic->bd", table_round, mod_round, preferred_element_type=jnp.float32)
    )
    sigmoid_cond = jax.nn.sigmoid(cond)
    grad_cond = grad_silu * sigmoid_cond * (1.0 + cond * (1.0 - sigmoid_cond))
    grad_qkv, grad_proj, grad_up, grad_down = (
        lax.psum_scatter(grad_qkv, "rows", scatter_dimension=0, tiled=True),
        lax.psum_scatter(grad_proj, "rows", scatter_dimension=0, tiled=True),
        lax.psum_scatter(grad_up, "rows", scatter_dimension=0, tiled=True),
        lax.psum_scatter(grad_down, "rows", scatter_dimension=0, tiled=True),
    )
    grad_proj = grad_proj[:, :, 0]
    next_mod, first_mod, second_mod = adam_step(w_mod, moments_mod, grad_mod)
    next_qkv, first_qkv, second_qkv = adam_step(w_qkv, moments_qkv, grad_qkv)
    next_proj, first_proj, second_proj = adam_step(w_proj, moments_proj, grad_proj)
    next_up, first_up, second_up = adam_step(w_up, moments_up, grad_up)
    next_down, first_down, second_down = adam_step(w_down, moments_down, grad_down)
    next_bias, first_bias, second_bias = adam_step(biases, moments_bias, grad_bias)
    return (
        output[:, :IMAGE_TOKENS],
        output[:, IMAGE_TOKENS:],
        grad_source[:, :IMAGE_TOKENS],
        grad_source[:, IMAGE_TOKENS:],
        grad_cond,
        grad_mod,
        grad_qkv,
        grad_proj,
        grad_up,
        grad_down,
        grad_bias,
        next_mod,
        next_qkv,
        next_proj,
        next_up,
        next_down,
        next_bias,
        first_mod,
        second_mod,
        jnp.stack([first_qkv, second_qkv]),
        jnp.stack([first_proj, second_proj]),
        jnp.stack([first_up, second_up]),
        jnp.stack([first_down, second_down]),
        first_bias,
        second_bias,
    )


def solution(mesh):
    in_specs = (
        P("rows", None, "cols"),
        P("rows", None, "cols"),
        P(None, "rows"),
        P("rows", None, "cols"),
        P("rows", None, "cols"),
        P("rows", None, None, "cols"),
        P("rows", None, None, "cols"),
        P("rows", None, "cols"),
        P("rows", None, None, "cols"),
        P("rows", None, None, "cols"),
        P(None, None, "cols"),
        P(None, "rows", None, None, "cols"),
        P(None, "rows", None, None, "cols"),
        P(None, "rows", None, "cols"),
        P(None, "rows", None, None, "cols"),
        P(None, "rows", None, None, "cols"),
        P(None, None, None, "cols"),
    )
    out_specs = (
        P("rows", None, "cols"),
        P("rows", None, "cols"),
        P("rows", None, "cols"),
        P("rows", None, "cols"),
        P(None, "rows"),
        P("rows", None, None, "cols"),
        P("rows", None, None, "cols"),
        P("rows", None, "cols"),
        P("rows", None, None, "cols"),
        P("rows", None, None, "cols"),
        P(None, None, "cols"),
        P("rows", None, None, "cols"),
        P("rows", None, None, "cols"),
        P("rows", None, "cols"),
        P("rows", None, None, "cols"),
        P("rows", None, None, "cols"),
        P(None, None, "cols"),
        P("rows", None, None, "cols"),
        P("rows", None, None, "cols"),
        P(None, "rows", None, None, "cols"),
        P(None, "rows", None, "cols"),
        P(None, "rows", None, None, "cols"),
        P(None, "rows", None, None, "cols"),
        P(None, None, "cols"),
        P(None, None, "cols"),
    )
    return jax.shard_map(shards, mesh=mesh, in_specs=in_specs, out_specs=out_specs, check_vma=False)
```

profile of v0, /device:TPU:0, one launch (start us, length us, event | category | flops | bytes accessed | tf_op | source)
XLA Modules:
  0.0 1995.7 jit_solution(12832509543996830996)
XLA Ops:
  14.0 13.0 all-reduce.4
  27.1 58.4 %all-reduce.7.cloned.1.call-done = f32[8,2,6,384]{3,1,2,0:T(2,128)} async-done(((f32[8,2,6,384]{3,1,2,0:T(2,128)}), f32[8,2,6,384]{3,1,2,0:T(2,128)}) %all-reduce.7.cloned.1.call-update) | async-done | bytes 147472
  93.0 28.3 %all-gather.11.cloned.1.call-done = bf16[1,1178,1536]{2,1,0:T(8,128)(2,1)} async-done(((bf16[1,1178,384]{2,1,0:T(8,128)(2,1)}), bf16[1,1178,1536]{2,1,0:T(8,128)(2,1)}) %all-gather.11.cloned.1.call-update) | async-done | bytes 3618832 | tf_op jit(solution)/shard_map/all_gather | solution.py:88
  121.3 111.8 %all-gather.13.cloned.1.call-done = bf16[1536,2,3,384]{3,0,2,1:T(8,128)(2,1)} async-done(((bf16[192,2,3,384]{3,0,2,1:T(8,128)(2,1)}), bf16[1536,2,3,384]{3,0,2,1:T(8,128)(2,1)}) %all-gather.13.cloned.1.call-update) | async-done | bytes 7077904 | tf_op jit(solution)/shard_map/all_gather | solution.py:299
  237.1 8.0 fusion.41
  246.3 5.0 fusion.13
  258.1 24.7 %while.36 = (s32[]{:T(128)}, bf16[1,1178,384]{1,2,0:T(8,128)(2,1)S(1)}, f32[3,1,2,1178,1]{3,2,4,1,0:T(2,128)}, bf16[1,1178,384]{1,2,0:T(8,128)(2,1)}, bf16[1,117...) while((s32[]{:T(128)}, ...), condition=%wide.region_8.9_spmd, body=%wide.region_5.8_spmd.sunk | while | flops 727294848 | bytes 37051836 | solution.py:197
  302.2 55.1 %reduce-scatter.9.cloned.1.call-done = f32[1,1178,384]{2,1,0:T(8,128)} async-done(((f32[1,1178,1536]{2,1,0:T(8,128)}), f32[1,1178,384]{2,1,0:T(8,128)}) %reduce-scatter.9.cloned.1.call-update) | async-done | bytes 1809424 | tf_op jit(solution)/shard_map/reduce_scatter | solution.py:92
  361.4 10.6 all-reduce.3
  376.3 14.4 all-gather.21.cloned.1.call-done
  390.7 140.9 %all-gather.19.cloned.1.call-done = bf16[1536,2,4,384]{3,0,2,1:T(8,128)(2,1)} async-done(((bf16[192,2,4,384]{3,0,2,1:T(8,128)(2,1)}), bf16[1536,2,4,384]{3,0,2,1:T(8,128)(2,1)}) %all-gather.19.cloned.1.call-update) | async-done | bytes 9437200 | tf_op jit(solution)/shard_map/all_gather | solution.py:302
  536.1 9.3 fusion.28
  545.4 125.3 %all-gather.17.cloned.1.call-done = bf16[1536,2,4,384]{3,0,2,1:T(8,128)(2,1)} async-done(((bf16[192,2,4,384]{3,0,2,1:T(8,128)(2,1)}), bf16[1536,2,4,384]{3,0,2,1:T(8,128)(2,1)}) %all-gather.17.cloned.1.call-update) | async-done | bytes 9437200 | tf_op jit(solution)/shard_map/all_gather | solution.py:301
  670.6 31.6 %all-gather.15.cloned.1.call-done = bf16[1,1178,1536]{2,1,0:T(8,128)(2,1)} async-done(((bf16[1,1178,384]{2,1,0:T(8,128)(2,1)}), bf16[1,1178,1536]{2,1,0:T(8,128)(2,1)}) %all-gather.15.cloned.1.call-update) | async-done | bytes 3618832 | tf_op jit(solution)/shard_map/all_gather | solution.py:88
  705.8 9.8 fusion.29
  716.9 12.2 fusion.117
  733.5 7.0 convolution_bitcast_fusion.8
  748.5 7.7 convolution_bitcast_fusion.7
  759.8 49.3 %reduce-scatter.11.cloned.1.call-done = f32[1,1178,384]{2,1,0:T(8,128)} async-done(((f32[1,1178,1536]{2,1,0:T(8,128)}), f32[1,1178,384]{2,1,0:T(8,128)}) %reduce-scatter.11.cloned.1.call-update) | async-done | bytes 1809424 | tf_op jit(solution)/shard_map/reduce_scatter | solution.py:92
  809.2 67.8 %reduce-scatter.13.cloned.1.call-done = f32[1,1178,384]{2,1,0:T(8,128)} async-done(((f32[1,1178,1536]{2,1,0:T(8,128)}), f32[1,1178,384]{2,1,0:T(8,128)}) %reduce-scatter.13.cloned.1.call-update) | async-done | bytes 1809424 | tf_op jit(solution)/shard_map/reduce_scatter | solution.py:92
  878.4 5.9 convert_multiply_fusion.1
  884.3 10.7 all-reduce.2
  895.8 4.7 fusion.54
  902.7 32.4 %all-gather.23.cloned.1.call-done = bf16[1,1178,1536]{2,1,0:T(8,128)(2,1)} async-done(((bf16[1,1178,384]{2,1,0:T(8,128)(2,1)}), bf16[1,1178,1536]{2,1,0:T(8,128)(2,1)}) %all-gather.23.cloned.1.call-update) | async-done | bytes 3618832 | tf_op jit(solution)/shard_map/all_gather | solution.py:88
  954.7 65.2 %while.37 = (s32[]{:T(128)}, f32[1,1178,384]{1,2,0:T(8,128)}, bf16[1,1178,384]{2,1,0:T(8,128)(2,1)}, f32[1,1178,384]{1,2,0:T(8,128)}, bf16[1,1178,384]{1,2,0:T(8...) while((s32[]{:T(128)}, f32[1,1178,384]{1,2,0:T(8,128)}, ...), condition=%wide.region_22.23_spmd, body=%wide.region_20.22_spmd.sunk | while | flops 1798888448 | bytes 100905440 | solution.py:248
  1042.0 5.1 convolution_bitcast_fusion.1
  1047.2 8.8 pad_maximum_fusion
  1059.5 5.1 convolution_bitcast_fusion
  1064.6 6.9 pad_maximum_fusion.1
  1071.6 5.3 convolution_bitcast_fusion.4
  1077.0 6.5 convolution_bitcast_fusion.5
  1083.5 11.1 pad_maximum_fusion.2
  1097.9 5.2 fusion.123
  1103.1 5.4 fusion.122
  1111.6 8.6 fusion.120
  1127.4 33.2 %all-gather.1 = f32[16,8,384]{2,1,0:T(8,128)S(1)} all-gather(f32[2,8,384]{2,1,0:T(8,128)S(1)} %concatenate.254), channel_id=3, replica_groups=mesh['rows'=8,'cols'=4] {'rows'}, dimensions={0}, use_global_device_ids=true | all-gather | bytes 221184 | tf_op jit(solution)/shard_map/all_gather | solution.py:365
  1172.9 32.3 %all_gather.38 = f32[8,2,6,384]{3,1,2,0:T(2,128)S(1)} all-gather(f32[1,2,6,384]{3,1,2,0:T(2,128)S(1)} %constant_dynamic-update-slice_fusion.4), channel_id=1, replica_groups=mesh['rows'=8,'cols'=4] {'rows'}, dimensions={0}, use_global_device_ids=true | all-gather | bytes 165888 | tf_op jit(solution)/shard_map/all_gather | solution.py:364
  1206.4 11.1 all-reduce.1
  1223.6 5.1 multiply_subtract_fusion
  1228.7 4.5 copy.357
  1237.1 6.5 copy.363
  1255.3 170.8 %reduce-scatter.21.cloned.1.call-done = f32[192,2,4,384]{3,0,2,1:T(8,128)} async-done(((f32[1536,2,4,384]{3,0,2,1:T(8,128)}), f32[192,2,4,384]{3,0,2,1:T(8,128)}) %reduce-scatter.21.cloned.1.call-update) | async-done | bytes 2359312 | tf_op jit(solution)/shard_map/reduce_scatter | solution.py:380
  1426.0 5.4 fusion.85
  1434.4 308.3 %reduce-scatter.23.cloned.1.call-done = f32[192,2,4,384]{3,0,2,1:T(8,128)} async-done(((f32[1536,2,4,384]{3,0,2,1:T(8,128)}), f32[192,2,4,384]{3,0,2,1:T(8,128)}) %reduce-scatter.23.cloned.1.call-update) | async-done | bytes 2359312 | tf_op jit(solution)/shard_map/reduce_scatter | solution.py:381
  1750.3 5.2 copy.373
  1756.0 5.2 copy.374
  1767.0 208.0 %reduce-scatter.17.cloned.1.call-done = f32[192,2,3,384]{3,0,2,1:T(8,128)} async-done(((f32[1536,2,3,384]{3,0,2,1:T(8,128)}), f32[192,2,3,384]{3,0,2,1:T(8,128)}) %reduce-scatter.17.cloned.1.call-update) | async-done | bytes 1769488 | tf_op jit(solution)/shard_map/reduce_scatter | solution.py:378
  1981.6 4.5 copy.371
  (511 shorter events, 291.1 us)
Async XLA Ops:
  7.2 78.3 %all-reduce.7.cloned.1.call-start = ((), (), s32[]{:S(2)}) async-start(), calls=%async_computation.24 | async-start | bytes 294912
  11.7 73.8 %copy-start.78 = (f32[2,14,384]{2,0,1:T(2,128)S(1)}, f32[2,14,384]{2,0,1:T(2,128)}, u32[]{:S(2)}) copy-start(f32[2,14,384]{2,0,1:T(2,128)} %param.31) | copy-start | bytes 129028
  12.8 108.4 %all-gather.11.cloned.1.call-start = ((), (), s32[]{:S(2)}) async-start(), calls=%async_computation.8 | async-start | bytes 4546560 | tf_op jit(solution)/shard_map/all_gather | solution.py:88
  27.0 63.7 %copy-start.76 = (f32[1178]{0:T(1024)}, f32[1178]{0:T(1024)S(1)}, u32[]{:S(2)}) copy-start(f32[1178]{0:T(1024)S(1)} %get-tuple-element.750) | copy-start | bytes 14140
  27.1 63.7 %copy-start.79 = (f32[1178]{0:T(1024)}, f32[1178]{0:T(1024)S(1)}, u32[]{:S(2)}) copy-start(f32[1178]{0:T(1024)S(1)} %add_rsqrt_fusion.1) | copy-start | bytes 14140
  90.8 142.3 %all-gather.13.cloned.1.call-start = ((), (), s32[]{:S(2)}) async-start(), calls=%async_computation.9 | async-start | bytes 7962624 | tf_op jit(solution)/shard_map/all_gather | solution.py:299
  91.9 194.2 %all-gather.25.cloned.1.call-start = ((), (), s32[]{:S(2)}) async-start(), calls=%async_computation.23 | async-start | bytes 2654208 | tf_op jit(solution)/shard_map/all_gather | solution.py:300
  92.7 264.6 %reduce-scatter.9.cloned.1.call-start = ((), (), s32[]{:S(2)}) async-start(), calls=%async_computation.10 | async-start | bytes 9093120 | tf_op jit(solution)/shard_map/reduce_scatter | solution.py:92
  282.8 7.1 copy-start.67
  293.6 97.1 %all-gather.21.cloned.1.call-start = ((), (), s32[]{:S(2)}) async-start(), calls=%async_computation.15 | async-start | bytes 4546560 | tf_op jit(solution)/shard_map/all_gather | solution.py:88
  296.6 235.0 %all-gather.19.cloned.1.call-start = ((), (), s32[]{:S(2)}) async-start(), calls=%async_computation.13 | async-start | bytes 10616832 | tf_op jit(solution)/shard_map/all_gather | solution.py:302
  300.6 370.0 %all-gather.17.cloned.1.call-start = ((), (), s32[]{:S(2)}) async-start(), calls=%async_computation.12 | async-start | bytes 10616832 | tf_op jit(solution)/shard_map/all_gather | solution.py:301
  302.1 400.2 %all-gather.15.cloned.1.call-start = ((), (), s32[]{:S(2)}) async-start(), calls=%async_computation.11 | async-start | bytes 4546560 | tf_op jit(solution)/shard_map/all_gather | solution.py:88
  375.4 433.8 %reduce-scatter.11.cloned.1.call-start = ((), (), s32[]{:S(2)}) async-start(), calls=%async_computation.14 | async-start | bytes 9093120 | tf_op jit(solution)/shard_map/reduce_scatter | solution.py:92
  702.3 13.9 slice-start.2
  705.8 10.3 slice-start.3
  744.0 133.1 %reduce-scatter.13.cloned.1.call-start = ((), (), s32[]{:S(2)}) async-start(), calls=%async_computation.16 | async-start | bytes 9093120 | tf_op jit(solution)/shard_map/reduce_scatter | solution.py:92
  759.8 117.4 %copy-start.70 = (bf16[1,154,384]{2,1,0:T(8,128)(2,1)S(1)}, bf16[1,154,384]{2,1,0:T(8,128)(2,1)}, u32[]{:S(2)}) copy-start(bf16[1,154,384]{2,1,0:T(8,128)(2,1)} %param.25) | copy-start | bytes 354820
  759.8 175.4 %all-gather.23.cloned.1.call-start = ((), (), s32[]{:S(2)}) async-start(), calls=%async_computation.17 | async-start | bytes 4546560 | tf_op jit(solution)/shard_map/all_gather | solution.py:88
  895.7 4.8 copy-start.20
  895.8 4.8 copy-start.37
  895.8 4.8 copy-start.50
  895.8 4.8 copy-start.66
  900.6 34.6 %copy-start.68 = (bf16[1,1178,384]{1,2,0:T(8,128)(2,1)S(1)}, bf16[1,1178,384]{1,2,0:T(8,128)(2,1)}, u32[]{:S(2)}) copy-start(bf16[1,1178,384]{1,2,0:T(8,128)(2,1)} %copy-done.67) | copy-start | bytes 2714116
  902.7 258.5 %reduce-scatter.19.cloned.1.call-start = ((), (), s32[]{:S(2)}) async-start(), calls=%async_computation.20 | async-start | bytes 5308416 | tf_op jit(solution)/shard_map/reduce_scatter | solution.py:379
  943.1 225.7 %reduce-scatter.15.cloned.1.call-start = ((), (), s32[]{:S(2)}) async-start(), calls=%async_computation.18 | async-start | bytes 9093120 | tf_op jit(solution)/shard_map/reduce_scatter | solution.py:92
  1025.4 5.2 copy-start.89
  1025.8 4.5 copy-start.60
  1038.4 387.7 %reduce-scatter.21.cloned.1.call-start = ((), (), s32[]{:S(2)}) async-start(), calls=%async_computation.21 | async-start | bytes 21233664 | tf_op jit(solution)/shard_map/reduce_scatter | solution.py:380
  1056.0 686.7 %reduce-scatter.23.cloned.1.call-start = ((), (), s32[]{:S(2)}) async-start(), calls=%async_computation.22 | async-start | bytes 21233664 | tf_op jit(solution)/shard_map/reduce_scatter | solution.py:381
  1071.6 903.5 %reduce-scatter.17.cloned.1.call-start = ((), (), s32[]{:S(2)}) async-start(), calls=%async_computation.19 | async-start | bytes 15925248 | tf_op jit(solution)/shard_map/reduce_scatter | solution.py:378
  1071.6 5.4 copy-start.61
  1071.6 5.4 copy-start.83
  1097.9 10.7 slice-start.4
  1103.1 5.4 slice-start.5
  1108.5 11.6 slice-start
  1111.6 8.6 slice-start.1
  1126.4 37.3 %copy-start.63 = (f32[192,2,384]{2,1,0:T(2,128)S(1)}, f32[192,2,384]{2,1,0:T(2,128)}, u32[]{:S(2)}) copy-start(f32[192,2,384]{2,1,0:T(2,128)} %param.28) | copy-start | bytes 1769476
  1172.3 33.6 %copy-start.17 = (bf16[192,2,6,384]{3,1,2,0:T(2,128)(2,1)S(1)}, bf16[192,2,6,384]{3,1,2,0:T(2,128)(2,1)}, u32[]{:S(2)}) copy-start(bf16[192,2,6,384]{3,1,2,0:T(2,128)(2,1)} %copy-done.16) | copy-start | bytes 5308420
  1217.5 5.5 copy-start.55
  1217.5 5.5 copy-start.57
  1244.3 4.5 copy-start.56
  1248.8 177.2 %copy-start.22 = (f32[192,2,4,384]{3,2,1,0:T(4,128)S(1)}, f32[192,2,4,384]{3,2,1,0:T(4,128)}, u32[]{:S(2)}) copy-start(f32[192,2,4,384]{3,2,1,0:T(4,128)} %param.29) | copy-start | bytes 7077892
  1431.5 311.2 %copy-start.23 = (f32[192,2,4,384]{3,2,1,0:T(4,128)S(1)}, f32[192,2,4,384]{3,2,1,0:T(4,128)}, u32[]{:S(2)}) copy-start(f32[192,2,4,384]{3,2,1,0:T(4,128)} %param.30) | copy-start | bytes 7077892
  1756.0 5.2 copy-start.24
  1764.1 211.0 %copy-start.39 = (f32[1,192,2,3,384]{4,2,3,1,0:T(2,128)S(1)}, f32[1,192,2,3,384]{4,2,3,1,0:T(2,128)}, u32[]{:S(2)}) copy-start(f32[1,192,2,3,384]{4,2,3,1,0:T(2,128)} %get-tuple-element.710) | copy-start | bytes 5308420
  1764.1 211.0 %copy-start.40 = (f32[1,192,2,3,384]{4,2,3,1,0:T(2,128)S(1)}, f32[1,192,2,3,384]{4,2,3,1,0:T(2,128)}, u32[]{:S(2)}) copy-start(f32[1,192,2,3,384]{4,2,3,1,0:T(2,128)} %get-tuple-element.711) | copy-start | bytes 5308420
  1981.6 4.5 copy-start.41
  (76 other events, 179.1 us)
Sparse Core Ops, SparseCore 0:
  12.9 72.5 all-reduce.6
  90.9 30.3 all-gather.10
  124.3 108.7 all-gather.12
  236.0 50.1 all-gather.24
  293.7 63.5 reduce-scatter.8
  359.3 31.3 all-gather.20
  393.5 138.0 all-gather.18
  534.3 136.2 all-gather.16
  672.8 29.4 all-gather.14
  744.1 65.0 reduce-scatter.10
  811.9 65.0 reduce-scatter.12
  902.8 32.2 all-gather.22
  943.2 95.2 reduce-scatter.18
  1040.9 64.8 reduce-scatter.14
  1110.0 316.0 reduce-scatter.20
  1430.3 312.4 reduce-scatter.22
  1746.7 228.3 reduce-scatter.16
where the time goes:
time: 2000 us
  waiting for transfers between devices  1410 us (70%)
  matrix products  165 us (8%)
  local copies, waits for them, and re-layouts  164 us (8%)
  other arithmetic  131 us (7%)
  blocking collectives  111 us (6%)
    reduce_scatter x1, waiting for transfers between devices, shards(): lax.psum_scatter(grad_down, 'rows', scatter_dimension=0, tiled=True)  308 us
    reduce_scatter x1, waiting for transfers between devices, shards(): lax.psum_scatter(grad_qkv, 'rows', scatter_dimension=0, tiled=True)  208 us
    reduce_scatter x4, waiting for transfers between devices, scatter_width(): lax.psum_scatter(partial_value, 'cols', scatter_dimension=2, tiled=True)  172 us
    reduce_scatter x1, waiting for transfers between devices, shards(): lax.psum_scatter(grad_up, 'rows', scatter_dimension=0, tiled=True)  171 us
    all_gather x1, waiting for transfers between devices, shards(): lax.all_gather(local_weights[3], 'rows', axis=0, tiled=True)  141 us
    all_gather x1, waiting for transfers between devices, shards(): lax.all_gather(local_weights[2], 'rows', axis=0, tiled=True)  125 us
    all_gather x1, waiting for transfers between devices, shards(): lax.all_gather(local_weights[0], 'rows', axis=0, tiled=True)  112 us
    all_gather x4, waiting for transfers between devices, gather_width(): return lax.all_gather(values, 'cols', axis=2, tiled=True)  107 us
  transfers between devices with their start and end apart: 17, of which 15 were waited for; matrix products, arithmetic and copies ran while one was open for 18% of the time, Pallas kernels for 0%

commit v1 on v0

v1 whole, which is shorter than its diff:
```python
import jax
import jax.numpy as jnp
from jax import lax
from jax.experimental import pallas as pl
from jax.experimental.pallas import tpu as pltpu
from jax.sharding import PartitionSpec as P

D = 1536
HEAD_FEATURES = 64
IMAGE_TOKENS = 1024
TXT = 154
STEP = 2


BETA_ONE = 0.9
BETA_TWO = 0.95
LEARN_RATE = 0.02
DECAY_RATE = 0.1
ADAM_EPS = 1e-08
NORM_EPS = 1e-06
GELU_COEF = 0.7978845608028654
GELU_CUBE = 0.044715
PADDED = IMAGE_TOKENS + (TXT + 15) // 16 * 16
TOKENS = IMAGE_TOKENS + TXT
STREAM_ROWS = ((0, 0, IMAGE_TOKENS), (1, IMAGE_TOKENS, PADDED))
PAIR = 2 * HEAD_FEATURES
VMEM_BYTES = 56 * 1024 * 1024
F32 = jnp.float32
BF16 = jnp.bfloat16


def narrow(values):
    return values.astype(jnp.bfloat16)


def gelu_value(inputs):
    return (
        0.5 * inputs * (1.0 + jnp.tanh(GELU_COEF * (inputs + GELU_CUBE * inputs * inputs * inputs)))
    )


def gelu_slope(inputs):
    tangent = jnp.tanh(GELU_COEF * (inputs + GELU_CUBE * inputs * inputs * inputs))
    return 0.5 * (1.0 + tangent) + 0.5 * inputs * (1.0 - tangent * tangent) * GELU_COEF * (
        1.0 + 3.0 * GELU_CUBE * inputs * inputs
    )


def adam_step(param, moments, gradient):
    first_moment = BETA_ONE * moments[0] + (1.0 - BETA_ONE) * gradient
    second_moment = BETA_TWO * moments[1] + (1.0 - BETA_TWO) * gradient * gradient
    update = (
        first_moment
        / (1.0 - BETA_ONE**STEP)
        / (jnp.sqrt(second_moment / (1.0 - BETA_TWO**STEP)) + ADAM_EPS)
    )
    return (param - LEARN_RATE * (update + DECAY_RATE * param), first_moment, second_moment)


def kernel_params():
    return pltpu.CompilerParams(vmem_limit_bytes=VMEM_BYTES)


def cost(flops, nbytes, transcendentals=0):
    return pl.CostEstimate(flops=flops, bytes_accessed=nbytes, transcendentals=transcendentals)


def whole(shape):
    return pl.BlockSpec(shape, lambda j: (0,) * len(shape))


def matmul_rows(acts, weight, epilogue, extras, extra_specs, out_types, out_specs, tile=384):
    rows, depth = acts.shape
    width = weight.shape[2]
    tile = min(tile, width)

    def kernel(acts_ref, weight_ref, *refs):
        for stream, low, high in STREAM_ROWS:
            product = jnp.dot(
                acts_ref[low:high], weight_ref[stream], preferred_element_type=F32
            )
            epilogue(product, stream, low, high, *refs)

    return pl.pallas_call(
        kernel,
        grid=(width // tile,),
        in_specs=[
            whole((rows, depth)),
            pl.BlockSpec((2, depth, tile), lambda j: (0, 0, j)),
            *extra_specs,
        ],
        out_specs=out_specs,
        out_shape=out_types,
        compiler_params=kernel_params(),
        cost_estimate=cost(
            2 * rows * depth * width, 2 * (rows * depth + 2 * depth * width + rows * width)
        ),
    )(acts, weight, *extras)


def column_spec(leading, tile=384):
    return pl.BlockSpec((leading, tile), lambda j: (0, j))


def project_triple(acts, weight, bias):
    def epilogue(product, stream, low, high, bias_ref, out_ref):
        out_ref[low:high] = (product + bias_ref[stream : stream + 1]).astype(BF16)

    rows, width = (acts.shape[0], weight.shape[2])
    return matmul_rows(
        acts,
        weight,
        epilogue,
        [bias],
        [column_spec(2)],
        jax.ShapeDtypeStruct((rows, width), BF16),
        column_spec(rows),
    )


def raise_hidden(acts, weight, bias):
    def epilogue(product, stream, low, high, bias_ref, act_ref, slope_ref):
        inputs = product + bias_ref[stream : stream + 1]
        square = inputs * inputs
        tangent = jnp.tanh(GELU_COEF * inputs * (1.0 + GELU_CUBE * square))
        act_ref[low:high] = (0.5 * inputs * (1.0 + tangent)).astype(BF16)
        slope_ref[low:high] = 0.5 * (1.0 + tangent) + 0.5 * inputs * (
            1.0 - tangent * tangent
        ) * GELU_COEF * (1.0 + 3.0 * GELU_CUBE * square)

    rows, width = (acts.shape[0], weight.shape[2])
    return matmul_rows(
        acts,
        weight,
        epilogue,
        [bias],
        [column_spec(2)],
        [jax.ShapeDtypeStruct((rows, width), BF16), jax.ShapeDtypeStruct((rows, width), F32)],
        [column_spec(rows), column_spec(rows)],
    )


def hidden_gradient(acts, weight, slope):
    def epilogue(product, stream, low, high, slope_ref, out_ref, sum_ref):
        gradient = product * slope_ref[low:high]
        out_ref[low:high] = gradient.astype(BF16)
        sum_ref[stream : stream + 1] = jnp.sum(gradient, axis=0, keepdims=True)

    rows, width = (acts.shape[0], weight.shape[2])
    return matmul_rows(
        acts,
        weight,
        epilogue,
        [slope],
        [column_spec(rows)],
        [jax.ShapeDtypeStruct((rows, width), BF16), jax.ShapeDtypeStruct((2, width), F32)],
        [column_spec(rows), column_spec(2)],
    )


def attended_gradient(acts, weight):
    def epilogue(product, stream, low, high, out_ref):
        out_ref[low:high] = product.astype(BF16)

    rows, width = (acts.shape[0], weight.shape[2])
    return matmul_rows(
        acts,
        weight,
        epilogue,
        [],
        [],
        jax.ShapeDtypeStruct((rows, width), BF16),
        column_spec(rows),
    )


def matmul_back(acts, weight, parity):
    rows, depth = acts.shape
    tile = weight.shape[1] // 4

    def kernel(acts_ref, weight_ref, out_ref):
        for stream, low, high in STREAM_ROWS:
            out_ref[low:high] = lax.dot_general(
                acts_ref[low:high],
                weight_ref[stream],
                (((1,), (1,)), ((), ())),
                preferred_element_type=F32,
            ).astype(BF16)

    return pl.pallas_call(
        kernel,
        grid=(2,),
        in_specs=[
            whole((rows, depth)),
            pl.BlockSpec((2, tile, depth), lambda j: (0, 2 * j + parity, 0)),
        ],
        out_specs=column_spec(rows, tile),
        out_shape=jax.ShapeDtypeStruct((rows, 2 * tile), BF16),
        compiler_params=kernel_params(),
        cost_estimate=cost(
            4 * rows * depth * tile, 2 * (rows * depth + 4 * depth * tile + 2 * rows * tile)
        ),
    )(acts, weight)


def weight_gradient(outer, inner, tile=384):
    rows, height = outer.shape
    width = inner.shape[1]

    def kernel(outer_ref, inner_ref, out_ref):
        for stream, low, high in STREAM_ROWS:
            out_ref[stream] = lax.dot_general(
                outer_ref[low:high],
                inner_ref[low:high],
                (((0,), (0,)), ((), ())),
                preferred_element_type=F32,
            ).astype(BF16)

    return pl.pallas_call(
        kernel,
        grid=(height // tile,),
        in_specs=[column_spec(rows, tile), whole((rows, width))],
        out_specs=pl.BlockSpec((2, tile, width), lambda j: (0, j, 0)),
        out_shape=jax.ShapeDtypeStruct((2, height, width), BF16),
        compiler_params=kernel_params(),
        cost_estimate=cost(
            2 * rows * height * width, 2 * (rows * height + rows * width + 2 * height * width)
        ),
    )(outer, inner)


def row_chunks(rows, size=256):
    return [(low, min(low + size, rows)) for low in range(0, rows, size)]


def attention(triple):
    rows, width = triple.shape
    pairs = width // (3 * PAIR)
    scale = HEAD_FEATURES ** (-0.5)

    def kernel(triple_ref, out_ref, total_ref):
        lane = lax.broadcasted_iota(jnp.int32, (1, PAIR), 1) // HEAD_FEATURES
        feature = lax.broadcasted_iota(jnp.int32, (PAIR, 1), 0) // HEAD_FEATURES
        key_index = lax.broadcasted_iota(jnp.int32, (rows, 1), 0)
        keys = triple_ref[:, PAIR : 2 * PAIR]
        values_turned = triple_ref[:, 2 * PAIR : 3 * PAIR].T
        for low, high in row_chunks(rows):
            queries = triple_ref[low:high, 0:PAIR] * jnp.asarray(scale, BF16)
            mixed = []
            for head in range(2):
                own = jnp.where(lane == head, queries, jnp.zeros_like(queries))
                scores = lax.dot_general(
                    keys, own, (((1,), (1,)), ((), ())), preferred_element_type=F32
                )
                scores = jnp.where(key_index < TOKENS, scores, -1e30)
                highest = jnp.max(scores, axis=0, keepdims=True)
                weights = jnp.exp(scores - highest)
                total = jnp.sum(weights, axis=0, keepdims=True)
                total_ref[0, head : head + 1, low:high] = highest + jnp.log(total)
                mixed.append(
                    jnp.dot(values_turned, weights.astype(BF16), preferred_element_type=F32)
                    / total
                )
            out_ref[low:high] = jnp.where(feature == 0, mixed[0], mixed[1]).T.astype(BF16)

    return pl.pallas_call(
        kernel,
        grid=(pairs,),
        in_specs=[pl.BlockSpec((rows, 3 * PAIR), lambda p: (0, p))],
        out_specs=[
            pl.BlockSpec((rows, PAIR), lambda p: (0, p)),
            pl.BlockSpec((1, 2, rows), lambda p: (p, 0, 0)),
        ],
        out_shape=[
            jax.ShapeDtypeStruct((rows, pairs * PAIR), BF16),
            jax.ShapeDtypeStruct((pairs, 2, rows), F32),
        ],
        compiler_params=kernel_params(),
        cost_estimate=cost(
            16 * pairs * PAIR * rows * rows, 8 * rows * width, 2 * pairs * rows * rows
        ),
    )(triple)


def attention_back(triple, totals, grad_mix):
    rows, width = triple.shape
    pairs = width // (3 * PAIR)
    scale = HEAD_FEATURES ** (-0.5)

    def kernel(triple_ref, total_ref, grad_ref, out_ref, sum_ref, key_acc, value_acc):
        lane = lax.broadcasted_iota(jnp.int32, (1, PAIR), 1) // HEAD_FEATURES
        feature = lax.broadcasted_iota(jnp.int32, (PAIR, 1), 0) // HEAD_FEATURES
        key_index = lax.broadcasted_iota(jnp.int32, (rows, 1), 0)
        keys = triple_ref[:, PAIR : 2 * PAIR]
        values = triple_ref[:, 2 * PAIR : 3 * PAIR]
        keys_turned = keys.T
        query_sums = [jnp.zeros((1, PAIR), F32), jnp.zeros((1, PAIR), F32)]
        for step, (low, high) in enumerate(row_chunks(rows)):
            queries = triple_ref[low:high, 0:PAIR] * jnp.asarray(scale, BF16)
            grads = grad_ref[low:high]
            turned = []
            for head in range(2):
                own = jnp.where(lane == head, queries, jnp.zeros_like(queries))
                own_grad = jnp.where(lane == head, grads, jnp.zeros_like(grads))
                scores = lax.dot_general(
                    keys, own, (((1,), (1,)), ((), ())), preferred_element_type=F32
                )
                soft = jnp.exp(scores - total_ref[0, head : head + 1, low:high])
                soft = jnp.where(key_index < TOKENS, soft, 0.0)
                grad_soft = lax.dot_general(
                    values, own_grad, (((1,), (1,)), ((), ())), preferred_element_type=F32
                )
                delta = jnp.sum(soft * grad_soft, axis=0, keepdims=True)
                score_round = (soft * (grad_soft - delta)).astype(BF16)
                turned.append(jnp.dot(keys_turned, score_round, preferred_element_type=F32))
                key_part = jnp.dot(score_round, own, preferred_element_type=F32)
                value_part = jnp.dot(soft.astype(BF16), own_grad, preferred_element_type=F32)
                if step == 0 and head == 0:
                    key_acc[...] = key_part
                    value_acc[...] = value_part
                else:
                    key_acc[...] += key_part
                    value_acc[...] += value_part
            grad_query = (jnp.where(feature == 0, turned[0], turned[1]) * scale).T
            out_ref[low:high, 0:PAIR] = grad_query.astype(BF16)
            stream = 0 if high <= IMAGE_TOKENS else 1
            query_sums[stream] += jnp.sum(grad_query, axis=0, keepdims=True)
        out_ref[:, PAIR : 2 * PAIR] = key_acc[...].astype(BF16)
        out_ref[:, 2 * PAIR : 3 * PAIR] = value_acc[...].astype(BF16)
        for stream, low, high in STREAM_ROWS:
            sum_ref[0, stream : stream + 1, 0:PAIR] = query_sums[stream]
            sum_ref[0, stream : stream + 1, PAIR : 2 * PAIR] = jnp.sum(
                value_acc[low:high], axis=0, keepdims=True
            )

    return pl.pallas_call(
        kernel,
        grid=(pairs,),
        in_specs=[
            pl.BlockSpec((rows, 3 * PAIR), lambda p: (0, p)),
            pl.BlockSpec((1, 2, rows), lambda p: (p, 0, 0)),
            pl.BlockSpec((rows, PAIR), lambda p: (0, p)),
        ],
        out_specs=[
            pl.BlockSpec((rows, 3 * PAIR), lambda p: (0, p)),
            pl.BlockSpec((1, 2, 2 * PAIR), lambda p: (p, 0, 0)),
        ],
        out_shape=[
            jax.ShapeDtypeStruct((rows, width), BF16),
            jax.ShapeDtypeStruct((pairs, 2, 2 * PAIR), F32),
        ],
        scratch_shapes=[pltpu.VMEM((rows, PAIR), F32), pltpu.VMEM((rows, PAIR), F32)],
        compiler_params=kernel_params(),
        cost_estimate=cost(
            40 * pairs * PAIR * rows * rows, 8 * rows * width, 2 * pairs * rows * rows
        ),
    )(triple, totals, grad_mix)


def per_token(table):
    row = lax.broadcasted_iota(jnp.int32, (PADDED, 1), 0)
    return jnp.where(row < IMAGE_TOKENS, table[0][None], table[1][None])


def stream_sums(values):
    return jnp.stack([jnp.sum(values[low:high], axis=0) for _, low, high in STREAM_ROWS])


def row_stats(total, square):
    center = total / D
    return (center, lax.rsqrt(square / D - center * center + NORM_EPS))


def join_tokens(image, text):
    blank = jnp.zeros((PADDED - TOKENS, image.shape[2]), image.dtype)
    return jnp.concatenate([image[0], text[0], blank], axis=0)


def make_shards(row_count, col_count):
    order = list(range(0, row_count, 2)) + list(range(row_count - 1, 0, -2))
    place = [order.index(device) for device in range(row_count)]
    ahead = [(order[i], order[(i + 1) % row_count]) for i in range(row_count)]
    behind = [(target, sender) for sender, target in ahead]
    near = [(device, device ^ 1) for device in range(col_count)]
    far = [(device, device ^ 2) for device in range(col_count)]
    share = row_count // col_count
    long_way = row_count // 2
    short_way = row_count - 1 - long_way

    def near_swap(values):
        return lax.ppermute(values, "cols", near)

    def far_swap(values):
        return lax.ppermute(values, "cols", far)

    def column_total(parts):
        parts = parts + near_swap(parts)
        return parts + far_swap(parts)

    def gather_width(values):
        away = far_swap(values)
        return jnp.concatenate([values, near_swap(values), away, near_swap(away)], axis=-1)

    def expand_rows(acts, weight):
        leaving = matmul_back(acts, weight, 1)
        arrived = near_swap(leaving)
        kept = matmul_back(acts, weight, 0)
        total = kept.astype(F32) + arrived.astype(F32)
        half = total.shape[1] // 2
        away = far_swap(narrow(total[:, half:]))
        return total[:, :half] + away.astype(F32)

    def owner(offset):
        here = jnp.asarray(place, jnp.int32)[lax.axis_index("rows")]
        return jnp.asarray(order, jnp.int32)[(here + offset) % row_count]

    def slot(offset):
        row = owner(offset)
        return (row // share ^ lax.axis_index("cols")) * share + row % share

    def ring_gather(block, forward_long):
        height = block.shape[1]
        complete = jnp.zeros((2, row_count * height, block.shape[2]), block.dtype)

        def put(state, piece, offset):
            return lax.dynamic_update_slice(state, piece, (0, slot(offset) * height, 0))

        complete = put(complete, block, 0)
        forward_hops, back_hops = (
            (long_way, short_way) if forward_long else (short_way, long_way)
        )
        forward = back = block
        for hop in range(1, long_way + 1):
            if hop <= forward_hops:
                forward = lax.ppermute(forward, "rows", ahead)
                complete = put(complete, forward, -hop)
            if hop <= back_hops:
                back = lax.ppermute(back, "rows", behind)
                complete = put(complete, back, hop)
        return complete

    def ring_scatter(partial, forward_long):
        height = partial.shape[1] // row_count

        def take(offset):
            return lax.dynamic_slice(
                partial, (0, slot(offset) * height, 0), (2, height, partial.shape[2])
            )

        forward_hops, back_hops = (
            (long_way, short_way) if forward_long else (short_way, long_way)
        )
        forward = take(forward_hops)
        back = take(-back_hops)
        for hop in range(1, long_way + 1):
            if hop <= forward_hops:
                forward = lax.ppermute(forward, "rows", ahead).astype(F32)
                forward = forward + take(forward_hops - hop).astype(F32)
                if hop < forward_hops:
                    forward = narrow(forward)
            if hop <= back_hops:
                back = lax.ppermute(back, "rows", behind)
                if hop < back_hops:
                    back = narrow(back.astype(F32) + take(hop - back_hops).astype(F32))
        return forward + back.astype(F32)

    def shards(
        x_img,
        x_txt,
        cond,
        back_img,
        back_txt,
        w_mod,
        w_qkv,
        w_proj,
        w_up,
        w_down,
        biases,
        moments_mod,
        moments_qkv,
        moments_proj,
        moments_up,
        moments_down,
        moments_bias,
    ):
        local_rows = w_qkv.shape[0]
        width = w_qkv.shape[3]
        pairs = width // PAIR

        def stream_major(weight):
            return narrow(weight).swapaxes(0, 1).reshape(2, local_rows, -1)

        qkv_local = (
            narrow(w_qkv)
            .reshape(local_rows, 2, 3, pairs, PAIR)
            .transpose(1, 0, 3, 2, 4)
            .reshape(2, local_rows, 3 * width)
        )
        triple_weight = ring_gather(qkv_local, True)
        project_weight = ring_gather(stream_major(w_proj), False)
        raise_weight = ring_gather(stream_major(w_up), True)
        lower_weight = ring_gather(stream_major(w_down), False)

        silu_cond = narrow(jax.nn.silu(cond))
        mod_round = narrow(w_mod)
        mod_parts = lax.all_to_all(
            jnp.einsum("bd,dsic->bsic", silu_cond, mod_round, preferred_element_type=F32),
            "rows",
            0,
            0,
            tiled=True,
        )
        modulation = jnp.sum(mod_parts, axis=0) + biases[:, 0:6]
        modulation_full = gather_width(modulation)
        scale_one, gate_one, scale_two, gate_two = [
            per_token(modulation[:, slot_index]) for slot_index in (1, 2, 4, 5)
        ]
        shift_two = per_token(modulation[:, 3])

        source_round = join_tokens(x_img, x_txt)
        source = source_round.astype(F32)
        source_full = gather_width(source_round).astype(F32)
        center_one, inverse_one = row_stats(
            jnp.sum(source_full, axis=1, keepdims=True),
            jnp.sum(source_full * source_full, axis=1, keepdims=True),
        )
        unit_one = (source - center_one) * inverse_one
        normed_one = narrow(
            (source_full - center_one)
            * inverse_one
            * (1.0 + per_token(modulation_full[:, 1]))
            + per_token(modulation_full[:, 0])
        )
        cotangent_round = join_tokens(back_img, back_txt)
        cotangent = cotangent_round.astype(F32)
        lowered_full = narrow(
            gather_width(cotangent_round).astype(F32) * per_token(modulation_full[:, 5])
        )

        triple_bias = (
            jnp.stack([biases[:, 6], jnp.zeros_like(biases[:, 6]), biases[:, 7]], axis=1)
            .reshape(2, 3, pairs, PAIR)
            .swapaxes(1, 2)
            .reshape(2, 3 * width)
        )
        triple = project_triple(normed_one, triple_weight, triple_bias)
        attended, log_totals = attention(triple)
        projected = expand_rows(attended, project_weight) + per_token(biases[:, 8])
        residual = source + gate_one * projected
        totals_two = column_total(
            jnp.stack([jnp.sum(residual, axis=1), jnp.sum(residual * residual, axis=1)])
        )
        center_two, inverse_two = row_stats(totals_two[0][:, None], totals_two[1][:, None])
        unit_two = (residual - center_two) * inverse_two
        normed_two = gather_width(narrow(unit_two * (1.0 + scale_two) + shift_two))
        hidden_act, hidden_slope = raise_hidden(
            normed_two, raise_weight, biases[:, 9:13].reshape(2, 4 * width)
        )
        grad_down = ring_scatter(weight_gradient(lowered_full, hidden_act), True)
        lowered = expand_rows(hidden_act, lower_weight) + per_token(biases[:, 13])
        output = narrow(residual + gate_two * lowered)
        grad_lowered = gate_two * cotangent

        hidden_round, hidden_sums = hidden_gradient(lowered_full, lower_weight, hidden_slope)
        grad_up = ring_scatter(weight_gradient(normed_two, hidden_round), False)
        grad_normed_two = expand_rows(hidden_round, raise_weight)

        def normalize_back(grad_unit, unit_rows, inverse):
            totals = column_total(
                jnp.stack([jnp.sum(grad_unit, axis=1), jnp.sum(grad_unit * unit_rows, axis=1)])
            )
            return inverse * (
                grad_unit - totals[0][:, None] / D - unit_rows * (totals[1][:, None] / D)
            )

        grad_residual = cotangent + normalize_back(
            grad_normed_two * (1.0 + scale_two), unit_two, inverse_two
        )
        grad_projected = gate_one * grad_residual
        projected_full = gather_width(narrow(grad_projected))
        grad_proj = ring_scatter(weight_gradient(projected_full, attended), True)
        grad_attended = attended_gradient(projected_full, project_weight)
        triple_round, triple_sums = attention_back(triple, log_totals, grad_attended)
        grad_qkv = ring_scatter(weight_gradient(normed_one, triple_round), False)
        grad_normed_one = expand_rows(triple_round, triple_weight)
        grad_source = grad_residual + normalize_back(
            grad_normed_one * (1.0 + scale_one), unit_one, inverse_one
        )

        head_sums = triple_sums.reshape(pairs, 2, 2, PAIR).transpose(1, 2, 0, 3)
        part = jnp.concatenate(
            [
                stream_sums(grad_normed_one)[:, None],
                stream_sums(grad_normed_one * unit_one)[:, None],
                stream_sums(grad_residual * projected)[:, None],
                stream_sums(grad_normed_two)[:, None],
                stream_sums(grad_normed_two * unit_two)[:, None],
                stream_sums(cotangent * lowered)[:, None],
                head_sums.reshape(2, 2, width),
                stream_sums(grad_projected)[:, None],
                hidden_sums.reshape(2, 4, width),
                stream_sums(grad_lowered)[:, None],
            ],
            axis=1,
        )
        part_all = lax.all_gather(part[None], "rows", axis=0, tiled=True)
        table_round = narrow(part_all[:, :, 0:6])
        grad_bias = jnp.sum(part_all, axis=0)
        grad_mod = jnp.einsum(
            "bd,bsic->dsic", silu_cond, table_round, preferred_element_type=F32
        )
        grad_silu = column_total(
            jnp.einsum("bsic,dsic->bd", table_round, mod_round, preferred_element_type=F32)
        )
        sigmoid_cond = jax.nn.sigmoid(cond)
        grad_cond = grad_silu * sigmoid_cond * (1.0 + cond * (1.0 - sigmoid_cond))
        grad_qkv = (
            grad_qkv.reshape(2, local_rows, pairs, 3, PAIR)
            .transpose(1, 0, 3, 2, 4)
            .reshape(w_qkv.shape)
        )
        grad_proj, grad_up, grad_down = [
            grad.swapaxes(0, 1).reshape(weight.shape)
            for grad, weight in ((grad_proj, w_proj), (grad_up, w_up), (grad_down, w_down))
        ]
        next_mod, first_mod, second_mod = adam_step(w_mod, moments_mod, grad_mod)
        next_qkv, first_qkv, second_qkv = adam_step(w_qkv, moments_qkv, grad_qkv)
        next_proj, first_proj, second_proj = adam_step(w_proj, moments_proj, grad_proj)
        next_up, first_up, second_up = adam_step(w_up, moments_up, grad_up)
        next_down, first_down, second_down = adam_step(w_down, moments_down, grad_down)
        next_bias, first_bias, second_bias = adam_step(biases, moments_bias, grad_bias)
        return (
            output[None, :IMAGE_TOKENS],
            output[None, IMAGE_TOKENS:TOKENS],
            grad_source[None, :IMAGE_TOKENS],
            grad_source[None, IMAGE_TOKENS:TOKENS],
            grad_cond,
            grad_mod,
            grad_qkv,
            grad_proj,
            grad_up,
            grad_down,
            grad_bias,
            next_mod,
            next_qkv,
            next_proj,
            next_up,
            next_down,
            next_bias,
            first_mod,
            second_mod,
            jnp.stack([first_qkv, second_qkv]),
            jnp.stack([first_proj, second_proj]),
            jnp.stack([first_up, second_up]),
            jnp.stack([first_down, second_down]),
            first_bias,
            second_bias,
        )

    return shards


def solution(mesh):
    in_specs = (
        P("rows", None, "cols"),
        P("rows", None, "cols"),
        P(None, "rows"),
        P("rows", None, "cols"),
        P("rows", None, "cols"),
        P("rows", None, None, "cols"),
        P("rows", None, None, "cols"),
        P("rows", None, "cols"),
        P("rows", None, None, "cols"),
        P("rows", None, None, "cols"),
        P(None, None, "cols"),
        P(None, "rows", None, None, "cols"),
        P(None, "rows", None, None, "cols"),
        P(None, "rows", None, "cols"),
        P(None, "rows", None, None, "cols"),
        P(None, "rows", None, None, "cols"),
        P(None, None, None, "cols"),
    )
    out_specs = (
        P("rows", None, "cols"),
        P("rows", None, "cols"),
        P("rows", None, "cols"),
        P("rows", None, "cols"),
        P(None, "rows"),
        P("rows", None, None, "cols"),
        P("rows", None, None, "cols"),
        P("rows", None, "cols"),
        P("rows", None, None, "cols"),
        P("rows", None, None, "cols"),
        P(None, None, "cols"),
        P("rows", None, None, "cols"),
        P("rows", None, None, "cols"),
        P("rows", None, "cols"),
        P("rows", None, None, "cols"),
        P("rows", None, None, "cols"),
        P(None, None, "cols"),
        P("rows", None, None, "cols"),
        P("rows", None, None, "cols"),
        P(None, "rows", None, None, "cols"),
        P(None, "rows", None, "cols"),
        P(None, "rows", None, None, "cols"),
        P(None, "rows", None, None, "cols"),
        P(None, None, "cols"),
        P(None, None, "cols"),
    )
    shards = make_shards(mesh.shape["rows"], mesh.shape["cols"])
    return jax.shard_map(shards, mesh=mesh, in_specs=in_specs, out_specs=out_specs, check_vma=False)
```

time: 2000 us -> 945 us (0.47)
  waiting for transfers between devices: 1410 us -> 288 us
  Pallas kernels: 0 us -> 196 us
  matrix products: 165 us -> 7.72 us
  starting transfers between devices: 1.52 us -> 87.1 us
  blocking collectives: 111 us -> 37.6 us
  other arithmetic: 131 us -> 91.6 us
  local copies, waits for them, and re-layouts: 164 us -> 194 us
    reduce_scatter x8 -> x0, waiting for transfers between devices: 859 us -> none  [the longest x1 308 us: shards(): lax.psum_scatter(grad_down, 'rows', scatter_dimension=0, tiled=True)]
    all_gather x8 -> x0, waiting for transfers between devices: 488 us -> none  [the longest x1 141 us: shards(): lax.all_gather(local_weights[3], 'rows', axis=0, tiled=True)]
    ppermute x0 -> x87, waiting for transfers between devices: none -> 288 us  [the longest x14 100 us: ring_gather(): back = lax.ppermute(back, 'rows', behind)]
    pallas_call x0 -> x18, Pallas kernels: none -> 196 us  [the longest x8 53.5 us: matmul_back(): pl.pallas_call(kernel, grid=(2,), in_specs=[whole((rows, depth)), pl.Bloc...]
    dot_general x45 -> x0, matrix products: 159 us -> none  [the longest x4 30.8 us: apply_rows(): jnp.einsum('xbq,qgu->xbgu', activations_complete[:, :IMAGE_TOKENS], weigh...]
    ppermute x0 -> x87, starting transfers between devices: none -> 80.9 us  [the longest x14 24.3 us: ring_gather(): forward = lax.ppermute(forward, 'rows', ahead)]
    unnamed x18 -> x0, waiting for transfers between devices: 58.7 us -> none
    psum x4 -> x0, blocking collectives: 45.3 us -> none  [column_total(): return lax.psum(parts, 'cols')]
  transfers between devices with their start and end apart: 17 -> 88, of which waited for: 15 -> 30; matrix products, arithmetic and copies ran while one was open for 18% -> 27% of each run, Pallas kernels for 0% -> 17%
where the time goes in v1:
time: 945 us; the launch traced here: 934 us
  waiting for transfers between devices  288 us (30%)
  Pallas kernels  196 us (21%)
  local copies, waits for them, and re-layouts  194 us (21%)
  other arithmetic  91.6 us (10%)
  starting transfers between devices  87.1 us (9%)
  blocking collectives  37.6 us (4%)
  between operations  33.3 us (4%)
    ppermute x14, waiting for transfers between devices, ring_gather(): back = lax.ppermute(back, 'rows', behind)  100 us
    ppermute x14, waiting for transfers between devices, ring_gather(): forward = lax.ppermute(forward, 'rows', ahead)  89.7 us
    unnamed x179, local copies, waits for them, and re-layouts  58.8 us
    pallas_call x8, Pallas kernels, matmul_back(): pl.pallas_call(kernel, grid=(2,), in_specs=[whole((rows, depth)), pl.Bloc...  53.5 us
    ppermute x14, waiting for transfers between devices, ring_scatter(): forward = lax.ppermute(forward, 'rows', ahead).astype(F32)  48.1 us
    pallas_call x4, Pallas kernels, matmul_rows(): pl.pallas_call(kernel, grid=(width // tile,), in_specs=[whole((rows, dept...  44.9 us
    dynamic_update_slice x30, local copies, waits for them, and re-layouts, put(): return lax.dynamic_update_slice(state, piece, (0, slot(offset) * height, 0))  42.1 us
    all_gather x1, blocking collectives, shards(): part_all = lax.all_gather(part[None], 'rows', axis=0, tiled=True)  37.6 us
  transfers between devices with their start and end apart: 88, of which 30 were waited for; matrix products, arithmetic and copies ran while one was open for 27% of the time, Pallas kernels for 17%

profile of v1, /device:TPU:0, one launch (start us, length us, event | category | flops | bytes accessed | tf_op | source)
XLA Modules:
  0.0 934.5 jit_solution(15406022893344530624)
XLA Ops:
  29.6 6.3 all-to-all-start
  39.3 5.0 fusion.90
  44.3 5.4 fusion.89
  120.6 18.6 %collective-permute-done.19 = bf16[2,192,384]{2,1,0:T(8,128)(2,1)S(1)} collective-permute-done((bf16[2,192,384]{2,1,0:T(8,128)(2,1)S(1)}, bf16[2,192,384]{2,1,0:T(8,128)(2,1)S(1)}, u32[]{:S(2)}, u32[]{:S(2)}) %collective-permute-start.19) | collective-permute-done | bytes 294944 | tf_op jit(solution)/shard_map/ppermute | solution.py:438
  153.3 12.8 %collective-permute-done.10 = bf16[2,192,1152]{2,1,0:T(8,128)(2,1)S(1)} collective-permute-done((bf16[2,192,1152]{2,1,0:T(8,128)(2,1)S(1)}, bf16[2,192,1152]{2,1,0:T(8,128)(2,1)S(1)}, u32[]{:S(2)}, u32[]{:S(2)}) %collective-permute-start.10) | collective-permute-done | bytes 884768 | tf_op jit(solution)/shard_map/ppermute | solution.py:435
  167.7 5.9 multiply_convert_fusion
  174.6 20.0 %collective-permute-done.11 = bf16[2,192,1152]{2,1,0:T(8,128)(2,1)S(1)} collective-permute-done((bf16[2,192,1152]{2,1,0:T(8,128)(2,1)S(1)}, bf16[2,192,1152]{2,1,0:T(8,128)(2,1)S(1)}, u32[]{:S(2)}, u32[]{:S(2)}) %collective-permute-start.11) | collective-permute-done | bytes 884768 | tf_op jit(solution)/shard_map/ppermute | solution.py:438
  196.3 38.9 %collective-permute-done.12 = bf16[2,192,1152]{2,1,0:T(8,128)(2,1)S(1)} collective-permute-done((bf16[2,192,1152]{2,1,0:T(8,128)(2,1)S(1)}, bf16[2,192,1152]{2,1,0:T(8,128)(2,1)S(1)}, u32[]{:S(2)}, u32[]{:S(2)}) %collective-permute-start.12) | collective-permute-done | bytes 884768 | tf_op jit(solution)/shard_map/ppermute | solution.py:435
  236.2 9.9 %shard_map.1512.triple_ref = bf16[1184,1152]{1,0:T(8,128)(2,1)} custom-call(bf16[1184,1536]{1,0:T(8,128)(2,1)} %get-tuple-element.276.acts_ref.outer_ref, bf16[2,1536,1152]{2,1,0:T(8,128)(2,1)} %constant_dynamic-update-slice_fusion.24.weight_ref, f32[2,1152]{1,0:T(2,128)} %reshape.452.refs_0_), custom_call_target="tpu_custom_call" | custom-call | flops 4190109696 | bytes 13443072 | tf_op jit(solution)/shard_map/pallas_call | solution.py:84
  246.0 24.6 %shard_map.1513 = (bf16[1184,384]{1,0:T(8,128)(2,1)}, f32[3,2,1184]{2,1,0:T(2,128)}) custom-call(bf16[1184,1152]{1,0:T(8,128)(2,1)} %shard_map.1512.triple_ref), custom_call_target="tpu_custom_call" | custom-call | flops 8613003264 | bytes 10911744 | tf_op jit(solution)/shard_map/pallas_call | solution.py:266
  276.5 5.6 fusion.88
  282.1 5.4 fusion.87
  309.1 8.0 collective-permute-done.29
  320.9 7.6 collective-permute-done.30
  331.3 11.1 %collective-permute-done.36 = bf16[2,192,1536]{2,1,0:T(8,128)(2,1)S(1)} collective-permute-done((bf16[2,192,1536]{2,1,0:T(8,128)(2,1)}, bf16[2,192,1536]{2,1,0:T(8,128)(2,1)S(1)}, u32[]{:S(2)}, u32[]{:S(2)}) %collective-permute-start.36) | collective-permute-done | bytes 1179680 | tf_op jit(solution)/shard_map/ppermute | solution.py:435
  343.9 9.8 %collective-permute-done.37 = bf16[2,192,1536]{2,1,0:T(8,128)(2,1)S(1)} collective-permute-done((bf16[2,192,1536]{2,1,0:T(8,128)(2,1)}, bf16[2,192,1536]{2,1,0:T(8,128)(2,1)S(1)}, u32[]{:S(2)}, u32[]{:S(2)}) %collective-permute-start.37) | collective-permute-done | bytes 1179680 | tf_op jit(solution)/shard_map/ppermute | solution.py:438
  357.7 10.0 %collective-permute-done.31 = bf16[2,192,1536]{2,1,0:T(8,128)(2,1)S(1)} collective-permute-done((bf16[2,192,1536]{2,1,0:T(8,128)(2,1)S(1)}, bf16[2,192,1536]{2,1,0:T(8,128)(2,1)S(1)}, u32[]{:S(2)}, u32[]{:S(2)}) %collective-permute-start.31) | collective-permute-done | bytes 1179680 | tf_op jit(solution)/shard_map/ppermute | solution.py:435
  370.3 32.9 %collective-permute-done.39 = bf16[2,192,1536]{2,1,0:T(8,128)(2,1)S(1)} collective-permute-done((bf16[2,192,1536]{2,1,0:T(8,128)(2,1)S(1)}, bf16[2,192,1536]{2,1,0:T(8,128)(2,1)S(1)}, u32[]{:S(2)}, u32[]{:S(2)}) %collective-permute-start.39) | collective-permute-done | bytes 1179680 | tf_op jit(solution)/shard_map/ppermute | solution.py:438
  408.9 8.9 collective-permute-done.33
  418.9 11.2 %collective-permute-done.40 = bf16[2,192,1536]{2,1,0:T(8,128)(2,1)S(1)} collective-permute-done((bf16[2,192,1536]{2,1,0:T(8,128)(2,1)S(1)}, bf16[2,192,1536]{2,1,0:T(8,128)(2,1)S(1)}, u32[]{:S(2)}, u32[]{:S(2)}) %collective-permute-start.40) | collective-permute-done | bytes 1179680 | tf_op jit(solution)/shard_map/ppermute | solution.py:438
  433.5 16.0 %shard_map.1516 = (bf16[1184,1536]{1,0:T(8,128)(2,1)}, f32[1184,1536]{1,0:T(8,128)}) custom-call(bf16[1184,1536]{1,0:T(8,128)(2,1)} %pad_maximum_fusion.3.acts_ref.outer_ref, bf16[2,1536,1536]{2,1,0:T(8,128)(2,1)} %constant_dynamic-update-slice_fusion.2.weight_ref, f32[2,1536]{1,0:T(2,128)} %bitcast.199), custom_call_target="tpu_custom_call" | custom-call | flops 5586812928 | bytes 16711680 | tf_op jit(solution)/shard_map/pallas_call | solution.py:84
  449.5 13.2 %shard_map.1519 = (bf16[1184,1536]{1,0:T(8,128)(2,1)}, f32[2,1536]{1,0:T(2,128)}) custom-call(bf16[1184,1536]{1,0:T(8,128)(2,1)} %get-tuple-element.275.acts_ref.outer_ref, bf16[2,1536,1536]{2,1,0:T(8,128)(2,1)} %constant_dynamic-update-slice_fusion.12.weight_ref, f32[1184,1536]{1,0:T(8,128)} %get-tuple-element.35.refs_0_), custom_call_target="tpu_custom_call" | custom-call | flops 5586812928 | bytes 16711680 | tf_op jit(solution)/shard_map/pallas_call | solution.py:84
  462.7 10.9 %shard_map.1528 = bf16[2,1536,1536]{2,1,0:T(8,128)(2,1)} custom-call(bf16[1184,1536]{1,0:T(8,128)(2,1)} %pad_maximum_fusion.3.acts_ref.outer_ref, bf16[1184,1536]{1,0:T(8,128)(2,1)} %get-tuple-element.36.acts_ref.inner_ref), custom_call_target="tpu_custom_call" | custom-call | flops 5586812928 | bytes 16711680 | tf_op jit(solution)/shard_map/pallas_call | solution.py:219
  477.5 10.8 %shard_map.1529 = bf16[2,1536,1536]{2,1,0:T(8,128)(2,1)} custom-call(bf16[1184,1536]{1,0:T(8,128)(2,1)} %get-tuple-element.275.acts_ref.outer_ref, bf16[1184,1536]{1,0:T(8,128)(2,1)} %get-tuple-element.34.acts_ref.inner_ref), custom_call_target="tpu_custom_call" | custom-call | flops 5586812928 | bytes 16711680 | tf_op jit(solution)/shard_map/pallas_call | solution.py:219
  488.3 7.9 shard_map.1518
  500.3 7.9 shard_map.1521
  510.1 7.9 shard_map.1517
  518.0 8.0 shard_map.1520
  538.8 14.5 %collective-permute-done.73 = bf16[2,192,1536]{2,1,0:T(8,128)(2,1)S(1)} collective-permute-done((bf16[2,192,1536]{2,1,0:T(8,128)(2,1)}, bf16[2,192,1536]{2,1,0:T(8,128)(2,1)S(1)}, u32[]{:S(2)}, u32[]{:S(2)}) %collective-permute-start.73) | collective-permute-done | bytes 1179680 | tf_op jit(solution)/shard_map/ppermute | solution.py:457
  554.8 24.3 %collective-permute-done.77 = bf16[2,192,1536]{2,1,0:T(8,128)(2,1)S(1)} collective-permute-done((bf16[2,192,1536]{2,1,0:T(8,128)(2,1)S(1)}, bf16[2,192,1536]{2,1,0:T(8,128)(2,1)S(1)}, u32[]{:S(2)}, u32[]{:S(2)}) %collective-permute-start.77) | collective-permute-done | bytes 1179680 | tf_op jit(solution)/shard_map/ppermute | solution.py:462
  602.0 8.4 collective-permute-done.74
  610.3 9.4 %collective-permute-done.51 = bf16[1184,384]{1,0:T(8,128)(2,1)S(1)} collective-permute-done((bf16[1184,384]{1,0:T(8,128)(2,1)S(1)}, bf16[1184,384]{1,0:T(8,128)(2,1)S(1)}, u32[]{:S(2)}, u32[]{:S(2)}) %collective-permute-start.51) | collective-permute-done | bytes 909344 | tf_op jit(solution)/shard_map/ppermute | solution.py:394
  623.6 10.1 %collective-permute-done.82 = bf16[2,192,1536]{2,1,0:T(8,128)(2,1)S(1)} collective-permute-done((bf16[2,192,1536]{2,1,0:T(8,128)(2,1)S(1)}, bf16[2,192,1536]{2,1,0:T(8,128)(2,1)S(1)}, u32[]{:S(2)}, u32[]{:S(2)}) %collective-permute-start.82) | collective-permute-done | bytes 1179680 | tf_op jit(solution)/shard_map/ppermute | solution.py:457
  643.5 5.7 shard_map.1522.grad_ref
  649.2 35.5 %shard_map.1523 = (bf16[1184,1152]{1,0:T(8,128)(2,1)}, f32[3,2,256]{2,1,0:T(2,128)}) custom-call(bf16[1184,1152]{1,0:T(8,128)(2,1)} %shard_map.1512.triple_ref, f32[3,2,1184]{2,1,0:T(2,128)} %get-tuple-element.37.total_ref, bf16[1184,384]{1,0:T(8,128)(2,1)} %shard_map.1522.grad_ref), custom_call_target="tpu_custom_call" | custom-call | flops 21532508160 | bytes 10911744 | tf_op jit(solution)/shard_map/pallas_call | solution.py:336
  684.7 7.0 shard_map.1525
  695.6 5.9 shard_map.1527
  701.5 9.7 %shard_map.1526 = bf16[2,1536,1152]{2,1,0:T(8,128)(2,1)} custom-call(bf16[1184,1536]{1,0:T(8,128)(2,1)} %get-tuple-element.276.acts_ref.outer_ref, bf16[1184,1152]{1,0:T(8,128)(2,1)} %get-tuple-element.38.acts_ref.inner_ref), custom_call_target="tpu_custom_call" | custom-call | flops 4190109696 | bytes 13443072 | tf_op jit(solution)/shard_map/pallas_call | solution.py:219
  713.2 6.8 shard_map.1524
  739.1 6.9 multiply_subtract_fusion.2
  792.2 5.2 copy.439
  797.9 5.2 copy.440
  817.7 7.0 collective-permute-done.60
  831.7 37.6 %all-gather = f32[16,14,384]{2,1,0:T(8,128)S(1)} all-gather(f32[2,14,384]{2,1,0:T(8,128)S(1)} %concatenate.31), channel_id=2, replica_groups=mesh['rows'=8,'cols'=4] {'rows'}, dimensions={0}, use_global_device_ids=true | all-gather | bytes 387072 | tf_op jit(solution)/shard_map/all_gather | solution.py:606
  872.3 6.8 multiply_subtract_fusion
  879.9 4.5 copy.425
  893.5 4.5 copy.436
  929.5 4.5 copy.437
  (542 shorter events, 341.1 us)
Async XLA Ops:
  6.4 101.7 %collective-permute-start.6 = (bf16[2,192,1152]{2,1,0:T(8,128)(2,1)}, bf16[2,192,1152]{2,1,0:T(8,128)(2,1)}, u32[]{:S(2)}, u32[]{:S(2)}) collective-permute-start(bf16[2,192,1152]{2,1,0:T(8,128)(2,1)} %reshape.450), channel_id=1, source_target_pairs={{0,8},{8,16},{16,24},{24,28},{28,20},{20,12},{12,4},{4,0},{1,9},{9... | collective-permute-start | bytes 2654216 | tf_op jit(solution)/shard_map/ppermute | solution.py:435
  9.4 100.9 %collective-permute-start.7 = (bf16[2,192,1152]{2,1,0:T(8,128)(2,1)}, bf16[2,192,1152]{2,1,0:T(8,128)(2,1)}, u32[]{:S(2)}, u32[]{:S(2)}) collective-permute-start(bf16[2,192,1152]{2,1,0:T(8,128)(2,1)} %reshape.450), channel_id=1, source_target_pairs={{8,0},{16,8},{24,16},{28,24},{20,28},{12,20},{4,12},{0,4},{9,1},{1... | collective-permute-start | bytes 2654216 | tf_op jit(solution)/shard_map/ppermute | solution.py:438
  24.1 46.7 %collective-permute-start.13 = (bf16[2,192,384]{2,1,0:T(8,128)(2,1)}, bf16[2,192,384]{2,1,0:T(8,128)(2,1)}, u32[]{:S(2)}, u32[]{:S(2)}) collective-permute-start(bf16[2,192,384]{2,1,0:T(8,128)(2,1)} %get-tuple-element.219), channel_id=1, source_target_pairs={{0,8},{8,16},{16,24},{24,28},{28,20},{20,12},{12,4},{4,0},{1,9},{9... | collective-permute-start | bytes 884744 | tf_op jit(solution)/shard_map/ppermute | solution.py:435
  26.1 46.6 %collective-permute-start.14 = (bf16[2,192,384]{2,1,0:T(8,128)(2,1)}, bf16[2,192,384]{2,1,0:T(8,128)(2,1)}, u32[]{:S(2)}, u32[]{:S(2)}) collective-permute-start(bf16[2,192,384]{2,1,0:T(8,128)(2,1)} %get-tuple-element.219), channel_id=1, source_target_pairs={{8,0},{16,8},{24,16},{28,24},{20,28},{12,20},{4,12},{0,4},{9,1},{1... | collective-permute-start | bytes 884744 | tf_op jit(solution)/shard_map/ppermute | solution.py:438
  29.6 36.2 %all-to-all-start = ((f32[8,2,6,384]{3,1,2,0:T(2,128)}), f32[8,2,6,384]{3,1,2,0:T(2,128)}, u32[]{:S(2)}, u32[]{:S(2)}) async-start(f32[8,2,6,384]{3,1,2,0:T(2,128)} %copy.375), calls=%async_computation | async-start | bytes 294912 | tf_op jit(solution)/shard_map/all_to_all | solution.py:506
  70.8 30.1 %collective-permute-start.15 = (bf16[2,192,384]{2,1,0:T(8,128)(2,1)}, bf16[2,192,384]{2,1,0:T(8,128)(2,1)}, u32[]{:S(2)}, u32[]{:S(2)}) collective-permute-start(bf16[2,192,384]{2,1,0:T(8,128)(2,1)} %collective-permute-done.13), channel_id=1, source_target_pairs={{0,8},{8,16},{16,24},{24,28},{28,20},{20,12},{12,4},{4,0},{1,9},{9... | collective-permute-start | bytes 884744 | tf_op jit(solution)/shard_map/ppermute | solution.py:435
  72.7 29.8 %collective-permute-start.16 = (bf16[2,192,384]{2,1,0:T(8,128)(2,1)}, bf16[2,192,384]{2,1,0:T(8,128)(2,1)}, u32[]{:S(2)}, u32[]{:S(2)}) collective-permute-start(bf16[2,192,384]{2,1,0:T(8,128)(2,1)} %collective-permute-done.14), channel_id=1, source_target_pairs={{8,0},{16,8},{24,16},{28,24},{20,28},{12,20},{4,12},{0,4},{9,1},{1... | collective-permute-start | bytes 884744 | tf_op jit(solution)/shard_map/ppermute | solution.py:438
  108.1 34.0 %collective-permute-start.44 = (bf16[1184,384]{1,0:T(8,128)(2,1)S(1)}, bf16[1184,384]{1,0:T(8,128)(2,1)S(1)}, u32[]{:S(2)}, u32[]{:S(2)}) collective-permute-start(bf16[1184,384]{1,0:T(8,128)(2,1)S(1)} %concatenate.28), channel_id=1, source_target_pairs={{0,2},{1,3},{2,0},{3,1},{4,6},{5,7},{6,4},{7,5},{8,10},{9,11},{10,... | collective-permute-start | bytes 2727944 | tf_op jit(solution)/shard_map/ppermute | solution.py:394
  110.3 32.3 %collective-permute-start.8 = (bf16[2,192,1152]{2,1,0:T(8,128)(2,1)}, bf16[2,192,1152]{2,1,0:T(8,128)(2,1)S(1)}, u32[]{:S(2)}, u32[]{:S(2)}) collective-permute-start(bf16[2,192,1152]{2,1,0:T(8,128)(2,1)} %collective-permute-done.6), channel_id=1, source_target_pairs={{0,8},{8,16},{16,24},{24,28},{28,20},{20,12},{12,4},{4,0},{1,9},{9... | collective-permute-start | bytes 2654216 | tf_op jit(solution)/shard_map/ppermute | solution.py:435
  112.0 31.7 %collective-permute-start.9 = (bf16[2,192,1152]{2,1,0:T(8,128)(2,1)}, bf16[2,192,1152]{2,1,0:T(8,128)(2,1)S(1)}, u32[]{:S(2)}, u32[]{:S(2)}) collective-permute-start(bf16[2,192,1152]{2,1,0:T(8,128)(2,1)} %collective-permute-done.7), channel_id=1, source_target_pairs={{8,0},{16,8},{24,16},{28,24},{20,28},{12,20},{4,12},{0,4},{9,1},{1... | collective-permute-start | bytes 2654216 | tf_op jit(solution)/shard_map/ppermute | solution.py:438
  146.2 141.9 %collective-permute-start.27 = (bf16[2,192,1536]{2,1,0:T(8,128)(2,1)}, bf16[2,192,1536]{2,1,0:T(8,128)(2,1)}, u32[]{:S(2)}, u32[]{:S(2)}) collective-permute-start(bf16[2,192,1536]{2,1,0:T(8,128)(2,1)} %get-tuple-element.268), channel_id=1, source_target_pairs={{0,8},{8,16},{16,24},{24,28},{28,20},{20,12},{12,4},{4,0},{1,9},{9... | collective-permute-start | bytes 3538952 | tf_op jit(solution)/shard_map/ppermute | solution.py:435
  147.7 151.7 %collective-permute-start.28 = (bf16[2,192,1536]{2,1,0:T(8,128)(2,1)}, bf16[2,192,1536]{2,1,0:T(8,128)(2,1)}, u32[]{:S(2)}, u32[]{:S(2)}) collective-permute-start(bf16[2,192,1536]{2,1,0:T(8,128)(2,1)} %get-tuple-element.268), channel_id=1, source_target_pairs={{8,0},{16,8},{24,16},{28,24},{20,28},{12,20},{4,12},{0,4},{9,1},{1... | collective-permute-start | bytes 3538952 | tf_op jit(solution)/shard_map/ppermute | solution.py:438
  151.2 148.7 %collective-permute-start.34 = (bf16[2,192,1536]{2,1,0:T(8,128)(2,1)}, bf16[2,192,1536]{2,1,0:T(8,128)(2,1)}, u32[]{:S(2)}, u32[]{:S(2)}) collective-permute-start(bf16[2,192,1536]{2,1,0:T(8,128)(2,1)} %get-tuple-element.266), channel_id=1, source_target_pairs={{0,8},{8,16},{16,24},{24,28},{28,20},{20,12},{12,4},{4,0},{1,9},{9... | collective-permute-start | bytes 3538952 | tf_op jit(solution)/shard_map/ppermute | solution.py:435
  152.7 41.8 %collective-permute-start.11 = (bf16[2,192,1152]{2,1,0:T(8,128)(2,1)S(1)}, bf16[2,192,1152]{2,1,0:T(8,128)(2,1)S(1)}, u32[]{:S(2)}, u32[]{:S(2)}) collective-permute-start(bf16[2,192,1152]{2,1,0:T(8,128)(2,1)S(1)} %collective-permute-done.9), channel_id=1, source_target_pairs={{8,0},{16,8},{24,16},{28,24},{20,28},{12,20},{4,12},{0,4},{9,1},{1... | collective-permute-start | bytes 2654216 | tf_op jit(solution)/shard_map/ppermute | solution.py:438
  166.1 69.1 %collective-permute-start.12 = (bf16[2,192,1152]{2,1,0:T(8,128)(2,1)S(1)}, bf16[2,192,1152]{2,1,0:T(8,128)(2,1)S(1)}, u32[]{:S(2)}, u32[]{:S(2)}) collective-permute-start(bf16[2,192,1152]{2,1,0:T(8,128)(2,1)S(1)} %collective-permute-done.10), channel_id=1, source_target_pairs={{0,8},{8,16},{16,24},{24,28},{28,20},{20,12},{12,4},{4,0},{1,9},{9... | collective-permute-start | bytes 2654216 | tf_op jit(solution)/shard_map/ppermute | solution.py:435
  194.6 111.6 %collective-permute-start.35 = (bf16[2,192,1536]{2,1,0:T(8,128)(2,1)}, bf16[2,192,1536]{2,1,0:T(8,128)(2,1)}, u32[]{:S(2)}, u32[]{:S(2)}) collective-permute-start(bf16[2,192,1536]{2,1,0:T(8,128)(2,1)} %get-tuple-element.266), channel_id=1, source_target_pairs={{8,0},{16,8},{24,16},{28,24},{20,28},{12,20},{4,12},{0,4},{9,1},{1... | collective-permute-start | bytes 3538952 | tf_op jit(solution)/shard_map/ppermute | solution.py:438
  299.9 42.4 %collective-permute-start.36 = (bf16[2,192,1536]{2,1,0:T(8,128)(2,1)}, bf16[2,192,1536]{2,1,0:T(8,128)(2,1)S(1)}, u32[]{:S(2)}, u32[]{:S(2)}) collective-permute-start(bf16[2,192,1536]{2,1,0:T(8,128)(2,1)} %collective-permute-done.34), channel_id=1, source_target_pairs={{0,8},{8,16},{16,24},{24,28},{28,20},{20,12},{12,4},{4,0},{1,9},{9... | collective-permute-start | bytes 3538952 | tf_op jit(solution)/shard_map/ppermute | solution.py:435
  306.2 47.5 %collective-permute-start.37 = (bf16[2,192,1536]{2,1,0:T(8,128)(2,1)}, bf16[2,192,1536]{2,1,0:T(8,128)(2,1)S(1)}, u32[]{:S(2)}, u32[]{:S(2)}) collective-permute-start(bf16[2,192,1536]{2,1,0:T(8,128)(2,1)} %collective-permute-done.35), channel_id=1, source_target_pairs={{8,0},{16,8},{24,16},{28,24},{20,28},{12,20},{4,12},{0,4},{9,1},{1... | collective-permute-start | bytes 3538952 | tf_op jit(solution)/shard_map/ppermute | solution.py:438
  317.1 50.6 %collective-permute-start.31 = (bf16[2,192,1536]{2,1,0:T(8,128)(2,1)S(1)}, bf16[2,192,1536]{2,1,0:T(8,128)(2,1)S(1)}, u32[]{:S(2)}, u32[]{:S(2)}) collective-permute-start(bf16[2,192,1536]{2,1,0:T(8,128)(2,1)S(1)} %collective-permute-done.29), channel_id=1, source_target_pairs={{0,8},{8,16},{16,24},{24,28},{28,20},{20,12},{12,4},{4,0},{1,9},{9... | collective-permute-start | bytes 3538952 | tf_op jit(solution)/shard_map/ppermute | solution.py:435
  328.5 79.3 %collective-permute-start.32 = (bf16[2,192,1536]{2,1,0:T(8,128)(2,1)S(1)}, bf16[2,192,1536]{2,1,0:T(8,128)(2,1)S(1)}, u32[]{:S(2)}, u32[]{:S(2)}) collective-permute-start(bf16[2,192,1536]{2,1,0:T(8,128)(2,1)S(1)} %collective-permute-done.30), channel_id=1, source_target_pairs={{8,0},{16,8},{24,16},{28,24},{20,28},{12,20},{4,12},{0,4},{9,1},{1... | collective-permute-start | bytes 3538952 | tf_op jit(solution)/shard_map/ppermute | solution.py:438
  342.4 62.6 %collective-permute-start.38 = (bf16[2,192,1536]{2,1,0:T(8,128)(2,1)S(1)}, bf16[2,192,1536]{2,1,0:T(8,128)(2,1)S(1)}, u32[]{:S(2)}, u32[]{:S(2)}) collective-permute-start(bf16[2,192,1536]{2,1,0:T(8,128)(2,1)S(1)} %collective-permute-done.36), channel_id=1, source_target_pairs={{0,8},{8,16},{16,24},{24,28},{28,20},{20,12},{12,4},{4,0},{1,9},{9... | collective-permute-start | bytes 3538952 | tf_op jit(solution)/shard_map/ppermute | solution.py:435
  353.8 49.4 %collective-permute-start.39 = (bf16[2,192,1536]{2,1,0:T(8,128)(2,1)S(1)}, bf16[2,192,1536]{2,1,0:T(8,128)(2,1)S(1)}, u32[]{:S(2)}, u32[]{:S(2)}) collective-permute-start(bf16[2,192,1536]{2,1,0:T(8,128)(2,1)S(1)} %collective-permute-done.37), channel_id=1, source_target_pairs={{8,0},{16,8},{24,16},{28,24},{20,28},{12,20},{4,12},{0,4},{9,1},{1... | collective-permute-start | bytes 3538952 | tf_op jit(solution)/shard_map/ppermute | solution.py:438
  355.4 50.7 %collective-permute-start.25 = (bf16[1184,384]{1,0:T(8,128)(2,1)S(1)}, bf16[1184,384]{1,0:T(8,128)(2,1)S(1)}, u32[]{:S(2)}, u32[]{:S(2)}) collective-permute-start(bf16[1184,384]{1,0:T(8,128)(2,1)S(1)} %add_convert_fusion.10), channel_id=1, source_target_pairs={{0,2},{1,3},{2,0},{3,1},{4,6},{5,7},{6,4},{7,5},{8,10},{9,11},{10,... | collective-permute-start | bytes 2727944 | tf_op jit(solution)/shard_map/ppermute | solution.py:394
  367.7 50.2 %collective-permute-start.33 = (bf16[2,192,1536]{2,1,0:T(8,128)(2,1)S(1)}, bf16[2,192,1536]{2,1,0:T(8,128)(2,1)S(1)}, u32[]{:S(2)}, u32[]{:S(2)}) collective-permute-start(bf16[2,192,1536]{2,1,0:T(8,128)(2,1)S(1)} %collective-permute-done.31), channel_id=1, source_target_pairs={{0,8},{8,16},{16,24},{24,28},{28,20},{20,12},{12,4},{4,0},{1,9},{9... | collective-permute-start | bytes 3538952 | tf_op jit(solution)/shard_map/ppermute | solution.py:435
  476.8 49.2 %collective-permute-start.76 = (bf16[2,192,1536]{2,1,0:T(8,128)(2,1)}, bf16[2,192,1536]{2,1,0:T(8,128)(2,1)}, u32[]{:S(2)}, u32[]{:S(2)}) collective-permute-start(bf16[2,192,1536]{2,1,0:T(8,128)(2,1)} %get-tuple-element.231), channel_id=1, source_target_pairs={{8,0},{16,8},{24,16},{28,24},{20,28},{12,20},{4,12},{0,4},{9,1},{1... | collective-permute-start | bytes 3538952 | tf_op jit(solution)/shard_map/ppermute | solution.py:462
  496.2 35.0 %collective-permute-start.41 = (bf16[1184,768]{1,0:T(8,128)(2,1)}, bf16[1184,768]{1,0:T(8,128)(2,1)}, u32[]{:S(2)}, u32[]{:S(2)}) collective-permute-start(bf16[1184,768]{1,0:T(8,128)(2,1)} %shard_map.1518), channel_id=1, source_target_pairs={{0,1},{1,0},{2,3},{3,2},{4,5},{5,4},{6,7},{7,6},{8,9},{9,8},{10,11... | collective-permute-start | bytes 5455880 | tf_op jit(solution)/shard_map/ppermute | solution.py:391
  499.0 29.4 %collective-permute-start.80 = (bf16[2,192,1536]{2,1,0:T(8,128)(2,1)}, bf16[2,192,1536]{2,1,0:T(8,128)(2,1)}, u32[]{:S(2)}, u32[]{:S(2)}) collective-permute-start(bf16[2,192,1536]{2,1,0:T(8,128)(2,1)} %get-tuple-element.224), channel_id=1, source_target_pairs={{0,8},{8,16},{16,24},{24,28},{28,20},{20,12},{12,4},{4,0},{1,9},{9... | collective-permute-start | bytes 3538952 | tf_op jit(solution)/shard_map/ppermute | solution.py:457
  508.5 44.8 %collective-permute-start.73 = (bf16[2,192,1536]{2,1,0:T(8,128)(2,1)}, bf16[2,192,1536]{2,1,0:T(8,128)(2,1)S(1)}, u32[]{:S(2)}, u32[]{:S(2)}) collective-permute-start(bf16[2,192,1536]{2,1,0:T(8,128)(2,1)} %get-tuple-element.230), channel_id=1, source_target_pairs={{0,8},{8,16},{16,24},{24,28},{28,20},{20,12},{12,4},{4,0},{1,9},{9... | collective-permute-start | bytes 3538952 | tf_op jit(solution)/shard_map/ppermute | solution.py:457
  526.0 56.8 %collective-permute-start.84 = (bf16[2,192,1536]{2,1,0:T(8,128)(2,1)S(1)}, bf16[2,192,1536]{2,1,0:T(8,128)(2,1)S(1)}, u32[]{:S(2)}, u32[]{:S(2)}) collective-permute-start(bf16[2,192,1536]{2,1,0:T(8,128)(2,1)S(1)} %get-tuple-element.225), channel_id=1, source_target_pairs={{8,0},{16,8},{24,16},{28,24},{20,28},{12,20},{4,12},{0,4},{9,1},{1... | collective-permute-start | bytes 3538952 | tf_op jit(solution)/shard_map/ppermute | solution.py:462
  528.4 50.7 %collective-permute-start.77 = (bf16[2,192,1536]{2,1,0:T(8,128)(2,1)S(1)}, bf16[2,192,1536]{2,1,0:T(8,128)(2,1)S(1)}, u32[]{:S(2)}, u32[]{:S(2)}) collective-permute-start(bf16[2,192,1536]{2,1,0:T(8,128)(2,1)S(1)} %add_convert_fusion.7), channel_id=1, source_target_pairs={{8,0},{16,8},{24,16},{28,24},{20,28},{12,20},{4,12},{0,4},{9,1},{1... | collective-permute-start | bytes 3538952 | tf_op jit(solution)/shard_map/ppermute | solution.py:462
  531.3 52.2 %collective-permute-start.81 = (bf16[2,192,1536]{2,1,0:T(8,128)(2,1)S(1)}, bf16[2,192,1536]{2,1,0:T(8,128)(2,1)S(1)}, u32[]{:S(2)}, u32[]{:S(2)}) collective-permute-start(bf16[2,192,1536]{2,1,0:T(8,128)(2,1)S(1)} %add_convert_fusion.4), channel_id=1, source_target_pairs={{0,8},{8,16},{16,24},{24,28},{28,20},{20,12},{12,4},{4,0},{1,9},{9... | collective-permute-start | bytes 3538952 | tf_op jit(solution)/shard_map/ppermute | solution.py:457
  534.9 51.8 %collective-permute-start.42 = (bf16[1184,384]{1,0:T(8,128)(2,1)S(1)}, bf16[1184,384]{1,0:T(8,128)(2,1)S(1)}, u32[]{:S(2)}, u32[]{:S(2)}) collective-permute-start(bf16[1184,384]{1,0:T(8,128)(2,1)S(1)} %slice.460), channel_id=1, source_target_pairs={{0,2},{1,3},{2,0},{3,1},{4,6},{5,7},{6,4},{7,5},{8,10},{9,11},{10,... | collective-permute-start | bytes 2727944 | tf_op jit(solution)/shard_map/ppermute | solution.py:394
  553.3 32.3 %collective-permute-start.47 = (bf16[1184,384]{1,0:T(8,128)(2,1)S(1)}, bf16[1184,384]{1,0:T(8,128)(2,1)S(1)}, u32[]{:S(2)}, u32[]{:S(2)}) collective-permute-start(bf16[1184,384]{1,0:T(8,128)(2,1)S(1)} %slice.459), channel_id=1, source_target_pairs={{0,2},{1,3},{2,0},{3,1},{4,6},{5,7},{6,4},{7,5},{8,10},{9,11},{10,... | collective-permute-start | bytes 2727944 | tf_op jit(solution)/shard_map/ppermute | solution.py:394
  582.8 36.9 %collective-permute-start.78 = (bf16[2,192,1536]{2,1,0:T(8,128)(2,1)S(1)}, bf16[2,192,1536]{2,1,0:T(8,128)(2,1)S(1)}, u32[]{:S(2)}, u32[]{:S(2)}) collective-permute-start(bf16[2,192,1536]{2,1,0:T(8,128)(2,1)S(1)} %get-tuple-element.229), channel_id=1, source_target_pairs={{8,0},{16,8},{24,16},{28,24},{20,28},{12,20},{4,12},{0,4},{9,1},{1... | collective-permute-start | bytes 3538952 | tf_op jit(solution)/shard_map/ppermute | solution.py:462
  584.1 49.6 %collective-permute-start.82 = (bf16[2,192,1536]{2,1,0:T(8,128)(2,1)S(1)}, bf16[2,192,1536]{2,1,0:T(8,128)(2,1)S(1)}, u32[]{:S(2)}, u32[]{:S(2)}) collective-permute-start(bf16[2,192,1536]{2,1,0:T(8,128)(2,1)S(1)} %get-tuple-element.222), channel_id=1, source_target_pairs={{0,8},{8,16},{16,24},{24,28},{28,20},{20,12},{12,4},{4,0},{1,9},{9... | collective-permute-start | bytes 3538952 | tf_op jit(solution)/shard_map/ppermute | solution.py:457
  585.6 51.4 %collective-permute-start.85 = (bf16[2,192,1536]{2,1,0:T(8,128)(2,1)S(1)}, bf16[2,192,1536]{2,1,0:T(8,128)(2,1)S(1)}, u32[]{:S(2)}, u32[]{:S(2)}) collective-permute-start(bf16[2,192,1536]{2,1,0:T(8,128)(2,1)S(1)} %get-tuple-element.223), channel_id=1, source_target_pairs={{8,0},{16,8},{24,16},{28,24},{20,28},{12,20},{4,12},{0,4},{9,1},{1... | collective-permute-start | bytes 3538952 | tf_op jit(solution)/shard_map/ppermute | solution.py:462
  623.1 99.6 %collective-permute-start.79 = (bf16[2,192,1536]{2,1,0:T(8,128)(2,1)}, bf16[2,192,1536]{2,1,0:T(8,128)(2,1)S(1)}, u32[]{:S(2)}, u32[]{:S(2)}) collective-permute-start(bf16[2,192,1536]{2,1,0:T(8,128)(2,1)} %get-tuple-element.227), channel_id=1, source_target_pairs={{8,0},{16,8},{24,16},{28,24},{20,28},{12,20},{4,12},{0,4},{9,1},{1... | collective-permute-start | bytes 3538952 | tf_op jit(solution)/shard_map/ppermute | solution.py:462
  633.7 89.6 %collective-permute-start.75 = (bf16[2,192,1536]{2,1,0:T(8,128)(2,1)S(1)}, bf16[2,192,1536]{2,1,0:T(8,128)(2,1)S(1)}, u32[]{:S(2)}, u32[]{:S(2)}) collective-permute-start(bf16[2,192,1536]{2,1,0:T(8,128)(2,1)S(1)} %get-tuple-element.226), channel_id=1, source_target_pairs={{0,8},{8,16},{16,24},{24,28},{28,20},{20,12},{12,4},{4,0},{1,9},{9... | collective-permute-start | bytes 3538952 | tf_op jit(solution)/shard_map/ppermute | solution.py:457
  639.0 90.6 %collective-permute-start.86 = (bf16[2,192,1536]{2,1,0:T(8,128)(2,1)}, bf16[2,192,1536]{2,1,0:T(8,128)(2,1)}, u32[]{:S(2)}, u32[]{:S(2)}) collective-permute-start(bf16[2,192,1536]{2,1,0:T(8,128)(2,1)} %get-tuple-element.221), channel_id=1, source_target_pairs={{8,0},{16,8},{24,16},{28,24},{20,28},{12,20},{4,12},{0,4},{9,1},{1... | collective-permute-start | bytes 3538952 | tf_op jit(solution)/shard_map/ppermute | solution.py:462
  639.7 90.6 %collective-permute-start.83 = (bf16[2,192,1536]{2,1,0:T(8,128)(2,1)}, bf16[2,192,1536]{2,1,0:T(8,128)(2,1)}, u32[]{:S(2)}, u32[]{:S(2)}) collective-permute-start(bf16[2,192,1536]{2,1,0:T(8,128)(2,1)} %get-tuple-element.220), channel_id=1, source_target_pairs={{0,8},{8,16},{16,24},{24,28},{28,20},{20,12},{12,4},{4,0},{1,9},{9... | collective-permute-start | bytes 3538952 | tf_op jit(solution)/shard_map/ppermute | solution.py:457
  691.7 118.2 %collective-permute-start.53 = (bf16[1184,768]{1,0:T(8,128)(2,1)}, bf16[1184,768]{1,0:T(8,128)(2,1)}, u32[]{:S(2)}, u32[]{:S(2)}) collective-permute-start(bf16[1184,768]{1,0:T(8,128)(2,1)} %shard_map.1525), channel_id=1, source_target_pairs={{0,1},{1,0},{2,3},{3,2},{4,5},{5,4},{6,7},{7,6},{8,9},{9,8},{10,11... | collective-permute-start | bytes 5455880 | tf_op jit(solution)/shard_map/ppermute | solution.py:391
  722.7 83.0 %collective-permute-start.59 = (bf16[2,192,1152]{2,1,0:T(8,128)(2,1)}, bf16[2,192,1152]{2,1,0:T(8,128)(2,1)}, u32[]{:S(2)}, u32[]{:S(2)}) collective-permute-start(bf16[2,192,1152]{2,1,0:T(8,128)(2,1)} %get-tuple-element.238), channel_id=1, source_target_pairs={{0,8},{8,16},{16,24},{24,28},{28,20},{20,12},{12,4},{4,0},{1,9},{9... | collective-permute-start | bytes 2654216 | tf_op jit(solution)/shard_map/ppermute | solution.py:457
  724.3 38.0 %collective-permute-start.62 = (bf16[2,192,1152]{2,1,0:T(8,128)(2,1)}, bf16[2,192,1152]{2,1,0:T(8,128)(2,1)}, u32[]{:S(2)}, u32[]{:S(2)}) collective-permute-start(bf16[2,192,1152]{2,1,0:T(8,128)(2,1)} %get-tuple-element.239), channel_id=1, source_target_pairs={{8,0},{16,8},{24,16},{28,24},{20,28},{12,20},{4,12},{0,4},{9,1},{1... | collective-permute-start | bytes 2654216 | tf_op jit(solution)/shard_map/ppermute | solution.py:462
  763.9 41.7 %collective-permute-start.63 = (bf16[2,192,1152]{2,1,0:T(8,128)(2,1)S(1)}, bf16[2,192,1152]{2,1,0:T(8,128)(2,1)}, u32[]{:S(2)}, u32[]{:S(2)}) collective-permute-start(bf16[2,192,1152]{2,1,0:T(8,128)(2,1)S(1)} %add_convert_fusion.13), channel_id=1, source_target_pairs={{8,0},{16,8},{24,16},{28,24},{20,28},{12,20},{4,12},{0,4},{9,1},{1... | collective-permute-start | bytes 2654216 | tf_op jit(solution)/shard_map/ppermute | solution.py:462
  771.8 31.4 %collective-permute-start.72 = (bf16[2,192,384]{2,1,0:T(8,128)(2,1)}, bf16[2,192,384]{2,1,0:T(8,128)(2,1)S(1)}, u32[]{:S(2)}, u32[]{:S(2)}) collective-permute-start(bf16[2,192,384]{2,1,0:T(8,128)(2,1)} %get-tuple-element.253), channel_id=1, source_target_pairs={{8,0},{16,8},{24,16},{28,24},{20,28},{12,20},{4,12},{0,4},{9,1},{1... | collective-permute-start | bytes 884744 | tf_op jit(solution)/shard_map/ppermute | solution.py:462
  773.2 30.0 %collective-permute-start.69 = (bf16[2,192,384]{2,1,0:T(8,128)(2,1)}, bf16[2,192,384]{2,1,0:T(8,128)(2,1)}, u32[]{:S(2)}, u32[]{:S(2)}) collective-permute-start(bf16[2,192,384]{2,1,0:T(8,128)(2,1)} %get-tuple-element.252), channel_id=1, source_target_pairs={{0,8},{8,16},{16,24},{24,28},{28,20},{20,12},{12,4},{4,0},{1,9},{9... | collective-permute-start | bytes 884744 | tf_op jit(solution)/shard_map/ppermute | solution.py:457
  828.2 79.2 %collective-permute-start.65 = (bf16[2,192,1152]{2,1,0:T(8,128)(2,1)}, bf16[2,192,1152]{2,1,0:T(8,128)(2,1)}, u32[]{:S(2)}, u32[]{:S(2)}) collective-permute-start(bf16[2,192,1152]{2,1,0:T(8,128)(2,1)} %get-tuple-element.235), channel_id=1, source_target_pairs={{8,0},{16,8},{24,16},{28,24},{20,28},{12,20},{4,12},{0,4},{9,1},{1... | collective-permute-start | bytes 2654216 | tf_op jit(solution)/shard_map/ppermute | solution.py:462
  829.6 77.9 %collective-permute-start.61 = (bf16[2,192,1152]{2,1,0:T(8,128)(2,1)}, bf16[2,192,1152]{2,1,0:T(8,128)(2,1)}, u32[]{:S(2)}, u32[]{:S(2)}) collective-permute-start(bf16[2,192,1152]{2,1,0:T(8,128)(2,1)} %get-tuple-element.234), channel_id=1, source_target_pairs={{0,8},{8,16},{16,24},{24,28},{28,20},{20,12},{12,4},{4,0},{1,9},{9... | collective-permute-start | bytes 2654216 | tf_op jit(solution)/shard_map/ppermute | solution.py:457
  (122 other events, 1750.7 us)

commit v2 on v1

v2 whole, which is shorter than its diff:
```python
import jax
import jax.numpy as jnp
from jax import lax
from jax.experimental import pallas as pl
from jax.experimental.pallas import tpu as pltpu
from jax.sharding import PartitionSpec as P

D = 1536
HEAD_FEATURES = 64
IMAGE_TOKENS = 1024
TXT = 154
STEP = 2


BETA_ONE = 0.9
BETA_TWO = 0.95
LEARN_RATE = 0.02
DECAY_RATE = 0.1
ADAM_EPS = 1e-08
NORM_EPS = 1e-06
GELU_COEF = 0.7978845608028654
GELU_CUBE = 0.044715
PADDED = IMAGE_TOKENS + (TXT + 15) // 16 * 16
TOKENS = IMAGE_TOKENS + TXT
STREAM_ROWS = ((0, 0, IMAGE_TOKENS), (1, IMAGE_TOKENS, PADDED))
PAIR = 2 * HEAD_FEATURES
VMEM_BYTES = 56 * 1024 * 1024
F32 = jnp.float32
BF16 = jnp.bfloat16
COST_SHARE = 1000


def narrow(values):
    return values.astype(jnp.bfloat16)


def gelu_value(inputs):
    return (
        0.5 * inputs * (1.0 + jnp.tanh(GELU_COEF * (inputs + GELU_CUBE * inputs * inputs * inputs)))
    )


def gelu_slope(inputs):
    tangent = jnp.tanh(GELU_COEF * (inputs + GELU_CUBE * inputs * inputs * inputs))
    return 0.5 * (1.0 + tangent) + 0.5 * inputs * (1.0 - tangent * tangent) * GELU_COEF * (
        1.0 + 3.0 * GELU_CUBE * inputs * inputs
    )


def adam_step(param, moments, gradient):
    first_moment = BETA_ONE * moments[0] + (1.0 - BETA_ONE) * gradient
    second_moment = BETA_TWO * moments[1] + (1.0 - BETA_TWO) * gradient * gradient
    update = (
        first_moment
        / (1.0 - BETA_ONE**STEP)
        / (jnp.sqrt(second_moment / (1.0 - BETA_TWO**STEP)) + ADAM_EPS)
    )
    return (param - LEARN_RATE * (update + DECAY_RATE * param), first_moment, second_moment)


STEP_ROWS = 48


def pieces(kind, index):
    if kind == "triple":
        return [((3 * pair + index) * PAIR, pair * PAIR, PAIR) for pair in range(3)]
    if kind == "attended":
        return [(9 * PAIR, 0, 3 * PAIR)]
    return [(index * 3 * PAIR, 0, 3 * PAIR)]


def plane(kind, stream, index):
    return (stream, index) if kind == "hidden" else (index, stream)


def row_view(kind, weight):
    if kind == "attended":
        return jnp.expand_dims(weight, -3)
    return weight if kind == "hidden" else jnp.swapaxes(weight, -3, -2)


def row_unview(kind, weight):
    if kind == "attended":
        return jnp.squeeze(weight, -3)
    return weight if kind == "hidden" else jnp.swapaxes(weight, -3, -2)


def travel_rows(kinds, weights):
    views = [row_view(kind, weight) for kind, weight in zip(kinds, weights)]
    height = views[0].shape[0]

    def kernel(*refs):
        out_ref = refs[-1]
        for kind, ref in zip(kinds, refs):
            for stream in range(2):
                for index in range(ref.shape[1 if kind != "hidden" else 2]):
                    one, two = plane(kind, stream, index)
                    for there, here, size in pieces(kind, index):
                        out_ref[stream, :, there : there + size] = ref[
                            :, one, two, here : here + size
                        ].astype(BF16)

    total = 12 * PAIR
    return pl.pallas_call(
        kernel,
        grid=(height // STEP_ROWS,),
        in_specs=[
            pl.BlockSpec((STEP_ROWS, *view.shape[1:]), lambda i: (i, 0, 0, 0)) for view in views
        ],
        out_specs=pl.BlockSpec((2, STEP_ROWS, total), lambda i: (0, i, 0)),
        out_shape=jax.ShapeDtypeStruct((2, height, total), BF16),
        compiler_params=kernel_params(),
        cost_estimate=cost(2 * height * total, 12 * height * total),
    )(*views)


def adam_rows(kind, param, moments, slot, partial, arrived):
    view, moment_view = (row_view(kind, param), row_view(kind, moments))
    height = view.shape[0]
    counts = view.shape[1:3]
    parts = height // STEP_ROWS

    def kernel(slot_ref, param_ref, moment_ref, *refs):
        grad_refs, (next_ref, grad_ref, moved_ref) = refs[:3], refs[3:]
        for stream in range(2):
            for index in range(counts[1] if kind == "hidden" else counts[0]):
                one, two = plane(kind, stream, index)
                gradient = jnp.concatenate(
                    [
                        sum(ref[stream, :, there : there + size].astype(F32) for ref in grad_refs)
                        for there, _, size in pieces(kind, index)
                    ],
                    axis=1,
                )
                result, first_moment, second_moment = adam_step(
                    param_ref[:, one, two],
                    (moment_ref[0, :, one, two], moment_ref[1, :, one, two]),
                    gradient,
                )
                next_ref[:, one, two] = result
                grad_ref[:, one, two] = gradient
                moved_ref[0, :, one, two] = first_moment
                moved_ref[1, :, one, two] = second_moment

    param_spec = pl.BlockSpec((STEP_ROWS, *counts, view.shape[3]), lambda i, slot: (i, 0, 0, 0))
    moment_spec = pl.BlockSpec(
        (2, STEP_ROWS, *counts, view.shape[3]), lambda i, slot: (0, i, 0, 0, 0)
    )
    total = partial.shape[2]
    grad_spec = pl.BlockSpec((2, STEP_ROWS, total), lambda i, slot: (0, i, 0))
    own_spec = pl.BlockSpec((2, STEP_ROWS, total), lambda i, slot: (0, slot[0] * parts + i, 0))
    next_param, grad, moved = pl.pallas_call(
        kernel,
        grid_spec=pltpu.PrefetchScalarGridSpec(
            num_scalar_prefetch=1,
            grid=(parts,),
            in_specs=[param_spec, moment_spec, own_spec, grad_spec, grad_spec],
            out_specs=[param_spec, param_spec, moment_spec],
        ),
        out_shape=[
            jax.ShapeDtypeStruct(view.shape, F32),
            jax.ShapeDtypeStruct(view.shape, F32),
            jax.ShapeDtypeStruct(moment_view.shape, F32),
        ],
        compiler_params=kernel_params(),
        cost_estimate=cost(20 * view.size, 40 * view.size),
    )(slot, view, moment_view, partial, *arrived)
    return [row_unview(kind, one) for one in (next_param, grad, moved)]


def adam_modulation(param, moments, rows, table):
    view, moment_view = (row_view("modulation", param), row_view("modulation", moments))
    height, count, streams, width = view.shape
    turned = jnp.swapaxes(table, 1, 2).reshape(table.shape[0], count * streams * width)

    def kernel(rows_ref, table_ref, param_ref, moment_ref, next_ref, grad_ref, *moved_refs):
        for index in range(count):
            for stream in range(streams):
                low = (index * streams + stream) * width
                gradient = jnp.dot(
                    rows_ref[...], table_ref[:, low : low + width], preferred_element_type=F32
                )
                result, first_moment, second_moment = adam_step(
                    param_ref[:, index, stream],
                    (moment_ref[0, :, index, stream], moment_ref[1, :, index, stream]),
                    gradient,
                )
                next_ref[:, index, stream] = result
                grad_ref[:, index, stream] = gradient
                moved_refs[0][:, index, stream] = first_moment
                moved_refs[1][:, index, stream] = second_moment

    param_spec = pl.BlockSpec((STEP_ROWS, count, streams, width), lambda i: (i, 0, 0, 0))
    moment_spec = pl.BlockSpec((2, STEP_ROWS, count, streams, width), lambda i: (0, i, 0, 0, 0))
    shape = jax.ShapeDtypeStruct(view.shape, F32)
    results = pl.pallas_call(
        kernel,
        grid=(height // STEP_ROWS,),
        in_specs=[
            pl.BlockSpec((STEP_ROWS, rows.shape[0]), lambda i: (i, 0)),
            whole(turned.shape),
            param_spec,
            moment_spec,
        ],
        out_specs=[param_spec] * 4,
        out_shape=[shape] * 4,
        compiler_params=kernel_params(),
        cost_estimate=cost(20 * view.size, 40 * view.size),
    )(rows.T, turned, view, moment_view)
    return [row_unview("modulation", one) for one in results]


def kernel_params():
    return pltpu.CompilerParams(vmem_limit_bytes=VMEM_BYTES)


def cost(flops, nbytes, transcendentals=0):
    return pl.CostEstimate(flops=flops // COST_SHARE, bytes_accessed=nbytes // COST_SHARE, transcendentals=transcendentals)


def whole(shape):
    return pl.BlockSpec(shape, lambda j: (0,) * len(shape))


def matmul_rows(acts, blocks, slots, span, epilogue, extras, extra_specs, out_types, out_specs):
    rows, depth = acts.shape
    count = len(blocks)
    height = blocks[0].shape[1]
    first, width = (span[0], span[1] - span[0])
    tile = 384
    tiles = width // tile

    def kernel(slots_ref, acts_ref, *refs):
        block_refs, refs = refs[:count], refs[count:]
        refs, weight, arrivals = refs[:-2], refs[-2], refs[-1]

        def copy(index, part):
            return pltpu.make_async_copy(
                block_refs[index].at[:, :, pl.ds(first + part * tile, tile)],
                weight.at[
                    part, :, pl.ds(pl.multiple_of(slots_ref[index] * height, height), height), :
                ],
                arrivals.at[part, index],
            )

        step = pl.program_id(0)

        @pl.when(step == 0)
        def _():
            for part in range(tiles):
                for index in range(count):
                    copy(index, part).start()

        for part in range(tiles):

            @pl.when(step == part)
            def _():
                for index in range(count):
                    copy(index, part).wait()

        for stream, low, high in STREAM_ROWS:
            product = jnp.dot(
                acts_ref[low:high], weight[step, stream], preferred_element_type=F32
            )
            epilogue(product, stream, low, high, *refs)

    return pl.pallas_call(
        kernel,
        grid=(tiles,),
        in_specs=[
            pl.BlockSpec(memory_space=pltpu.SMEM),
            whole((rows, depth)),
            *[pl.BlockSpec(memory_space=pl.ANY)] * count,
            *extra_specs,
        ],
        out_specs=out_specs,
        out_shape=out_types,
        scratch_shapes=[
            pltpu.VMEM((tiles, 2, depth, tile), BF16),
            pltpu.SemaphoreType.DMA((tiles, count)),
        ],
        compiler_params=kernel_params(),
        cost_estimate=cost(
            2 * rows * depth * width, 2 * (rows * depth + 2 * depth * width + rows * width)
        ),
    )(slots, acts, *blocks, *extras)


def column_spec(leading, tile=384):
    return pl.BlockSpec((leading, tile), lambda j: (0, j))


def project_triple(acts, blocks, slots, span, bias):
    def epilogue(product, stream, low, high, bias_ref, out_ref):
        out_ref[low:high] = (product + bias_ref[stream : stream + 1]).astype(BF16)

    rows, width = (acts.shape[0], span[1] - span[0])
    return matmul_rows(
        acts,
        blocks,
        slots,
        span,
        epilogue,
        [bias],
        [column_spec(2)],
        jax.ShapeDtypeStruct((rows, width), BF16),
        column_spec(rows),
    )


def raise_hidden(acts, blocks, slots, span, bias):
    def epilogue(product, stream, low, high, bias_ref, act_ref, slope_ref):
        inputs = product + bias_ref[stream : stream + 1]
        square = inputs * inputs
        tangent = jnp.tanh(GELU_COEF * inputs * (1.0 + GELU_CUBE * square))
        act_ref[low:high] = (0.5 * inputs * (1.0 + tangent)).astype(BF16)
        slope_ref[low:high] = 0.5 * (1.0 + tangent) + 0.5 * inputs * (
            1.0 - tangent * tangent
        ) * GELU_COEF * (1.0 + 3.0 * GELU_CUBE * square)

    rows, width = (acts.shape[0], span[1] - span[0])
    return matmul_rows(
        acts,
        blocks,
        slots,
        span,
        epilogue,
        [bias],
        [column_spec(2)],
        [jax.ShapeDtypeStruct((rows, width), BF16), jax.ShapeDtypeStruct((rows, width), F32)],
        [column_spec(rows), column_spec(rows)],
    )


def hidden_gradient(acts, blocks, slots, span, slope):
    def epilogue(product, stream, low, high, slope_ref, out_ref, sum_ref):
        gradient = product * slope_ref[low:high]
        out_ref[low:high] = gradient.astype(BF16)
        sum_ref[stream : stream + 1] = jnp.sum(gradient, axis=0, keepdims=True)

    rows, width = (acts.shape[0], span[1] - span[0])
    return matmul_rows(
        acts,
        blocks,
        slots,
        span,
        epilogue,
        [slope],
        [column_spec(rows)],
        [jax.ShapeDtypeStruct((rows, width), BF16), jax.ShapeDtypeStruct((2, width), F32)],
        [column_spec(rows), column_spec(2)],
    )


def attended_gradient(acts, blocks, slots, span):
    def epilogue(product, stream, low, high, out_ref):
        out_ref[low:high] = product.astype(BF16)

    rows, width = (acts.shape[0], span[1] - span[0])
    return matmul_rows(
        acts,
        blocks,
        slots,
        span,
        epilogue,
        [],
        [],
        jax.ShapeDtypeStruct((rows, width), BF16),
        column_spec(rows),
    )


def matmul_back(acts, blocks, slots, span, parity):
    rows, depth = acts.shape
    count = len(blocks)
    height = blocks[0].shape[1]
    share = count // 4
    tile = share * height

    def kernel(slots_ref, acts_ref, *refs):
        block_refs, (*out_refs, weight, arrivals) = refs[:count], refs[count:]

        def copy(index):
            slot = slots_ref[index]
            row = pl.multiple_of(slot % share * height, height)
            return pltpu.make_async_copy(
                block_refs[index].at[:, :, pl.ds(span[0], depth)],
                weight.at[slot // share // 2, :, pl.ds(row, height), :],
                arrivals.at[index],
            )

        def each(action, wanted):
            for index in range(count):
                pl.when(wanted(slots_ref[index] // share))(lambda index=index: action(copy(index)))

        step = pl.program_id(0)

        @pl.when(step == 0)
        def _():
            for part in range(2):
                each(lambda job: job.start(), lambda group: group == 2 * part + parity)

        each(lambda job: job.wait(), lambda group: group == 2 * step + parity)
        for part, out_ref in enumerate(out_refs):

            @pl.when(step == part)
            def _():
                for stream, low, high in STREAM_ROWS:
                    out_ref[low:high] = lax.dot_general(
                        acts_ref[low:high],
                        weight[part, stream],
                        (((1,), (1,)), ((), ())),
                        preferred_element_type=F32,
                    ).astype(BF16)

    return pl.pallas_call(
        kernel,
        grid=(2,),
        in_specs=[
            pl.BlockSpec(memory_space=pltpu.SMEM),
            whole((rows, depth)),
            *[pl.BlockSpec(memory_space=pl.ANY)] * count,
        ],
        out_specs=[whole((rows, tile))] * 2,
        out_shape=[jax.ShapeDtypeStruct((rows, tile), BF16)] * 2,
        scratch_shapes=[
            pltpu.VMEM((2, 2, tile, depth), BF16),
            pltpu.SemaphoreType.DMA((count,)),
        ],
        compiler_params=kernel_params(),
        cost_estimate=cost(
            4 * rows * depth * tile, 2 * (rows * depth + 4 * depth * tile + 2 * rows * tile)
        ),
    )(slots, acts, *blocks)


def weight_gradient(outer, inner, full_width, first=0, *so_far, tile=384):
    rows, height = outer.shape
    width = inner.shape[1]

    def kernel(outer_ref, inner_ref, *refs):
        out_ref = refs[-1]
        for stream, low, high in STREAM_ROWS:
            out_ref[stream] = lax.dot_general(
                outer_ref[low:high],
                inner_ref[low:high],
                (((0,), (0,)), ((), ())),
                preferred_element_type=F32,
            ).astype(BF16)

    return pl.pallas_call(
        kernel,
        grid=(height // tile,),
        in_specs=[
            column_spec(rows, tile),
            whole((rows, width)),
            *[pl.BlockSpec(memory_space=pl.ANY)] * len(so_far),
        ],
        out_specs=pl.BlockSpec((2, tile, width), lambda j: (0, j, first // width)),
        out_shape=jax.ShapeDtypeStruct((2, height, full_width), BF16),
        input_output_aliases={2 + index: index for index in range(len(so_far))},
        compiler_params=kernel_params(),
        cost_estimate=cost(
            2 * rows * height * width, 2 * (rows * height + rows * width + 2 * height * width)
        ),
    )(outer, inner, *so_far)


def row_chunks(rows, size=256):
    return [(low, min(low + size, rows)) for low in range(0, rows, size)]


def attention(triple, first, last, *so_far):
    rows, width = triple.shape
    pairs = width // (3 * PAIR)
    scale = HEAD_FEATURES ** (-0.5)

    def kernel(triple_ref, *refs):
        out_ref, total_ref = refs[-2:]
        lane = lax.broadcasted_iota(jnp.int32, (1, PAIR), 1) // HEAD_FEATURES
        feature = lax.broadcasted_iota(jnp.int32, (PAIR, 1), 0) // HEAD_FEATURES
        key_index = lax.broadcasted_iota(jnp.int32, (rows, 1), 0)
        keys = triple_ref[:, PAIR : 2 * PAIR]
        values_turned = triple_ref[:, 2 * PAIR : 3 * PAIR].T
        for low, high in row_chunks(rows):
            queries = triple_ref[low:high, 0:PAIR] * jnp.asarray(scale, BF16)
            mixed = []
            for head in range(2):
                own = jnp.where(lane == head, queries, jnp.zeros_like(queries))
                scores = lax.dot_general(
                    keys, own, (((1,), (1,)), ((), ())), preferred_element_type=F32
                )
                scores = jnp.where(key_index < TOKENS, scores, -1e30)
                highest = jnp.max(scores, axis=0, keepdims=True)
                weights = jnp.exp(scores - highest)
                total = jnp.sum(weights, axis=0, keepdims=True)
                total_ref[0, head : head + 1, low:high] = highest + jnp.log(total)
                mixed.append(
                    jnp.dot(values_turned, weights.astype(BF16), preferred_element_type=F32)
                    / total
                )
            out_ref[low:high] = jnp.where(feature == 0, mixed[0], mixed[1]).T.astype(BF16)

    return pl.pallas_call(
        kernel,
        grid=(last - first,),
        in_specs=[
            pl.BlockSpec((rows, 3 * PAIR), lambda p: (0, p + first)),
            *[pl.BlockSpec(memory_space=pl.ANY)] * len(so_far),
        ],
        input_output_aliases={1 + index: index for index in range(len(so_far))},
        out_specs=[
            pl.BlockSpec((rows, PAIR), lambda p: (0, p + first)),
            pl.BlockSpec((1, 2, rows), lambda p: (p + first, 0, 0)),
        ],
        out_shape=[
            jax.ShapeDtypeStruct((rows, pairs * PAIR), BF16),
            jax.ShapeDtypeStruct((pairs, 2, rows), F32),
        ],
        compiler_params=kernel_params(),
        cost_estimate=cost(
            16 * pairs * PAIR * rows * rows, 8 * rows * width, 2 * pairs * rows * rows
        ),
    )(triple, *so_far)


def attention_back(triple, totals, grad_mix, first, last, *so_far):
    rows, width = triple.shape
    pairs = width // (3 * PAIR)
    scale = HEAD_FEATURES ** (-0.5)

    def kernel(triple_ref, total_ref, grad_ref, *refs):
        out_ref, sum_ref, key_acc, value_acc = refs[-4:]
        lane = lax.broadcasted_iota(jnp.int32, (1, PAIR), 1) // HEAD_FEATURES
        feature = lax.broadcasted_iota(jnp.int32, (PAIR, 1), 0) // HEAD_FEATURES
        key_index = lax.broadcasted_iota(jnp.int32, (rows, 1), 0)
        keys = triple_ref[:, PAIR : 2 * PAIR]
        values = triple_ref[:, 2 * PAIR : 3 * PAIR]
        keys_turned = keys.T
        query_sums = [jnp.zeros((1, PAIR), F32), jnp.zeros((1, PAIR), F32)]
        for step, (low, high) in enumerate(row_chunks(rows)):
            queries = triple_ref[low:high, 0:PAIR] * jnp.asarray(scale, BF16)
            grads = grad_ref[low:high]
            turned = []
            for head in range(2):
                own = jnp.where(lane == head, queries, jnp.zeros_like(queries))
                own_grad = jnp.where(lane == head, grads, jnp.zeros_like(grads))
                scores = lax.dot_general(
                    keys, own, (((1,), (1,)), ((), ())), preferred_element_type=F32
                )
                soft = jnp.exp(scores - total_ref[0, head : head + 1, low:high])
                soft = jnp.where(key_index < TOKENS, soft, 0.0)
                grad_soft = lax.dot_general(
                    values, own_grad, (((1,), (1,)), ((), ())), preferred_element_type=F32
                )
                delta = jnp.sum(soft * grad_soft, axis=0, keepdims=True)
                score_round = (soft * (grad_soft - delta)).astype(BF16)
                turned.append(jnp.dot(keys_turned, score_round, preferred_element_type=F32))
                key_part = jnp.dot(score_round, own, preferred_element_type=F32)
                value_part = jnp.dot(soft.astype(BF16), own_grad, preferred_element_type=F32)
                if step == 0 and head == 0:
                    key_acc[...] = key_part
                    value_acc[...] = value_part
                else:
                    key_acc[...] += key_part
                    value_acc[...] += value_part
            grad_query = (jnp.where(feature == 0, turned[0], turned[1]) * scale).T
            out_ref[low:high, 0:PAIR] = grad_query.astype(BF16)
            stream = 0 if high <= IMAGE_TOKENS else 1
            query_sums[stream] += jnp.sum(grad_query, axis=0, keepdims=True)
        out_ref[:, PAIR : 2 * PAIR] = key_acc[...].astype(BF16)
        out_ref[:, 2 * PAIR : 3 * PAIR] = value_acc[...].astype(BF16)
        for stream, low, high in STREAM_ROWS:
            sum_ref[0, stream : stream + 1, 0:PAIR] = query_sums[stream]
            sum_ref[0, stream : stream + 1, PAIR : 2 * PAIR] = jnp.sum(
                value_acc[low:high], axis=0, keepdims=True
            )

    return pl.pallas_call(
        kernel,
        grid=(last - first,),
        in_specs=[
            pl.BlockSpec((rows, 3 * PAIR), lambda p: (0, p + first)),
            pl.BlockSpec((1, 2, rows), lambda p: (p + first, 0, 0)),
            pl.BlockSpec((rows, PAIR), lambda p: (0, p + first)),
            *[pl.BlockSpec(memory_space=pl.ANY)] * len(so_far),
        ],
        input_output_aliases={3 + index: index for index in range(len(so_far))},
        out_specs=[
            pl.BlockSpec((rows, 3 * PAIR), lambda p: (0, p + first)),
            pl.BlockSpec((1, 2, 2 * PAIR), lambda p: (p + first, 0, 0)),
        ],
        out_shape=[
            jax.ShapeDtypeStruct((rows, width), BF16),
            jax.ShapeDtypeStruct((pairs, 2, 2 * PAIR), F32),
        ],
        scratch_shapes=[pltpu.VMEM((rows, PAIR), F32), pltpu.VMEM((rows, PAIR), F32)],
        compiler_params=kernel_params(),
        cost_estimate=cost(
            40 * pairs * PAIR * rows * rows, 8 * rows * width, 2 * pairs * rows * rows
        ),
    )(triple, totals, grad_mix, *so_far)


def per_token(table):
    row = lax.broadcasted_iota(jnp.int32, (PADDED, 1), 0)
    return jnp.where(row < IMAGE_TOKENS, table[0][None], table[1][None])


def stream_sums(values):
    return jnp.stack([jnp.sum(values[low:high], axis=0) for _, low, high in STREAM_ROWS])


def row_stats(total, square):
    center = total / D
    return (center, lax.rsqrt(square / D - center * center + NORM_EPS))


def join_tokens(image, text):
    blank = jnp.zeros((PADDED - TOKENS, image.shape[2]), image.dtype)
    return jnp.concatenate([image[0], text[0], blank], axis=0)


def add_halves(kept, arrived):
    own, other = [one.astype(F32) + two.astype(F32) for one, two in zip(kept, arrived)]
    return (own, narrow(other))


def make_shards(row_count, col_count):
    order = list(range(0, row_count, 2)) + list(range(row_count - 1, 0, -2))
    place = [order.index(device) for device in range(row_count)]
    ahead = [(order[i], order[(i + 1) % row_count]) for i in range(row_count)]
    behind = [(target, sender) for sender, target in ahead]
    near = [(device, device ^ 1) for device in range(col_count)]
    far = [(device, device ^ 2) for device in range(col_count)]
    across = [(device, device ^ 3) for device in range(col_count)]
    share = row_count // col_count
    long_way = row_count // 2
    short_way = row_count - 1 - long_way

    slots = [
        [
            [
                (row // share ^ col) * share + row % share
                for row in (order[(place[here] + offset) % row_count] for offset in range(row_count))
            ]
            for col in range(col_count)
        ]
        for here in range(row_count)
    ]

    class Order:
        def __init__(self):
            self.last = []

        def tie(self, *values):
            if self.last:
                values, _ = lax.optimization_barrier((values, tuple(self.last)))
            return values

        def mark(self, *values):
            self.last = list(values)

        def add(self, *values):
            self.last += values

        def run(self, step, *values):
            result = step(*self.tie(*values))
            self.mark(*jax.tree.leaves(result))
            return result

    class Swap:
        def __init__(self, steps, value, pairs):
            (value,) = steps.tie(value)
            self.steps = steps
            self.value = lax.ppermute(value, "cols", pairs)

        def land(self):
            (self.value,) = self.steps.tie(self.value)
            self.steps.mark(self.value)
            return self.value

    def shift_pairs(offset):
        return [(row, (row + offset) % row_count) for row in range(row_count)]

    def rotate(values, start):
        return lax.dynamic_slice_in_dim(
            jnp.concatenate([values, values]), start, values.shape[0], 0
        )

    class Ring:
        def __init__(self, order_of_steps, slot_row, hops):
            self.steps = order_of_steps
            self.slot_row = slot_row
            self.hops = dict(zip((1, -1), hops))
            self.done = {1: 0, -1: 0}
            self.held = {}

        def send(self, ways=(1, -1)):
            for way in ways:
                if self.done[way] < self.hops[way]:
                    (value,) = self.steps.tie(self.held[way])
                    pairs = ahead if way == 1 else behind
                    self.held[way] = lax.ppermute(value, "rows", pairs)

        def land(self, ways=(1, -1)):
            here = [way for way in ways if self.done[way] < self.hops[way]]
            if not here:
                return
            values = self.steps.tie(*[self.held[way] for way in here])
            self.steps.mark(*values)
            for way, value in zip(here, values):
                self.held[way] = value
                self.done[way] += 1
                self.take(way)

        def left(self):
            return max(self.hops[way] - self.done[way] for way in (1, -1))

        def step(self, ways=(1, -1)):
            self.land(ways)
            self.send(ways)

        def finish(self):
            while self.left():
                self.step()

        def slot(self, offset):
            return self.slot_row[offset % row_count]

    class Lanes:
        def __init__(self):
            self.queue = {1: [], -1: []}
            self.flying = {}

        def push(self, ring, ahead_of=None):
            for way in (1, -1):
                queue = self.queue[way]
                place_at = queue.index(ahead_of) if ahead_of in queue else len(queue)
                queue[place_at:place_at] = [ring] * ring.hops[way]

        def tick(self):
            landed = list(self.flying.items())
            if landed:
                steps = landed[0][1].steps
                values = steps.tie(*[ring.held[way] for way, ring in landed])
                steps.mark(*values)
                for (way, ring), value in zip(landed, values):
                    ring.held[way] = value
                    ring.done[way] += 1
                for way, ring in landed:
                    ring.take(way)
            self.flying = {}
            for way in (1, -1):
                if self.queue[way]:
                    self.flying[way] = self.queue[way].pop(0)
                    self.flying[way].send((way,))

        def until(self, ring, left=0):
            while ring.left() > left:
                self.tick()

    class RingGather(Ring):
        def __init__(self, order_of_steps, slot_row, block, hops):
            super().__init__(order_of_steps, slot_row, hops)
            self.blocks = [block] * row_count
            self.held = {1: block, -1: block}

        def take(self, way):
            self.blocks[-way * self.done[way] % row_count] = self.held[way]

    class RingScatter(Ring):
        def __init__(self, order_of_steps, slot_row, partial, hops):
            super().__init__(order_of_steps, slot_row, hops)
            self.partial = partial
            self.height = partial.shape[1] // row_count
            self.held = {way: self.part(way * self.hops[way]) for way in (1, -1)}

        def part(self, offset):
            return lax.dynamic_slice(
                self.partial,
                (0, self.slot(offset) * self.height, 0),
                (2, self.height, self.partial.shape[2]),
            )

        def take(self, way):
            left = self.hops[way] - self.done[way]
            if left:
                self.held[way] = narrow(
                    self.held[way].astype(F32) + self.part(way * left).astype(F32)
                )
                self.steps.add(self.held[way])

    def shards(
        x_img,
        x_txt,
        cond,
        back_img,
        back_txt,
        w_mod,
        w_qkv,
        w_proj,
        w_up,
        w_down,
        biases,
        moments_mod,
        moments_qkv,
        moments_proj,
        moments_up,
        moments_down,
        moments_bias,
    ):
        local_rows = w_qkv.shape[0]
        width = w_qkv.shape[3]
        pairs = width // PAIR
        slot_row = lax.dynamic_slice(
            jnp.asarray(slots, jnp.int32),
            (lax.axis_index("rows"), lax.axis_index("cols"), 0),
            (1, 1, row_count),
        )[0, 0]
        slot_list = [slot_row[offset] for offset in range(row_count)]
        steps = Order()
        more_ahead, more_behind = ((long_way, short_way), (short_way, long_way))

        def gather(block, hops):
            return RingGather(steps, slot_list, block, hops)

        def scatter(partial, hops):
            return RingScatter(steps, slot_list, partial, hops)

        def update(kind, ring, param, moments):
            return steps.run(
                lambda *values: adam_rows(
                    kind, *values[:2], ring.slot(0).reshape(1), values[2], values[3:]
                ),
                param,
                moments,
                ring.partial,
                ring.held[1],
                ring.held[-1],
            )

        def far_swap(value):
            return Swap(steps, value, far)

        def near_swap(value):
            return Swap(steps, value, near)

        def send_around(value):
            return [value] + [Swap(steps, value, pairs) for pairs in (near, far, across)]

        def land_around(parts):
            return [parts[0]] + [part.land() for part in parts[1:]]

        def total_around(parts):
            one, two, three, four = land_around(parts)
            return (one + two) + (three + four)

        triple_span, attended_span, hidden_span = (
            (0, 3 * width),
            (3 * width, 4 * width),
            (0, 4 * width),
        )

        def run(step, acts, ring, span, *rest):
            return steps.run(
                lambda acts, *rest: step(acts, ring.blocks, slot_row, span, *rest), acts, *rest
            )

        def weight_part(outer, inner, *rest):
            return steps.run(
                lambda a, b, *so_far: weight_gradient(a, b, 4 * width, *rest[:1], *so_far),
                outer,
                inner,
                *rest[1:],
            )

        def send_halves(acts, ring, span, between=lambda: None):
            leaving = run(lambda *args: matmul_back(*args, 1), acts, ring, span)
            between()
            arriving = [near_swap(half) for half in leaving]
            return run(lambda *args: matmul_back(*args, 0), acts, ring, span), arriving

        def send_away(kept, arriving):
            own, other = steps.run(add_halves, kept, [half.land() for half in arriving])
            return own, far_swap(other)

        def start_width(value):
            return (value, far_swap(value), near_swap(value))

        def middle_width(parts):
            return (*parts, near_swap(parts[1].land()))

        def end_width(parts):
            value, away, beside, diagonal = parts
            diagonal.land()
            beside.land()
            return jnp.concatenate(
                [value, beside.value, away.value, diagonal.value], axis=-1
            )

        lanes = Lanes()

        def queued(ring, ahead_of=None):
            lanes.push(ring, ahead_of)
            return ring

        source_round = steps.run(join_tokens, x_img, x_txt)
        source_parts = start_width(source_round)
        silu_cond = narrow(jax.nn.silu(cond))
        mod_round = narrow(w_mod)
        (mod_terms,) = steps.tie(
            jnp.einsum("bd,dsic->bsic", silu_cond, mod_round, preferred_element_type=F32)
        )
        mod_parts = lax.all_to_all(mod_terms, "rows", 0, 0, tiled=True)
        first_local = travel_rows(("triple", "attended"), (w_qkv, w_proj))
        steps.mark(mod_parts, first_local)
        ring_first = queued(gather(first_local, more_ahead))
        lanes.tick()
        modulation = jnp.sum(mod_parts, axis=0) + biases[:, 0:6]
        mod_around = send_around(modulation)
        ring_up = queued(
            gather(steps.run(lambda w: travel_rows(("hidden",), (w,)), w_up), more_behind)
        )
        cotangent_round = steps.run(join_tokens, back_img, back_txt)
        lanes.tick()
        modulation_full = jnp.concatenate(land_around(mod_around), axis=-1)
        source_parts = middle_width(source_parts)
        cotangent_parts = start_width(cotangent_round)
        source_full = end_width(source_parts).astype(F32)
        scale_one, gate_one, scale_two, gate_two = [
            per_token(modulation[:, slot_index]) for slot_index in (1, 2, 4, 5)
        ]
        shift_two = per_token(modulation[:, 3])
        source = source_round.astype(F32)
        cotangent = cotangent_round.astype(F32)

        def first_norm(full, full_modulation):
            center, inverse = row_stats(
                jnp.sum(full, axis=1, keepdims=True),
                jnp.sum(full * full, axis=1, keepdims=True),
            )
            normed = narrow(
                (full - center) * inverse * (1.0 + per_token(full_modulation[:, 1]))
                + per_token(full_modulation[:, 0])
            )
            return center, inverse, normed

        center_one, inverse_one, normed_one = steps.run(first_norm, source_full, modulation_full)
        unit_one = (source - center_one) * inverse_one
        ring_down = queued(
            gather(steps.run(lambda w: travel_rows(("hidden",), (w,)), w_down), more_ahead)
        )
        lanes.tick()
        cotangent_parts = middle_width(cotangent_parts)
        lanes.until(ring_first)
        cotangent_full = end_width(cotangent_parts)
        triple_bias = (
            jnp.stack([biases[:, 6], jnp.zeros_like(biases[:, 6]), biases[:, 7]], axis=1)
            .reshape(2, 3, pairs, PAIR)
            .swapaxes(1, 2)
            .reshape(2, 3 * width)
        )
        triple = run(project_triple, normed_one, ring_first, triple_span, triple_bias)
        so_far = ()
        for pair in range(pairs):
            so_far = steps.run(
                lambda t, *rest, pair=pair: attention(t, pair, pair + 1, *rest), triple, *so_far
            )
            if pair == 0:
                lanes.tick()
        attended, log_totals = so_far
        halves = send_halves(attended, ring_first, attended_span)
        lanes.tick()
        own, away = send_away(*halves)
        lanes.tick()

        def residual_terms(own, away, source):
            projected = own + away.astype(F32) + per_token(biases[:, 8])
            residual = source + gate_one * projected
            sums = jnp.stack([jnp.sum(residual, axis=1), jnp.sum(residual * residual, axis=1)])
            return projected, residual, sums

        projected, residual, sums = steps.run(residual_terms, own, away.land(), source)
        sums_around = send_around(sums)
        lanes.tick()
        totals_two = total_around(sums_around)
        center_two, inverse_two = row_stats(totals_two[0][:, None], totals_two[1][:, None])
        unit_two = (residual - center_two) * inverse_two
        normed_own = narrow(unit_two * (1.0 + scale_two) + shift_two)
        steps.mark(normed_own)
        normed_parts = start_width(normed_own)
        lanes.tick()
        lanes.until(ring_up)
        lowered_full = steps.run(
            lambda full, gate: narrow(full.astype(F32) * per_token(gate)),
            cotangent_full,
            modulation_full[:, 5],
        )
        normed_two = end_width(middle_width(normed_parts))
        hidden_act, hidden_slope = run(
            raise_hidden, normed_two, ring_up, hidden_span, biases[:, 9:13].reshape(2, 4 * width)
        )
        lanes.tick()
        ring_grad_down = queued(
            scatter(weight_part(lowered_full, hidden_act), more_behind)
        )
        lanes.until(ring_down)
        hidden_round, hidden_sums = run(
            hidden_gradient, lowered_full, ring_down, hidden_span, hidden_slope
        )
        halves = send_halves(hidden_round, ring_up, hidden_span, lanes.tick)
        own, away = send_away(*halves)
        lanes.tick()
        ring_grad_up = queued(
            scatter(weight_part(normed_two, hidden_round), more_ahead)
        )

        def back_sums(grad_unit, unit_rows):
            return jnp.stack([jnp.sum(grad_unit, axis=1), jnp.sum(grad_unit * unit_rows, axis=1)])

        def normalize_back(grad_unit, unit_rows, inverse, totals):
            return inverse * (
                grad_unit - totals[0][:, None] / D - unit_rows * (totals[1][:, None] / D)
            )

        grad_normed_two = own + away.land().astype(F32)
        grad_unit_two = grad_normed_two * (1.0 + scale_two)
        sums = back_sums(grad_unit_two, unit_two)
        steps.mark(sums)
        sums_around = send_around(sums)
        lanes.tick()
        totals = total_around(sums_around)
        grad_residual = cotangent + normalize_back(grad_unit_two, unit_two, inverse_two, totals)
        grad_projected = gate_one * grad_residual
        projected_own = narrow(grad_projected)
        steps.mark(projected_own)
        projected_parts = start_width(projected_own)
        lowered_leaving = run(
            lambda *args: matmul_back(*args, 1), hidden_act, ring_down, hidden_span
        )
        lowered_kept = run(
            lambda *args: matmul_back(*args, 0), hidden_act, ring_down, hidden_span
        )
        arriving = [near_swap(half) for half in lowered_leaving]
        lanes.tick()
        projected_full = end_width(middle_width(projected_parts))
        grad_attended = run(attended_gradient, projected_full, ring_first, attended_span)
        partial_first = weight_part(projected_full, attended, 3 * width)
        own_lowered, away_lowered = send_away(lowered_kept, arriving)
        lanes.tick()
        so_far = ()
        for pair in range(pairs):
            so_far = steps.run(
                lambda t, l, g, *rest, pair=pair: attention_back(t, l, g, pair, pair + 1, *rest),
                triple,
                log_totals,
                grad_attended,
                *so_far,
            )
            if pair == pairs - 2:
                lanes.tick()
        triple_round, triple_sums = so_far
        partial_first = weight_part(normed_one, triple_round, 0, partial_first)
        ring_grad_first = queued(scatter(partial_first, more_behind))
        lanes.tick()
        halves = send_halves(triple_round, ring_first, triple_span)
        own, away = send_away(*halves)
        lowered = own_lowered + away_lowered.land().astype(F32) + per_token(biases[:, 13])
        output = narrow(residual + gate_two * lowered)
        grad_lowered = gate_two * cotangent
        steps.add(output)
        next_down, grad_down, moved_down = update(
            "hidden", ring_grad_down, w_down, moments_down
        )
        lanes.tick()
        grad_normed_one = own + away.land().astype(F32)
        grad_unit_one = grad_normed_one * (1.0 + scale_one)
        sums = back_sums(grad_unit_one, unit_one)
        steps.mark(sums)
        sums_around = send_around(sums)
        head_sums = triple_sums.reshape(pairs, 2, 2, PAIR).transpose(1, 2, 0, 3)
        part = jnp.concatenate(
            [
                stream_sums(grad_normed_one)[:, None],
                stream_sums(grad_normed_one * unit_one)[:, None],
                stream_sums(grad_residual * projected)[:, None],
                stream_sums(grad_normed_two)[:, None],
                stream_sums(grad_normed_two * unit_two)[:, None],
                stream_sums(cotangent * lowered)[:, None],
                head_sums.reshape(2, 2, width),
                stream_sums(grad_projected)[:, None],
                hidden_sums.reshape(2, 4, width),
                stream_sums(grad_lowered)[:, None],
            ],
            axis=1,
        )
        steps.mark(part)
        lanes.tick()
        (part,) = steps.tie(part)
        part_all = lax.all_to_all(
            jnp.broadcast_to(part[None], (row_count,) + part.shape), "rows", 0, 0, tiled=True
        )
        steps.mark(part_all)
        totals = total_around(sums_around)
        grad_source = grad_residual + normalize_back(grad_unit_one, unit_one, inverse_one, totals)
        steps.add(grad_source)
        table_round = narrow(part_all[:, :, 0:6])
        grad_bias = jnp.sum(part_all, axis=0)
        silu_terms = jnp.einsum("bsic,dsic->bd", table_round, mod_round, preferred_element_type=F32)
        steps.mark(silu_terms)
        silu_around = send_around(silu_terms)
        lanes.until(ring_grad_up)
        next_up, grad_up, moved_up = update("hidden", ring_grad_up, w_up, moments_up)
        lanes.until(ring_grad_first, 1)
        grad_silu = total_around(silu_around)
        sigmoid_cond = jax.nn.sigmoid(cond)
        grad_cond = grad_silu * sigmoid_cond * (1.0 + cond * (1.0 - sigmoid_cond))
        next_mod, grad_mod, first_mod, second_mod = steps.run(
            adam_modulation, w_mod, moments_mod, silu_cond, table_round
        )
        next_bias, first_bias, second_bias = adam_step(biases, moments_bias, grad_bias)
        steps.add(next_bias, first_bias, second_bias, grad_cond)
        lanes.until(ring_grad_first)
        next_qkv, grad_qkv, moved_qkv = update("triple", ring_grad_first, w_qkv, moments_qkv)
        next_proj, grad_proj, moved_proj = update(
            "attended", ring_grad_first, w_proj, moments_proj
        )
        return (
            output[None, :IMAGE_TOKENS],
            output[None, IMAGE_TOKENS:TOKENS],
            grad_source[None, :IMAGE_TOKENS],
            grad_source[None, IMAGE_TOKENS:TOKENS],
            grad_cond,
            grad_mod,
            grad_qkv,
            grad_proj,
            grad_up,
            grad_down,
            grad_bias,
            next_mod,
            next_qkv,
            next_proj,
            next_up,
            next_down,
            next_bias,
            first_mod,
            second_mod,
            moved_qkv,
            moved_proj,
            moved_up,
            moved_down,
            first_bias,
            second_bias,
        )

    return shards


def solution(mesh):
    in_specs = (
        P("rows", None, "cols"),
        P("rows", None, "cols"),
        P(None, "rows"),
        P("rows", None, "cols"),
        P("rows", None, "cols"),
        P("rows", None, None, "cols"),
        P("rows", None, None, "cols"),
        P("rows", None, "cols"),
        P("rows", None, None, "cols"),
        P("rows", None, None, "cols"),
        P(None, None, "cols"),
        P(None, "rows", None, None, "cols"),
        P(None, "rows", None, None, "cols"),
        P(None, "rows", None, "cols"),
        P(None, "rows", None, None, "cols"),
        P(None, "rows", None, None, "cols"),
        P(None, None, None, "cols"),
    )
    out_specs = (
        P("rows", None, "cols"),
        P("rows", None, "cols"),
        P("rows", None, "cols"),
        P("rows", None, "cols"),
        P(None, "rows"),
        P("rows", None, None, "cols"),
        P("rows", None, None, "cols"),
        P("rows", None, "cols"),
        P("rows", None, None, "cols"),
        P("rows", None, None, "cols"),
        P(None, None, "cols"),
        P("rows", None, None, "cols"),
        P("rows", None, None, "cols"),
        P("rows", None, "cols"),
        P("rows", None, None, "cols"),
        P("rows", None, None, "cols"),
        P(None, None, "cols"),
        P("rows", None, None, "cols"),
        P("rows", None, None, "cols"),
        P(None, "rows", None, None, "cols"),
        P(None, "rows", None, "cols"),
        P(None, "rows", None, None, "cols"),
        P(None, "rows", None, None, "cols"),
        P(None, None, "cols"),
        P(None, None, "cols"),
    )
    shards = make_shards(mesh.shape["rows"], mesh.shape["cols"])
    return jax.shard_map(shards, mesh=mesh, in_specs=in_specs, out_specs=out_specs, check_vma=False)
```

time: 945 us -> 750 us (0.79)
  local copies, waits for them, and re-layouts: 194 us -> 35.9 us
  Pallas kernels: 196 us -> 287 us
  waiting for transfers between devices: 288 us -> 234 us
  blocking collectives: 37.6 us -> 0 us
  between operations: 33.3 us -> 6.72 us
  starting transfers between devices: 87.1 us -> 75.8 us
    pallas_call x14 -> x26, Pallas kernels: 159 us -> 250 us  [the longest x8 64.5 us: matmul_back(): pl.pallas_call(kernel, grid=(2,), in_specs=[pl.BlockSpec(memory_space=plt...]
    ppermute x87 -> x81, waiting for transfers between devices: 288 us -> 228 us  [the longest x42 195 us: send(): self.held[way] = lax.ppermute(value, 'rows', pairs)]
    unnamed x179 -> x100, local copies, waits for them, and re-layouts: 58.8 us -> 7.67 us
    dynamic_update_slice x30 -> x0, local copies, waits for them, and re-layouts: 42.1 us -> none  [put(): return lax.dynamic_update_slice(state, piece, (0, slot(offset) * height, 0))]
    all_gather x1 -> x0, blocking collectives: 37.6 us -> none  [shards(): part_all = lax.all_gather(part[None], 'rows', axis=0, tiled=True)]
    convert_element_type x17 -> x18, other arithmetic: 29.2 us -> 60.1 us  [narrow(): return values.astype(jnp.bfloat16)]
    reshape x13 -> x0, local copies, waits for them, and re-layouts: 25.4 us -> none  [the longest x4 11.3 us: shards(): grad.swapaxes(0, 1).reshape(weight.shape)]
    slice x9 -> x3, local copies, waits for them, and re-layouts: 23.1 us -> 1.26 us  [the longest x1 0.64 us: shards(): table_round = narrow(part_all[:, :, 0:6])]
  transfers between devices with their start and end apart: 88 -> 83, of which waited for: 30 -> 35; matrix products, arithmetic and copies ran while one was open for 27% -> 14% of each run, Pallas kernels for 17% -> 36%
where the time goes in v2:
time: 750 us; the launch traced here: 740 us
  Pallas kernels  287 us (38%)
  waiting for transfers between devices  234 us (31%)
  other arithmetic  96.9 us (13%)
  starting transfers between devices  75.8 us (10%)
  local copies, waits for them, and re-layouts  35.9 us (5%)
    ppermute x42, waiting for transfers between devices, send(): self.held[way] = lax.ppermute(value, 'rows', pairs)  195 us
    pallas_call x8, Pallas kernels, matmul_back(): pl.pallas_call(kernel, grid=(2,), in_specs=[pl.BlockSpec(memory_space=plt...  64.5 us
    convert_element_type x18, other arithmetic, narrow(): return values.astype(jnp.bfloat16)  60.1 us
    pallas_call x4, Pallas kernels, matmul_rows(): pl.pallas_call(kernel, grid=(tiles,), in_specs=[pl.BlockSpec(memory_space...  49.4 us
    ppermute x42, starting transfers between devices, send(): self.held[way] = lax.ppermute(value, 'rows', pairs)  44.6 us
    pallas_call x3, Pallas kernels, attention_back(): pl.pallas_call(kernel, grid=(last - first,), in_specs=[pl.BlockSpec((rows...  40 us
    pallas_call x4, Pallas kernels, weight_gradient(): pl.pallas_call(kernel, grid=(height // tile,), in_specs=[column_spec(rows...  37.8 us
    pallas_call x4, Pallas kernels, adam_rows(): pl.pallas_call(kernel, grid_spec=pltpu.PrefetchScalarGridSpec(num_scalar_...  37.4 us
  transfers between devices with their start and end apart: 83, of which 35 were waited for; matrix products, arithmetic and copies ran while one was open for 14% of the time, Pallas kernels for 36%

profile of v2, /device:TPU:0, one launch (start us, length us, event | category | flops | bytes accessed | tf_op | source)
XLA Modules:
  0.0 739.5 jit_solution(12753763084340556659)
XLA Ops:
  7.8 7.3 all-to-all-start
  15.1 4.8 shard_map.369.refs_0_
  26.8 22.2 %collective-permute-done.6.refs_1_ = bf16[2,192,1536]{2,1,0:T(8,128)(2,1)S(1)} collective-permute-done((bf16[2,192,1536]{2,1,0:T(8,128)(2,1)}, bf16[2,192,1536]{2,1,0:T(8,128)(2,1)S(1)}, u32[]{:S(2)}, u32[]{:S(2)}) %collective-permute-start.6) | collective-permute-done | bytes 1179680 | tf_op jit(solution)/shard_map/ppermute | solution.py:704
  49.0 5.2 shard_map.370.refs_0_
  54.2 7.1 concatenate.25
  69.0 9.9 %add_convert_fusion.acts_ref.outer_ref = bf16[1184,1536]{1,0:T(8,128)(2,1)} fusion(f32[1184,1536]{1,0:T(8,128)S(1)} %maximum_convert_fusion, f32[1536]{0:T(1024)S(1)} %get-tuple-element.716, f32[1536]{0:T(1024)S(1)} %get-tuple-element.717, f32[1536]{0:T(1024)S(1)} %get-tuple-element.718, f32[1536]{0:T(1024)S(1)} %get-tuple-element.715, ...), kind=kLoop, calls=%fused_computation.1 | loop fusion | flops 14548992 | bytes 10946976 | tf_op jit(solution)/shard_map/convert_element_type | solution.py:34
  79.0 4.8 shard_map.371.refs_0_
  83.8 7.3 collective-permute-done.10.refs_6_
  94.6 21.0 %collective-permute-done.9 = bf16[1184,384]{1,0:T(8,128)(2,1)} collective-permute-done((bf16[1184,384]{1,0:T(8,128)(2,1)}, bf16[1184,384]{1,0:T(8,128)(2,1)}, u32[]{:S(2)}, u32[]{:S(2)}) %collective-permute-start.9) | collective-permute-done | bytes 909344 | tf_op jit(solution)/shard_map/ppermute | solution.py:676
  121.7 24.6 %collective-permute-done.15.refs_4_ = bf16[2,192,1536]{2,1,0:T(8,128)(2,1)S(1)} collective-permute-done((bf16[2,192,1536]{2,1,0:T(8,128)(2,1)S(1)}, bf16[2,192,1536]{2,1,0:T(8,128)(2,1)S(1)}, u32[]{:S(2)}, u32[]{:S(2)}) %collective-permute-start.15) | collective-permute-done | bytes 1179680 | tf_op jit(solution)/shard_map/ppermute | solution.py:704
  153.6 11.1 %shard_map.372.triple_ref = bf16[1184,1152]{1,0:T(8,128)(2,1)} custom-call(s32[8]{0:T(128)} %fusion.32.slots_ref, bf16[1184,1536]{1,0:T(8,128)(2,1)} %add_convert_fusion.acts_ref.outer_ref, bf16[2,192,1536]{2,1,0:T(8,128)(2,1)} %shard_map.369.refs_0_, bf16[2,192,1536]{2,1,0:T(8,128)(2,1)} %copy-done, bf16[2,192,1536]{2,1,0:T(8,128)(2,1)} %copy-done.3, ...), custom_call_target="tpu_custom_call" | custom-call | flops 4190109 | bytes 13443 | tf_op jit(solution)/shard_map/pallas_call | solution.py:267
  164.7 9.5 %shard_map.373 = (bf16[1184,384]{1,0:T(8,128)(2,1)}, f32[3,2,1184]{2,1,0:T(2,128)}) custom-call(bf16[1184,1152]{1,0:T(8,128)(2,1)} %shard_map.372.triple_ref), custom_call_target="tpu_custom_call" | custom-call | flops 8613003 | bytes 10911 | tf_op jit(solution)/shard_map/pallas_call | solution.py:504
  176.5 9.5 %shard_map.374 = (bf16[1184,384]{1,0:T(8,128)(2,1)}, f32[3,2,1184]{2,1,0:T(2,128)}) custom-call(bf16[1184,1152]{1,0:T(8,128)(2,1)} %shard_map.372.triple_ref, bf16[1184,384]{1,0:T(8,128)(2,1)} %get-tuple-element.362.refs_0_, f32[3,2,1184]{2,1,0:T(2,128)} %get-tuple-element.363.refs_1_), custom_call_target="tpu_custom_call", output_to_operand_aliasing={{0}: (1, {}), {1}: (2, {})} | custom-call | flops 8613003 | bytes 10911 | tf_op jit(solution)/shard_map/pallas_call | solution.py:504
  186.0 9.9 %shard_map.375 = (bf16[1184,384]{1,0:T(8,128)(2,1)}, f32[3,2,1184]{2,1,0:T(2,128)}) custom-call(bf16[1184,1152]{1,0:T(8,128)(2,1)} %shard_map.372.triple_ref, bf16[1184,384]{1,0:T(8,128)(2,1)} %get-tuple-element.367.refs_0_, f32[3,2,1184]{2,1,0:T(2,128)} %get-tuple-element.368.refs_1_), custom_call_target="tpu_custom_call", output_to_operand_aliasing={{0}: (1, {}), {1}: (2, {})} | custom-call | flops 8613003 | bytes 10911 | tf_op jit(solution)/shard_map/pallas_call | solution.py:504
  195.8 5.3 shard_map.376
  201.7 5.3 shard_map.377
  211.9 23.1 %collective-permute-done.24.refs_5_ = bf16[2,192,1536]{2,1,0:T(8,128)(2,1)S(1)} collective-permute-done((bf16[2,192,1536]{2,1,0:T(8,128)(2,1)S(1)}, bf16[2,192,1536]{2,1,0:T(8,128)(2,1)S(1)}, u32[]{:S(2)}, u32[]{:S(2)}) %collective-permute-start.24) | collective-permute-done | bytes 1179680 | tf_op jit(solution)/shard_map/ppermute | solution.py:704
  243.9 18.8 %collective-permute-done.28.refs_1_ = bf16[2,192,1536]{2,1,0:T(8,128)(2,1)S(1)} collective-permute-done((bf16[2,192,1536]{2,1,0:T(8,128)(2,1)S(1)}, bf16[2,192,1536]{2,1,0:T(8,128)(2,1)S(1)}, u32[]{:S(2)}, u32[]{:S(2)}) %collective-permute-start.28) | collective-permute-done | bytes 1179680 | tf_op jit(solution)/shard_map/ppermute | solution.py:704
  266.8 22.5 %collective-permute-done.33.refs_6_ = bf16[2,192,1536]{2,1,0:T(8,128)(2,1)S(1)} collective-permute-done((bf16[2,192,1536]{2,1,0:T(8,128)(2,1)S(1)}, bf16[2,192,1536]{2,1,0:T(8,128)(2,1)S(1)}, u32[]{:S(2)}, u32[]{:S(2)}) %collective-permute-start.33) | collective-permute-done | bytes 1179680 | tf_op jit(solution)/shard_map/ppermute | solution.py:704
  298.8 17.5 %shard_map.378 = (bf16[1184,1536]{1,0:T(8,128)(2,1)}, f32[1184,1536]{1,0:T(8,128)}) custom-call(s32[8]{0:T(128)} %fusion.32.slots_ref, bf16[1184,1536]{1,0:T(8,128)(2,1)} %pad_maximum_fusion.1.acts_ref.outer_ref, bf16[2,192,1536]{2,1,0:T(8,128)(2,1)} %shard_map.370.refs_0_, bf16[2,192,1536]{2,1,0:T(8,128)(2,1)} %collective-permute-done.16.refs_1_, ...), custom_call_target="tpu_custom_call" | custom-call | flops 5586812 | bytes 16711 | tf_op jit(solution)/shard_map/pallas_call | solution.py:267
  316.3 5.2 collective-permute-done.36.refs_5_
  327.3 11.0 %shard_map.379.refs_0_ = bf16[2,1536,1536]{2,1,0:T(8,128)(2,1)} custom-call(bf16[1184,1536]{1,0:T(8,128)(2,1)} %multiply_convert_fusion.outer_ref.acts_ref, bf16[1184,1536]{1,0:T(8,128)(2,1)} %get-tuple-element.469.inner_ref.acts_ref), custom_call_target="tpu_custom_call" | custom-call | flops 5586812 | bytes 16711 | tf_op jit(solution)/shard_map/pallas_call | solution.py:451
  341.5 9.4 %collective-permute-done.38.refs_4_ = bf16[2,192,1536]{2,1,0:T(8,128)(2,1)} collective-permute-done((bf16[2,192,1536]{2,1,0:T(8,128)(2,1)}, bf16[2,192,1536]{2,1,0:T(8,128)(2,1)}, u32[]{:S(2)}, u32[]{:S(2)}) %collective-permute-start.38) | collective-permute-done | bytes 1179680 | tf_op jit(solution)/shard_map/ppermute | solution.py:704
  354.2 14.1 %shard_map.380 = (bf16[1184,1536]{1,0:T(8,128)(2,1)}, f32[2,1536]{1,0:T(2,128)}) custom-call(s32[8]{0:T(128)} %fusion.32.slots_ref, bf16[1184,1536]{1,0:T(8,128)(2,1)} %multiply_convert_fusion.outer_ref.acts_ref, bf16[2,192,1536]{2,1,0:T(8,128)(2,1)} %shard_map.371.refs_0_, bf16[2,192,1536]{2,1,0:T(8,128)(2,1)} %copy-done.13, ...), custom_call_target="tpu_custom_call" | custom-call | flops 5586812 | bytes 16711 | tf_op jit(solution)/shard_map/pallas_call | solution.py:267
  368.3 9.4 %shard_map.381 = (bf16[1184,384]{1,0:T(8,128)(2,1)}, bf16[1184,384]{1,0:T(8,128)(2,1)}) custom-call(s32[8]{0:T(128)} %fusion.32.slots_ref, bf16[1184,1536]{1,0:T(8,128)(2,1)} %get-tuple-element.456.acts_ref.inner_ref, bf16[2,192,1536]{2,1,0:T(8,128)(2,1)} %shard_map.370.refs_0_, bf16[2,192,1536]{2,1,0:T(8,128)(2,1)} %collective-permute-done.16.refs_1_, ...), custom_call_target="tpu_custom_call" | custom-call | flops 2793406 | bytes 10174 | tf_op jit(solution)/shard_map/pallas_call | solution.py:416
  386.8 9.4 %shard_map.382 = (bf16[1184,384]{1,0:T(8,128)(2,1)}, bf16[1184,384]{1,0:T(8,128)(2,1)}) custom-call(s32[8]{0:T(128)} %fusion.32.slots_ref, bf16[1184,1536]{1,0:T(8,128)(2,1)} %get-tuple-element.456.acts_ref.inner_ref, bf16[2,192,1536]{2,1,0:T(8,128)(2,1)} %shard_map.370.refs_0_, bf16[2,192,1536]{2,1,0:T(8,128)(2,1)} %collective-permute-done.16.refs_1_, ...), custom_call_target="tpu_custom_call" | custom-call | flops 2793406 | bytes 10174 | tf_op jit(solution)/shard_map/pallas_call | solution.py:416
  398.8 12.0 %collective-permute-done.44 = bf16[2,192,1536]{2,1,0:T(8,128)(2,1)} collective-permute-done((bf16[2,192,1536]{2,1,0:T(8,128)(2,1)}, bf16[2,192,1536]{2,1,0:T(8,128)(2,1)}, u32[]{:S(2)}, u32[]{:S(2)}) %collective-permute-start.44) | collective-permute-done | bytes 1179680 | tf_op jit(solution)/shard_map/ppermute | solution.py:704
  417.7 10.9 %shard_map.383.refs_0_ = bf16[2,1536,1536]{2,1,0:T(8,128)(2,1)} custom-call(bf16[1184,1536]{1,0:T(8,128)(2,1)} %pad_maximum_fusion.1.acts_ref.outer_ref, bf16[1184,1536]{1,0:T(8,128)(2,1)} %get-tuple-element.456.acts_ref.inner_ref), custom_call_target="tpu_custom_call" | custom-call | flops 5586812 | bytes 16711 | tf_op jit(solution)/shard_map/pallas_call | solution.py:451
  436.8 5.9 collective-permute-done.47.refs_1_
  453.3 9.3 %shard_map.384 = (bf16[1184,384]{1,0:T(8,128)(2,1)}, bf16[1184,384]{1,0:T(8,128)(2,1)}) custom-call(s32[8]{0:T(128)} %fusion.32.slots_ref, bf16[1184,1536]{1,0:T(8,128)(2,1)} %get-tuple-element.469.inner_ref.acts_ref, bf16[2,192,1536]{2,1,0:T(8,128)(2,1)} %shard_map.371.refs_0_, bf16[2,192,1536]{2,1,0:T(8,128)(2,1)} %copy-done.13, ...), custom_call_target="tpu_custom_call" | custom-call | flops 2793406 | bytes 10174 | tf_op jit(solution)/shard_map/pallas_call | solution.py:416
  462.6 9.4 %shard_map.385 = (bf16[1184,384]{1,0:T(8,128)(2,1)}, bf16[1184,384]{1,0:T(8,128)(2,1)}) custom-call(s32[8]{0:T(128)} %fusion.32.slots_ref, bf16[1184,1536]{1,0:T(8,128)(2,1)} %get-tuple-element.469.inner_ref.acts_ref, bf16[2,192,1536]{2,1,0:T(8,128)(2,1)} %shard_map.371.refs_0_, bf16[2,192,1536]{2,1,0:T(8,128)(2,1)} %copy-done.13, ...), custom_call_target="tpu_custom_call" | custom-call | flops 2793406 | bytes 10174 | tf_op jit(solution)/shard_map/pallas_call | solution.py:416
  482.2 6.7 shard_map.386.grad_ref
  488.9 6.0 shard_map.387.refs_0_
  497.2 5.8 collective-permute-done.59
  511.6 13.3 %shard_map.388 = (bf16[1184,1152]{1,0:T(8,128)(2,1)}, f32[3,2,256]{2,1,0:T(2,128)}) custom-call(bf16[1184,1152]{1,0:T(8,128)(2,1)} %shard_map.372.triple_ref, f32[3,2,1184]{2,1,0:T(2,128)} %get-tuple-element.514.total_ref, bf16[1184,384]{1,0:T(8,128)(2,1)} %shard_map.386.grad_ref), custom_call_target="tpu_custom_call" | custom-call | flops 21532508 | bytes 10911 | tf_op jit(solution)/shard_map/pallas_call | solution.py:579
  524.9 13.5 %shard_map.389 = (bf16[1184,1152]{1,0:T(8,128)(2,1)}, f32[3,2,256]{2,1,0:T(2,128)}) custom-call(bf16[1184,1152]{1,0:T(8,128)(2,1)} %shard_map.372.triple_ref, f32[3,2,1184]{2,1,0:T(2,128)} %get-tuple-element.514.total_ref, bf16[1184,384]{1,0:T(8,128)(2,1)} %shard_map.386.grad_ref, ...), custom_call_target="tpu_custom_call", output_to_operand_aliasing={{0}: (3, {}), {1}: (4, {})} | custom-call | flops 21532508 | bytes 10911 | tf_op jit(solution)/shard_map/pallas_call | solution.py:579
  548.6 13.3 %shard_map.390 = (bf16[1184,1152]{1,0:T(8,128)(2,1)}, f32[3,2,256]{2,1,0:T(2,128)}) custom-call(bf16[1184,1152]{1,0:T(8,128)(2,1)} %shard_map.372.triple_ref, f32[3,2,1184]{2,1,0:T(2,128)} %get-tuple-element.514.total_ref, bf16[1184,384]{1,0:T(8,128)(2,1)} %shard_map.386.grad_ref, ...), custom_call_target="tpu_custom_call", output_to_operand_aliasing={{0}: (3, {}), {1}: (4, {})} | custom-call | flops 21532508 | bytes 10911 | tf_op jit(solution)/shard_map/pallas_call | solution.py:579
  561.8 9.9 %shard_map.391.refs_0_ = bf16[2,1536,1536]{2,1,0:T(8,128)(2,1)} custom-call(bf16[1184,1536]{1,0:T(8,128)(2,1)} %add_convert_fusion.acts_ref.outer_ref, bf16[1184,1152]{1,0:T(8,128)(2,1)} %get-tuple-element.530.inner_ref.acts_ref, bf16[2,1536,1536]{2,1,0:T(8,128)(2,1)} %shard_map.387.refs_0_), custom_call_target="tpu_custom_call", output_to_operand_aliasing={{}: (2, {})} | custom-call | flops 4190109 | bytes 13443 | tf_op jit(solution)/shard_map/pallas_call | solution.py:451
  571.8 8.3 %shard_map.392 = (bf16[1184,384]{1,0:T(8,128)(2,1)}, bf16[1184,384]{1,0:T(8,128)(2,1)}) custom-call(s32[8]{0:T(128)} %fusion.32.slots_ref, bf16[1184,1152]{1,0:T(8,128)(2,1)} %get-tuple-element.530.inner_ref.acts_ref, bf16[2,192,1536]{2,1,0:T(8,128)(2,1)} %shard_map.369.refs_0_, bf16[2,192,1536]{2,1,0:T(8,128)(2,1)} %copy-done, ...), custom_call_target="tpu_custom_call" | custom-call | flops 2095054 | bytes 8085 | tf_op jit(solution)/shard_map/pallas_call | solution.py:416
  587.1 8.2 %shard_map.393 = (bf16[1184,384]{1,0:T(8,128)(2,1)}, bf16[1184,384]{1,0:T(8,128)(2,1)}) custom-call(s32[8]{0:T(128)} %fusion.32.slots_ref, bf16[1184,1152]{1,0:T(8,128)(2,1)} %get-tuple-element.530.inner_ref.acts_ref, bf16[2,192,1536]{2,1,0:T(8,128)(2,1)} %shard_map.369.refs_0_, bf16[2,192,1536]{2,1,0:T(8,128)(2,1)} %copy-done, ...), custom_call_target="tpu_custom_call" | custom-call | flops 2095054 | bytes 8085 | tf_op jit(solution)/shard_map/pallas_call | solution.py:416
  598.0 5.9 collective-permute-done.58
  608.8 11.2 %shard_map.394 = (f32[192,2,4,384]{3,2,1,0:T(4,128)}, f32[192,2,4,384]{3,2,1,0:T(4,128)}, f32[2,192,2,4,384]{4,3,2,1,0:T(4,128)}) custom-call(s32[1]{0:T(128)} %bitcast.19.slot_ref, f32[192,2,4,384]{3,2,1,0:T(4,128)} %param_ref, f32[2,192,2,4,384]{4,3,2,1,0:T(4,128)} %moment_ref, bf16[2,1536,1536]{2,1,0:T(8,128)(2,1)} %shard_map.379.refs_0_, ...), custom_call_target="tpu_custom_call" | custom-call | flops 11796 | bytes 23592 | tf_op jit(solution)/shard_map/pallas_call | solution.py:152
  631.6 20.6 %collective-permute-done.71 = bf16[2,192,1536]{2,1,0:T(8,128)(2,1)} collective-permute-done((bf16[2,192,1536]{2,1,0:T(8,128)(2,1)}, bf16[2,192,1536]{2,1,0:T(8,128)(2,1)}, u32[]{:S(2)}, u32[]{:S(2)}) %collective-permute-start.71) | collective-permute-done | bytes 1179680 | tf_op jit(solution)/shard_map/ppermute | solution.py:704
  657.7 4.4 all-to-all-start.1
  675.6 11.2 %shard_map.395 = (f32[192,2,4,384]{3,2,1,0:T(4,128)}, f32[192,2,4,384]{3,2,1,0:T(4,128)}, f32[2,192,2,4,384]{4,3,2,1,0:T(4,128)}) custom-call(s32[1]{0:T(128)} %bitcast.19.slot_ref, f32[192,2,4,384]{3,2,1,0:T(4,128)} %param_ref.1, f32[2,192,2,4,384]{4,3,2,1,0:T(4,128)} %moment_ref.1, bf16[2,1536,1536]{2,1,0:T(8,128)(2,1)} %shard_map.383.refs_0_, ...), custom_call_target="tpu_custom_call" | custom-call | flops 11796 | bytes 23592 | tf_op jit(solution)/shard_map/pallas_call | solution.py:152
  707.1 14.7 %shard_map.396 = (f32[192,6,2,384]{3,2,1,0:T(2,128)}, f32[192,6,2,384]{3,2,1,0:T(2,128)}, f32[192,6,2,384]{3,2,1,0:T(2,128)}, f32[192,6,2,384]{3,2,1,0:T(2,128)}) custom-call(bf16[192,8]{1,0:T(8,128)(2,1)} %bitcast.79, bf16[8,4608]{1,0:T(8,128)(2,1)} %bitcast.80, f32[192,6,2,384]{3,2,1,0:T(2,128)} %bitcast.69, f32[2,192,6,2,384]{4,3,2,1,0:T(2,128)} %bitcast.72), custom_call_target="tpu_custom_call" | custom-call | flops 17694 | bytes 35389 | tf_op jit(solution)/shard_map/pallas_call | solution.py:196
  724.2 9.3 %shard_map.397 = (f32[192,3,2,384]{3,2,1,0:T(2,128)}, f32[192,3,2,384]{3,2,1,0:T(2,128)}, f32[2,192,3,2,384]{4,3,2,1,0:T(2,128)}) custom-call(s32[1]{0:T(128)} %bitcast.19.slot_ref, f32[192,3,2,384]{3,2,1,0:T(2,128)} %bitcast.71, f32[2,192,3,2,384]{4,3,2,1,0:T(2,128)} %bitcast.73, bf16[2,1536,1536]{2,1,0:T(8,128)(2,1)} %shard_map.391.refs_0_, ...), custom_call_target="tpu_custom_call" | custom-call | flops 8847 | bytes 17694 | tf_op jit(solution)/shard_map/pallas_call | solution.py:152
  733.5 5.8 shard_map.398
  (397 shorter events, 212.3 us)
Async XLA Ops:
  22.5 26.5 %collective-permute-start.6 = (bf16[2,192,1536]{2,1,0:T(8,128)(2,1)}, bf16[2,192,1536]{2,1,0:T(8,128)(2,1)S(1)}, u32[]{:S(2)}, u32[]{:S(2)}) collective-permute-start(bf16[2,192,1536]{2,1,0:T(8,128)(2,1)} %shard_map.369.refs_0_), channel_id=1, source_target_pairs={{8,0},{16,8},{24,16},{28,24},{20,28},{12,20},{4,12},{0,4},{9,1},{1... | collective-permute-start | bytes 3538952 | tf_op jit(solution)/shard_map/ppermute | solution.py:704
  22.8 38.5 %collective-permute-start.5 = (bf16[2,192,1536]{2,1,0:T(8,128)(2,1)}, bf16[2,192,1536]{2,1,0:T(8,128)(2,1)S(1)}, u32[]{:S(2)}, u32[]{:S(2)}) collective-permute-start(bf16[2,192,1536]{2,1,0:T(8,128)(2,1)} %shard_map.369.refs_0_), channel_id=1, source_target_pairs={{0,8},{8,16},{16,24},{24,28},{28,20},{20,12},{12,4},{4,0},{1,9},{9... | collective-permute-start | bytes 3538952 | tf_op jit(solution)/shard_map/ppermute | solution.py:704
  24.5 36.8 %collective-permute-start.1 = (bf16[1184,384]{1,0:T(8,128)(2,1)S(1)}, bf16[1184,384]{1,0:T(8,128)(2,1)}, u32[]{:S(2)}, u32[]{:S(2)}) collective-permute-start(bf16[1184,384]{1,0:T(8,128)(2,1)S(1)} %concatenate.24), channel_id=1, source_target_pairs={{0,2},{1,3},{2,0},{3,1},{4,6},{5,7},{6,4},{7,5},{8,10},{9,11},{10,... | collective-permute-start | bytes 2727944 | tf_op jit(solution)/shard_map/ppermute | solution.py:676
  26.2 35.2 %collective-permute-start.4 = (f32[2,6,384]{2,1,0:T(8,128)S(1)}, f32[2,6,384]{2,1,0:T(8,128)S(1)}, u32[]{:S(2)}, u32[]{:S(2)}) collective-permute-start(f32[2,6,384]{2,1,0:T(8,128)S(1)} %copy_add_fusion), channel_id=1, source_target_pairs={{0,1},{1,0},{2,3},{3,2},{4,5},{5,4},{6,7},{7,6},{8,9},{9,8},{10,11... | collective-permute-start | bytes 55304 | tf_op jit(solution)/shard_map/ppermute | solution.py:676
  26.2 35.1 %collective-permute-start.3 = (f32[2,6,384]{2,1,0:T(8,128)S(1)}, f32[2,6,384]{2,1,0:T(8,128)S(1)}, u32[]{:S(2)}, u32[]{:S(2)}) collective-permute-start(f32[2,6,384]{2,1,0:T(8,128)S(1)} %copy_add_fusion), channel_id=1, source_target_pairs={{0,2},{1,3},{2,0},{3,1},{4,6},{5,7},{6,4},{7,5},{8,10},{9,11},{10,... | collective-permute-start | bytes 55304 | tf_op jit(solution)/shard_map/ppermute | solution.py:676
  62.7 28.3 %collective-permute-start.10 = (bf16[2,192,1536]{2,1,0:T(8,128)(2,1)S(1)}, bf16[2,192,1536]{2,1,0:T(8,128)(2,1)S(1)}, u32[]{:S(2)}, u32[]{:S(2)}) collective-permute-start(bf16[2,192,1536]{2,1,0:T(8,128)(2,1)S(1)} %collective-permute-done.5.refs_7_), channel_id=1, source_target_pairs={{0,8},{8,16},{16,24},{24,28},{28,20},{20,12},{12,4},{4,0},{1,9},{9... | collective-permute-start | bytes 3538952 | tf_op jit(solution)/shard_map/ppermute | solution.py:704
  62.9 28.2 %collective-permute-start.11 = (bf16[2,192,1536]{2,1,0:T(8,128)(2,1)S(1)}, bf16[2,192,1536]{2,1,0:T(8,128)(2,1)S(1)}, u32[]{:S(2)}, u32[]{:S(2)}) collective-permute-start(bf16[2,192,1536]{2,1,0:T(8,128)(2,1)S(1)} %collective-permute-done.6.refs_1_), channel_id=1, source_target_pairs={{8,0},{16,8},{24,16},{28,24},{20,28},{12,20},{4,12},{0,4},{9,1},{1... | collective-permute-start | bytes 3538952 | tf_op jit(solution)/shard_map/ppermute | solution.py:704
  92.1 27.5 %collective-permute-start.13 = (bf16[2,192,1536]{2,1,0:T(8,128)(2,1)S(1)}, bf16[2,192,1536]{2,1,0:T(8,128)(2,1)S(1)}, u32[]{:S(2)}, u32[]{:S(2)}) collective-permute-start(bf16[2,192,1536]{2,1,0:T(8,128)(2,1)S(1)} %collective-permute-done.10.refs_6_), channel_id=1, source_target_pairs={{0,8},{8,16},{16,24},{24,28},{28,20},{20,12},{12,4},{4,0},{1,9},{9... | collective-permute-start | bytes 3538952 | tf_op jit(solution)/shard_map/ppermute | solution.py:704
  92.5 27.2 %collective-permute-start.14 = (bf16[2,192,1536]{2,1,0:T(8,128)(2,1)S(1)}, bf16[2,192,1536]{2,1,0:T(8,128)(2,1)S(1)}, u32[]{:S(2)}, u32[]{:S(2)}) collective-permute-start(bf16[2,192,1536]{2,1,0:T(8,128)(2,1)S(1)} %collective-permute-done.11.refs_2_), channel_id=1, source_target_pairs={{8,0},{16,8},{24,16},{28,24},{20,28},{12,20},{4,12},{0,4},{9,1},{1... | collective-permute-start | bytes 3538952 | tf_op jit(solution)/shard_map/ppermute | solution.py:704
  119.7 26.7 %collective-permute-start.15 = (bf16[2,192,1536]{2,1,0:T(8,128)(2,1)S(1)}, bf16[2,192,1536]{2,1,0:T(8,128)(2,1)S(1)}, u32[]{:S(2)}, u32[]{:S(2)}) collective-permute-start(bf16[2,192,1536]{2,1,0:T(8,128)(2,1)S(1)} %collective-permute-done.13.refs_5_), channel_id=1, source_target_pairs={{0,8},{8,16},{16,24},{24,28},{28,20},{20,12},{12,4},{4,0},{1,9},{9... | collective-permute-start | bytes 3538952 | tf_op jit(solution)/shard_map/ppermute | solution.py:704
  121.0 26.3 %collective-permute-start.16 = (bf16[2,192,1536]{2,1,0:T(8,128)(2,1)}, bf16[2,192,1536]{2,1,0:T(8,128)(2,1)}, u32[]{:S(2)}, u32[]{:S(2)}) collective-permute-start(bf16[2,192,1536]{2,1,0:T(8,128)(2,1)} %shard_map.370.refs_0_), channel_id=1, source_target_pairs={{8,0},{16,8},{24,16},{28,24},{20,28},{12,20},{4,12},{0,4},{9,1},{1... | collective-permute-start | bytes 3538952 | tf_op jit(solution)/shard_map/ppermute | solution.py:704
  147.3 26.9 %collective-permute-start.17 = (bf16[2,192,1536]{2,1,0:T(8,128)(2,1)}, bf16[2,192,1536]{2,1,0:T(8,128)(2,1)}, u32[]{:S(2)}, u32[]{:S(2)}) collective-permute-start(bf16[2,192,1536]{2,1,0:T(8,128)(2,1)} %shard_map.370.refs_0_), channel_id=1, source_target_pairs={{0,8},{8,16},{16,24},{24,28},{28,20},{20,12},{12,4},{4,0},{1,9},{9... | collective-permute-start | bytes 3538952 | tf_op jit(solution)/shard_map/ppermute | solution.py:704
  148.6 25.6 %collective-permute-start.18 = (bf16[2,192,1536]{2,1,0:T(8,128)(2,1)}, bf16[2,192,1536]{2,1,0:T(8,128)(2,1)}, u32[]{:S(2)}, u32[]{:S(2)}) collective-permute-start(bf16[2,192,1536]{2,1,0:T(8,128)(2,1)} %collective-permute-done.16.refs_1_), channel_id=1, source_target_pairs={{8,0},{16,8},{24,16},{28,24},{20,28},{12,20},{4,12},{0,4},{9,1},{1... | collective-permute-start | bytes 3538952 | tf_op jit(solution)/shard_map/ppermute | solution.py:704
  174.2 32.7 %collective-permute-start.20 = (bf16[2,192,1536]{2,1,0:T(8,128)(2,1)}, bf16[2,192,1536]{2,1,0:T(8,128)(2,1)S(1)}, u32[]{:S(2)}, u32[]{:S(2)}) collective-permute-start(bf16[2,192,1536]{2,1,0:T(8,128)(2,1)} %collective-permute-done.17.refs_7_), channel_id=1, source_target_pairs={{0,8},{8,16},{16,24},{24,28},{28,20},{20,12},{12,4},{4,0},{1,9},{9... | collective-permute-start | bytes 3538952 | tf_op jit(solution)/shard_map/ppermute | solution.py:704
  175.6 31.4 %collective-permute-start.21 = (bf16[2,192,1536]{2,1,0:T(8,128)(2,1)}, bf16[2,192,1536]{2,1,0:T(8,128)(2,1)S(1)}, u32[]{:S(2)}, u32[]{:S(2)}) collective-permute-start(bf16[2,192,1536]{2,1,0:T(8,128)(2,1)} %collective-permute-done.18.refs_2_), channel_id=1, source_target_pairs={{8,0},{16,8},{24,16},{28,24},{20,28},{12,20},{4,12},{0,4},{9,1},{1... | collective-permute-start | bytes 3538952 | tf_op jit(solution)/shard_map/ppermute | solution.py:704
  207.0 28.0 %collective-permute-start.24 = (bf16[2,192,1536]{2,1,0:T(8,128)(2,1)S(1)}, bf16[2,192,1536]{2,1,0:T(8,128)(2,1)S(1)}, u32[]{:S(2)}, u32[]{:S(2)}) collective-permute-start(bf16[2,192,1536]{2,1,0:T(8,128)(2,1)S(1)} %collective-permute-done.20.refs_6_), channel_id=1, source_target_pairs={{0,8},{8,16},{16,24},{24,28},{28,20},{20,12},{12,4},{4,0},{1,9},{9... | collective-permute-start | bytes 3538952 | tf_op jit(solution)/shard_map/ppermute | solution.py:704
  208.4 27.6 %collective-permute-start.25 = (bf16[2,192,1536]{2,1,0:T(8,128)(2,1)S(1)}, bf16[2,192,1536]{2,1,0:T(8,128)(2,1)S(1)}, u32[]{:S(2)}, u32[]{:S(2)}) collective-permute-start(bf16[2,192,1536]{2,1,0:T(8,128)(2,1)S(1)} %collective-permute-done.21.refs_3_), channel_id=1, source_target_pairs={{8,0},{16,8},{24,16},{28,24},{20,28},{12,20},{4,12},{0,4},{9,1},{1... | collective-permute-start | bytes 3538952 | tf_op jit(solution)/shard_map/ppermute | solution.py:704
  211.0 27.0 %collective-permute-start.23 = (bf16[1184,384]{1,0:T(8,128)(2,1)S(1)}, bf16[1184,384]{1,0:T(8,128)(2,1)S(1)}, u32[]{:S(2)}, u32[]{:S(2)}) collective-permute-start(bf16[1184,384]{1,0:T(8,128)(2,1)S(1)} %get-tuple-element.389), channel_id=1, source_target_pairs={{0,2},{1,3},{2,0},{3,1},{4,6},{5,7},{6,4},{7,5},{8,10},{9,11},{10,... | collective-permute-start | bytes 2727944 | tf_op jit(solution)/shard_map/ppermute | solution.py:676
  236.0 26.8 %collective-permute-start.28 = (bf16[2,192,1536]{2,1,0:T(8,128)(2,1)S(1)}, bf16[2,192,1536]{2,1,0:T(8,128)(2,1)S(1)}, u32[]{:S(2)}, u32[]{:S(2)}) collective-permute-start(bf16[2,192,1536]{2,1,0:T(8,128)(2,1)S(1)} %copy-done.9), channel_id=1, source_target_pairs={{8,0},{16,8},{24,16},{28,24},{20,28},{12,20},{4,12},{0,4},{9,1},{1... | collective-permute-start | bytes 3538952 | tf_op jit(solution)/shard_map/ppermute | solution.py:704
  236.7 26.7 %collective-permute-start.27 = (bf16[2,192,1536]{2,1,0:T(8,128)(2,1)S(1)}, bf16[2,192,1536]{2,1,0:T(8,128)(2,1)S(1)}, u32[]{:S(2)}, u32[]{:S(2)}) collective-permute-start(bf16[2,192,1536]{2,1,0:T(8,128)(2,1)S(1)} %copy-done.9), channel_id=1, source_target_pairs={{0,8},{8,16},{16,24},{24,28},{28,20},{20,12},{12,4},{4,0},{1,9},{9... | collective-permute-start | bytes 3538952 | tf_op jit(solution)/shard_map/ppermute | solution.py:704
  263.5 25.8 %collective-permute-start.33 = (bf16[2,192,1536]{2,1,0:T(8,128)(2,1)S(1)}, bf16[2,192,1536]{2,1,0:T(8,128)(2,1)S(1)}, u32[]{:S(2)}, u32[]{:S(2)}) collective-permute-start(bf16[2,192,1536]{2,1,0:T(8,128)(2,1)S(1)} %collective-permute-done.27.refs_7_), channel_id=1, source_target_pairs={{0,8},{8,16},{16,24},{24,28},{28,20},{20,12},{12,4},{4,0},{1,9},{9... | collective-permute-start | bytes 3538952 | tf_op jit(solution)/shard_map/ppermute | solution.py:704
  266.7 26.3 %collective-permute-start.32 = (bf16[1184,384]{1,0:T(8,128)(2,1)S(1)}, bf16[1184,384]{1,0:T(8,128)(2,1)S(1)}, u32[]{:S(2)}, u32[]{:S(2)}) collective-permute-start(bf16[1184,384]{1,0:T(8,128)(2,1)S(1)} %add_convert_fusion.19), channel_id=1, source_target_pairs={{0,2},{1,3},{2,0},{3,1},{4,6},{5,7},{6,4},{7,5},{8,10},{9,11},{10,... | collective-permute-start | bytes 2727944 | tf_op jit(solution)/shard_map/ppermute | solution.py:676
  293.6 28.0 %collective-permute-start.36 = (bf16[2,192,1536]{2,1,0:T(8,128)(2,1)S(1)}, bf16[2,192,1536]{2,1,0:T(8,128)(2,1)}, u32[]{:S(2)}, u32[]{:S(2)}) collective-permute-start(bf16[2,192,1536]{2,1,0:T(8,128)(2,1)S(1)} %collective-permute-done.33.refs_6_), channel_id=1, source_target_pairs={{0,8},{8,16},{16,24},{24,28},{28,20},{20,12},{12,4},{4,0},{1,9},{9... | collective-permute-start | bytes 3538952 | tf_op jit(solution)/shard_map/ppermute | solution.py:704
  295.0 27.7 %collective-permute-start.37 = (bf16[2,192,1536]{2,1,0:T(8,128)(2,1)S(1)}, bf16[2,192,1536]{2,1,0:T(8,128)(2,1)S(1)}, u32[]{:S(2)}, u32[]{:S(2)}) collective-permute-start(bf16[2,192,1536]{2,1,0:T(8,128)(2,1)S(1)} %collective-permute-done.34.refs_2_), channel_id=1, source_target_pairs={{8,0},{16,8},{24,16},{28,24},{20,28},{12,20},{4,12},{0,4},{9,1},{1... | collective-permute-start | bytes 3538952 | tf_op jit(solution)/shard_map/ppermute | solution.py:704
  323.8 27.1 %collective-permute-start.38 = (bf16[2,192,1536]{2,1,0:T(8,128)(2,1)}, bf16[2,192,1536]{2,1,0:T(8,128)(2,1)}, u32[]{:S(2)}, u32[]{:S(2)}) collective-permute-start(bf16[2,192,1536]{2,1,0:T(8,128)(2,1)} %collective-permute-done.36.refs_5_), channel_id=1, source_target_pairs={{0,8},{8,16},{16,24},{24,28},{28,20},{20,12},{12,4},{4,0},{1,9},{9... | collective-permute-start | bytes 3538952 | tf_op jit(solution)/shard_map/ppermute | solution.py:704
  350.9 26.9 %collective-permute-start.39 = (bf16[2,192,1536]{2,1,0:T(8,128)(2,1)}, bf16[2,192,1536]{2,1,0:T(8,128)(2,1)}, u32[]{:S(2)}, u32[]{:S(2)}) collective-permute-start(bf16[2,192,1536]{2,1,0:T(8,128)(2,1)} %get-tuple-element.431), channel_id=1, source_target_pairs={{0,8},{8,16},{16,24},{24,28},{28,20},{20,12},{12,4},{4,0},{1,9},{9... | collective-permute-start | bytes 3538952 | tf_op jit(solution)/shard_map/ppermute | solution.py:704
  351.8 25.9 %collective-permute-start.40 = (bf16[2,192,1536]{2,1,0:T(8,128)(2,1)}, bf16[2,192,1536]{2,1,0:T(8,128)(2,1)}, u32[]{:S(2)}, u32[]{:S(2)}) collective-permute-start(bf16[2,192,1536]{2,1,0:T(8,128)(2,1)} %get-tuple-element.432), channel_id=1, source_target_pairs={{8,0},{16,8},{24,16},{28,24},{20,28},{12,20},{4,12},{0,4},{9,1},{1... | collective-permute-start | bytes 3538952 | tf_op jit(solution)/shard_map/ppermute | solution.py:704
  382.6 28.2 %collective-permute-start.44 = (bf16[2,192,1536]{2,1,0:T(8,128)(2,1)}, bf16[2,192,1536]{2,1,0:T(8,128)(2,1)}, u32[]{:S(2)}, u32[]{:S(2)}) collective-permute-start(bf16[2,192,1536]{2,1,0:T(8,128)(2,1)} %get-tuple-element.451), channel_id=1, source_target_pairs={{0,8},{8,16},{16,24},{24,28},{28,20},{20,12},{12,4},{4,0},{1,9},{9... | collective-permute-start | bytes 3538952 | tf_op jit(solution)/shard_map/ppermute | solution.py:704
  383.6 28.1 %collective-permute-start.45 = (bf16[2,192,1536]{2,1,0:T(8,128)(2,1)}, bf16[2,192,1536]{2,1,0:T(8,128)(2,1)}, u32[]{:S(2)}, u32[]{:S(2)}) collective-permute-start(bf16[2,192,1536]{2,1,0:T(8,128)(2,1)} %get-tuple-element.452), channel_id=1, source_target_pairs={{8,0},{16,8},{24,16},{28,24},{20,28},{12,20},{4,12},{0,4},{9,1},{1... | collective-permute-start | bytes 3538952 | tf_op jit(solution)/shard_map/ppermute | solution.py:704
  398.8 31.6 %collective-permute-start.43 = (bf16[1184,384]{1,0:T(8,128)(2,1)}, bf16[1184,384]{1,0:T(8,128)(2,1)S(1)}, u32[]{:S(2)}, u32[]{:S(2)}) collective-permute-start(bf16[1184,384]{1,0:T(8,128)(2,1)} %add_convert_fusion.18), channel_id=1, source_target_pairs={{0,2},{1,3},{2,0},{3,1},{4,6},{5,7},{6,4},{7,5},{8,10},{9,11},{10,... | collective-permute-start | bytes 2727944 | tf_op jit(solution)/shard_map/ppermute | solution.py:676
  415.7 27.0 %collective-permute-start.47 = (bf16[2,192,1536]{2,1,0:T(8,128)(2,1)}, bf16[2,192,1536]{2,1,0:T(8,128)(2,1)}, u32[]{:S(2)}, u32[]{:S(2)}) collective-permute-start(bf16[2,192,1536]{2,1,0:T(8,128)(2,1)} %get-tuple-element.459), channel_id=1, source_target_pairs={{0,8},{8,16},{16,24},{24,28},{28,20},{20,12},{12,4},{4,0},{1,9},{9... | collective-permute-start | bytes 3538952 | tf_op jit(solution)/shard_map/ppermute | solution.py:704
  416.4 26.5 %collective-permute-start.48 = (bf16[2,192,1536]{2,1,0:T(8,128)(2,1)S(1)}, bf16[2,192,1536]{2,1,0:T(8,128)(2,1)}, u32[]{:S(2)}, u32[]{:S(2)}) collective-permute-start(bf16[2,192,1536]{2,1,0:T(8,128)(2,1)S(1)} %get-tuple-element.460), channel_id=1, source_target_pairs={{8,0},{16,8},{24,16},{28,24},{20,28},{12,20},{4,12},{0,4},{9,1},{1... | collective-permute-start | bytes 3538952 | tf_op jit(solution)/shard_map/ppermute | solution.py:704
  445.0 27.0 %collective-permute-start.55 = (bf16[2,192,1536]{2,1,0:T(8,128)(2,1)S(1)}, bf16[2,192,1536]{2,1,0:T(8,128)(2,1)}, u32[]{:S(2)}, u32[]{:S(2)}) collective-permute-start(bf16[2,192,1536]{2,1,0:T(8,128)(2,1)S(1)} %add_convert_fusion.11), channel_id=1, source_target_pairs={{8,0},{16,8},{24,16},{28,24},{20,28},{12,20},{4,12},{0,4},{9,1},{1... | collective-permute-start | bytes 3538952 | tf_op jit(solution)/shard_map/ppermute | solution.py:704
  446.3 25.8 %collective-permute-start.54 = (bf16[2,192,1536]{2,1,0:T(8,128)(2,1)S(1)}, bf16[2,192,1536]{2,1,0:T(8,128)(2,1)}, u32[]{:S(2)}, u32[]{:S(2)}) collective-permute-start(bf16[2,192,1536]{2,1,0:T(8,128)(2,1)S(1)} %get-tuple-element.474), channel_id=1, source_target_pairs={{0,8},{8,16},{16,24},{24,28},{28,20},{20,12},{12,4},{4,0},{1,9},{9... | collective-permute-start | bytes 3538952 | tf_op jit(solution)/shard_map/ppermute | solution.py:704
  475.0 28.0 %collective-permute-start.59 = (bf16[2,192,1536]{2,1,0:T(8,128)(2,1)S(1)}, bf16[2,192,1536]{2,1,0:T(8,128)(2,1)S(1)}, u32[]{:S(2)}, u32[]{:S(2)}) collective-permute-start(bf16[2,192,1536]{2,1,0:T(8,128)(2,1)S(1)} %add_convert_fusion.10), channel_id=1, source_target_pairs={{0,8},{8,16},{16,24},{24,28},{28,20},{20,12},{12,4},{4,0},{1,9},{9... | collective-permute-start | bytes 3538952 | tf_op jit(solution)/shard_map/ppermute | solution.py:704
  477.2 28.1 %collective-permute-start.60 = (bf16[2,192,1536]{2,1,0:T(8,128)(2,1)S(1)}, bf16[2,192,1536]{2,1,0:T(8,128)(2,1)}, u32[]{:S(2)}, u32[]{:S(2)}) collective-permute-start(bf16[2,192,1536]{2,1,0:T(8,128)(2,1)S(1)} %get-tuple-element.494), channel_id=1, source_target_pairs={{8,0},{16,8},{24,16},{28,24},{20,28},{12,20},{4,12},{0,4},{9,1},{1... | collective-permute-start | bytes 3538952 | tf_op jit(solution)/shard_map/ppermute | solution.py:704
  509.3 29.0 %collective-permute-start.61 = (bf16[2,192,1536]{2,1,0:T(8,128)(2,1)}, bf16[2,192,1536]{2,1,0:T(8,128)(2,1)}, u32[]{:S(2)}, u32[]{:S(2)}) collective-permute-start(bf16[2,192,1536]{2,1,0:T(8,128)(2,1)} %get-tuple-element.509), channel_id=1, source_target_pairs={{0,8},{8,16},{16,24},{24,28},{28,20},{20,12},{12,4},{4,0},{1,9},{9... | collective-permute-start | bytes 3538952 | tf_op jit(solution)/shard_map/ppermute | solution.py:704
  510.2 28.1 %collective-permute-start.62 = (bf16[2,192,1536]{2,1,0:T(8,128)(2,1)}, bf16[2,192,1536]{2,1,0:T(8,128)(2,1)}, u32[]{:S(2)}, u32[]{:S(2)}) collective-permute-start(bf16[2,192,1536]{2,1,0:T(8,128)(2,1)} %get-tuple-element.510), channel_id=1, source_target_pairs={{8,0},{16,8},{24,16},{28,24},{20,28},{12,20},{4,12},{0,4},{9,1},{1... | collective-permute-start | bytes 3538952 | tf_op jit(solution)/shard_map/ppermute | solution.py:704
  542.7 29.0 %collective-permute-start.63 = (bf16[2,192,1536]{2,1,0:T(8,128)(2,1)}, bf16[2,192,1536]{2,1,0:T(8,128)(2,1)}, u32[]{:S(2)}, u32[]{:S(2)}) collective-permute-start(bf16[2,192,1536]{2,1,0:T(8,128)(2,1)} %get-tuple-element.519), channel_id=1, source_target_pairs={{0,8},{8,16},{16,24},{24,28},{28,20},{20,12},{12,4},{4,0},{1,9},{9... | collective-permute-start | bytes 3538952 | tf_op jit(solution)/shard_map/ppermute | solution.py:704
  543.6 28.1 %collective-permute-start.64 = (bf16[2,192,1536]{2,1,0:T(8,128)(2,1)}, bf16[2,192,1536]{2,1,0:T(8,128)(2,1)}, u32[]{:S(2)}, u32[]{:S(2)}) collective-permute-start(bf16[2,192,1536]{2,1,0:T(8,128)(2,1)} %get-tuple-element.520), channel_id=1, source_target_pairs={{8,0},{16,8},{24,16},{28,24},{20,28},{12,20},{4,12},{0,4},{9,1},{1... | collective-permute-start | bytes 3538952 | tf_op jit(solution)/shard_map/ppermute | solution.py:704
  585.0 35.9 %collective-permute-start.68 = (bf16[2,192,1536]{2,1,0:T(8,128)(2,1)S(1)}, bf16[2,192,1536]{2,1,0:T(8,128)(2,1)S(1)}, u32[]{:S(2)}, u32[]{:S(2)}) collective-permute-start(bf16[2,192,1536]{2,1,0:T(8,128)(2,1)S(1)} %get-tuple-element.543), channel_id=1, source_target_pairs={{0,8},{8,16},{16,24},{24,28},{28,20},{20,12},{12,4},{4,0},{1,9},{9... | collective-permute-start | bytes 3538952 | tf_op jit(solution)/shard_map/ppermute | solution.py:704
  585.7 35.3 %collective-permute-start.69 = (bf16[2,192,1536]{2,1,0:T(8,128)(2,1)S(1)}, bf16[2,192,1536]{2,1,0:T(8,128)(2,1)}, u32[]{:S(2)}, u32[]{:S(2)}) collective-permute-start(bf16[2,192,1536]{2,1,0:T(8,128)(2,1)S(1)} %get-tuple-element.544), channel_id=1, source_target_pairs={{8,0},{16,8},{24,16},{28,24},{20,28},{12,20},{4,12},{0,4},{9,1},{1... | collective-permute-start | bytes 3538952 | tf_op jit(solution)/shard_map/ppermute | solution.py:704
  625.0 27.1 %collective-permute-start.71 = (bf16[2,192,1536]{2,1,0:T(8,128)(2,1)}, bf16[2,192,1536]{2,1,0:T(8,128)(2,1)}, u32[]{:S(2)}, u32[]{:S(2)}) collective-permute-start(bf16[2,192,1536]{2,1,0:T(8,128)(2,1)} %get-tuple-element.557), channel_id=1, source_target_pairs={{0,8},{8,16},{16,24},{24,28},{28,20},{20,12},{12,4},{4,0},{1,9},{9... | collective-permute-start | bytes 3538952 | tf_op jit(solution)/shard_map/ppermute | solution.py:704
  625.7 26.9 %collective-permute-start.72 = (bf16[2,192,1536]{2,1,0:T(8,128)(2,1)}, bf16[2,192,1536]{2,1,0:T(8,128)(2,1)}, u32[]{:S(2)}, u32[]{:S(2)}) collective-permute-start(bf16[2,192,1536]{2,1,0:T(8,128)(2,1)} %get-tuple-element.558), channel_id=1, source_target_pairs={{8,0},{16,8},{24,16},{28,24},{20,28},{12,20},{4,12},{0,4},{9,1},{1... | collective-permute-start | bytes 3538952 | tf_op jit(solution)/shard_map/ppermute | solution.py:704
  663.7 28.7 %collective-permute-start.76 = (bf16[2,192,1536]{2,1,0:T(8,128)(2,1)}, bf16[2,192,1536]{2,1,0:T(8,128)(2,1)}, u32[]{:S(2)}, u32[]{:S(2)}) collective-permute-start(bf16[2,192,1536]{2,1,0:T(8,128)(2,1)} %get-tuple-element.566), channel_id=1, source_target_pairs={{0,8},{8,16},{16,24},{24,28},{28,20},{20,12},{12,4},{4,0},{1,9},{9... | collective-permute-start | bytes 3538952 | tf_op jit(solution)/shard_map/ppermute | solution.py:704
  665.7 28.5 %collective-permute-start.77 = (bf16[2,192,1536]{2,1,0:T(8,128)(2,1)}, bf16[2,192,1536]{2,1,0:T(8,128)(2,1)}, u32[]{:S(2)}, u32[]{:S(2)}) collective-permute-start(bf16[2,192,1536]{2,1,0:T(8,128)(2,1)} %get-tuple-element.567), channel_id=1, source_target_pairs={{8,0},{16,8},{24,16},{28,24},{20,28},{12,20},{4,12},{0,4},{9,1},{1... | collective-permute-start | bytes 3538952 | tf_op jit(solution)/shard_map/ppermute | solution.py:704
  675.5 31.6 %collective-permute-start.79 = (f32[8,192]{0,1:T(8,128)S(1)}, f32[8,192]{0,1:T(8,128)}, u32[]{:S(2)}, u32[]{:S(2)}) collective-permute-start(f32[8,192]{0,1:T(8,128)S(1)} %copy.122), channel_id=1, source_target_pairs={{0,3},{1,2},{2,1},{3,0},{4,7},{5,6},{6,5},{7,4},{8,11},{9,10},{10,... | collective-permute-start | bytes 18440 | tf_op jit(solution)/shard_map/ppermute | solution.py:676
  697.2 27.1 %collective-permute-start.80 = (bf16[2,192,1536]{2,1,0:T(8,128)(2,1)}, bf16[2,192,1536]{2,1,0:T(8,128)(2,1)}, u32[]{:S(2)}, u32[]{:S(2)}) collective-permute-start(bf16[2,192,1536]{2,1,0:T(8,128)(2,1)} %add_convert_fusion.1), channel_id=1, source_target_pairs={{8,0},{16,8},{24,16},{28,24},{20,28},{12,20},{4,12},{0,4},{9,1},{1... | collective-permute-start | bytes 3538952 | tf_op jit(solution)/shard_map/ppermute | solution.py:704
  (84 other events, 908.4 us)

commit v3 on v2

--- a/solution.py
+++ b/solution.py
@@ -114,58 +114,75 @@
     )(*views)
 
 
-def adam_rows(kind, param, moments, slot, partial, arrived):
-    view, moment_view = (row_view(kind, param), row_view(kind, moments))
-    height = view.shape[0]
-    counts = view.shape[1:3]
-    parts = height // STEP_ROWS
-
-    def kernel(slot_ref, param_ref, moment_ref, *refs):
-        grad_refs, (next_ref, grad_ref, moved_ref) = refs[:3], refs[3:]
-        for stream in range(2):
-            for index in range(counts[1] if kind == "hidden" else counts[0]):
-                one, two = plane(kind, stream, index)
-                gradient = jnp.concatenate(
-                    [
-                        sum(ref[stream, :, there : there + size].astype(F32) for ref in grad_refs)
-                        for there, _, size in pieces(kind, index)
-                    ],
-                    axis=1,
-                )
-                result, first_moment, second_moment = adam_step(
-                    param_ref[:, one, two],
-                    (moment_ref[0, :, one, two], moment_ref[1, :, one, two]),
-                    gradient,
-                )
-                next_ref[:, one, two] = result
-                grad_ref[:, one, two] = gradient
-                moved_ref[0, :, one, two] = first_moment
-                moved_ref[1, :, one, two] = second_moment
-
-    param_spec = pl.BlockSpec((STEP_ROWS, *counts, view.shape[3]), lambda i, slot: (i, 0, 0, 0))
-    moment_spec = pl.BlockSpec(
-        (2, STEP_ROWS, *counts, view.shape[3]), lambda i, slot: (0, i, 0, 0, 0)
-    )
+def adam_rows(kinds, params, moments, slot, partial, arrived):
+    count = len(kinds)
+    views = [row_view(kind, one) for kind, one in zip(kinds, params)]
+    moment_views = [row_view(kind, one) for kind, one in zip(kinds, moments)]
+    parts = views[0].shape[0] // STEP_ROWS
+
+    def kernel(slot_ref, *refs):
+        param_refs, refs = refs[:count], refs[count:]
+        moment_refs, refs = refs[:count], refs[count:]
+        grad_refs, refs = refs[:3], refs[3:]
+        for place, kind in enumerate(kinds):
+            next_ref, grad_ref, moved_ref = refs[3 * place : 3 * place + 3]
+            param_ref, moment_ref = param_refs[place], moment_refs[place]
+            for stream in range(2):
+                for index in range(param_ref.shape[2 if kind == "hidden" else 1]):
+                    one, two = plane(kind, stream, index)
+                    gradient = jnp.concatenate(
+                        [
+                            sum(
+                                ref[stream, :, there : there + size].astype(F32)
+                                for ref in grad_refs
+                            )
+                            for there, _, size in pieces(kind, index)
+                        ],
+                        axis=1,
+                    )
+                    result, first_moment, second_moment = adam_step(
+                        param_ref[:, one, two],
+                        (moment_ref[0, :, one, two], moment_ref[1, :, one, two]),
+                        gradient,
+                    )
+                    next_ref[:, one, two] = result
+                    grad_ref[:, one, two] = gradient
+                    moved_ref[0, :, one, two] = first_moment
+                    moved_ref[1, :, one, two] = second_moment
+
+    param_specs = [
+        pl.BlockSpec((STEP_ROWS, *view.shape[1:]), lambda i, slot: (i, 0, 0, 0)) for view in views
+    ]
+    moment_specs = [
+        pl.BlockSpec((2, STEP_ROWS, *view.shape[1:]), lambda i, slot: (0, i, 0, 0, 0))
+        for view in views
+    ]
     total = partial.shape[2]
     grad_spec = pl.BlockSpec((2, STEP_ROWS, total), lambda i, slot: (0, i, 0))
     own_spec = pl.BlockSpec((2, STEP_ROWS, total), lambda i, slot: (0, slot[0] * parts + i, 0))
-    next_param, grad, moved = pl.pallas_call(
+    out_specs, out_shape = [], []
+    for place, view in enumerate(views):
+        out_specs += [param_specs[place], param_specs[place], moment_specs[place]]
+        out_shape += [
+            jax.ShapeDtypeStruct(one.shape, F32) for one in (view, view, moment_views[place])
+        ]
+    size = sum(view.size for view in views)
+    results = pl.pallas_call(
         kernel,
         grid_spec=pltpu.PrefetchScalarGridSpec(
             num_scalar_prefetch=1,
             grid=(parts,),
-            in_specs=[param_spec, moment_spec, own_spec, grad_spec, grad_spec],
-            out_specs=[param_spec, param_spec, moment_spec],
+            in_specs=[*param_specs, *moment_specs, own_spec, grad_spec, grad_spec],
+            out_specs=out_specs,
         ),
-        out_shape=[
-            jax.ShapeDtypeStruct(view.shape, F32),
-            jax.ShapeDtypeStruct(view.shape, F32),
-            jax.ShapeDtypeStruct(moment_view.shape, F32),
-        ],
+        out_shape=out_shape,
         compiler_params=kernel_params(),
-        cost_estimate=cost(20 * view.size, 40 * view.size),
-    )(slot, view, moment_view, partial, *arrived)
-    return [row_unview(kind, one) for one in (next_param, grad, moved)]
+        cost_estimate=cost(20 * size, 40 * size),
+    )(slot, *views, *moment_views, partial, *arrived)
+    return [
+        [row_unview(kind, one) for one in results[3 * place : 3 * place + 3]]
+        for place, kind in enumerate(kinds)
+    ]
 
 
 def adam_modulation(param, moments, rows, table):
@@ -222,6 +239,14 @@
     return pl.BlockSpec(shape, lambda j: (0,) * len(shape))
 
 
+def arrivals_of(refs):
+    count = len(refs) - 1
+    half_way = count // 2
+    offsets = [offset for offset in range(count) if offset != half_way]
+    moves = [(offset, ref, 0, 2) for offset, ref in zip(offsets, refs)]
+    return moves + [(half_way, refs[-2], 0, 1), (half_way, refs[-1], 1, 1)]
+
+
 def matmul_rows(acts, blocks, slots, span, epilogue, extras, extra_specs, out_types, out_specs):
     rows, depth = acts.shape
     count = len(blocks)
@@ -234,12 +259,14 @@
         block_refs, refs = refs[:count], refs[count:]
         refs, weight, arrivals = refs[:-2], refs[-2], refs[-1]
 
+        moves = arrivals_of(block_refs)
+
         def copy(index, part):
+            offset, ref, stream, streams = moves[index]
+            row = pl.multiple_of(slots_ref[offset] * height, height)
             return pltpu.make_async_copy(
-                block_refs[index].at[:, :, pl.ds(first + part * tile, tile)],
-                weight.at[
-                    part, :, pl.ds(pl.multiple_of(slots_ref[index] * height, height), height), :
-                ],
+                ref.at[:, :, pl.ds(first + part * tile, tile)],
+                weight.at[part, pl.ds(stream, streams), pl.ds(row, height), :],
                 arrivals.at[part, index],
             )
 
@@ -374,24 +401,29 @@
     rows, depth = acts.shape
     count = len(blocks)
     height = blocks[0].shape[1]
-    share = count // 4
+    share = (count - 1) // 4
     tile = share * height
 
     def kernel(slots_ref, acts_ref, *refs):
         block_refs, (*out_refs, weight, arrivals) = refs[:count], refs[count:]
 
+        moves = arrivals_of(block_refs)
+
         def copy(index):
-            slot = slots_ref[index]
+            offset, ref, stream, streams = moves[index]
+            slot = slots_ref[offset]
             row = pl.multiple_of(slot % share * height, height)
             return pltpu.make_async_copy(
-                block_refs[index].at[:, :, pl.ds(span[0], depth)],
-                weight.at[slot // share // 2, :, pl.ds(row, height), :],
+                ref.at[:, :, pl.ds(span[0], depth)],
+                weight.at[slot // share // 2, pl.ds(stream, streams), pl.ds(row, height), :],
                 arrivals.at[index],
             )
 
         def each(action, wanted):
             for index in range(count):
-                pl.when(wanted(slots_ref[index] // share))(lambda index=index: action(copy(index)))
+                pl.when(wanted(slots_ref[moves[index][0]] // share))(
+                    lambda index=index: action(copy(index))
+                )
 
         step = pl.program_id(0)
 
@@ -635,8 +667,7 @@
     far = [(device, device ^ 2) for device in range(col_count)]
     across = [(device, device ^ 3) for device in range(col_count)]
     share = row_count // col_count
-    long_way = row_count // 2
-    short_way = row_count - 1 - long_way
+    half_way = row_count // 2
 
     slots = [
         [
@@ -689,41 +720,24 @@
         )
 
     class Ring:
-        def __init__(self, order_of_steps, slot_row, hops):
+        def __init__(self, order_of_steps, slot_row):
             self.steps = order_of_steps
             self.slot_row = slot_row
-            self.hops = dict(zip((1, -1), hops))
+            self.hops = {1: half_way, -1: half_way}
             self.done = {1: 0, -1: 0}
             self.held = {}
 
-        def send(self, ways=(1, -1)):
-            for way in ways:
-                if self.done[way] < self.hops[way]:
-                    (value,) = self.steps.tie(self.held[way])
-                    pairs = ahead if way == 1 else behind
-                    self.held[way] = lax.ppermute(value, "rows", pairs)
-
-        def land(self, ways=(1, -1)):
-            here = [way for way in ways if self.done[way] < self.hops[way]]
-            if not here:
-                return
-            values = self.steps.tie(*[self.held[way] for way in here])
-            self.steps.mark(*values)
-            for way, value in zip(here, values):
-                self.held[way] = value
-                self.done[way] += 1
-                self.take(way)
+        def send(self, way):
+            (value,) = self.steps.tie(self.held[way])
+            self.held[way] = lax.ppermute(value, "rows", ahead if way == 1 else behind)
+
+        def land(self, way, value):
+            self.held[way] = value
+            self.done[way] += 1
+            self.take(way)
 
         def left(self):
             return max(self.hops[way] - self.done[way] for way in (1, -1))
-
-        def step(self, ways=(1, -1)):
-            self.land(ways)
-            self.send(ways)
-
-        def finish(self):
-            while self.left():
-                self.step()
 
         def slot(self, offset):
             return self.slot_row[offset % row_count]
@@ -740,56 +754,79 @@
                 queue[place_at:place_at] = [ring] * ring.hops[way]
 
         def tick(self):
-            landed = list(self.flying.items())
-            if landed:
-                steps = landed[0][1].steps
-                values = steps.tie(*[ring.held[way] for way, ring in landed])
+            flying, self.flying = list(self.flying.items()), {}
+            if flying:
+                steps = flying[0][1].steps
+                values = steps.tie(*[ring.held[way] for way, ring in flying])
                 steps.mark(*values)
-                for (way, ring), value in zip(landed, values):
-                    ring.held[way] = value
-                    ring.done[way] += 1
-                for way, ring in landed:
-                    ring.take(way)
-            self.flying = {}
+                for (way, ring), value in zip(flying, values):
+                    ring.land(way, value)
             for way in (1, -1):
                 if self.queue[way]:
                     self.flying[way] = self.queue[way].pop(0)
-                    self.flying[way].send((way,))
+                    self.flying[way].send(way)
 
         def until(self, ring, left=0):
             while ring.left() > left:
                 self.tick()
 
     class RingGather(Ring):
-        def __init__(self, order_of_steps, slot_row, block, hops):
-            super().__init__(order_of_steps, slot_row, hops)
+        def __init__(self, order_of_steps, slot_row, block):
+            super().__init__(order_of_steps, slot_row)
             self.blocks = [block] * row_count
+            self.halves = {}
             self.held = {1: block, -1: block}
 
         def take(self, way):
+            if self.done[way] == half_way:
+                self.halves[way] = self.held[way]
+                return
             self.blocks[-way * self.done[way] % row_count] = self.held[way]
+            if self.done[way] == half_way - 1:
+                stream = 0 if way == 1 else 1
+                self.held[way] = self.held[way][stream : stream + 1]
+
+        def arrays(self):
+            whole_blocks = self.blocks[:half_way] + self.blocks[half_way + 1 :]
+            return [*whole_blocks, self.halves[1], self.halves[-1]]
 
     class RingScatter(Ring):
-        def __init__(self, order_of_steps, slot_row, partial, hops):
-            super().__init__(order_of_steps, slot_row, hops)
+        def __init__(self, order_of_steps, slot_row, partial, long_way=None):
+            super().__init__(order_of_steps, slot_row)
             self.partial = partial
             self.height = partial.shape[1] // row_count
-            self.held = {way: self.part(way * self.hops[way]) for way in (1, -1)}
-
-        def part(self, offset):
+            self.halved = long_way is None
+            if self.halved:
+                starts = (self.part(half_way, 0, 1), self.part(-half_way, 1, 1))
+            else:
+                self.hops[-long_way] -= 1
+                starts = [self.part(way * self.hops[way]) for way in (1, -1)]
+            starts = self.steps.tie(*starts)
+            self.steps.mark(*starts)
+            self.held = dict(zip((1, -1), starts))
+
+        def part(self, offset, stream=0, streams=2):
             return lax.dynamic_slice(
                 self.partial,
-                (0, self.slot(offset) * self.height, 0),
-                (2, self.height, self.partial.shape[2]),
+                (stream, self.slot(offset) * self.height, 0),
+                (streams, self.height, self.partial.shape[2]),
             )
 
         def take(self, way):
             left = self.hops[way] - self.done[way]
-            if left:
-                self.held[way] = narrow(
-                    self.held[way].astype(F32) + self.part(way * left).astype(F32)
-                )
-                self.steps.add(self.held[way])
+            if not left:
+                return
+            own = self.part(way * left).astype(F32)
+            arrived = self.held[way].astype(F32)
+            if self.halved and self.done[way] == 1:
+                stream = 0 if way == 1 else 1
+                with_arrived = own[stream : stream + 1] + arrived
+                other = own[1 - stream : 2 - stream]
+                pair = (with_arrived, other) if stream == 0 else (other, with_arrived)
+                self.held[way] = narrow(jnp.concatenate(pair))
+            else:
+                self.held[way] = narrow(own + arrived)
+            self.steps.add(self.held[way])
 
     def shards(
         x_img,
@@ -820,20 +857,19 @@
         )[0, 0]
         slot_list = [slot_row[offset] for offset in range(row_count)]
         steps = Order()
-        more_ahead, more_behind = ((long_way, short_way), (short_way, long_way))
-
-        def gather(block, hops):
-            return RingGather(steps, slot_list, block, hops)
-
-        def scatter(partial, hops):
-            return RingScatter(steps, slot_list, partial, hops)
-
-        def update(kind, ring, param, moments):
+
+        def gather(block):
+            return RingGather(steps, slot_list, block)
+
+        def scatter(partial, long_way=None):
+            return RingScatter(steps, slot_list, partial, long_way)
+
+        def update(kinds, ring, params, moments):
             return steps.run(
-                lambda *values: adam_rows(
-                    kind, *values[:2], ring.slot(0).reshape(1), values[2], values[3:]
+                lambda params, moments, *values: adam_rows(
+                    kinds, params, moments, ring.slot(0).reshape(1), values[0], values[1:]
                 ),
-                param,
+                params,
                 moments,
                 ring.partial,
                 ring.held[1],
@@ -864,7 +900,7 @@
 
         def run(step, acts, ring, span, *rest):
             return steps.run(
-                lambda acts, *rest: step(acts, ring.blocks, slot_row, span, *rest), acts, *rest
+                lambda acts, *rest: step(acts, ring.arrays(), slot_row, span, *rest), acts, *rest
             )
 
         def weight_part(outer, inner, *rest):
@@ -915,25 +951,19 @@
         mod_parts = lax.all_to_all(mod_terms, "rows", 0, 0, tiled=True)
         first_local = travel_rows(("triple", "attended"), (w_qkv, w_proj))
         steps.mark(mod_parts, first_local)
-        ring_first = queued(gather(first_local, more_ahead))
+        ring_first = queued(gather(first_local))
         lanes.tick()
         modulation = jnp.sum(mod_parts, axis=0) + biases[:, 0:6]
         mod_around = send_around(modulation)
-        ring_up = queued(
-            gather(steps.run(lambda w: travel_rows(("hidden",), (w,)), w_up), more_behind)
-        )
-        cotangent_round = steps.run(join_tokens, back_img, back_txt)
         lanes.tick()
         modulation_full = jnp.concatenate(land_around(mod_around), axis=-1)
         source_parts = middle_width(source_parts)
-        cotangent_parts = start_width(cotangent_round)
         source_full = end_width(source_parts).astype(F32)
         scale_one, gate_one, scale_two, gate_two = [
             per_token(modulation[:, slot_index]) for slot_index in (1, 2, 4, 5)
         ]
         shift_two = per_token(modulation[:, 3])
         source = source_round.astype(F32)
-        cotangent = cotangent_round.astype(F32)
 
         def first_norm(full, full_modulation):
             center, inverse = row_stats(
@@ -947,9 +977,16 @@
             return center, inverse, normed
 
         center_one, inverse_one, normed_one = steps.run(first_norm, source_full, modulation_full)
+        cotangent_round = steps.run(join_tokens, back_img, back_txt)
+        cotangent = cotangent_round.astype(F32)
         unit_one = (source - center_one) * inverse_one
+        lanes.tick()
+        cotangent_parts = start_width(cotangent_round)
+        ring_up = queued(
+            gather(steps.run(lambda w: travel_rows(("hidden",), (w,)), w_up))
+        )
         ring_down = queued(
-            gather(steps.run(lambda w: travel_rows(("hidden",), (w,)), w_down), more_ahead)
+            gather(steps.run(lambda w: travel_rows(("hidden",), (w,)), w_down))
         )
         lanes.tick()
         cotangent_parts = middle_width(cotangent_parts)
@@ -1003,7 +1040,7 @@
         )
         lanes.tick()
         ring_grad_down = queued(
-            scatter(weight_part(lowered_full, hidden_act), more_behind)
+            scatter(weight_part(lowered_full, hidden_act), 1)
         )
         lanes.until(ring_down)
         hidden_round, hidden_sums = run(
@@ -1011,10 +1048,10 @@
         )
         halves = send_halves(hidden_round, ring_up, hidden_span, lanes.tick)
         own, away = send_away(*halves)
-        lanes.tick()
         ring_grad_up = queued(
-            scatter(weight_part(normed_two, hidden_round), more_ahead)
-        )
+            scatter(weight_part(normed_two, hidden_round), -1)
+        )
+        lanes.tick()
 
         def back_sums(grad_unit, unit_rows):
             return jnp.stack([jnp.sum(grad_unit, axis=1), jnp.sum(grad_unit * unit_rows, axis=1)])
@@ -1046,9 +1083,6 @@
         lanes.tick()
         projected_full = end_width(middle_width(projected_parts))
         grad_attended = run(attended_gradient, projected_full, ring_first, attended_span)
-        partial_first = weight_part(projected_full, attended, 3 * width)
-        own_lowered, away_lowered = send_away(lowered_kept, arriving)
-        lanes.tick()
         so_far = ()
         for pair in range(pairs):
             so_far = steps.run(
@@ -1058,22 +1092,27 @@
                 grad_attended,
                 *so_far,
             )
-            if pair == pairs - 2:
+            if pair == 0:
+                own_lowered, away_lowered = send_away(lowered_kept, arriving)
                 lanes.tick()
+        lowered_away = away_lowered.land()
+        lanes.tick()
         triple_round, triple_sums = so_far
-        partial_first = weight_part(normed_one, triple_round, 0, partial_first)
-        ring_grad_first = queued(scatter(partial_first, more_behind))
-        lanes.tick()
-        halves = send_halves(triple_round, ring_first, triple_span)
+        partial_first = weight_part(normed_one, triple_round, 0)
+        partial_first = weight_part(projected_full, attended, 3 * width, partial_first)
+        ring_grad_first = queued(scatter(partial_first), ring_grad_up)
+        halves = send_halves(triple_round, ring_first, triple_span, lanes.tick)
         own, away = send_away(*halves)
-        lowered = own_lowered + away_lowered.land().astype(F32) + per_token(biases[:, 13])
-        output = narrow(residual + gate_two * lowered)
+        lanes.tick()
+        ((next_down, grad_down, moved_down),) = update(
+            ("hidden",), ring_grad_down, (w_down,), (moments_down,)
+        )
+        lanes.until(ring_grad_up)
+        ((next_up, grad_up, moved_up),) = update(
+            ("hidden",), ring_grad_up, (w_up,), (moments_up,)
+        )
+        lowered = own_lowered + lowered_away.astype(F32) + per_token(biases[:, 13])
         grad_lowered = gate_two * cotangent
-        steps.add(output)
-        next_down, grad_down, moved_down = update(
-            "hidden", ring_grad_down, w_down, moments_down
-        )
-        lanes.tick()
         grad_normed_one = own + away.land().astype(F32)
         grad_unit_one = grad_normed_one * (1.0 + scale_one)
         sums = back_sums(grad_unit_one, unit_one)
@@ -1110,21 +1149,27 @@
         silu_terms = jnp.einsum("bsic,dsic->bd", table_round, mod_round, preferred_element_type=F32)
         steps.mark(silu_terms)
         silu_around = send_around(silu_terms)
-        lanes.until(ring_grad_up)
-        next_up, grad_up, moved_up = update("hidden", ring_grad_up, w_up, moments_up)
-        lanes.until(ring_grad_first, 1)
         grad_silu = total_around(silu_around)
         sigmoid_cond = jax.nn.sigmoid(cond)
         grad_cond = grad_silu * sigmoid_cond * (1.0 + cond * (1.0 - sigmoid_cond))
+        next_bias, first_bias, second_bias = adam_step(biases, moments_bias, grad_bias)
+        steps.add(next_bias, first_bias, second_bias, grad_cond)
         next_mod, grad_mod, first_mod, second_mod = steps.run(
             adam_modulation, w_mod, moments_mod, silu_cond, table_round
         )
-        next_bias, first_bias, second_bias = adam_step(biases, moments_bias, grad_bias)
-        steps.add(next_bias, first_bias, second_bias, grad_cond)
+        lanes.until(ring_grad_first, 1)
+        own_lowered, lowered_away = steps.tie(own_lowered, lowered_away)
+        output = narrow(
+            residual
+            + gate_two * (own_lowered + lowered_away.astype(F32) + per_token(biases[:, 13]))
+        )
+        steps.add(output)
         lanes.until(ring_grad_first)
-        next_qkv, grad_qkv, moved_qkv = update("triple", ring_grad_first, w_qkv, moments_qkv)
-        next_proj, grad_proj, moved_proj = update(
-            "attended", ring_grad_first, w_proj, moments_proj
+        (next_qkv, grad_qkv, moved_qkv), (next_proj, grad_proj, moved_proj) = update(
+            ("triple", "attended"),
+            ring_grad_first,
+            (w_qkv, w_proj),
+            (moments_qkv, moments_proj),
         )
         return (
             output[None, :IMAGE_TOKENS],

time: 750 us -> 733 us (0.977)
  waiting for transfers between devices: 234 us -> 211 us
    ppermute x39, waiting for transfers between devices: 32.3 us -> 12.7 us  [__init__(): self.value = lax.ppermute(value, 'cols', pairs)]
    ppermute x42 -> x46, starting transfers between devices: 44.6 us -> 49.4 us  [send(): self.held[way] = lax.ppermute(value, 'rows', ahead if way == 1 else behind)]
    ppermute x42 -> x46, waiting for transfers between devices: 195 us -> 191 us  [send(): self.held[way] = lax.ppermute(value, 'rows', ahead if way == 1 else behind)]
    convert_element_type x18 -> x17, other arithmetic: 60.1 us -> 55.6 us  [narrow(): return values.astype(jnp.bfloat16)]
    pallas_call x4 -> x3, Pallas kernels: 37.4 us -> 33.7 us  [adam_rows(): pl.pallas_call(kernel, grid_spec=pltpu.PrefetchScalarGridSpec(num_scalar_...]
  transfers between devices with their start and end apart: 83 -> 87, of which waited for: 35 -> 39; matrix products, arithmetic and copies ran while one was open for 14% -> 14% of each run, Pallas kernels for 36% -> 38%
where the time goes in v3:
time: 733 us; the launch traced here: 722 us
  Pallas kernels  283 us (39%)
  waiting for transfers between devices  211 us (29%)
  other arithmetic  96.7 us (13%)
  starting transfers between devices  81.9 us (11%)
  local copies, waits for them, and re-layouts  39.3 us (5%)
    ppermute x46, waiting for transfers between devices, send(): self.held[way] = lax.ppermute(value, 'rows', ahead if way == 1 else behind)  191 us
    pallas_call x8, Pallas kernels, matmul_back(): pl.pallas_call(kernel, grid=(2,), in_specs=[pl.BlockSpec(memory_space=plt...  64.7 us
    convert_element_type x17, other arithmetic, narrow(): return values.astype(jnp.bfloat16)  55.6 us
    pallas_call x4, Pallas kernels, matmul_rows(): pl.pallas_call(kernel, grid=(tiles,), in_specs=[pl.BlockSpec(memory_space...  49.5 us
    ppermute x46, starting transfers between devices, send(): self.held[way] = lax.ppermute(value, 'rows', ahead if way == 1 else behind)  49.4 us
    pallas_call x3, Pallas kernels, attention_back(): pl.pallas_call(kernel, grid=(last - first,), in_specs=[pl.BlockSpec((rows...  40.3 us
    pallas_call x4, Pallas kernels, weight_gradient(): pl.pallas_call(kernel, grid=(height // tile,), in_specs=[column_spec(rows...  37.4 us
    pallas_call x3, Pallas kernels, adam_rows(): pl.pallas_call(kernel, grid_spec=pltpu.PrefetchScalarGridSpec(num_scalar_...  33.7 us
  transfers between devices with their start and end apart: 87, of which 39 were waited for; matrix products, arithmetic and copies ran while one was open for 14% of the time, Pallas kernels for 38%

profile of v3, /device:TPU:0, one launch (start us, length us, event | category | flops | bytes accessed | tf_op | source)
XLA Modules:
  0.0 722.0 jit_solution(17405158994514678876)
XLA Ops:
  12.7 7.3 %all-to-all-start = ((f32[8,2,6,384]{3,1,2,0:T(2,128)}), f32[8,2,6,384]{3,1,2,0:T(2,128)S(1)}, u32[]{:S(2)}, u32[]{:S(2)}) async-start(f32[8,2,6,384]{3,1,2,0:T(2,128)} %copy.113), calls=%async_computation | async-start | bytes 294912 | tf_op jit(solution)/shard_map/all_to_all | solution.py:951
  19.9 4.8 shard_map.369.refs_0_
  31.7 22.2 %collective-permute-done.6.refs_1_ = bf16[2,192,1536]{2,1,0:T(8,128)(2,1)S(1)} collective-permute-done((bf16[2,192,1536]{2,1,0:T(8,128)(2,1)}, bf16[2,192,1536]{2,1,0:T(8,128)(2,1)S(1)}, u32[]{:S(2)}, u32[]{:S(2)}) %collective-permute-start.6) | collective-permute-done | bytes 1179680 | tf_op jit(solution)/shard_map/ppermute | solution.py:732
  64.5 9.9 %add_convert_fusion.acts_ref.outer_ref = bf16[1184,1536]{1,0:T(8,128)(2,1)} fusion(f32[1184,1536]{1,0:T(8,128)S(1)} %maximum_convert_fusion, f32[1536]{0:T(1024)S(1)} %get-tuple-element.740, f32[1536]{0:T(1024)S(1)} %get-tuple-element.741, f32[1536]{0:T(1024)S(1)} %get-tuple-element.742, f32[1536]{0:T(1024)S(1)} %get-tuple-element.739, ...), kind=kLoop, calls=%fused_computation.1 | loop fusion | flops 14548992 | bytes 10946976 | tf_op jit(solution)/shard_map/convert_element_type | solution.py:34
  74.4 6.2 concatenate.35
  80.6 5.4 collective-permute-done.8.refs_5_
  89.3 4.8 shard_map.370.refs_0_
  94.1 4.8 shard_map.371.refs_0_
  98.8 14.5 %collective-permute-done.12.refs_4_ = bf16[2,192,1536]{2,1,0:T(8,128)(2,1)S(1)} collective-permute-done((bf16[2,192,1536]{2,1,0:T(8,128)(2,1)}, bf16[2,192,1536]{2,1,0:T(8,128)(2,1)S(1)}, u32[]{:S(2)}, u32[]{:S(2)}) %collective-permute-start.12) | collective-permute-done | bytes 1179680 | tf_op jit(solution)/shard_map/ppermute | solution.py:732
  116.3 11.0 %collective-permute-done.16.refs_8_ = bf16[1,192,1536]{2,1,0:T(8,128)(2,1)S(1)} collective-permute-done((bf16[1,192,1536]{2,1,0:T(8,128)(2,1)S(1)}, bf16[1,192,1536]{2,1,0:T(8,128)(2,1)S(1)}, u32[]{:S(2)}, u32[]{:S(2)}) %collective-permute-start.16) | collective-permute-done | bytes 589856 | tf_op jit(solution)/shard_map/ppermute | solution.py:732
  134.7 11.1 %shard_map.372.triple_ref = bf16[1184,1152]{1,0:T(8,128)(2,1)} custom-call(s32[8]{0:T(128)} %fusion.32.slots_ref, bf16[1184,1536]{1,0:T(8,128)(2,1)} %add_convert_fusion.acts_ref.outer_ref, bf16[2,192,1536]{2,1,0:T(8,128)(2,1)} %shard_map.369.refs_0_, bf16[2,192,1536]{2,1,0:T(8,128)(2,1)} %copy-done.2, bf16[2,192,1536]{2,1,0:T(8,128)(2,1)} %collective-permute-done.9.refs_2_, ...), custom_call_target="tpu_custom_call" | custom-call | flops 4190109 | bytes 13443 | tf_op jit(solution)/shard_map/pallas_call | solution.py:294
  145.8 9.5 %shard_map.373 = (bf16[1184,384]{1,0:T(8,128)(2,1)}, f32[3,2,1184]{2,1,0:T(2,128)}) custom-call(bf16[1184,1152]{1,0:T(8,128)(2,1)} %shard_map.372.triple_ref), custom_call_target="tpu_custom_call" | custom-call | flops 8613003 | bytes 10911 | tf_op jit(solution)/shard_map/pallas_call | solution.py:536
  157.8 9.5 %shard_map.374 = (bf16[1184,384]{1,0:T(8,128)(2,1)}, f32[3,2,1184]{2,1,0:T(2,128)}) custom-call(bf16[1184,1152]{1,0:T(8,128)(2,1)} %shard_map.372.triple_ref, bf16[1184,384]{1,0:T(8,128)(2,1)} %get-tuple-element.373.refs_0_, f32[3,2,1184]{2,1,0:T(2,128)} %get-tuple-element.374.refs_1_), custom_call_target="tpu_custom_call", output_to_operand_aliasing={{0}: (1, {}), {1}: (2, {})} | custom-call | flops 8613003 | bytes 10911 | tf_op jit(solution)/shard_map/pallas_call | solution.py:536
  167.3 9.6 %shard_map.375 = (bf16[1184,384]{1,0:T(8,128)(2,1)}, f32[3,2,1184]{2,1,0:T(2,128)}) custom-call(bf16[1184,1152]{1,0:T(8,128)(2,1)} %shard_map.372.triple_ref, bf16[1184,384]{1,0:T(8,128)(2,1)} %get-tuple-element.378.refs_0_, f32[3,2,1184]{2,1,0:T(2,128)} %get-tuple-element.379.refs_1_), custom_call_target="tpu_custom_call", output_to_operand_aliasing={{0}: (1, {}), {1}: (2, {})} | custom-call | flops 8613003 | bytes 10911 | tf_op jit(solution)/shard_map/pallas_call | solution.py:536
  176.9 5.2 shard_map.376
  182.7 5.3 shard_map.377
  193.7 22.3 %collective-permute-done.24.refs_4_ = bf16[2,192,1536]{2,1,0:T(8,128)(2,1)S(1)} collective-permute-done((bf16[2,192,1536]{2,1,0:T(8,128)(2,1)S(1)}, bf16[2,192,1536]{2,1,0:T(8,128)(2,1)S(1)}, u32[]{:S(2)}, u32[]{:S(2)}) %collective-permute-start.24) | collective-permute-done | bytes 1179680 | tf_op jit(solution)/shard_map/ppermute | solution.py:732
  225.0 11.1 %collective-permute-done.28.refs_8_ = bf16[1,192,1536]{2,1,0:T(8,128)(2,1)S(1)} collective-permute-done((bf16[1,192,1536]{2,1,0:T(8,128)(2,1)S(1)}, bf16[1,192,1536]{2,1,0:T(8,128)(2,1)S(1)}, u32[]{:S(2)}, u32[]{:S(2)}) %collective-permute-start.28) | collective-permute-done | bytes 589856 | tf_op jit(solution)/shard_map/ppermute | solution.py:732
  241.4 22.3 %collective-permute-done.34.refs_1_ = bf16[2,192,1536]{2,1,0:T(8,128)(2,1)S(1)} collective-permute-done((bf16[2,192,1536]{2,1,0:T(8,128)(2,1)S(1)}, bf16[2,192,1536]{2,1,0:T(8,128)(2,1)S(1)}, u32[]{:S(2)}, u32[]{:S(2)}) %collective-permute-start.34) | collective-permute-done | bytes 1179680 | tf_op jit(solution)/shard_map/ppermute | solution.py:732
  272.9 17.5 %shard_map.378 = (bf16[1184,1536]{1,0:T(8,128)(2,1)}, f32[1184,1536]{1,0:T(8,128)}) custom-call(s32[8]{0:T(128)} %fusion.32.slots_ref, bf16[1184,1536]{1,0:T(8,128)(2,1)} %pad_maximum_fusion.1.acts_ref.outer_ref, bf16[2,192,1536]{2,1,0:T(8,128)(2,1)} %shard_map.370.refs_0_, bf16[2,192,1536]{2,1,0:T(8,128)(2,1)} %collective-permute-done.18.refs_1_, ...), custom_call_target="tpu_custom_call" | custom-call | flops 5586812 | bytes 16711 | tf_op jit(solution)/shard_map/pallas_call | solution.py:294
  290.4 5.3 collective-permute-done.36.refs_5_
  301.5 10.9 %shard_map.379.refs_2_ = bf16[2,1536,1536]{2,1,0:T(8,128)(2,1)} custom-call(bf16[1184,1536]{1,0:T(8,128)(2,1)} %multiply_convert_fusion.outer_ref.acts_ref, bf16[1184,1536]{1,0:T(8,128)(2,1)} %get-tuple-element.490.inner_ref.acts_ref), custom_call_target="tpu_custom_call" | custom-call | flops 5586812 | bytes 16711 | tf_op jit(solution)/shard_map/pallas_call | solution.py:483
  315.5 8.3 %collective-permute-done.38.refs_4_ = bf16[2,192,1536]{2,1,0:T(8,128)(2,1)} collective-permute-done((bf16[2,192,1536]{2,1,0:T(8,128)(2,1)}, bf16[2,192,1536]{2,1,0:T(8,128)(2,1)}, u32[]{:S(2)}, u32[]{:S(2)}) %collective-permute-start.38) | collective-permute-done | bytes 1179680 | tf_op jit(solution)/shard_map/ppermute | solution.py:732
  328.7 10.9 %collective-permute-done.41.refs_8_ = bf16[1,192,1536]{2,1,0:T(8,128)(2,1)S(1)} collective-permute-done((bf16[1,192,1536]{2,1,0:T(8,128)(2,1)S(1)}, bf16[1,192,1536]{2,1,0:T(8,128)(2,1)S(1)}, u32[]{:S(2)}, u32[]{:S(2)}) %collective-permute-start.41) | collective-permute-done | bytes 589856 | tf_op jit(solution)/shard_map/ppermute | solution.py:732
  344.5 14.2 %shard_map.380 = (bf16[1184,1536]{1,0:T(8,128)(2,1)}, f32[2,1536]{1,0:T(2,128)}) custom-call(s32[8]{0:T(128)} %fusion.32.slots_ref, bf16[1184,1536]{1,0:T(8,128)(2,1)} %multiply_convert_fusion.outer_ref.acts_ref, bf16[2,192,1536]{2,1,0:T(8,128)(2,1)} %shard_map.371.refs_0_, bf16[2,192,1536]{2,1,0:T(8,128)(2,1)} %copy-done.16, ...), custom_call_target="tpu_custom_call" | custom-call | flops 5586812 | bytes 16711 | tf_op jit(solution)/shard_map/pallas_call | solution.py:294
  358.7 9.4 %shard_map.381 = (bf16[1184,384]{1,0:T(8,128)(2,1)}, bf16[1184,384]{1,0:T(8,128)(2,1)}) custom-call(s32[8]{0:T(128)} %fusion.32.slots_ref, bf16[1184,1536]{1,0:T(8,128)(2,1)} %get-tuple-element.473.acts_ref.inner_ref, bf16[2,192,1536]{2,1,0:T(8,128)(2,1)} %shard_map.370.refs_0_, bf16[2,192,1536]{2,1,0:T(8,128)(2,1)} %collective-permute-done.18.refs_1_, ...), custom_call_target="tpu_custom_call" | custom-call | flops 2793406 | bytes 10174 | tf_op jit(solution)/shard_map/pallas_call | solution.py:448
  368.1 4.4 add_convert_fusion.13
  377.3 9.4 %shard_map.382 = (bf16[1184,384]{1,0:T(8,128)(2,1)}, bf16[1184,384]{1,0:T(8,128)(2,1)}) custom-call(s32[8]{0:T(128)} %fusion.32.slots_ref, bf16[1184,1536]{1,0:T(8,128)(2,1)} %get-tuple-element.473.acts_ref.inner_ref, bf16[2,192,1536]{2,1,0:T(8,128)(2,1)} %shard_map.370.refs_0_, bf16[2,192,1536]{2,1,0:T(8,128)(2,1)} %collective-permute-done.18.refs_1_, ...), custom_call_target="tpu_custom_call" | custom-call | flops 2793406 | bytes 10174 | tf_op jit(solution)/shard_map/pallas_call | solution.py:448
  390.4 10.8 %shard_map.383.refs_2_ = bf16[2,1536,1536]{2,1,0:T(8,128)(2,1)} custom-call(bf16[1184,1536]{1,0:T(8,128)(2,1)} %pad_maximum_fusion.1.acts_ref.outer_ref, bf16[1184,1536]{1,0:T(8,128)(2,1)} %get-tuple-element.473.acts_ref.inner_ref), custom_call_target="tpu_custom_call" | custom-call | flops 5586812 | bytes 16711 | tf_op jit(solution)/shard_map/pallas_call | solution.py:483
  417.7 15.7 %collective-permute-done.50 = bf16[2,192,1536]{2,1,0:T(8,128)(2,1)S(1)} collective-permute-done((bf16[2,192,1536]{2,1,0:T(8,128)(2,1)S(1)}, bf16[2,192,1536]{2,1,0:T(8,128)(2,1)S(1)}, u32[]{:S(2)}, u32[]{:S(2)}) %collective-permute-start.50) | collective-permute-done | bytes 1179680 | tf_op jit(solution)/shard_map/ppermute | solution.py:732
  446.7 9.4 %shard_map.384 = (bf16[1184,384]{1,0:T(8,128)(2,1)}, bf16[1184,384]{1,0:T(8,128)(2,1)}) custom-call(s32[8]{0:T(128)} %fusion.32.slots_ref, bf16[1184,1536]{1,0:T(8,128)(2,1)} %get-tuple-element.490.inner_ref.acts_ref, bf16[2,192,1536]{2,1,0:T(8,128)(2,1)} %shard_map.371.refs_0_, bf16[2,192,1536]{2,1,0:T(8,128)(2,1)} %copy-done.16, ...), custom_call_target="tpu_custom_call" | custom-call | flops 2793406 | bytes 10174 | tf_op jit(solution)/shard_map/pallas_call | solution.py:448
  456.2 9.5 %shard_map.385 = (bf16[1184,384]{1,0:T(8,128)(2,1)}, bf16[1184,384]{1,0:T(8,128)(2,1)}) custom-call(s32[8]{0:T(128)} %fusion.32.slots_ref, bf16[1184,1536]{1,0:T(8,128)(2,1)} %get-tuple-element.490.inner_ref.acts_ref, bf16[2,192,1536]{2,1,0:T(8,128)(2,1)} %shard_map.371.refs_0_, bf16[2,192,1536]{2,1,0:T(8,128)(2,1)} %copy-done.16, ...), custom_call_target="tpu_custom_call" | custom-call | flops 2793406 | bytes 10174 | tf_op jit(solution)/shard_map/pallas_call | solution.py:448
  477.3 6.7 shard_map.386.grad_ref
  484.0 13.3 %shard_map.387 = (bf16[1184,1152]{1,0:T(8,128)(2,1)}, f32[3,2,256]{2,1,0:T(2,128)}) custom-call(bf16[1184,1152]{1,0:T(8,128)(2,1)} %shard_map.372.triple_ref, f32[3,2,1184]{2,1,0:T(2,128)} %get-tuple-element.529.total_ref, bf16[1184,384]{1,0:T(8,128)(2,1)} %shard_map.386.grad_ref), custom_call_target="tpu_custom_call" | custom-call | flops 21532508 | bytes 10911 | tf_op jit(solution)/shard_map/pallas_call | solution.py:611
  508.1 13.3 %shard_map.388 = (bf16[1184,1152]{1,0:T(8,128)(2,1)}, f32[3,2,256]{2,1,0:T(2,128)}) custom-call(bf16[1184,1152]{1,0:T(8,128)(2,1)} %shard_map.372.triple_ref, f32[3,2,1184]{2,1,0:T(2,128)} %get-tuple-element.529.total_ref, bf16[1184,384]{1,0:T(8,128)(2,1)} %shard_map.386.grad_ref, ...), custom_call_target="tpu_custom_call", output_to_operand_aliasing={{0}: (3, {}), {1}: (4, {})} | custom-call | flops 21532508 | bytes 10911 | tf_op jit(solution)/shard_map/pallas_call | solution.py:611
  521.3 13.7 %shard_map.389 = (bf16[1184,1152]{1,0:T(8,128)(2,1)}, f32[3,2,256]{2,1,0:T(2,128)}) custom-call(bf16[1184,1152]{1,0:T(8,128)(2,1)} %shard_map.372.triple_ref, f32[3,2,1184]{2,1,0:T(2,128)} %get-tuple-element.529.total_ref, bf16[1184,384]{1,0:T(8,128)(2,1)} %shard_map.386.grad_ref, ...), custom_call_target="tpu_custom_call", output_to_operand_aliasing={{0}: (3, {}), {1}: (4, {})} | custom-call | flops 21532508 | bytes 10911 | tf_op jit(solution)/shard_map/pallas_call | solution.py:611
  544.6 9.8 %shard_map.390.refs_0_ = bf16[2,1536,1536]{2,1,0:T(8,128)(2,1)} custom-call(bf16[1184,1536]{1,0:T(8,128)(2,1)} %add_convert_fusion.acts_ref.outer_ref, bf16[1184,1152]{1,0:T(8,128)(2,1)} %get-tuple-element.556.inner_ref.acts_ref), custom_call_target="tpu_custom_call" | custom-call | flops 4190109 | bytes 13443 | tf_op jit(solution)/shard_map/pallas_call | solution.py:483
  554.3 5.9 shard_map.391.refs_4_
  563.1 8.3 %shard_map.392 = (bf16[1184,384]{1,0:T(8,128)(2,1)}, bf16[1184,384]{1,0:T(8,128)(2,1)}) custom-call(s32[8]{0:T(128)} %fusion.32.slots_ref, bf16[1184,1152]{1,0:T(8,128)(2,1)} %get-tuple-element.556.inner_ref.acts_ref, bf16[2,192,1536]{2,1,0:T(8,128)(2,1)} %shard_map.369.refs_0_, bf16[2,192,1536]{2,1,0:T(8,128)(2,1)} %copy-done.2, ...), custom_call_target="tpu_custom_call" | custom-call | flops 2095054 | bytes 8085 | tf_op jit(solution)/shard_map/pallas_call | solution.py:448
  575.3 8.2 %shard_map.393 = (bf16[1184,384]{1,0:T(8,128)(2,1)}, bf16[1184,384]{1,0:T(8,128)(2,1)}) custom-call(s32[8]{0:T(128)} %fusion.32.slots_ref, bf16[1184,1152]{1,0:T(8,128)(2,1)} %get-tuple-element.556.inner_ref.acts_ref, bf16[2,192,1536]{2,1,0:T(8,128)(2,1)} %shard_map.369.refs_0_, bf16[2,192,1536]{2,1,0:T(8,128)(2,1)} %copy-done.2, ...), custom_call_target="tpu_custom_call" | custom-call | flops 2095054 | bytes 8085 | tf_op jit(solution)/shard_map/pallas_call | solution.py:448
  594.0 11.1 %shard_map.394 = (f32[192,2,4,384]{3,2,1,0:T(4,128)}, f32[192,2,4,384]{3,2,1,0:T(4,128)}, f32[2,192,2,4,384]{4,3,2,1,0:T(4,128)}) custom-call(s32[1]{0:T(128)} %bitcast.17.slot_ref, f32[192,2,4,384]{3,2,1,0:T(4,128)} %refs_0_.2, f32[2,192,2,4,384]{4,3,2,1,0:T(4,128)} %refs_1_, bf16[2,1536,1536]{2,1,0:T(8,128)(2,1)} %shard_map.379.refs_2_, ...), custom_call_target="tpu_custom_call" | custom-call | flops 11796 | bytes 23592 | tf_op jit(solution)/shard_map/pallas_call | solution.py:170
  607.4 11.1 %shard_map.395 = (f32[192,2,4,384]{3,2,1,0:T(4,128)}, f32[192,2,4,384]{3,2,1,0:T(4,128)}, f32[2,192,2,4,384]{4,3,2,1,0:T(4,128)}) custom-call(s32[1]{0:T(128)} %bitcast.17.slot_ref, f32[192,2,4,384]{3,2,1,0:T(4,128)} %refs_0_.3, f32[2,192,2,4,384]{4,3,2,1,0:T(4,128)} %refs_1_.1, bf16[2,1536,1536]{2,1,0:T(8,128)(2,1)} %shard_map.383.refs_2_, ...), custom_call_target="tpu_custom_call" | custom-call | flops 11796 | bytes 23592 | tf_op jit(solution)/shard_map/pallas_call | solution.py:170
  624.1 7.4 %collective-permute-done.72 = bf16[2,192,1536]{2,1,0:T(8,128)(2,1)} collective-permute-done((bf16[2,192,1536]{2,1,0:T(8,128)(2,1)}, bf16[2,192,1536]{2,1,0:T(8,128)(2,1)}, u32[]{:S(2)}, u32[]{:S(2)}) %collective-permute-start.72) | collective-permute-done | bytes 1179680 | tf_op jit(solution)/shard_map/ppermute | solution.py:732
  632.6 4.4 add_convert_fusion.3
  645.5 4.9 all-to-all-done.1
  661.5 14.7 %shard_map.396 = (f32[192,6,2,384]{3,2,1,0:T(2,128)}, f32[192,6,2,384]{3,2,1,0:T(2,128)}, f32[192,6,2,384]{3,2,1,0:T(2,128)}, f32[192,6,2,384]{3,2,1,0:T(2,128)}) custom-call(bf16[192,8]{1,0:T(8,128)(2,1)} %bitcast.79, bf16[8,4608]{1,0:T(8,128)(2,1)} %bitcast.80, f32[192,6,2,384]{3,2,1,0:T(2,128)} %bitcast.69, f32[2,192,6,2,384]{4,3,2,1,0:T(2,128)} %bitcast.70), custom_call_target="tpu_custom_call" | custom-call | flops 17694 | bytes 35389 | tf_op jit(solution)/shard_map/pallas_call | solution.py:213
  688.2 20.4 %collective-permute-done.83.refs_5_ = bf16[2,192,1536]{2,1,0:T(8,128)(2,1)S(1)} collective-permute-done((bf16[2,192,1536]{2,1,0:T(8,128)(2,1)S(1)}, bf16[2,192,1536]{2,1,0:T(8,128)(2,1)S(1)}, u32[]{:S(2)}, u32[]{:S(2)}) %collective-permute-start.83) | collective-permute-done | bytes 1179680 | tf_op jit(solution)/shard_map/ppermute | solution.py:732
  710.0 11.5 %shard_map.397 = (f32[192,3,2,384]{3,2,1,0:T(2,128)}, f32[192,3,2,384]{3,2,1,0:T(2,128)}, f32[2,192,3,2,384]{4,3,2,1,0:T(2,128)}, f32[192,1,2,384]{3,2,1,0:T(2,1...) custom-call(s32[1]{0:T(128)} %bitcast.17.slot_ref, f32[192,3,2,384]{3,2,1,0:T(2,128)} %bitcast.72, ...), custom_call_target="tpu_custom_call" | custom-call | flops 11796 | bytes 23592 | tf_op jit(solution)/shard_map/pallas_call | solution.py:170
  (452 shorter events, 217.6 us)
Async XLA Ops:
  27.4 26.5 %collective-permute-start.6 = (bf16[2,192,1536]{2,1,0:T(8,128)(2,1)}, bf16[2,192,1536]{2,1,0:T(8,128)(2,1)S(1)}, u32[]{:S(2)}, u32[]{:S(2)}) collective-permute-start(bf16[2,192,1536]{2,1,0:T(8,128)(2,1)} %shard_map.369.refs_0_), channel_id=1, source_target_pairs={{8,0},{16,8},{24,16},{28,24},{20,28},{12,20},{4,12},{0,4},{9,1},{1... | collective-permute-start | bytes 3538952 | tf_op jit(solution)/shard_map/ppermute | solution.py:732
  27.7 26.2 %collective-permute-start.5 = (bf16[2,192,1536]{2,1,0:T(8,128)(2,1)}, bf16[2,192,1536]{2,1,0:T(8,128)(2,1)S(1)}, u32[]{:S(2)}, u32[]{:S(2)}) collective-permute-start(bf16[2,192,1536]{2,1,0:T(8,128)(2,1)} %shard_map.369.refs_0_), channel_id=1, source_target_pairs={{0,8},{8,16},{16,24},{24,28},{28,20},{20,12},{12,4},{4,0},{1,9},{9... | collective-permute-start | bytes 3538952 | tf_op jit(solution)/shard_map/ppermute | solution.py:732
  29.4 27.9 %collective-permute-start.1 = (bf16[1184,384]{1,0:T(8,128)(2,1)}, bf16[1184,384]{1,0:T(8,128)(2,1)}, u32[]{:S(2)}, u32[]{:S(2)}) collective-permute-start(bf16[1184,384]{1,0:T(8,128)(2,1)} %concatenate.32), channel_id=1, source_target_pairs={{0,2},{1,3},{2,0},{3,1},{4,6},{5,7},{6,4},{7,5},{8,10},{9,11},{10,... | collective-permute-start | bytes 2727944 | tf_op jit(solution)/shard_map/ppermute | solution.py:707
  31.0 22.9 %collective-permute-start.4 = (f32[2,6,384]{2,1,0:T(8,128)S(1)}, f32[2,6,384]{2,1,0:T(8,128)S(1)}, u32[]{:S(2)}, u32[]{:S(2)}) collective-permute-start(f32[2,6,384]{2,1,0:T(8,128)S(1)} %copy_add_fusion), channel_id=1, source_target_pairs={{0,1},{1,0},{2,3},{3,2},{4,5},{5,4},{6,7},{7,6},{8,9},{9,8},{10,11... | collective-permute-start | bytes 55304 | tf_op jit(solution)/shard_map/ppermute | solution.py:707
  31.1 22.8 %collective-permute-start.3 = (f32[2,6,384]{2,1,0:T(8,128)S(1)}, f32[2,6,384]{2,1,0:T(8,128)S(1)}, u32[]{:S(2)}, u32[]{:S(2)}) collective-permute-start(f32[2,6,384]{2,1,0:T(8,128)S(1)} %copy_add_fusion), channel_id=1, source_target_pairs={{0,2},{1,3},{2,0},{3,1},{4,6},{5,7},{6,4},{7,5},{8,10},{9,11},{10,... | collective-permute-start | bytes 55304 | tf_op jit(solution)/shard_map/ppermute | solution.py:707
  57.9 28.1 %collective-permute-start.8 = (bf16[2,192,1536]{2,1,0:T(8,128)(2,1)S(1)}, bf16[2,192,1536]{2,1,0:T(8,128)(2,1)}, u32[]{:S(2)}, u32[]{:S(2)}) collective-permute-start(bf16[2,192,1536]{2,1,0:T(8,128)(2,1)S(1)} %collective-permute-done.5.refs_6_), channel_id=1, source_target_pairs={{0,8},{8,16},{16,24},{24,28},{28,20},{20,12},{12,4},{4,0},{1,9},{9... | collective-permute-start | bytes 3538952 | tf_op jit(solution)/shard_map/ppermute | solution.py:732
  58.1 27.9 %collective-permute-start.9 = (bf16[2,192,1536]{2,1,0:T(8,128)(2,1)S(1)}, bf16[2,192,1536]{2,1,0:T(8,128)(2,1)}, u32[]{:S(2)}, u32[]{:S(2)}) collective-permute-start(bf16[2,192,1536]{2,1,0:T(8,128)(2,1)S(1)} %collective-permute-done.6.refs_1_), channel_id=1, source_target_pairs={{8,0},{16,8},{24,16},{28,24},{20,28},{12,20},{4,12},{0,4},{9,1},{1... | collective-permute-start | bytes 3538952 | tf_op jit(solution)/shard_map/ppermute | solution.py:732
  86.0 27.4 %collective-permute-start.12 = (bf16[2,192,1536]{2,1,0:T(8,128)(2,1)}, bf16[2,192,1536]{2,1,0:T(8,128)(2,1)S(1)}, u32[]{:S(2)}, u32[]{:S(2)}) collective-permute-start(bf16[2,192,1536]{2,1,0:T(8,128)(2,1)} %collective-permute-done.8.refs_5_), channel_id=1, source_target_pairs={{0,8},{8,16},{16,24},{24,28},{28,20},{20,12},{12,4},{4,0},{1,9},{9... | collective-permute-start | bytes 3538952 | tf_op jit(solution)/shard_map/ppermute | solution.py:732
  87.4 26.8 %collective-permute-start.13 = (bf16[2,192,1536]{2,1,0:T(8,128)(2,1)}, bf16[2,192,1536]{2,1,0:T(8,128)(2,1)S(1)}, u32[]{:S(2)}, u32[]{:S(2)}) collective-permute-start(bf16[2,192,1536]{2,1,0:T(8,128)(2,1)} %collective-permute-done.9.refs_2_), channel_id=1, source_target_pairs={{8,0},{16,8},{24,16},{28,24},{20,28},{12,20},{4,12},{0,4},{9,1},{1... | collective-permute-start | bytes 3538952 | tf_op jit(solution)/shard_map/ppermute | solution.py:732
  88.0 28.3 %collective-permute-start.11 = (bf16[1184,384]{1,0:T(8,128)(2,1)}, bf16[1184,384]{1,0:T(8,128)(2,1)}, u32[]{:S(2)}, u32[]{:S(2)}) collective-permute-start(bf16[1184,384]{1,0:T(8,128)(2,1)} %concatenate.35), channel_id=1, source_target_pairs={{0,2},{1,3},{2,0},{3,1},{4,6},{5,7},{6,4},{7,5},{8,10},{9,11},{10,... | collective-permute-start | bytes 2727944 | tf_op jit(solution)/shard_map/ppermute | solution.py:707
  128.4 26.9 %collective-permute-start.18 = (bf16[2,192,1536]{2,1,0:T(8,128)(2,1)}, bf16[2,192,1536]{2,1,0:T(8,128)(2,1)}, u32[]{:S(2)}, u32[]{:S(2)}) collective-permute-start(bf16[2,192,1536]{2,1,0:T(8,128)(2,1)} %shard_map.370.refs_0_), channel_id=1, source_target_pairs={{8,0},{16,8},{24,16},{28,24},{20,28},{12,20},{4,12},{0,4},{9,1},{1... | collective-permute-start | bytes 3538952 | tf_op jit(solution)/shard_map/ppermute | solution.py:732
  129.5 25.8 %collective-permute-start.17 = (bf16[2,192,1536]{2,1,0:T(8,128)(2,1)}, bf16[2,192,1536]{2,1,0:T(8,128)(2,1)}, u32[]{:S(2)}, u32[]{:S(2)}) collective-permute-start(bf16[2,192,1536]{2,1,0:T(8,128)(2,1)} %shard_map.370.refs_0_), channel_id=1, source_target_pairs={{0,8},{8,16},{16,24},{24,28},{28,20},{20,12},{12,4},{4,0},{1,9},{9... | collective-permute-start | bytes 3538952 | tf_op jit(solution)/shard_map/ppermute | solution.py:732
  155.3 32.7 %collective-permute-start.20 = (bf16[2,192,1536]{2,1,0:T(8,128)(2,1)}, bf16[2,192,1536]{2,1,0:T(8,128)(2,1)S(1)}, u32[]{:S(2)}, u32[]{:S(2)}) collective-permute-start(bf16[2,192,1536]{2,1,0:T(8,128)(2,1)} %collective-permute-done.17.refs_6_), channel_id=1, source_target_pairs={{0,8},{8,16},{16,24},{24,28},{28,20},{20,12},{12,4},{4,0},{1,9},{9... | collective-permute-start | bytes 3538952 | tf_op jit(solution)/shard_map/ppermute | solution.py:732
  156.1 31.9 %collective-permute-start.21 = (bf16[2,192,1536]{2,1,0:T(8,128)(2,1)}, bf16[2,192,1536]{2,1,0:T(8,128)(2,1)S(1)}, u32[]{:S(2)}, u32[]{:S(2)}) collective-permute-start(bf16[2,192,1536]{2,1,0:T(8,128)(2,1)} %collective-permute-done.18.refs_1_), channel_id=1, source_target_pairs={{8,0},{16,8},{24,16},{28,24},{20,28},{12,20},{4,12},{0,4},{9,1},{1... | collective-permute-start | bytes 3538952 | tf_op jit(solution)/shard_map/ppermute | solution.py:732
  188.1 28.0 %collective-permute-start.24 = (bf16[2,192,1536]{2,1,0:T(8,128)(2,1)S(1)}, bf16[2,192,1536]{2,1,0:T(8,128)(2,1)S(1)}, u32[]{:S(2)}, u32[]{:S(2)}) collective-permute-start(bf16[2,192,1536]{2,1,0:T(8,128)(2,1)S(1)} %collective-permute-done.20.refs_5_), channel_id=1, source_target_pairs={{0,8},{8,16},{16,24},{24,28},{28,20},{20,12},{12,4},{4,0},{1,9},{9... | collective-permute-start | bytes 3538952 | tf_op jit(solution)/shard_map/ppermute | solution.py:732
  189.0 27.9 %collective-permute-start.25 = (bf16[2,192,1536]{2,1,0:T(8,128)(2,1)S(1)}, bf16[2,192,1536]{2,1,0:T(8,128)(2,1)S(1)}, u32[]{:S(2)}, u32[]{:S(2)}) collective-permute-start(bf16[2,192,1536]{2,1,0:T(8,128)(2,1)S(1)} %collective-permute-done.21.refs_2_), channel_id=1, source_target_pairs={{8,0},{16,8},{24,16},{28,24},{20,28},{12,20},{4,12},{0,4},{9,1},{1... | collective-permute-start | bytes 3538952 | tf_op jit(solution)/shard_map/ppermute | solution.py:732
  192.3 24.6 %collective-permute-start.23 = (bf16[1184,384]{1,0:T(8,128)(2,1)S(1)}, bf16[1184,384]{1,0:T(8,128)(2,1)S(1)}, u32[]{:S(2)}, u32[]{:S(2)}) collective-permute-start(bf16[1184,384]{1,0:T(8,128)(2,1)S(1)} %get-tuple-element.400), channel_id=1, source_target_pairs={{0,2},{1,3},{2,0},{3,1},{4,6},{5,7},{6,4},{7,5},{8,10},{9,11},{10,... | collective-permute-start | bytes 2727944 | tf_op jit(solution)/shard_map/ppermute | solution.py:707
  237.0 26.7 %collective-permute-start.34 = (bf16[2,192,1536]{2,1,0:T(8,128)(2,1)S(1)}, bf16[2,192,1536]{2,1,0:T(8,128)(2,1)S(1)}, u32[]{:S(2)}, u32[]{:S(2)}) collective-permute-start(bf16[2,192,1536]{2,1,0:T(8,128)(2,1)S(1)} %copy-done.10), channel_id=1, source_target_pairs={{8,0},{16,8},{24,16},{28,24},{20,28},{12,20},{4,12},{0,4},{9,1},{1... | collective-permute-start | bytes 3538952 | tf_op jit(solution)/shard_map/ppermute | solution.py:732
  237.9 26.4 %collective-permute-start.33 = (bf16[2,192,1536]{2,1,0:T(8,128)(2,1)S(1)}, bf16[2,192,1536]{2,1,0:T(8,128)(2,1)S(1)}, u32[]{:S(2)}, u32[]{:S(2)}) collective-permute-start(bf16[2,192,1536]{2,1,0:T(8,128)(2,1)S(1)} %copy-done.10), channel_id=1, source_target_pairs={{0,8},{8,16},{16,24},{24,28},{28,20},{20,12},{12,4},{4,0},{1,9},{9... | collective-permute-start | bytes 3538952 | tf_op jit(solution)/shard_map/ppermute | solution.py:732
  240.2 26.9 %collective-permute-start.32 = (bf16[1184,384]{1,0:T(8,128)(2,1)S(1)}, bf16[1184,384]{1,0:T(8,128)(2,1)S(1)}, u32[]{:S(2)}, u32[]{:S(2)}) collective-permute-start(bf16[1184,384]{1,0:T(8,128)(2,1)S(1)} %add_convert_fusion.18), channel_id=1, source_target_pairs={{0,2},{1,3},{2,0},{3,1},{4,6},{5,7},{6,4},{7,5},{8,10},{9,11},{10,... | collective-permute-start | bytes 2727944 | tf_op jit(solution)/shard_map/ppermute | solution.py:707
  267.7 28.1 %collective-permute-start.36 = (bf16[2,192,1536]{2,1,0:T(8,128)(2,1)S(1)}, bf16[2,192,1536]{2,1,0:T(8,128)(2,1)}, u32[]{:S(2)}, u32[]{:S(2)}) collective-permute-start(bf16[2,192,1536]{2,1,0:T(8,128)(2,1)S(1)} %collective-permute-done.33.refs_6_), channel_id=1, source_target_pairs={{0,8},{8,16},{16,24},{24,28},{28,20},{20,12},{12,4},{4,0},{1,9},{9... | collective-permute-start | bytes 3538952 | tf_op jit(solution)/shard_map/ppermute | solution.py:732
  268.8 28.0 %collective-permute-start.37 = (bf16[2,192,1536]{2,1,0:T(8,128)(2,1)S(1)}, bf16[2,192,1536]{2,1,0:T(8,128)(2,1)}, u32[]{:S(2)}, u32[]{:S(2)}) collective-permute-start(bf16[2,192,1536]{2,1,0:T(8,128)(2,1)S(1)} %collective-permute-done.34.refs_1_), channel_id=1, source_target_pairs={{8,0},{16,8},{24,16},{28,24},{20,28},{12,20},{4,12},{0,4},{9,1},{1... | collective-permute-start | bytes 3538952 | tf_op jit(solution)/shard_map/ppermute | solution.py:732
  296.8 27.1 %collective-permute-start.38 = (bf16[2,192,1536]{2,1,0:T(8,128)(2,1)}, bf16[2,192,1536]{2,1,0:T(8,128)(2,1)}, u32[]{:S(2)}, u32[]{:S(2)}) collective-permute-start(bf16[2,192,1536]{2,1,0:T(8,128)(2,1)} %collective-permute-done.36.refs_5_), channel_id=1, source_target_pairs={{0,8},{8,16},{16,24},{24,28},{28,20},{20,12},{12,4},{4,0},{1,9},{9... | collective-permute-start | bytes 3538952 | tf_op jit(solution)/shard_map/ppermute | solution.py:732
  297.6 26.8 %collective-permute-start.39 = (bf16[2,192,1536]{2,1,0:T(8,128)(2,1)}, bf16[2,192,1536]{2,1,0:T(8,128)(2,1)}, u32[]{:S(2)}, u32[]{:S(2)}) collective-permute-start(bf16[2,192,1536]{2,1,0:T(8,128)(2,1)} %collective-permute-done.37.refs_2_), channel_id=1, source_target_pairs={{8,0},{16,8},{24,16},{28,24},{20,28},{12,20},{4,12},{0,4},{9,1},{1... | collective-permute-start | bytes 3538952 | tf_op jit(solution)/shard_map/ppermute | solution.py:732
  341.2 26.9 %collective-permute-start.42 = (bf16[2,192,1536]{2,1,0:T(8,128)(2,1)}, bf16[2,192,1536]{2,1,0:T(8,128)(2,1)}, u32[]{:S(2)}, u32[]{:S(2)}) collective-permute-start(bf16[2,192,1536]{2,1,0:T(8,128)(2,1)} %get-tuple-element.450), channel_id=1, source_target_pairs={{0,8},{8,16},{16,24},{24,28},{28,20},{20,12},{12,4},{4,0},{1,9},{9... | collective-permute-start | bytes 3538952 | tf_op jit(solution)/shard_map/ppermute | solution.py:732
  342.0 26.1 %collective-permute-start.43 = (bf16[2,192,1536]{2,1,0:T(8,128)(2,1)}, bf16[2,192,1536]{2,1,0:T(8,128)(2,1)}, u32[]{:S(2)}, u32[]{:S(2)}) collective-permute-start(bf16[2,192,1536]{2,1,0:T(8,128)(2,1)} %get-tuple-element.451), channel_id=1, source_target_pairs={{8,0},{16,8},{24,16},{28,24},{20,28},{12,20},{4,12},{0,4},{9,1},{1... | collective-permute-start | bytes 3538952 | tf_op jit(solution)/shard_map/ppermute | solution.py:732
  375.0 28.1 %collective-permute-start.47 = (bf16[2,192,1536]{2,1,0:T(8,128)(2,1)}, bf16[2,192,1536]{2,1,0:T(8,128)(2,1)S(1)}, u32[]{:S(2)}, u32[]{:S(2)}) collective-permute-start(bf16[2,192,1536]{2,1,0:T(8,128)(2,1)} %get-tuple-element.470), channel_id=1, source_target_pairs={{0,8},{8,16},{16,24},{24,28},{28,20},{20,12},{12,4},{4,0},{1,9},{9... | collective-permute-start | bytes 3538952 | tf_op jit(solution)/shard_map/ppermute | solution.py:732
  375.9 28.1 %collective-permute-start.48 = (bf16[2,192,1536]{2,1,0:T(8,128)(2,1)}, bf16[2,192,1536]{2,1,0:T(8,128)(2,1)}, u32[]{:S(2)}, u32[]{:S(2)}) collective-permute-start(bf16[2,192,1536]{2,1,0:T(8,128)(2,1)} %get-tuple-element.471), channel_id=1, source_target_pairs={{8,0},{16,8},{24,16},{28,24},{20,28},{12,20},{4,12},{0,4},{9,1},{1... | collective-permute-start | bytes 3538952 | tf_op jit(solution)/shard_map/ppermute | solution.py:732
  406.7 26.8 %collective-permute-start.50 = (bf16[2,192,1536]{2,1,0:T(8,128)(2,1)S(1)}, bf16[2,192,1536]{2,1,0:T(8,128)(2,1)S(1)}, u32[]{:S(2)}, u32[]{:S(2)}) collective-permute-start(bf16[2,192,1536]{2,1,0:T(8,128)(2,1)S(1)} %get-tuple-element.480), channel_id=1, source_target_pairs={{0,8},{8,16},{16,24},{24,28},{28,20},{20,12},{12,4},{4,0},{1,9},{9... | collective-permute-start | bytes 3538952 | tf_op jit(solution)/shard_map/ppermute | solution.py:732
  408.1 26.4 %collective-permute-start.51 = (bf16[2,192,1536]{2,1,0:T(8,128)(2,1)S(1)}, bf16[2,192,1536]{2,1,0:T(8,128)(2,1)S(1)}, u32[]{:S(2)}, u32[]{:S(2)}) collective-permute-start(bf16[2,192,1536]{2,1,0:T(8,128)(2,1)S(1)} %get-tuple-element.481), channel_id=1, source_target_pairs={{8,0},{16,8},{24,16},{28,24},{20,28},{12,20},{4,12},{0,4},{9,1},{1... | collective-permute-start | bytes 3538952 | tf_op jit(solution)/shard_map/ppermute | solution.py:732
  437.6 28.1 %collective-permute-start.57 = (bf16[2,192,1536]{2,1,0:T(8,128)(2,1)}, bf16[2,192,1536]{2,1,0:T(8,128)(2,1)}, u32[]{:S(2)}, u32[]{:S(2)}) collective-permute-start(bf16[2,192,1536]{2,1,0:T(8,128)(2,1)} %add_convert_fusion.10), channel_id=1, source_target_pairs={{0,8},{8,16},{16,24},{24,28},{28,20},{20,12},{12,4},{4,0},{1,9},{9... | collective-permute-start | bytes 3538952 | tf_op jit(solution)/shard_map/ppermute | solution.py:732
  438.9 26.8 %collective-permute-start.58 = (bf16[2,192,1536]{2,1,0:T(8,128)(2,1)S(1)}, bf16[2,192,1536]{2,1,0:T(8,128)(2,1)}, u32[]{:S(2)}, u32[]{:S(2)}) collective-permute-start(bf16[2,192,1536]{2,1,0:T(8,128)(2,1)S(1)} %get-tuple-element.496), channel_id=1, source_target_pairs={{8,0},{16,8},{24,16},{28,24},{20,28},{12,20},{4,12},{0,4},{9,1},{1... | collective-permute-start | bytes 3538952 | tf_op jit(solution)/shard_map/ppermute | solution.py:732
  468.2 29.2 %collective-permute-start.54 = (bf16[1184,384]{1,0:T(8,128)(2,1)}, bf16[1184,384]{1,0:T(8,128)(2,1)S(1)}, u32[]{:S(2)}, u32[]{:S(2)}) collective-permute-start(bf16[1184,384]{1,0:T(8,128)(2,1)} %get-tuple-element.493), channel_id=1, source_target_pairs={{0,1},{1,0},{2,3},{3,2},{4,5},{5,4},{6,7},{7,6},{8,9},{9,8},{10,11... | collective-permute-start | bytes 2727944 | tf_op jit(solution)/shard_map/ppermute | solution.py:707
  468.3 29.1 %collective-permute-start.60 = (bf16[1184,384]{1,0:T(8,128)(2,1)}, bf16[1184,384]{1,0:T(8,128)(2,1)}, u32[]{:S(2)}, u32[]{:S(2)}) collective-permute-start(bf16[1184,384]{1,0:T(8,128)(2,1)} %get-tuple-element.510), channel_id=1, source_target_pairs={{0,1},{1,0},{2,3},{3,2},{4,5},{5,4},{6,7},{7,6},{8,9},{9,8},{10,11... | collective-permute-start | bytes 2727944 | tf_op jit(solution)/shard_map/ppermute | solution.py:707
  468.7 33.0 %collective-permute-start.62 = (bf16[2,192,1536]{2,1,0:T(8,128)(2,1)S(1)}, bf16[2,192,1536]{2,1,0:T(8,128)(2,1)}, u32[]{:S(2)}, u32[]{:S(2)}) collective-permute-start(bf16[2,192,1536]{2,1,0:T(8,128)(2,1)S(1)} %get-tuple-element.517), channel_id=1, source_target_pairs={{0,8},{8,16},{16,24},{24,28},{28,20},{20,12},{12,4},{4,0},{1,9},{9... | collective-permute-start | bytes 3538952 | tf_op jit(solution)/shard_map/ppermute | solution.py:732
  470.8 30.9 %collective-permute-start.63 = (bf16[2,192,1536]{2,1,0:T(8,128)(2,1)S(1)}, bf16[2,192,1536]{2,1,0:T(8,128)(2,1)}, u32[]{:S(2)}, u32[]{:S(2)}) collective-permute-start(bf16[2,192,1536]{2,1,0:T(8,128)(2,1)S(1)} %add_convert_fusion.9), channel_id=1, source_target_pairs={{8,0},{16,8},{24,16},{28,24},{20,28},{12,20},{4,12},{0,4},{9,1},{1... | collective-permute-start | bytes 3538952 | tf_op jit(solution)/shard_map/ppermute | solution.py:732
  504.7 30.3 %collective-permute-start.64 = (bf16[2,192,1536]{2,1,0:T(8,128)(2,1)S(1)}, bf16[2,192,1536]{2,1,0:T(8,128)(2,1)S(1)}, u32[]{:S(2)}, u32[]{:S(2)}) collective-permute-start(bf16[2,192,1536]{2,1,0:T(8,128)(2,1)S(1)} %get-tuple-element.536), channel_id=1, source_target_pairs={{0,8},{8,16},{16,24},{24,28},{28,20},{20,12},{12,4},{4,0},{1,9},{9... | collective-permute-start | bytes 3538952 | tf_op jit(solution)/shard_map/ppermute | solution.py:732
  506.2 28.9 %collective-permute-start.65 = (bf16[2,192,1536]{2,1,0:T(8,128)(2,1)S(1)}, bf16[2,192,1536]{2,1,0:T(8,128)(2,1)}, u32[]{:S(2)}, u32[]{:S(2)}) collective-permute-start(bf16[2,192,1536]{2,1,0:T(8,128)(2,1)S(1)} %get-tuple-element.537), channel_id=1, source_target_pairs={{8,0},{16,8},{24,16},{28,24},{20,28},{12,20},{4,12},{0,4},{9,1},{1... | collective-permute-start | bytes 3538952 | tf_op jit(solution)/shard_map/ppermute | solution.py:732
  506.8 28.2 %collective-permute-start.61 = (bf16[1184,384]{1,0:T(8,128)(2,1)}, bf16[1184,384]{1,0:T(8,128)(2,1)S(1)}, u32[]{:S(2)}, u32[]{:S(2)}) collective-permute-start(bf16[1184,384]{1,0:T(8,128)(2,1)} %add_convert_fusion.16), channel_id=1, source_target_pairs={{0,2},{1,3},{2,0},{3,1},{4,6},{5,7},{6,4},{7,5},{8,10},{9,11},{10,... | collective-permute-start | bytes 2727944 | tf_op jit(solution)/shard_map/ppermute | solution.py:707
  539.4 32.1 %collective-permute-start.66 = (bf16[2,192,1536]{2,1,0:T(8,128)(2,1)}, bf16[2,192,1536]{2,1,0:T(8,128)(2,1)}, u32[]{:S(2)}, u32[]{:S(2)}) collective-permute-start(bf16[2,192,1536]{2,1,0:T(8,128)(2,1)} %get-tuple-element.546), channel_id=1, source_target_pairs={{0,8},{8,16},{16,24},{24,28},{28,20},{20,12},{12,4},{4,0},{1,9},{9... | collective-permute-start | bytes 3538952 | tf_op jit(solution)/shard_map/ppermute | solution.py:732
  540.6 30.8 %collective-permute-start.67 = (bf16[2,192,1536]{2,1,0:T(8,128)(2,1)}, bf16[2,192,1536]{2,1,0:T(8,128)(2,1)}, u32[]{:S(2)}, u32[]{:S(2)}) collective-permute-start(bf16[2,192,1536]{2,1,0:T(8,128)(2,1)} %get-tuple-element.547), channel_id=1, source_target_pairs={{8,0},{16,8},{24,16},{28,24},{20,28},{12,20},{4,12},{0,4},{9,1},{1... | collective-permute-start | bytes 3538952 | tf_op jit(solution)/shard_map/ppermute | solution.py:732
  589.3 29.2 %collective-permute-start.74 = (bf16[1184,384]{1,0:T(8,128)(2,1)}, bf16[1184,384]{1,0:T(8,128)(2,1)S(1)}, u32[]{:S(2)}, u32[]{:S(2)}) collective-permute-start(bf16[1184,384]{1,0:T(8,128)(2,1)} %add_convert_fusion.15), channel_id=1, source_target_pairs={{0,2},{1,3},{2,0},{3,1},{4,6},{5,7},{6,4},{7,5},{8,10},{9,11},{10,... | collective-permute-start | bytes 2727944 | tf_op jit(solution)/shard_map/ppermute | solution.py:707
  605.1 26.4 %collective-permute-start.72 = (bf16[2,192,1536]{2,1,0:T(8,128)(2,1)}, bf16[2,192,1536]{2,1,0:T(8,128)(2,1)}, u32[]{:S(2)}, u32[]{:S(2)}) collective-permute-start(bf16[2,192,1536]{2,1,0:T(8,128)(2,1)} %pad_maximum_fusion.3), channel_id=1, source_target_pairs={{0,8},{8,16},{16,24},{24,28},{28,20},{20,12},{12,4},{4,0},{1,9},{9... | collective-permute-start | bytes 3538952 | tf_op jit(solution)/shard_map/ppermute | solution.py:732
  606.3 26.3 %collective-permute-start.73 = (bf16[2,192,1536]{2,1,0:T(8,128)(2,1)}, bf16[2,192,1536]{2,1,0:T(8,128)(2,1)}, u32[]{:S(2)}, u32[]{:S(2)}) collective-permute-start(bf16[2,192,1536]{2,1,0:T(8,128)(2,1)} %pad_maximum_fusion.4), channel_id=1, source_target_pairs={{8,0},{16,8},{24,16},{28,24},{20,28},{12,20},{4,12},{0,4},{9,1},{1... | collective-permute-start | bytes 3538952 | tf_op jit(solution)/shard_map/ppermute | solution.py:732
  643.4 33.5 %collective-permute-start.75 = (bf16[2,192,1536]{2,1,0:T(8,128)(2,1)}, bf16[2,192,1536]{2,1,0:T(8,128)(2,1)}, u32[]{:S(2)}, u32[]{:S(2)}) collective-permute-start(bf16[2,192,1536]{2,1,0:T(8,128)(2,1)} %get-tuple-element.591), channel_id=1, source_target_pairs={{0,8},{8,16},{16,24},{24,28},{28,20},{20,12},{12,4},{4,0},{1,9},{9... | collective-permute-start | bytes 3538952 | tf_op jit(solution)/shard_map/ppermute | solution.py:732
  645.4 31.5 %collective-permute-start.76 = (bf16[2,192,1536]{2,1,0:T(8,128)(2,1)}, bf16[2,192,1536]{2,1,0:T(8,128)(2,1)}, u32[]{:S(2)}, u32[]{:S(2)}) collective-permute-start(bf16[2,192,1536]{2,1,0:T(8,128)(2,1)} %get-tuple-element.592), channel_id=1, source_target_pairs={{8,0},{16,8},{24,16},{28,24},{20,28},{12,20},{4,12},{0,4},{9,1},{1... | collective-permute-start | bytes 3538952 | tf_op jit(solution)/shard_map/ppermute | solution.py:732
  680.1 28.4 %collective-permute-start.83 = (bf16[2,192,1536]{2,1,0:T(8,128)(2,1)S(1)}, bf16[2,192,1536]{2,1,0:T(8,128)(2,1)S(1)}, u32[]{:S(2)}, u32[]{:S(2)}) collective-permute-start(bf16[2,192,1536]{2,1,0:T(8,128)(2,1)S(1)} %get-tuple-element.614), channel_id=1, source_target_pairs={{0,8},{8,16},{16,24},{24,28},{28,20},{20,12},{12,4},{4,0},{1,9},{9... | collective-permute-start | bytes 3538952 | tf_op jit(solution)/shard_map/ppermute | solution.py:732
  680.2 28.7 %collective-permute-start.84 = (bf16[2,192,1536]{2,1,0:T(8,128)(2,1)S(1)}, bf16[2,192,1536]{2,1,0:T(8,128)(2,1)S(1)}, u32[]{:S(2)}, u32[]{:S(2)}) collective-permute-start(bf16[2,192,1536]{2,1,0:T(8,128)(2,1)S(1)} %get-tuple-element.615), channel_id=1, source_target_pairs={{8,0},{16,8},{24,16},{28,24},{20,28},{12,20},{4,12},{0,4},{9,1},{1... | collective-permute-start | bytes 3538952 | tf_op jit(solution)/shard_map/ppermute | solution.py:732
  (108 other events, 3156.7 us)

commit v4 on v3

--- a/solution.py
+++ b/solution.py
@@ -941,18 +941,27 @@
             lanes.push(ring, ahead_of)
             return ring
 
+        ring_first = queued(
+            gather(
+                steps.run(
+                    lambda *weights: travel_rows(("triple", "attended"), weights), w_qkv, w_proj
+                )
+            )
+        )
+        lanes.tick()
+        silu_cond = narrow(jax.nn.silu(cond))
+        mod_round = narrow(w_mod)
+        mod_terms = steps.run(
+            lambda rows, weight: jnp.einsum(
+                "bd,dsic->bsic", rows, weight, preferred_element_type=F32
+            ),
+            silu_cond,
+            mod_round,
+        )
+        mod_parts = lax.all_to_all(mod_terms, "rows", 0, 0, tiled=True)
         source_round = steps.run(join_tokens, x_img, x_txt)
         source_parts = start_width(source_round)
-        silu_cond = narrow(jax.nn.silu(cond))
-        mod_round = narrow(w_mod)
-        (mod_terms,) = steps.tie(
-            jnp.einsum("bd,dsic->bsic", silu_cond, mod_round, preferred_element_type=F32)
-        )
-        mod_parts = lax.all_to_all(mod_terms, "rows", 0, 0, tiled=True)
-        first_local = travel_rows(("triple", "attended"), (w_qkv, w_proj))
-        steps.mark(mod_parts, first_local)
-        ring_first = queued(gather(first_local))
-        lanes.tick()
+        steps.add(mod_parts)
         modulation = jnp.sum(mod_parts, axis=0) + biases[:, 0:6]
         mod_around = send_around(modulation)
         lanes.tick()
@@ -1007,8 +1016,7 @@
             if pair == 0:
                 lanes.tick()
         attended, log_totals = so_far
-        halves = send_halves(attended, ring_first, attended_span)
-        lanes.tick()
+        halves = send_halves(attended, ring_first, attended_span, lanes.tick)
         own, away = send_away(*halves)
         lanes.tick()
 
@@ -1108,9 +1116,6 @@
             ("hidden",), ring_grad_down, (w_down,), (moments_down,)
         )
         lanes.until(ring_grad_up)
-        ((next_up, grad_up, moved_up),) = update(
-            ("hidden",), ring_grad_up, (w_up,), (moments_up,)
-        )
         lowered = own_lowered + lowered_away.astype(F32) + per_token(biases[:, 13])
         grad_lowered = gate_two * cotangent
         grad_normed_one = own + away.land().astype(F32)
@@ -1154,8 +1159,8 @@
         grad_cond = grad_silu * sigmoid_cond * (1.0 + cond * (1.0 - sigmoid_cond))
         next_bias, first_bias, second_bias = adam_step(biases, moments_bias, grad_bias)
         steps.add(next_bias, first_bias, second_bias, grad_cond)
-        next_mod, grad_mod, first_mod, second_mod = steps.run(
-            adam_modulation, w_mod, moments_mod, silu_cond, table_round
+        ((next_up, grad_up, moved_up),) = update(
+            ("hidden",), ring_grad_up, (w_up,), (moments_up,)
         )
         lanes.until(ring_grad_first, 1)
         own_lowered, lowered_away = steps.tie(own_lowered, lowered_away)
@@ -1163,7 +1168,10 @@
             residual
             + gate_two * (own_lowered + lowered_away.astype(F32) + per_token(biases[:, 13]))
         )
-        steps.add(output)
+        steps.add(output, grad_source)
+        next_mod, grad_mod, first_mod, second_mod = steps.run(
+            adam_modulation, w_mod, moments_mod, silu_cond, table_round
+        )
         lanes.until(ring_grad_first)
         (next_qkv, grad_qkv, moved_qkv), (next_proj, grad_proj, moved_proj) = update(
             ("triple", "attended"),

time: 733 us -> 698 us (0.952)
  waiting for transfers between devices: 211 us -> 176 us
    ppermute x46, waiting for transfers between devices: 191 us -> 143 us  [send(): self.held[way] = lax.ppermute(value, 'rows', ahead if way == 1 else behind)]
    all_to_all x1, waiting for transfers between devices: 2.66 us -> 12.4 us  [shards(): mod_parts = lax.all_to_all(mod_terms, 'rows', 0, 0, tiled=True)]
  transfers between devices with their start and end apart: 87 -> 87, of which waited for: 39 -> 45; matrix products, arithmetic and copies ran while one was open for 14% -> 16% of each run, Pallas kernels for 38% -> 39%
where the time goes in v4:
time: 698 us; the launch traced here: 687 us
  Pallas kernels  284 us (41%)
  waiting for transfers between devices  176 us (25%)
  other arithmetic  98.1 us (14%)
  starting transfers between devices  80.9 us (12%)
  local copies, waits for them, and re-layouts  38.7 us (6%)
  between operations  7.08 us (1%)
    ppermute x46, waiting for transfers between devices, send(): self.held[way] = lax.ppermute(value, 'rows', ahead if way == 1 else behind)  143 us
    pallas_call x8, Pallas kernels, matmul_back(): pl.pallas_call(kernel, grid=(2,), in_specs=[pl.BlockSpec(memory_space=plt...  64.6 us
    convert_element_type x17, other arithmetic, narrow(): return values.astype(jnp.bfloat16)  57.1 us
    ppermute x46, starting transfers between devices, send(): self.held[way] = lax.ppermute(value, 'rows', ahead if way == 1 else behind)  49.5 us
    pallas_call x4, Pallas kernels, matmul_rows(): pl.pallas_call(kernel, grid=(tiles,), in_specs=[pl.BlockSpec(memory_space...  49.4 us
    pallas_call x3, Pallas kernels, attention_back(): pl.pallas_call(kernel, grid=(last - first,), in_specs=[pl.BlockSpec((rows...  40.3 us
    pallas_call x4, Pallas kernels, weight_gradient(): pl.pallas_call(kernel, grid=(height // tile,), in_specs=[column_spec(rows...  37.4 us
    pallas_call x3, Pallas kernels, adam_rows(): pl.pallas_call(kernel, grid_spec=pltpu.PrefetchScalarGridSpec(num_scalar_...  34.3 us
  transfers between devices with their start and end apart: 87, of which 45 were waited for; matrix products, arithmetic and copies ran while one was open for 16% of the time, Pallas kernels for 39%

profile of v4, /device:TPU:0, one launch (start us, length us, event | category | flops | bytes accessed | tf_op | source)
XLA Modules:
  0.0 687.3 jit_solution(2236764181269199106)
XLA Ops:
  0.7 4.8 shard_map.369.refs_0_
  14.1 6.1 concatenate.32
  23.0 5.8 all-to-all-start
  28.8 12.4 %all-to-all-done = f32[8,2,6,384]{3,1,2,0:T(2,128)S(1)} async-done(((f32[8,2,6,384]{3,1,2,0:T(2,128)}), f32[8,2,6,384]{3,1,2,0:T(2,128)S(1)}, u32[]{:S(2)}, u32[]{:S(2)}) %all-to-all-start) | async-done | bytes 147488 | tf_op jit(solution)/shard_map/all_to_all | solution.py:961
  53.4 9.9 %add_convert_fusion.acts_ref.outer_ref = bf16[1184,1536]{1,0:T(8,128)(2,1)} fusion(f32[1184,1536]{1,0:T(8,128)S(1)} %maximum_convert_fusion, f32[1536]{0:T(1024)S(1)} %get-tuple-element.746, f32[1536]{0:T(1024)S(1)} %get-tuple-element.747, f32[1536]{0:T(1024)S(1)} %get-tuple-element.748, f32[1536]{0:T(1024)S(1)} %get-tuple-element.745, ...), kind=kLoop, calls=%fused_computation.1 | loop fusion | flops 14548992 | bytes 10946976 | tf_op jit(solution)/shard_map/convert_element_type | solution.py:34
  63.4 6.2 concatenate.35
  69.5 5.4 collective-permute-done.8.refs_5_
  77.7 4.8 shard_map.370.refs_0_
  82.5 4.8 shard_map.371.refs_0_
  87.3 15.1 %collective-permute-done.12.refs_4_ = bf16[2,192,1536]{2,1,0:T(8,128)(2,1)S(1)} collective-permute-done((bf16[2,192,1536]{2,1,0:T(8,128)(2,1)}, bf16[2,192,1536]{2,1,0:T(8,128)(2,1)S(1)}, u32[]{:S(2)}, u32[]{:S(2)}) %collective-permute-start.12) | collective-permute-done | bytes 1179680 | tf_op jit(solution)/shard_map/ppermute | solution.py:732
  104.8 11.3 %collective-permute-done.16.refs_8_ = bf16[1,192,1536]{2,1,0:T(8,128)(2,1)S(1)} collective-permute-done((bf16[1,192,1536]{2,1,0:T(8,128)(2,1)S(1)}, bf16[1,192,1536]{2,1,0:T(8,128)(2,1)S(1)}, u32[]{:S(2)}, u32[]{:S(2)}) %collective-permute-start.16) | collective-permute-done | bytes 589856 | tf_op jit(solution)/shard_map/ppermute | solution.py:732
  123.8 11.1 %shard_map.372.triple_ref = bf16[1184,1152]{1,0:T(8,128)(2,1)} custom-call(s32[8]{0:T(128)} %fusion.32.slots_ref, bf16[1184,1536]{1,0:T(8,128)(2,1)} %add_convert_fusion.acts_ref.outer_ref, bf16[2,192,1536]{2,1,0:T(8,128)(2,1)} %shard_map.369.refs_0_, bf16[2,192,1536]{2,1,0:T(8,128)(2,1)} %copy-done.2, bf16[2,192,1536]{2,1,0:T(8,128)(2,1)} %collective-permute-done.9.refs_2_, ...), custom_call_target="tpu_custom_call" | custom-call | flops 4190109 | bytes 13443 | tf_op jit(solution)/shard_map/pallas_call | solution.py:294
  134.9 9.5 %shard_map.373 = (bf16[1184,384]{1,0:T(8,128)(2,1)}, f32[3,2,1184]{2,1,0:T(2,128)}) custom-call(bf16[1184,1152]{1,0:T(8,128)(2,1)} %shard_map.372.triple_ref), custom_call_target="tpu_custom_call" | custom-call | flops 8613003 | bytes 10911 | tf_op jit(solution)/shard_map/pallas_call | solution.py:536
  146.8 9.5 %shard_map.374 = (bf16[1184,384]{1,0:T(8,128)(2,1)}, f32[3,2,1184]{2,1,0:T(2,128)}) custom-call(bf16[1184,1152]{1,0:T(8,128)(2,1)} %shard_map.372.triple_ref, bf16[1184,384]{1,0:T(8,128)(2,1)} %get-tuple-element.379.refs_0_, f32[3,2,1184]{2,1,0:T(2,128)} %get-tuple-element.380.refs_1_), custom_call_target="tpu_custom_call", output_to_operand_aliasing={{0}: (1, {}), {1}: (2, {})} | custom-call | flops 8613003 | bytes 10911 | tf_op jit(solution)/shard_map/pallas_call | solution.py:536
  156.3 9.7 %shard_map.375 = (bf16[1184,384]{1,0:T(8,128)(2,1)}, f32[3,2,1184]{2,1,0:T(2,128)}) custom-call(bf16[1184,1152]{1,0:T(8,128)(2,1)} %shard_map.372.triple_ref, bf16[1184,384]{1,0:T(8,128)(2,1)} %get-tuple-element.384.refs_0_, f32[3,2,1184]{2,1,0:T(2,128)} %get-tuple-element.385.refs_1_), custom_call_target="tpu_custom_call", output_to_operand_aliasing={{0}: (1, {}), {1}: (2, {})} | custom-call | flops 8613003 | bytes 10911 | tf_op jit(solution)/shard_map/pallas_call | solution.py:536
  166.0 5.2 shard_map.376
  175.8 5.3 shard_map.377
  184.3 17.4 %collective-permute-done.24.refs_4_ = bf16[2,192,1536]{2,1,0:T(8,128)(2,1)S(1)} collective-permute-done((bf16[2,192,1536]{2,1,0:T(8,128)(2,1)S(1)}, bf16[2,192,1536]{2,1,0:T(8,128)(2,1)S(1)}, u32[]{:S(2)}, u32[]{:S(2)}) %collective-permute-start.24) | collective-permute-done | bytes 1179680 | tf_op jit(solution)/shard_map/ppermute | solution.py:732
  210.8 5.4 collective-permute-done.28.refs_8_
  221.3 21.7 %collective-permute-done.34.refs_1_ = bf16[2,192,1536]{2,1,0:T(8,128)(2,1)S(1)} collective-permute-done((bf16[2,192,1536]{2,1,0:T(8,128)(2,1)S(1)}, bf16[2,192,1536]{2,1,0:T(8,128)(2,1)S(1)}, u32[]{:S(2)}, u32[]{:S(2)}) %collective-permute-start.34) | collective-permute-done | bytes 1179680 | tf_op jit(solution)/shard_map/ppermute | solution.py:732
  252.7 17.4 %shard_map.378 = (bf16[1184,1536]{1,0:T(8,128)(2,1)}, f32[1184,1536]{1,0:T(8,128)}) custom-call(s32[8]{0:T(128)} %fusion.32.slots_ref, bf16[1184,1536]{1,0:T(8,128)(2,1)} %pad_maximum_fusion.1.acts_ref.outer_ref, bf16[2,192,1536]{2,1,0:T(8,128)(2,1)} %shard_map.370.refs_0_, bf16[2,192,1536]{2,1,0:T(8,128)(2,1)} %collective-permute-done.18.refs_1_, ...), custom_call_target="tpu_custom_call" | custom-call | flops 5586812 | bytes 16711 | tf_op jit(solution)/shard_map/pallas_call | solution.py:294
  270.2 5.3 collective-permute-done.36.refs_5_
  280.7 10.9 %shard_map.379.refs_2_ = bf16[2,1536,1536]{2,1,0:T(8,128)(2,1)} custom-call(bf16[1184,1536]{1,0:T(8,128)(2,1)} %multiply_convert_fusion.outer_ref.acts_ref, bf16[1184,1536]{1,0:T(8,128)(2,1)} %get-tuple-element.496.inner_ref.acts_ref), custom_call_target="tpu_custom_call" | custom-call | flops 5586812 | bytes 16711 | tf_op jit(solution)/shard_map/pallas_call | solution.py:483
  294.8 8.3 %collective-permute-done.38.refs_4_ = bf16[2,192,1536]{2,1,0:T(8,128)(2,1)} collective-permute-done((bf16[2,192,1536]{2,1,0:T(8,128)(2,1)}, bf16[2,192,1536]{2,1,0:T(8,128)(2,1)}, u32[]{:S(2)}, u32[]{:S(2)}) %collective-permute-start.38) | collective-permute-done | bytes 1179680 | tf_op jit(solution)/shard_map/ppermute | solution.py:732
  307.7 10.9 %collective-permute-done.41.refs_8_ = bf16[1,192,1536]{2,1,0:T(8,128)(2,1)S(1)} collective-permute-done((bf16[1,192,1536]{2,1,0:T(8,128)(2,1)S(1)}, bf16[1,192,1536]{2,1,0:T(8,128)(2,1)S(1)}, u32[]{:S(2)}, u32[]{:S(2)}) %collective-permute-start.41) | collective-permute-done | bytes 589856 | tf_op jit(solution)/shard_map/ppermute | solution.py:732
  323.8 14.2 %shard_map.380 = (bf16[1184,1536]{1,0:T(8,128)(2,1)}, f32[2,1536]{1,0:T(2,128)}) custom-call(s32[8]{0:T(128)} %fusion.32.slots_ref, bf16[1184,1536]{1,0:T(8,128)(2,1)} %multiply_convert_fusion.outer_ref.acts_ref, bf16[2,192,1536]{2,1,0:T(8,128)(2,1)} %shard_map.371.refs_0_, bf16[2,192,1536]{2,1,0:T(8,128)(2,1)} %copy-done.16, ...), custom_call_target="tpu_custom_call" | custom-call | flops 5586812 | bytes 16711 | tf_op jit(solution)/shard_map/pallas_call | solution.py:294
  337.9 9.4 %shard_map.381 = (bf16[1184,384]{1,0:T(8,128)(2,1)}, bf16[1184,384]{1,0:T(8,128)(2,1)}) custom-call(s32[8]{0:T(128)} %fusion.32.slots_ref, bf16[1184,1536]{1,0:T(8,128)(2,1)} %get-tuple-element.479.acts_ref.inner_ref, bf16[2,192,1536]{2,1,0:T(8,128)(2,1)} %shard_map.370.refs_0_, bf16[2,192,1536]{2,1,0:T(8,128)(2,1)} %collective-permute-done.18.refs_1_, ...), custom_call_target="tpu_custom_call" | custom-call | flops 2793406 | bytes 10174 | tf_op jit(solution)/shard_map/pallas_call | solution.py:448
  356.5 9.3 %shard_map.382 = (bf16[1184,384]{1,0:T(8,128)(2,1)}, bf16[1184,384]{1,0:T(8,128)(2,1)}) custom-call(s32[8]{0:T(128)} %fusion.32.slots_ref, bf16[1184,1536]{1,0:T(8,128)(2,1)} %get-tuple-element.479.acts_ref.inner_ref, bf16[2,192,1536]{2,1,0:T(8,128)(2,1)} %shard_map.370.refs_0_, bf16[2,192,1536]{2,1,0:T(8,128)(2,1)} %collective-permute-done.18.refs_1_, ...), custom_call_target="tpu_custom_call" | custom-call | flops 2793406 | bytes 10174 | tf_op jit(solution)/shard_map/pallas_call | solution.py:448
  369.1 10.8 %shard_map.383.refs_2_ = bf16[2,1536,1536]{2,1,0:T(8,128)(2,1)} custom-call(bf16[1184,1536]{1,0:T(8,128)(2,1)} %pad_maximum_fusion.1.acts_ref.outer_ref, bf16[1184,1536]{1,0:T(8,128)(2,1)} %get-tuple-element.479.acts_ref.inner_ref), custom_call_target="tpu_custom_call" | custom-call | flops 5586812 | bytes 16711 | tf_op jit(solution)/shard_map/pallas_call | solution.py:483
  396.9 15.4 %collective-permute-done.50 = bf16[2,192,1536]{2,1,0:T(8,128)(2,1)S(1)} collective-permute-done((bf16[2,192,1536]{2,1,0:T(8,128)(2,1)S(1)}, bf16[2,192,1536]{2,1,0:T(8,128)(2,1)S(1)}, u32[]{:S(2)}, u32[]{:S(2)}) %collective-permute-start.50) | collective-permute-done | bytes 1179680 | tf_op jit(solution)/shard_map/ppermute | solution.py:732
  425.8 9.4 %shard_map.384 = (bf16[1184,384]{1,0:T(8,128)(2,1)}, bf16[1184,384]{1,0:T(8,128)(2,1)}) custom-call(s32[8]{0:T(128)} %fusion.32.slots_ref, bf16[1184,1536]{1,0:T(8,128)(2,1)} %get-tuple-element.496.inner_ref.acts_ref, bf16[2,192,1536]{2,1,0:T(8,128)(2,1)} %shard_map.371.refs_0_, bf16[2,192,1536]{2,1,0:T(8,128)(2,1)} %copy-done.16, ...), custom_call_target="tpu_custom_call" | custom-call | flops 2793406 | bytes 10174 | tf_op jit(solution)/shard_map/pallas_call | solution.py:448
  435.2 9.4 %shard_map.385 = (bf16[1184,384]{1,0:T(8,128)(2,1)}, bf16[1184,384]{1,0:T(8,128)(2,1)}) custom-call(s32[8]{0:T(128)} %fusion.32.slots_ref, bf16[1184,1536]{1,0:T(8,128)(2,1)} %get-tuple-element.496.inner_ref.acts_ref, bf16[2,192,1536]{2,1,0:T(8,128)(2,1)} %shard_map.371.refs_0_, bf16[2,192,1536]{2,1,0:T(8,128)(2,1)} %copy-done.16, ...), custom_call_target="tpu_custom_call" | custom-call | flops 2793406 | bytes 10174 | tf_op jit(solution)/shard_map/pallas_call | solution.py:448
  456.2 6.7 shard_map.386.grad_ref
  462.9 13.4 %shard_map.387 = (bf16[1184,1152]{1,0:T(8,128)(2,1)}, f32[3,2,256]{2,1,0:T(2,128)}) custom-call(bf16[1184,1152]{1,0:T(8,128)(2,1)} %shard_map.372.triple_ref, f32[3,2,1184]{2,1,0:T(2,128)} %get-tuple-element.535.total_ref, bf16[1184,384]{1,0:T(8,128)(2,1)} %shard_map.386.grad_ref), custom_call_target="tpu_custom_call" | custom-call | flops 21532508 | bytes 10911 | tf_op jit(solution)/shard_map/pallas_call | solution.py:611
  486.5 13.3 %shard_map.388 = (bf16[1184,1152]{1,0:T(8,128)(2,1)}, f32[3,2,256]{2,1,0:T(2,128)}) custom-call(bf16[1184,1152]{1,0:T(8,128)(2,1)} %shard_map.372.triple_ref, f32[3,2,1184]{2,1,0:T(2,128)} %get-tuple-element.535.total_ref, bf16[1184,384]{1,0:T(8,128)(2,1)} %shard_map.386.grad_ref, ...), custom_call_target="tpu_custom_call", output_to_operand_aliasing={{0}: (3, {}), {1}: (4, {})} | custom-call | flops 21532508 | bytes 10911 | tf_op jit(solution)/shard_map/pallas_call | solution.py:611
  499.7 13.7 %shard_map.389 = (bf16[1184,1152]{1,0:T(8,128)(2,1)}, f32[3,2,256]{2,1,0:T(2,128)}) custom-call(bf16[1184,1152]{1,0:T(8,128)(2,1)} %shard_map.372.triple_ref, f32[3,2,1184]{2,1,0:T(2,128)} %get-tuple-element.535.total_ref, bf16[1184,384]{1,0:T(8,128)(2,1)} %shard_map.386.grad_ref, ...), custom_call_target="tpu_custom_call", output_to_operand_aliasing={{0}: (3, {}), {1}: (4, {})} | custom-call | flops 21532508 | bytes 10911 | tf_op jit(solution)/shard_map/pallas_call | solution.py:611
  523.0 9.8 %shard_map.390.refs_0_ = bf16[2,1536,1536]{2,1,0:T(8,128)(2,1)} custom-call(bf16[1184,1536]{1,0:T(8,128)(2,1)} %add_convert_fusion.acts_ref.outer_ref, bf16[1184,1152]{1,0:T(8,128)(2,1)} %get-tuple-element.562.inner_ref.acts_ref), custom_call_target="tpu_custom_call" | custom-call | flops 4190109 | bytes 13443 | tf_op jit(solution)/shard_map/pallas_call | solution.py:483
  532.8 5.9 shard_map.391.refs_4_
  541.5 8.3 %shard_map.392 = (bf16[1184,384]{1,0:T(8,128)(2,1)}, bf16[1184,384]{1,0:T(8,128)(2,1)}) custom-call(s32[8]{0:T(128)} %fusion.32.slots_ref, bf16[1184,1152]{1,0:T(8,128)(2,1)} %get-tuple-element.562.inner_ref.acts_ref, bf16[2,192,1536]{2,1,0:T(8,128)(2,1)} %shard_map.369.refs_0_, bf16[2,192,1536]{2,1,0:T(8,128)(2,1)} %copy-done.2, ...), custom_call_target="tpu_custom_call" | custom-call | flops 2095054 | bytes 8085 | tf_op jit(solution)/shard_map/pallas_call | solution.py:448
  553.7 8.2 %shard_map.393 = (bf16[1184,384]{1,0:T(8,128)(2,1)}, bf16[1184,384]{1,0:T(8,128)(2,1)}) custom-call(s32[8]{0:T(128)} %fusion.32.slots_ref, bf16[1184,1152]{1,0:T(8,128)(2,1)} %get-tuple-element.562.inner_ref.acts_ref, bf16[2,192,1536]{2,1,0:T(8,128)(2,1)} %shard_map.369.refs_0_, bf16[2,192,1536]{2,1,0:T(8,128)(2,1)} %copy-done.2, ...), custom_call_target="tpu_custom_call" | custom-call | flops 2095054 | bytes 8085 | tf_op jit(solution)/shard_map/pallas_call | solution.py:448
  574.6 11.5 %shard_map.394 = (f32[192,2,4,384]{3,2,1,0:T(4,128)}, f32[192,2,4,384]{3,2,1,0:T(4,128)}, f32[2,192,2,4,384]{4,3,2,1,0:T(4,128)}) custom-call(s32[1]{0:T(128)} %bitcast.17.slot_ref, f32[192,2,4,384]{3,2,1,0:T(4,128)} %refs_0_.2, f32[2,192,2,4,384]{4,3,2,1,0:T(4,128)} %refs_1_, bf16[2,1536,1536]{2,1,0:T(8,128)(2,1)} %shard_map.379.refs_2_, ...), custom_call_target="tpu_custom_call" | custom-call | flops 11796 | bytes 23592 | tf_op jit(solution)/shard_map/pallas_call | solution.py:170
  593.7 5.0 collective-permute-done.72
  612.9 4.9 all-to-all-done.1
  629.1 11.2 %shard_map.395 = (f32[192,2,4,384]{3,2,1,0:T(4,128)}, f32[192,2,4,384]{3,2,1,0:T(4,128)}, f32[2,192,2,4,384]{4,3,2,1,0:T(4,128)}) custom-call(s32[1]{0:T(128)} %bitcast.17.slot_ref, f32[192,2,4,384]{3,2,1,0:T(4,128)} %refs_0_.3, f32[2,192,2,4,384]{4,3,2,1,0:T(4,128)} %refs_1_.1, bf16[2,1536,1536]{2,1,0:T(8,128)(2,1)} %shard_map.383.refs_2_, ...), custom_call_target="tpu_custom_call" | custom-call | flops 11796 | bytes 23592 | tf_op jit(solution)/shard_map/pallas_call | solution.py:170
  641.5 4.5 add_convert_fusion.1
  650.2 14.7 %shard_map.396 = (f32[192,6,2,384]{3,2,1,0:T(2,128)}, f32[192,6,2,384]{3,2,1,0:T(2,128)}, f32[192,6,2,384]{3,2,1,0:T(2,128)}, f32[192,6,2,384]{3,2,1,0:T(2,128)}) custom-call(bf16[192,8]{1,0:T(8,128)(2,1)} %bitcast.79, bf16[8,4608]{1,0:T(8,128)(2,1)} %bitcast.80, f32[192,6,2,384]{3,2,1,0:T(2,128)} %bitcast.69, f32[2,192,6,2,384]{4,3,2,1,0:T(2,128)} %bitcast.70), custom_call_target="tpu_custom_call" | custom-call | flops 17694 | bytes 35389 | tf_op jit(solution)/shard_map/pallas_call | solution.py:213
  668.7 5.4 collective-permute-done.83.refs_5_
  675.2 11.6 %shard_map.397 = (f32[192,3,2,384]{3,2,1,0:T(2,128)}, f32[192,3,2,384]{3,2,1,0:T(2,128)}, f32[2,192,3,2,384]{4,3,2,1,0:T(2,128)}, f32[192,1,2,384]{3,2,1,0:T(2,1...) custom-call(s32[1]{0:T(128)} %bitcast.17.slot_ref, f32[192,3,2,384]{3,2,1,0:T(2,128)} %bitcast.72, ...), custom_call_target="tpu_custom_call" | custom-call | flops 11796 | bytes 23592 | tf_op jit(solution)/shard_map/pallas_call | solution.py:170
  (446 shorter events, 219.9 us)
Async XLA Ops:
  5.5 37.5 %collective-permute-start.6 = (bf16[2,192,1536]{2,1,0:T(8,128)(2,1)}, bf16[2,192,1536]{2,1,0:T(8,128)(2,1)S(1)}, u32[]{:S(2)}, u32[]{:S(2)}) collective-permute-start(bf16[2,192,1536]{2,1,0:T(8,128)(2,1)} %shard_map.369.refs_0_), channel_id=1, source_target_pairs={{8,0},{16,8},{24,16},{28,24},{20,28},{12,20},{4,12},{0,4},{9,1},{1... | collective-permute-start | bytes 3538952 | tf_op jit(solution)/shard_map/ppermute | solution.py:732
  8.4 34.9 %collective-permute-start.5 = (bf16[2,192,1536]{2,1,0:T(8,128)(2,1)}, bf16[2,192,1536]{2,1,0:T(8,128)(2,1)S(1)}, u32[]{:S(2)}, u32[]{:S(2)}) collective-permute-start(bf16[2,192,1536]{2,1,0:T(8,128)(2,1)} %shard_map.369.refs_0_), channel_id=1, source_target_pairs={{0,8},{8,16},{16,24},{24,28},{28,20},{20,12},{12,4},{4,0},{1,9},{9... | collective-permute-start | bytes 3538952 | tf_op jit(solution)/shard_map/ppermute | solution.py:732
  20.3 26.0 %collective-permute-start.1 = (bf16[1184,384]{1,0:T(8,128)(2,1)}, bf16[1184,384]{1,0:T(8,128)(2,1)}, u32[]{:S(2)}, u32[]{:S(2)}) collective-permute-start(bf16[1184,384]{1,0:T(8,128)(2,1)} %concatenate.32), channel_id=1, source_target_pairs={{0,2},{1,3},{2,0},{3,1},{4,6},{5,7},{6,4},{7,5},{8,10},{9,11},{10,... | collective-permute-start | bytes 2727944 | tf_op jit(solution)/shard_map/ppermute | solution.py:707
  46.8 28.1 %collective-permute-start.8 = (bf16[2,192,1536]{2,1,0:T(8,128)(2,1)S(1)}, bf16[2,192,1536]{2,1,0:T(8,128)(2,1)}, u32[]{:S(2)}, u32[]{:S(2)}) collective-permute-start(bf16[2,192,1536]{2,1,0:T(8,128)(2,1)S(1)} %collective-permute-done.5.refs_6_), channel_id=1, source_target_pairs={{0,8},{8,16},{16,24},{24,28},{28,20},{20,12},{12,4},{4,0},{1,9},{9... | collective-permute-start | bytes 3538952 | tf_op jit(solution)/shard_map/ppermute | solution.py:732
  46.8 28.1 %collective-permute-start.9 = (bf16[2,192,1536]{2,1,0:T(8,128)(2,1)S(1)}, bf16[2,192,1536]{2,1,0:T(8,128)(2,1)}, u32[]{:S(2)}, u32[]{:S(2)}) collective-permute-start(bf16[2,192,1536]{2,1,0:T(8,128)(2,1)S(1)} %collective-permute-done.6.refs_1_), channel_id=1, source_target_pairs={{8,0},{16,8},{24,16},{28,24},{20,28},{12,20},{4,12},{0,4},{9,1},{1... | collective-permute-start | bytes 3538952 | tf_op jit(solution)/shard_map/ppermute | solution.py:732
  74.9 27.4 %collective-permute-start.12 = (bf16[2,192,1536]{2,1,0:T(8,128)(2,1)}, bf16[2,192,1536]{2,1,0:T(8,128)(2,1)S(1)}, u32[]{:S(2)}, u32[]{:S(2)}) collective-permute-start(bf16[2,192,1536]{2,1,0:T(8,128)(2,1)} %collective-permute-done.8.refs_5_), channel_id=1, source_target_pairs={{0,8},{8,16},{16,24},{24,28},{28,20},{20,12},{12,4},{4,0},{1,9},{9... | collective-permute-start | bytes 3538952 | tf_op jit(solution)/shard_map/ppermute | solution.py:732
  75.6 27.1 %collective-permute-start.13 = (bf16[2,192,1536]{2,1,0:T(8,128)(2,1)}, bf16[2,192,1536]{2,1,0:T(8,128)(2,1)S(1)}, u32[]{:S(2)}, u32[]{:S(2)}) collective-permute-start(bf16[2,192,1536]{2,1,0:T(8,128)(2,1)} %collective-permute-done.9.refs_2_), channel_id=1, source_target_pairs={{8,0},{16,8},{24,16},{28,24},{20,28},{12,20},{4,12},{0,4},{9,1},{1... | collective-permute-start | bytes 3538952 | tf_op jit(solution)/shard_map/ppermute | solution.py:732
  76.9 27.9 %collective-permute-start.11 = (bf16[1184,384]{1,0:T(8,128)(2,1)}, bf16[1184,384]{1,0:T(8,128)(2,1)}, u32[]{:S(2)}, u32[]{:S(2)}) collective-permute-start(bf16[1184,384]{1,0:T(8,128)(2,1)} %concatenate.35), channel_id=1, source_target_pairs={{0,2},{1,3},{2,0},{3,1},{4,6},{5,7},{6,4},{7,5},{8,10},{9,11},{10,... | collective-permute-start | bytes 2727944 | tf_op jit(solution)/shard_map/ppermute | solution.py:707
  117.4 27.0 %collective-permute-start.18 = (bf16[2,192,1536]{2,1,0:T(8,128)(2,1)}, bf16[2,192,1536]{2,1,0:T(8,128)(2,1)}, u32[]{:S(2)}, u32[]{:S(2)}) collective-permute-start(bf16[2,192,1536]{2,1,0:T(8,128)(2,1)} %shard_map.370.refs_0_), channel_id=1, source_target_pairs={{8,0},{16,8},{24,16},{28,24},{20,28},{12,20},{4,12},{0,4},{9,1},{1... | collective-permute-start | bytes 3538952 | tf_op jit(solution)/shard_map/ppermute | solution.py:732
  118.5 25.8 %collective-permute-start.17 = (bf16[2,192,1536]{2,1,0:T(8,128)(2,1)}, bf16[2,192,1536]{2,1,0:T(8,128)(2,1)}, u32[]{:S(2)}, u32[]{:S(2)}) collective-permute-start(bf16[2,192,1536]{2,1,0:T(8,128)(2,1)} %shard_map.370.refs_0_), channel_id=1, source_target_pairs={{0,8},{8,16},{16,24},{24,28},{28,20},{20,12},{12,4},{4,0},{1,9},{9... | collective-permute-start | bytes 3538952 | tf_op jit(solution)/shard_map/ppermute | solution.py:732
  144.4 28.3 %collective-permute-start.19 = (bf16[2,192,1536]{2,1,0:T(8,128)(2,1)}, bf16[2,192,1536]{2,1,0:T(8,128)(2,1)S(1)}, u32[]{:S(2)}, u32[]{:S(2)}) collective-permute-start(bf16[2,192,1536]{2,1,0:T(8,128)(2,1)} %collective-permute-done.17.refs_6_), channel_id=1, source_target_pairs={{0,8},{8,16},{16,24},{24,28},{28,20},{20,12},{12,4},{4,0},{1,9},{9... | collective-permute-start | bytes 3538952 | tf_op jit(solution)/shard_map/ppermute | solution.py:732
  145.0 28.3 %collective-permute-start.20 = (bf16[2,192,1536]{2,1,0:T(8,128)(2,1)}, bf16[2,192,1536]{2,1,0:T(8,128)(2,1)S(1)}, u32[]{:S(2)}, u32[]{:S(2)}) collective-permute-start(bf16[2,192,1536]{2,1,0:T(8,128)(2,1)} %collective-permute-done.18.refs_1_), channel_id=1, source_target_pairs={{8,0},{16,8},{24,16},{28,24},{20,28},{12,20},{4,12},{0,4},{9,1},{1... | collective-permute-start | bytes 3538952 | tf_op jit(solution)/shard_map/ppermute | solution.py:732
  173.8 27.9 %collective-permute-start.24 = (bf16[2,192,1536]{2,1,0:T(8,128)(2,1)S(1)}, bf16[2,192,1536]{2,1,0:T(8,128)(2,1)S(1)}, u32[]{:S(2)}, u32[]{:S(2)}) collective-permute-start(bf16[2,192,1536]{2,1,0:T(8,128)(2,1)S(1)} %collective-permute-done.19.refs_5_), channel_id=1, source_target_pairs={{0,8},{8,16},{16,24},{24,28},{28,20},{20,12},{12,4},{4,0},{1,9},{9... | collective-permute-start | bytes 3538952 | tf_op jit(solution)/shard_map/ppermute | solution.py:732
  174.4 27.6 %collective-permute-start.25 = (bf16[2,192,1536]{2,1,0:T(8,128)(2,1)S(1)}, bf16[2,192,1536]{2,1,0:T(8,128)(2,1)S(1)}, u32[]{:S(2)}, u32[]{:S(2)}) collective-permute-start(bf16[2,192,1536]{2,1,0:T(8,128)(2,1)S(1)} %collective-permute-done.20.refs_2_), channel_id=1, source_target_pairs={{8,0},{16,8},{24,16},{28,24},{20,28},{12,20},{4,12},{0,4},{9,1},{1... | collective-permute-start | bytes 3538952 | tf_op jit(solution)/shard_map/ppermute | solution.py:732
  183.4 21.6 %collective-permute-start.23 = (bf16[1184,384]{1,0:T(8,128)(2,1)S(1)}, bf16[1184,384]{1,0:T(8,128)(2,1)S(1)}, u32[]{:S(2)}, u32[]{:S(2)}) collective-permute-start(bf16[1184,384]{1,0:T(8,128)(2,1)S(1)} %get-tuple-element.406), channel_id=1, source_target_pairs={{0,2},{1,3},{2,0},{3,1},{4,6},{5,7},{6,4},{7,5},{8,10},{9,11},{10,... | collective-permute-start | bytes 2727944 | tf_op jit(solution)/shard_map/ppermute | solution.py:707
  217.4 25.5 %collective-permute-start.34 = (bf16[2,192,1536]{2,1,0:T(8,128)(2,1)S(1)}, bf16[2,192,1536]{2,1,0:T(8,128)(2,1)S(1)}, u32[]{:S(2)}, u32[]{:S(2)}) collective-permute-start(bf16[2,192,1536]{2,1,0:T(8,128)(2,1)S(1)} %copy-done.10), channel_id=1, source_target_pairs={{8,0},{16,8},{24,16},{28,24},{20,28},{12,20},{4,12},{0,4},{9,1},{1... | collective-permute-start | bytes 3538952 | tf_op jit(solution)/shard_map/ppermute | solution.py:732
  218.8 25.2 %collective-permute-start.33 = (bf16[2,192,1536]{2,1,0:T(8,128)(2,1)S(1)}, bf16[2,192,1536]{2,1,0:T(8,128)(2,1)S(1)}, u32[]{:S(2)}, u32[]{:S(2)}) collective-permute-start(bf16[2,192,1536]{2,1,0:T(8,128)(2,1)S(1)} %copy-done.10), channel_id=1, source_target_pairs={{0,8},{8,16},{16,24},{24,28},{28,20},{20,12},{12,4},{4,0},{1,9},{9... | collective-permute-start | bytes 3538952 | tf_op jit(solution)/shard_map/ppermute | solution.py:732
  220.6 26.2 %collective-permute-start.32 = (bf16[1184,384]{1,0:T(8,128)(2,1)S(1)}, bf16[1184,384]{1,0:T(8,128)(2,1)S(1)}, u32[]{:S(2)}, u32[]{:S(2)}) collective-permute-start(bf16[1184,384]{1,0:T(8,128)(2,1)S(1)} %add_convert_fusion.18), channel_id=1, source_target_pairs={{0,2},{1,3},{2,0},{3,1},{4,6},{5,7},{6,4},{7,5},{8,10},{9,11},{10,... | collective-permute-start | bytes 2727944 | tf_op jit(solution)/shard_map/ppermute | solution.py:707
  247.4 28.1 %collective-permute-start.36 = (bf16[2,192,1536]{2,1,0:T(8,128)(2,1)S(1)}, bf16[2,192,1536]{2,1,0:T(8,128)(2,1)}, u32[]{:S(2)}, u32[]{:S(2)}) collective-permute-start(bf16[2,192,1536]{2,1,0:T(8,128)(2,1)S(1)} %collective-permute-done.33.refs_6_), channel_id=1, source_target_pairs={{0,8},{8,16},{16,24},{24,28},{28,20},{20,12},{12,4},{4,0},{1,9},{9... | collective-permute-start | bytes 3538952 | tf_op jit(solution)/shard_map/ppermute | solution.py:732
  248.1 28.0 %collective-permute-start.37 = (bf16[2,192,1536]{2,1,0:T(8,128)(2,1)S(1)}, bf16[2,192,1536]{2,1,0:T(8,128)(2,1)}, u32[]{:S(2)}, u32[]{:S(2)}) collective-permute-start(bf16[2,192,1536]{2,1,0:T(8,128)(2,1)S(1)} %collective-permute-done.34.refs_1_), channel_id=1, source_target_pairs={{8,0},{16,8},{24,16},{28,24},{20,28},{12,20},{4,12},{0,4},{9,1},{1... | collective-permute-start | bytes 3538952 | tf_op jit(solution)/shard_map/ppermute | solution.py:732
  276.1 27.1 %collective-permute-start.38 = (bf16[2,192,1536]{2,1,0:T(8,128)(2,1)}, bf16[2,192,1536]{2,1,0:T(8,128)(2,1)}, u32[]{:S(2)}, u32[]{:S(2)}) collective-permute-start(bf16[2,192,1536]{2,1,0:T(8,128)(2,1)} %collective-permute-done.36.refs_5_), channel_id=1, source_target_pairs={{0,8},{8,16},{16,24},{24,28},{28,20},{20,12},{12,4},{4,0},{1,9},{9... | collective-permute-start | bytes 3538952 | tf_op jit(solution)/shard_map/ppermute | solution.py:732
  276.6 26.8 %collective-permute-start.39 = (bf16[2,192,1536]{2,1,0:T(8,128)(2,1)}, bf16[2,192,1536]{2,1,0:T(8,128)(2,1)}, u32[]{:S(2)}, u32[]{:S(2)}) collective-permute-start(bf16[2,192,1536]{2,1,0:T(8,128)(2,1)} %collective-permute-done.37.refs_2_), channel_id=1, source_target_pairs={{8,0},{16,8},{24,16},{28,24},{20,28},{12,20},{4,12},{0,4},{9,1},{1... | collective-permute-start | bytes 3538952 | tf_op jit(solution)/shard_map/ppermute | solution.py:732
  320.5 26.9 %collective-permute-start.42 = (bf16[2,192,1536]{2,1,0:T(8,128)(2,1)}, bf16[2,192,1536]{2,1,0:T(8,128)(2,1)}, u32[]{:S(2)}, u32[]{:S(2)}) collective-permute-start(bf16[2,192,1536]{2,1,0:T(8,128)(2,1)} %get-tuple-element.456), channel_id=1, source_target_pairs={{0,8},{8,16},{16,24},{24,28},{28,20},{20,12},{12,4},{4,0},{1,9},{9... | collective-permute-start | bytes 3538952 | tf_op jit(solution)/shard_map/ppermute | solution.py:732
  321.0 26.3 %collective-permute-start.43 = (bf16[2,192,1536]{2,1,0:T(8,128)(2,1)}, bf16[2,192,1536]{2,1,0:T(8,128)(2,1)}, u32[]{:S(2)}, u32[]{:S(2)}) collective-permute-start(bf16[2,192,1536]{2,1,0:T(8,128)(2,1)} %get-tuple-element.457), channel_id=1, source_target_pairs={{8,0},{16,8},{24,16},{28,24},{20,28},{12,20},{4,12},{0,4},{9,1},{1... | collective-permute-start | bytes 3538952 | tf_op jit(solution)/shard_map/ppermute | solution.py:732
  354.2 28.1 %collective-permute-start.47 = (bf16[2,192,1536]{2,1,0:T(8,128)(2,1)}, bf16[2,192,1536]{2,1,0:T(8,128)(2,1)S(1)}, u32[]{:S(2)}, u32[]{:S(2)}) collective-permute-start(bf16[2,192,1536]{2,1,0:T(8,128)(2,1)} %get-tuple-element.476), channel_id=1, source_target_pairs={{0,8},{8,16},{16,24},{24,28},{28,20},{20,12},{12,4},{4,0},{1,9},{9... | collective-permute-start | bytes 3538952 | tf_op jit(solution)/shard_map/ppermute | solution.py:732
  354.8 28.1 %collective-permute-start.48 = (bf16[2,192,1536]{2,1,0:T(8,128)(2,1)}, bf16[2,192,1536]{2,1,0:T(8,128)(2,1)}, u32[]{:S(2)}, u32[]{:S(2)}) collective-permute-start(bf16[2,192,1536]{2,1,0:T(8,128)(2,1)} %get-tuple-element.477), channel_id=1, source_target_pairs={{8,0},{16,8},{24,16},{28,24},{20,28},{12,20},{4,12},{0,4},{9,1},{1... | collective-permute-start | bytes 3538952 | tf_op jit(solution)/shard_map/ppermute | solution.py:732
  368.5 21.8 %collective-permute-start.46 = (bf16[1184,384]{1,0:T(8,128)(2,1)}, bf16[1184,384]{1,0:T(8,128)(2,1)}, u32[]{:S(2)}, u32[]{:S(2)}) collective-permute-start(bf16[1184,384]{1,0:T(8,128)(2,1)} %add_convert_fusion.17), channel_id=1, source_target_pairs={{0,2},{1,3},{2,0},{3,1},{4,6},{5,7},{6,4},{7,5},{8,10},{9,11},{10,... | collective-permute-start | bytes 2727944 | tf_op jit(solution)/shard_map/ppermute | solution.py:707
  385.6 26.8 %collective-permute-start.50 = (bf16[2,192,1536]{2,1,0:T(8,128)(2,1)S(1)}, bf16[2,192,1536]{2,1,0:T(8,128)(2,1)S(1)}, u32[]{:S(2)}, u32[]{:S(2)}) collective-permute-start(bf16[2,192,1536]{2,1,0:T(8,128)(2,1)S(1)} %get-tuple-element.486), channel_id=1, source_target_pairs={{0,8},{8,16},{16,24},{24,28},{28,20},{20,12},{12,4},{4,0},{1,9},{9... | collective-permute-start | bytes 3538952 | tf_op jit(solution)/shard_map/ppermute | solution.py:732
  386.6 26.4 %collective-permute-start.51 = (bf16[2,192,1536]{2,1,0:T(8,128)(2,1)S(1)}, bf16[2,192,1536]{2,1,0:T(8,128)(2,1)S(1)}, u32[]{:S(2)}, u32[]{:S(2)}) collective-permute-start(bf16[2,192,1536]{2,1,0:T(8,128)(2,1)S(1)} %get-tuple-element.487), channel_id=1, source_target_pairs={{8,0},{16,8},{24,16},{28,24},{20,28},{12,20},{4,12},{0,4},{9,1},{1... | collective-permute-start | bytes 3538952 | tf_op jit(solution)/shard_map/ppermute | solution.py:732
  395.0 21.0 %collective-permute-start.53 = (f32[2,1184]{1,0:T(2,128)S(1)}, f32[2,1184]{1,0:T(2,128)S(1)}, u32[]{:S(2)}, u32[]{:S(2)}) collective-permute-start(f32[2,1184]{1,0:T(2,128)S(1)} %pad_maximum_fusion.7), channel_id=1, source_target_pairs={{0,3},{1,2},{2,1},{3,0},{4,7},{5,6},{6,5},{7,4},{8,11},{9,10},{10,... | collective-permute-start | bytes 28424 | tf_op jit(solution)/shard_map/ppermute | solution.py:707
  416.1 28.6 %collective-permute-start.57 = (bf16[2,192,1536]{2,1,0:T(8,128)(2,1)}, bf16[2,192,1536]{2,1,0:T(8,128)(2,1)}, u32[]{:S(2)}, u32[]{:S(2)}) collective-permute-start(bf16[2,192,1536]{2,1,0:T(8,128)(2,1)} %add_convert_fusion.10), channel_id=1, source_target_pairs={{0,8},{8,16},{16,24},{24,28},{28,20},{20,12},{12,4},{4,0},{1,9},{9... | collective-permute-start | bytes 3538952 | tf_op jit(solution)/shard_map/ppermute | solution.py:732
  417.1 27.5 %collective-permute-start.58 = (bf16[2,192,1536]{2,1,0:T(8,128)(2,1)S(1)}, bf16[2,192,1536]{2,1,0:T(8,128)(2,1)}, u32[]{:S(2)}, u32[]{:S(2)}) collective-permute-start(bf16[2,192,1536]{2,1,0:T(8,128)(2,1)S(1)} %get-tuple-element.502), channel_id=1, source_target_pairs={{8,0},{16,8},{24,16},{28,24},{20,28},{12,20},{4,12},{0,4},{9,1},{1... | collective-permute-start | bytes 3538952 | tf_op jit(solution)/shard_map/ppermute | solution.py:732
  424.4 22.2 %collective-permute-start.56 = (bf16[1184,384]{1,0:T(8,128)(2,1)S(1)}, bf16[1184,384]{1,0:T(8,128)(2,1)}, u32[]{:S(2)}, u32[]{:S(2)}) collective-permute-start(bf16[1184,384]{1,0:T(8,128)(2,1)S(1)} %get-tuple-element.500), channel_id=1, source_target_pairs={{0,2},{1,3},{2,0},{3,1},{4,6},{5,7},{6,4},{7,5},{8,10},{9,11},{10,... | collective-permute-start | bytes 2727944 | tf_op jit(solution)/shard_map/ppermute | solution.py:707
  447.1 29.2 %collective-permute-start.54 = (bf16[1184,384]{1,0:T(8,128)(2,1)}, bf16[1184,384]{1,0:T(8,128)(2,1)S(1)}, u32[]{:S(2)}, u32[]{:S(2)}) collective-permute-start(bf16[1184,384]{1,0:T(8,128)(2,1)} %get-tuple-element.499), channel_id=1, source_target_pairs={{0,1},{1,0},{2,3},{3,2},{4,5},{5,4},{6,7},{7,6},{8,9},{9,8},{10,11... | collective-permute-start | bytes 2727944 | tf_op jit(solution)/shard_map/ppermute | solution.py:707
  447.2 29.1 %collective-permute-start.60 = (bf16[1184,384]{1,0:T(8,128)(2,1)}, bf16[1184,384]{1,0:T(8,128)(2,1)}, u32[]{:S(2)}, u32[]{:S(2)}) collective-permute-start(bf16[1184,384]{1,0:T(8,128)(2,1)} %get-tuple-element.516), channel_id=1, source_target_pairs={{0,1},{1,0},{2,3},{3,2},{4,5},{5,4},{6,7},{7,6},{8,9},{9,8},{10,11... | collective-permute-start | bytes 2727944 | tf_op jit(solution)/shard_map/ppermute | solution.py:707
  447.6 33.1 %collective-permute-start.62 = (bf16[2,192,1536]{2,1,0:T(8,128)(2,1)S(1)}, bf16[2,192,1536]{2,1,0:T(8,128)(2,1)}, u32[]{:S(2)}, u32[]{:S(2)}) collective-permute-start(bf16[2,192,1536]{2,1,0:T(8,128)(2,1)S(1)} %get-tuple-element.523), channel_id=1, source_target_pairs={{0,8},{8,16},{16,24},{24,28},{28,20},{20,12},{12,4},{4,0},{1,9},{9... | collective-permute-start | bytes 3538952 | tf_op jit(solution)/shard_map/ppermute | solution.py:732
  449.8 30.9 %collective-permute-start.63 = (bf16[2,192,1536]{2,1,0:T(8,128)(2,1)S(1)}, bf16[2,192,1536]{2,1,0:T(8,128)(2,1)}, u32[]{:S(2)}, u32[]{:S(2)}) collective-permute-start(bf16[2,192,1536]{2,1,0:T(8,128)(2,1)S(1)} %add_convert_fusion.9), channel_id=1, source_target_pairs={{8,0},{16,8},{24,16},{28,24},{20,28},{12,20},{4,12},{0,4},{9,1},{1... | collective-permute-start | bytes 3538952 | tf_op jit(solution)/shard_map/ppermute | solution.py:732
  483.7 29.7 %collective-permute-start.64 = (bf16[2,192,1536]{2,1,0:T(8,128)(2,1)S(1)}, bf16[2,192,1536]{2,1,0:T(8,128)(2,1)S(1)}, u32[]{:S(2)}, u32[]{:S(2)}) collective-permute-start(bf16[2,192,1536]{2,1,0:T(8,128)(2,1)S(1)} %get-tuple-element.542), channel_id=1, source_target_pairs={{0,8},{8,16},{16,24},{24,28},{28,20},{20,12},{12,4},{4,0},{1,9},{9... | collective-permute-start | bytes 3538952 | tf_op jit(solution)/shard_map/ppermute | solution.py:732
  484.6 28.9 %collective-permute-start.65 = (bf16[2,192,1536]{2,1,0:T(8,128)(2,1)S(1)}, bf16[2,192,1536]{2,1,0:T(8,128)(2,1)}, u32[]{:S(2)}, u32[]{:S(2)}) collective-permute-start(bf16[2,192,1536]{2,1,0:T(8,128)(2,1)S(1)} %get-tuple-element.543), channel_id=1, source_target_pairs={{8,0},{16,8},{24,16},{28,24},{20,28},{12,20},{4,12},{0,4},{9,1},{1... | collective-permute-start | bytes 3538952 | tf_op jit(solution)/shard_map/ppermute | solution.py:732
  485.8 27.6 %collective-permute-start.61 = (bf16[1184,384]{1,0:T(8,128)(2,1)}, bf16[1184,384]{1,0:T(8,128)(2,1)S(1)}, u32[]{:S(2)}, u32[]{:S(2)}) collective-permute-start(bf16[1184,384]{1,0:T(8,128)(2,1)} %add_convert_fusion.16), channel_id=1, source_target_pairs={{0,2},{1,3},{2,0},{3,1},{4,6},{5,7},{6,4},{7,5},{8,10},{9,11},{10,... | collective-permute-start | bytes 2727944 | tf_op jit(solution)/shard_map/ppermute | solution.py:707
  517.8 32.0 %collective-permute-start.66 = (bf16[2,192,1536]{2,1,0:T(8,128)(2,1)}, bf16[2,192,1536]{2,1,0:T(8,128)(2,1)}, u32[]{:S(2)}, u32[]{:S(2)}) collective-permute-start(bf16[2,192,1536]{2,1,0:T(8,128)(2,1)} %get-tuple-element.552), channel_id=1, source_target_pairs={{0,8},{8,16},{16,24},{24,28},{28,20},{20,12},{12,4},{4,0},{1,9},{9... | collective-permute-start | bytes 3538952 | tf_op jit(solution)/shard_map/ppermute | solution.py:732
  518.8 31.1 %collective-permute-start.67 = (bf16[2,192,1536]{2,1,0:T(8,128)(2,1)}, bf16[2,192,1536]{2,1,0:T(8,128)(2,1)}, u32[]{:S(2)}, u32[]{:S(2)}) collective-permute-start(bf16[2,192,1536]{2,1,0:T(8,128)(2,1)} %get-tuple-element.553), channel_id=1, source_target_pairs={{8,0},{16,8},{24,16},{28,24},{20,28},{12,20},{4,12},{0,4},{9,1},{1... | collective-permute-start | bytes 3538952 | tf_op jit(solution)/shard_map/ppermute | solution.py:732
  572.4 26.4 %collective-permute-start.72 = (bf16[2,192,1536]{2,1,0:T(8,128)(2,1)}, bf16[2,192,1536]{2,1,0:T(8,128)(2,1)}, u32[]{:S(2)}, u32[]{:S(2)}) collective-permute-start(bf16[2,192,1536]{2,1,0:T(8,128)(2,1)} %pad_maximum_fusion.3), channel_id=1, source_target_pairs={{0,8},{8,16},{16,24},{24,28},{28,20},{20,12},{12,4},{4,0},{1,9},{9... | collective-permute-start | bytes 3538952 | tf_op jit(solution)/shard_map/ppermute | solution.py:732
  573.2 26.3 %collective-permute-start.73 = (bf16[2,192,1536]{2,1,0:T(8,128)(2,1)}, bf16[2,192,1536]{2,1,0:T(8,128)(2,1)}, u32[]{:S(2)}, u32[]{:S(2)}) collective-permute-start(bf16[2,192,1536]{2,1,0:T(8,128)(2,1)} %pad_maximum_fusion.4), channel_id=1, source_target_pairs={{8,0},{16,8},{24,16},{28,24},{20,28},{12,20},{4,12},{0,4},{9,1},{1... | collective-permute-start | bytes 3538952 | tf_op jit(solution)/shard_map/ppermute | solution.py:732
  610.9 30.1 %collective-permute-start.75 = (bf16[2,192,1536]{2,1,0:T(8,128)(2,1)}, bf16[2,192,1536]{2,1,0:T(8,128)(2,1)}, u32[]{:S(2)}, u32[]{:S(2)}) collective-permute-start(bf16[2,192,1536]{2,1,0:T(8,128)(2,1)} %get-tuple-element.589), channel_id=1, source_target_pairs={{0,8},{8,16},{16,24},{24,28},{28,20},{20,12},{12,4},{4,0},{1,9},{9... | collective-permute-start | bytes 3538952 | tf_op jit(solution)/shard_map/ppermute | solution.py:732
  612.9 28.6 %collective-permute-start.76 = (bf16[2,192,1536]{2,1,0:T(8,128)(2,1)}, bf16[2,192,1536]{2,1,0:T(8,128)(2,1)}, u32[]{:S(2)}, u32[]{:S(2)}) collective-permute-start(bf16[2,192,1536]{2,1,0:T(8,128)(2,1)} %get-tuple-element.590), channel_id=1, source_target_pairs={{8,0},{16,8},{24,16},{28,24},{20,28},{12,20},{4,12},{0,4},{9,1},{1... | collective-permute-start | bytes 3538952 | tf_op jit(solution)/shard_map/ppermute | solution.py:732
  646.1 28.0 %collective-permute-start.83 = (bf16[2,192,1536]{2,1,0:T(8,128)(2,1)}, bf16[2,192,1536]{2,1,0:T(8,128)(2,1)}, u32[]{:S(2)}, u32[]{:S(2)}) collective-permute-start(bf16[2,192,1536]{2,1,0:T(8,128)(2,1)} %get-tuple-element.617), channel_id=1, source_target_pairs={{0,8},{8,16},{16,24},{24,28},{28,20},{20,12},{12,4},{4,0},{1,9},{9... | collective-permute-start | bytes 3538952 | tf_op jit(solution)/shard_map/ppermute | solution.py:732
  647.5 27.7 %collective-permute-start.84 = (bf16[2,192,1536]{2,1,0:T(8,128)(2,1)}, bf16[2,192,1536]{2,1,0:T(8,128)(2,1)}, u32[]{:S(2)}, u32[]{:S(2)}) collective-permute-start(bf16[2,192,1536]{2,1,0:T(8,128)(2,1)} %get-tuple-element.618), channel_id=1, source_target_pairs={{8,0},{16,8},{24,16},{28,24},{20,28},{12,20},{4,12},{0,4},{9,1},{1... | collective-permute-start | bytes 3538952 | tf_op jit(solution)/shard_map/ppermute | solution.py:732
  (105 other events, 3019.5 us)

commit v5 on v4

--- a/solution.py
+++ b/solution.py
@@ -58,7 +58,8 @@
     return (param - LEARN_RATE * (update + DECAY_RATE * param), first_moment, second_moment)
 
 
-STEP_ROWS = 48
+def rows_per_step(height):
+    return 96 if height % 96 == 0 else 48
 
 
 def pieces(kind, index):
@@ -88,6 +89,7 @@
 def travel_rows(kinds, weights):
     views = [row_view(kind, weight) for kind, weight in zip(kinds, weights)]
     height = views[0].shape[0]
+    step_rows = rows_per_step(height)
 
     def kernel(*refs):
         out_ref = refs[-1]
@@ -103,11 +105,11 @@
     total = 12 * PAIR
     return pl.pallas_call(
         kernel,
-        grid=(height // STEP_ROWS,),
+        grid=(height // step_rows,),
         in_specs=[
-            pl.BlockSpec((STEP_ROWS, *view.shape[1:]), lambda i: (i, 0, 0, 0)) for view in views
+            pl.BlockSpec((step_rows, *view.shape[1:]), lambda i: (i, 0, 0, 0)) for view in views
         ],
-        out_specs=pl.BlockSpec((2, STEP_ROWS, total), lambda i: (0, i, 0)),
+        out_specs=pl.BlockSpec((2, step_rows, total), lambda i: (0, i, 0)),
         out_shape=jax.ShapeDtypeStruct((2, height, total), BF16),
         compiler_params=kernel_params(),
         cost_estimate=cost(2 * height * total, 12 * height * total),
@@ -118,7 +120,8 @@
     count = len(kinds)
     views = [row_view(kind, one) for kind, one in zip(kinds, params)]
     moment_views = [row_view(kind, one) for kind, one in zip(kinds, moments)]
-    parts = views[0].shape[0] // STEP_ROWS
+    step_rows = rows_per_step(views[0].shape[0])
+    parts = views[0].shape[0] // step_rows
 
     def kernel(slot_ref, *refs):
         param_refs, refs = refs[:count], refs[count:]
@@ -151,15 +154,15 @@
                     moved_ref[1, :, one, two] = second_moment
 
     param_specs = [
-        pl.BlockSpec((STEP_ROWS, *view.shape[1:]), lambda i, slot: (i, 0, 0, 0)) for view in views
+        pl.BlockSpec((step_rows, *view.shape[1:]), lambda i, slot: (i, 0, 0, 0)) for view in views
     ]
     moment_specs = [
-        pl.BlockSpec((2, STEP_ROWS, *view.shape[1:]), lambda i, slot: (0, i, 0, 0, 0))
+        pl.BlockSpec((2, step_rows, *view.shape[1:]), lambda i, slot: (0, i, 0, 0, 0))
         for view in views
     ]
     total = partial.shape[2]
-    grad_spec = pl.BlockSpec((2, STEP_ROWS, total), lambda i, slot: (0, i, 0))
-    own_spec = pl.BlockSpec((2, STEP_ROWS, total), lambda i, slot: (0, slot[0] * parts + i, 0))
+    grad_spec = pl.BlockSpec((2, step_rows, total), lambda i, slot: (0, i, 0))
+    own_spec = pl.BlockSpec((2, step_rows, total), lambda i, slot: (0, slot[0] * parts + i, 0))
     out_specs, out_shape = [], []
     for place, view in enumerate(views):
         out_specs += [param_specs[place], param_specs[place], moment_specs[place]]
@@ -188,6 +191,7 @@
 def adam_modulation(param, moments, rows, table):
     view, moment_view = (row_view("modulation", param), row_view("modulation", moments))
     height, count, streams, width = view.shape
+    step_rows = rows_per_step(height)
     turned = jnp.swapaxes(table, 1, 2).reshape(table.shape[0], count * streams * width)
 
     def kernel(rows_ref, table_ref, param_ref, moment_ref, next_ref, grad_ref, *moved_refs):
@@ -207,14 +211,14 @@
                 moved_refs[0][:, index, stream] = first_moment
                 moved_refs[1][:, index, stream] = second_moment
 
-    param_spec = pl.BlockSpec((STEP_ROWS, count, streams, width), lambda i: (i, 0, 0, 0))
-    moment_spec = pl.BlockSpec((2, STEP_ROWS, count, streams, width), lambda i: (0, i, 0, 0, 0))
+    param_spec = pl.BlockSpec((step_rows, count, streams, width), lambda i: (i, 0, 0, 0))
+    moment_spec = pl.BlockSpec((2, step_rows, count, streams, width), lambda i: (0, i, 0, 0, 0))
     shape = jax.ShapeDtypeStruct(view.shape, F32)
     results = pl.pallas_call(
         kernel,
-        grid=(height // STEP_ROWS,),
+        grid=(height // step_rows,),
         in_specs=[
-            pl.BlockSpec((STEP_ROWS, rows.shape[0]), lambda i: (i, 0)),
+            pl.BlockSpec((step_rows, rows.shape[0]), lambda i: (i, 0)),
             whole(turned.shape),
             param_spec,
             moment_spec,

time: 698 us -> 697 us (level)
  transfers between devices with their start and end apart: 87 -> 87, of which waited for: 45 -> 44; matrix products, arithmetic and copies ran while one was open for 16% -> 16% of each run, Pallas kernels for 39% -> 39%
where the time goes in v5:
time: 697 us; the launch traced here: 688 us
  Pallas kernels  286 us (41%)
  waiting for transfers between devices  174 us (25%)
  other arithmetic  98.1 us (14%)
  starting transfers between devices  80.9 us (12%)
  local copies, waits for them, and re-layouts  38.7 us (6%)
  between operations  7.1 us (1%)
    ppermute x46, waiting for transfers between devices, send(): self.held[way] = lax.ppermute(value, 'rows', ahead if way == 1 else behind)  141 us
    pallas_call x8, Pallas kernels, matmul_back(): pl.pallas_call(kernel, grid=(2,), in_specs=[pl.BlockSpec(memory_space=plt...  64.6 us
    convert_element_type x17, other arithmetic, narrow(): return values.astype(jnp.bfloat16)  57.1 us
    pallas_call x4, Pallas kernels, matmul_rows(): pl.pallas_call(kernel, grid=(tiles,), in_specs=[pl.BlockSpec(memory_space...  49.4 us
    ppermute x46, starting transfers between devices, send(): self.held[way] = lax.ppermute(value, 'rows', ahead if way == 1 else behind)  49.4 us
    pallas_call x3, Pallas kernels, attention_back(): pl.pallas_call(kernel, grid=(last - first,), in_specs=[pl.BlockSpec((rows...  40.3 us
    pallas_call x4, Pallas kernels, weight_gradient(): pl.pallas_call(kernel, grid=(height // tile,), in_specs=[column_spec(rows...  37.4 us
    pallas_call x3, Pallas kernels, adam_rows(): pl.pallas_call(kernel, grid_spec=pltpu.PrefetchScalarGridSpec(num_scalar_...  36.4 us
  transfers between devices with their start and end apart: 87, of which 44 were waited for; matrix products, arithmetic and copies ran while one was open for 16% of the time, Pallas kernels for 39%

profile of v5, /device:TPU:0, one launch (start us, length us, event | category | flops | bytes accessed | tf_op | source)
XLA Modules:
  0.0 687.6 jit_solution(13352753837755020205)
XLA Ops:
  0.7 4.4 shard_map.369.refs_0_
  13.8 6.1 concatenate.32
  22.6 5.8 all-to-all-start
  28.5 12.4 %all-to-all-done = f32[8,2,6,384]{3,1,2,0:T(2,128)S(1)} async-done(((f32[8,2,6,384]{3,1,2,0:T(2,128)}), f32[8,2,6,384]{3,1,2,0:T(2,128)S(1)}, u32[]{:S(2)}, u32[]{:S(2)}) %all-to-all-start) | async-done | bytes 147488 | tf_op jit(solution)/shard_map/all_to_all | solution.py:965
  53.1 9.9 %add_convert_fusion.acts_ref.outer_ref = bf16[1184,1536]{1,0:T(8,128)(2,1)} fusion(f32[1184,1536]{1,0:T(8,128)S(1)} %maximum_convert_fusion, f32[1536]{0:T(1024)S(1)} %get-tuple-element.746, f32[1536]{0:T(1024)S(1)} %get-tuple-element.747, f32[1536]{0:T(1024)S(1)} %get-tuple-element.748, f32[1536]{0:T(1024)S(1)} %get-tuple-element.745, ...), kind=kLoop, calls=%fused_computation.1 | loop fusion | flops 14548992 | bytes 10946976 | tf_op jit(solution)/shard_map/convert_element_type | solution.py:34
  63.0 6.2 concatenate.35
  69.2 5.4 collective-permute-done.8.refs_5_
  77.5 4.4 shard_map.370.refs_0_
  82.0 4.4 shard_map.371.refs_0_
  86.4 15.6 %collective-permute-done.12.refs_4_ = bf16[2,192,1536]{2,1,0:T(8,128)(2,1)S(1)} collective-permute-done((bf16[2,192,1536]{2,1,0:T(8,128)(2,1)}, bf16[2,192,1536]{2,1,0:T(8,128)(2,1)S(1)}, u32[]{:S(2)}, u32[]{:S(2)}) %collective-permute-start.12) | collective-permute-done | bytes 1179680 | tf_op jit(solution)/shard_map/ppermute | solution.py:736
  104.7 11.3 %collective-permute-done.16.refs_8_ = bf16[1,192,1536]{2,1,0:T(8,128)(2,1)S(1)} collective-permute-done((bf16[1,192,1536]{2,1,0:T(8,128)(2,1)S(1)}, bf16[1,192,1536]{2,1,0:T(8,128)(2,1)S(1)}, u32[]{:S(2)}, u32[]{:S(2)}) %collective-permute-start.16) | collective-permute-done | bytes 589856 | tf_op jit(solution)/shard_map/ppermute | solution.py:736
  123.4 11.1 %shard_map.372.triple_ref = bf16[1184,1152]{1,0:T(8,128)(2,1)} custom-call(s32[8]{0:T(128)} %fusion.32.slots_ref, bf16[1184,1536]{1,0:T(8,128)(2,1)} %add_convert_fusion.acts_ref.outer_ref, bf16[2,192,1536]{2,1,0:T(8,128)(2,1)} %shard_map.369.refs_0_, bf16[2,192,1536]{2,1,0:T(8,128)(2,1)} %copy-done.2, bf16[2,192,1536]{2,1,0:T(8,128)(2,1)} %collective-permute-done.9.refs_2_, ...), custom_call_target="tpu_custom_call" | custom-call | flops 4190109 | bytes 13443 | tf_op jit(solution)/shard_map/pallas_call | solution.py:298
  134.6 9.5 %shard_map.373 = (bf16[1184,384]{1,0:T(8,128)(2,1)}, f32[3,2,1184]{2,1,0:T(2,128)}) custom-call(bf16[1184,1152]{1,0:T(8,128)(2,1)} %shard_map.372.triple_ref), custom_call_target="tpu_custom_call" | custom-call | flops 8613003 | bytes 10911 | tf_op jit(solution)/shard_map/pallas_call | solution.py:540
  146.5 9.5 %shard_map.374 = (bf16[1184,384]{1,0:T(8,128)(2,1)}, f32[3,2,1184]{2,1,0:T(2,128)}) custom-call(bf16[1184,1152]{1,0:T(8,128)(2,1)} %shard_map.372.triple_ref, bf16[1184,384]{1,0:T(8,128)(2,1)} %get-tuple-element.379.refs_0_, f32[3,2,1184]{2,1,0:T(2,128)} %get-tuple-element.380.refs_1_), custom_call_target="tpu_custom_call", output_to_operand_aliasing={{0}: (1, {}), {1}: (2, {})} | custom-call | flops 8613003 | bytes 10911 | tf_op jit(solution)/shard_map/pallas_call | solution.py:540
  156.0 9.7 %shard_map.375 = (bf16[1184,384]{1,0:T(8,128)(2,1)}, f32[3,2,1184]{2,1,0:T(2,128)}) custom-call(bf16[1184,1152]{1,0:T(8,128)(2,1)} %shard_map.372.triple_ref, bf16[1184,384]{1,0:T(8,128)(2,1)} %get-tuple-element.384.refs_0_, f32[3,2,1184]{2,1,0:T(2,128)} %get-tuple-element.385.refs_1_), custom_call_target="tpu_custom_call", output_to_operand_aliasing={{0}: (1, {}), {1}: (2, {})} | custom-call | flops 8613003 | bytes 10911 | tf_op jit(solution)/shard_map/pallas_call | solution.py:540
  165.7 5.2 shard_map.376
  175.5 5.3 shard_map.377
  183.9 17.4 %collective-permute-done.24.refs_4_ = bf16[2,192,1536]{2,1,0:T(8,128)(2,1)S(1)} collective-permute-done((bf16[2,192,1536]{2,1,0:T(8,128)(2,1)S(1)}, bf16[2,192,1536]{2,1,0:T(8,128)(2,1)S(1)}, u32[]{:S(2)}, u32[]{:S(2)}) %collective-permute-start.24) | collective-permute-done | bytes 1179680 | tf_op jit(solution)/shard_map/ppermute | solution.py:736
  210.5 5.4 collective-permute-done.28.refs_8_
  220.9 21.7 %collective-permute-done.34.refs_1_ = bf16[2,192,1536]{2,1,0:T(8,128)(2,1)S(1)} collective-permute-done((bf16[2,192,1536]{2,1,0:T(8,128)(2,1)S(1)}, bf16[2,192,1536]{2,1,0:T(8,128)(2,1)S(1)}, u32[]{:S(2)}, u32[]{:S(2)}) %collective-permute-start.34) | collective-permute-done | bytes 1179680 | tf_op jit(solution)/shard_map/ppermute | solution.py:736
  252.4 17.4 %shard_map.378 = (bf16[1184,1536]{1,0:T(8,128)(2,1)}, f32[1184,1536]{1,0:T(8,128)}) custom-call(s32[8]{0:T(128)} %fusion.32.slots_ref, bf16[1184,1536]{1,0:T(8,128)(2,1)} %pad_maximum_fusion.1.acts_ref.outer_ref, bf16[2,192,1536]{2,1,0:T(8,128)(2,1)} %shard_map.370.refs_0_, bf16[2,192,1536]{2,1,0:T(8,128)(2,1)} %collective-permute-done.18.refs_1_, ...), custom_call_target="tpu_custom_call" | custom-call | flops 5586812 | bytes 16711 | tf_op jit(solution)/shard_map/pallas_call | solution.py:298
  269.8 5.3 collective-permute-done.36.refs_5_
  280.4 10.9 %shard_map.379.refs_2_ = bf16[2,1536,1536]{2,1,0:T(8,128)(2,1)} custom-call(bf16[1184,1536]{1,0:T(8,128)(2,1)} %multiply_convert_fusion.outer_ref.acts_ref, bf16[1184,1536]{1,0:T(8,128)(2,1)} %get-tuple-element.496.inner_ref.acts_ref), custom_call_target="tpu_custom_call" | custom-call | flops 5586812 | bytes 16711 | tf_op jit(solution)/shard_map/pallas_call | solution.py:487
  294.5 8.3 %collective-permute-done.38.refs_4_ = bf16[2,192,1536]{2,1,0:T(8,128)(2,1)} collective-permute-done((bf16[2,192,1536]{2,1,0:T(8,128)(2,1)}, bf16[2,192,1536]{2,1,0:T(8,128)(2,1)}, u32[]{:S(2)}, u32[]{:S(2)}) %collective-permute-start.38) | collective-permute-done | bytes 1179680 | tf_op jit(solution)/shard_map/ppermute | solution.py:736
  307.6 10.9 %collective-permute-done.41.refs_8_ = bf16[1,192,1536]{2,1,0:T(8,128)(2,1)S(1)} collective-permute-done((bf16[1,192,1536]{2,1,0:T(8,128)(2,1)S(1)}, bf16[1,192,1536]{2,1,0:T(8,128)(2,1)S(1)}, u32[]{:S(2)}, u32[]{:S(2)}) %collective-permute-start.41) | collective-permute-done | bytes 589856 | tf_op jit(solution)/shard_map/ppermute | solution.py:736
  323.4 14.2 %shard_map.380 = (bf16[1184,1536]{1,0:T(8,128)(2,1)}, f32[2,1536]{1,0:T(2,128)}) custom-call(s32[8]{0:T(128)} %fusion.32.slots_ref, bf16[1184,1536]{1,0:T(8,128)(2,1)} %multiply_convert_fusion.outer_ref.acts_ref, bf16[2,192,1536]{2,1,0:T(8,128)(2,1)} %shard_map.371.refs_0_, bf16[2,192,1536]{2,1,0:T(8,128)(2,1)} %copy-done.16, ...), custom_call_target="tpu_custom_call" | custom-call | flops 5586812 | bytes 16711 | tf_op jit(solution)/shard_map/pallas_call | solution.py:298
  337.6 9.4 %shard_map.381 = (bf16[1184,384]{1,0:T(8,128)(2,1)}, bf16[1184,384]{1,0:T(8,128)(2,1)}) custom-call(s32[8]{0:T(128)} %fusion.32.slots_ref, bf16[1184,1536]{1,0:T(8,128)(2,1)} %get-tuple-element.479.acts_ref.inner_ref, bf16[2,192,1536]{2,1,0:T(8,128)(2,1)} %shard_map.370.refs_0_, bf16[2,192,1536]{2,1,0:T(8,128)(2,1)} %collective-permute-done.18.refs_1_, ...), custom_call_target="tpu_custom_call" | custom-call | flops 2793406 | bytes 10174 | tf_op jit(solution)/shard_map/pallas_call | solution.py:452
  347.0 4.4 add_convert_fusion.13
  356.2 9.3 %shard_map.382 = (bf16[1184,384]{1,0:T(8,128)(2,1)}, bf16[1184,384]{1,0:T(8,128)(2,1)}) custom-call(s32[8]{0:T(128)} %fusion.32.slots_ref, bf16[1184,1536]{1,0:T(8,128)(2,1)} %get-tuple-element.479.acts_ref.inner_ref, bf16[2,192,1536]{2,1,0:T(8,128)(2,1)} %shard_map.370.refs_0_, bf16[2,192,1536]{2,1,0:T(8,128)(2,1)} %collective-permute-done.18.refs_1_, ...), custom_call_target="tpu_custom_call" | custom-call | flops 2793406 | bytes 10174 | tf_op jit(solution)/shard_map/pallas_call | solution.py:452
  368.8 10.8 %shard_map.383.refs_2_ = bf16[2,1536,1536]{2,1,0:T(8,128)(2,1)} custom-call(bf16[1184,1536]{1,0:T(8,128)(2,1)} %pad_maximum_fusion.1.acts_ref.outer_ref, bf16[1184,1536]{1,0:T(8,128)(2,1)} %get-tuple-element.479.acts_ref.inner_ref), custom_call_target="tpu_custom_call" | custom-call | flops 5586812 | bytes 16711 | tf_op jit(solution)/shard_map/pallas_call | solution.py:487
  396.6 15.6 %collective-permute-done.50 = bf16[2,192,1536]{2,1,0:T(8,128)(2,1)S(1)} collective-permute-done((bf16[2,192,1536]{2,1,0:T(8,128)(2,1)S(1)}, bf16[2,192,1536]{2,1,0:T(8,128)(2,1)S(1)}, u32[]{:S(2)}, u32[]{:S(2)}) %collective-permute-start.50) | collective-permute-done | bytes 1179680 | tf_op jit(solution)/shard_map/ppermute | solution.py:736
  425.6 9.4 %shard_map.384 = (bf16[1184,384]{1,0:T(8,128)(2,1)}, bf16[1184,384]{1,0:T(8,128)(2,1)}) custom-call(s32[8]{0:T(128)} %fusion.32.slots_ref, bf16[1184,1536]{1,0:T(8,128)(2,1)} %get-tuple-element.496.inner_ref.acts_ref, bf16[2,192,1536]{2,1,0:T(8,128)(2,1)} %shard_map.371.refs_0_, bf16[2,192,1536]{2,1,0:T(8,128)(2,1)} %copy-done.16, ...), custom_call_target="tpu_custom_call" | custom-call | flops 2793406 | bytes 10174 | tf_op jit(solution)/shard_map/pallas_call | solution.py:452
  435.0 9.5 %shard_map.385 = (bf16[1184,384]{1,0:T(8,128)(2,1)}, bf16[1184,384]{1,0:T(8,128)(2,1)}) custom-call(s32[8]{0:T(128)} %fusion.32.slots_ref, bf16[1184,1536]{1,0:T(8,128)(2,1)} %get-tuple-element.496.inner_ref.acts_ref, bf16[2,192,1536]{2,1,0:T(8,128)(2,1)} %shard_map.371.refs_0_, bf16[2,192,1536]{2,1,0:T(8,128)(2,1)} %copy-done.16, ...), custom_call_target="tpu_custom_call" | custom-call | flops 2793406 | bytes 10174 | tf_op jit(solution)/shard_map/pallas_call | solution.py:452
  456.1 6.7 shard_map.386.grad_ref
  462.8 13.4 %shard_map.387 = (bf16[1184,1152]{1,0:T(8,128)(2,1)}, f32[3,2,256]{2,1,0:T(2,128)}) custom-call(bf16[1184,1152]{1,0:T(8,128)(2,1)} %shard_map.372.triple_ref, f32[3,2,1184]{2,1,0:T(2,128)} %get-tuple-element.535.total_ref, bf16[1184,384]{1,0:T(8,128)(2,1)} %shard_map.386.grad_ref), custom_call_target="tpu_custom_call" | custom-call | flops 21532508 | bytes 10911 | tf_op jit(solution)/shard_map/pallas_call | solution.py:615
  486.1 13.3 %shard_map.388 = (bf16[1184,1152]{1,0:T(8,128)(2,1)}, f32[3,2,256]{2,1,0:T(2,128)}) custom-call(bf16[1184,1152]{1,0:T(8,128)(2,1)} %shard_map.372.triple_ref, f32[3,2,1184]{2,1,0:T(2,128)} %get-tuple-element.535.total_ref, bf16[1184,384]{1,0:T(8,128)(2,1)} %shard_map.386.grad_ref, ...), custom_call_target="tpu_custom_call", output_to_operand_aliasing={{0}: (3, {}), {1}: (4, {})} | custom-call | flops 21532508 | bytes 10911 | tf_op jit(solution)/shard_map/pallas_call | solution.py:615
  499.4 13.7 %shard_map.389 = (bf16[1184,1152]{1,0:T(8,128)(2,1)}, f32[3,2,256]{2,1,0:T(2,128)}) custom-call(bf16[1184,1152]{1,0:T(8,128)(2,1)} %shard_map.372.triple_ref, f32[3,2,1184]{2,1,0:T(2,128)} %get-tuple-element.535.total_ref, bf16[1184,384]{1,0:T(8,128)(2,1)} %shard_map.386.grad_ref, ...), custom_call_target="tpu_custom_call", output_to_operand_aliasing={{0}: (3, {}), {1}: (4, {})} | custom-call | flops 21532508 | bytes 10911 | tf_op jit(solution)/shard_map/pallas_call | solution.py:615
  522.7 9.8 %shard_map.390.refs_0_ = bf16[2,1536,1536]{2,1,0:T(8,128)(2,1)} custom-call(bf16[1184,1536]{1,0:T(8,128)(2,1)} %add_convert_fusion.acts_ref.outer_ref, bf16[1184,1152]{1,0:T(8,128)(2,1)} %get-tuple-element.562.inner_ref.acts_ref), custom_call_target="tpu_custom_call" | custom-call | flops 4190109 | bytes 13443 | tf_op jit(solution)/shard_map/pallas_call | solution.py:487
  532.4 5.9 shard_map.391.refs_4_
  541.2 8.3 %shard_map.392 = (bf16[1184,384]{1,0:T(8,128)(2,1)}, bf16[1184,384]{1,0:T(8,128)(2,1)}) custom-call(s32[8]{0:T(128)} %fusion.32.slots_ref, bf16[1184,1152]{1,0:T(8,128)(2,1)} %get-tuple-element.562.inner_ref.acts_ref, bf16[2,192,1536]{2,1,0:T(8,128)(2,1)} %shard_map.369.refs_0_, bf16[2,192,1536]{2,1,0:T(8,128)(2,1)} %copy-done.2, ...), custom_call_target="tpu_custom_call" | custom-call | flops 2095054 | bytes 8085 | tf_op jit(solution)/shard_map/pallas_call | solution.py:452
  553.4 8.2 %shard_map.393 = (bf16[1184,384]{1,0:T(8,128)(2,1)}, bf16[1184,384]{1,0:T(8,128)(2,1)}) custom-call(s32[8]{0:T(128)} %fusion.32.slots_ref, bf16[1184,1152]{1,0:T(8,128)(2,1)} %get-tuple-element.562.inner_ref.acts_ref, bf16[2,192,1536]{2,1,0:T(8,128)(2,1)} %shard_map.369.refs_0_, bf16[2,192,1536]{2,1,0:T(8,128)(2,1)} %copy-done.2, ...), custom_call_target="tpu_custom_call" | custom-call | flops 2095054 | bytes 8085 | tf_op jit(solution)/shard_map/pallas_call | solution.py:452
  574.4 12.3 %shard_map.394 = (f32[192,2,4,384]{3,2,1,0:T(4,128)}, f32[192,2,4,384]{3,2,1,0:T(4,128)}, f32[2,192,2,4,384]{4,3,2,1,0:T(4,128)}) custom-call(s32[1]{0:T(128)} %bitcast.17.slot_ref, f32[192,2,4,384]{3,2,1,0:T(4,128)} %refs_0_.2, f32[2,192,2,4,384]{4,3,2,1,0:T(4,128)} %refs_1_, bf16[2,1536,1536]{2,1,0:T(8,128)(2,1)} %shard_map.379.refs_2_, ...), custom_call_target="tpu_custom_call" | custom-call | flops 11796 | bytes 23592 | tf_op jit(solution)/shard_map/pallas_call | solution.py:173
  593.4 5.1 collective-permute-done.72
  612.6 5.0 all-to-all-done.1
  628.8 11.9 %shard_map.395 = (f32[192,2,4,384]{3,2,1,0:T(4,128)}, f32[192,2,4,384]{3,2,1,0:T(4,128)}, f32[2,192,2,4,384]{4,3,2,1,0:T(4,128)}) custom-call(s32[1]{0:T(128)} %bitcast.17.slot_ref, f32[192,2,4,384]{3,2,1,0:T(4,128)} %refs_0_.3, f32[2,192,2,4,384]{4,3,2,1,0:T(4,128)} %refs_1_.1, bf16[2,1536,1536]{2,1,0:T(8,128)(2,1)} %shard_map.383.refs_2_, ...), custom_call_target="tpu_custom_call" | custom-call | flops 11796 | bytes 23592 | tf_op jit(solution)/shard_map/pallas_call | solution.py:173
  641.5 4.5 add_convert_fusion.1
  650.2 16.2 %shard_map.396 = (f32[192,6,2,384]{3,2,1,0:T(2,128)}, f32[192,6,2,384]{3,2,1,0:T(2,128)}, f32[192,6,2,384]{3,2,1,0:T(2,128)}, f32[192,6,2,384]{3,2,1,0:T(2,128)}) custom-call(bf16[192,8]{1,0:T(8,128)(2,1)} %bitcast.79, bf16[8,4608]{1,0:T(8,128)(2,1)} %bitcast.80, f32[192,6,2,384]{3,2,1,0:T(2,128)} %bitcast.69, f32[2,192,6,2,384]{4,3,2,1,0:T(2,128)} %bitcast.70), custom_call_target="tpu_custom_call" | custom-call | flops 17694 | bytes 35389 | tf_op jit(solution)/shard_map/pallas_call | solution.py:217
  674.9 12.2 %shard_map.397 = (f32[192,3,2,384]{3,2,1,0:T(2,128)}, f32[192,3,2,384]{3,2,1,0:T(2,128)}, f32[2,192,3,2,384]{4,3,2,1,0:T(2,128)}, f32[192,1,2,384]{3,2,1,0:T(2,1...) custom-call(s32[1]{0:T(128)} %bitcast.17.slot_ref, f32[192,3,2,384]{3,2,1,0:T(2,128)} %bitcast.72, ...), custom_call_target="tpu_custom_call" | custom-call | flops 11796 | bytes 23592 | tf_op jit(solution)/shard_map/pallas_call | solution.py:173
  (446 shorter events, 217.8 us)
Async XLA Ops:
  5.1 37.5 %collective-permute-start.6 = (bf16[2,192,1536]{2,1,0:T(8,128)(2,1)}, bf16[2,192,1536]{2,1,0:T(8,128)(2,1)S(1)}, u32[]{:S(2)}, u32[]{:S(2)}) collective-permute-start(bf16[2,192,1536]{2,1,0:T(8,128)(2,1)} %shard_map.369.refs_0_), channel_id=1, source_target_pairs={{8,0},{16,8},{24,16},{28,24},{20,28},{12,20},{4,12},{0,4},{9,1},{1... | collective-permute-start | bytes 3538952 | tf_op jit(solution)/shard_map/ppermute | solution.py:736
  8.1 34.9 %collective-permute-start.5 = (bf16[2,192,1536]{2,1,0:T(8,128)(2,1)}, bf16[2,192,1536]{2,1,0:T(8,128)(2,1)S(1)}, u32[]{:S(2)}, u32[]{:S(2)}) collective-permute-start(bf16[2,192,1536]{2,1,0:T(8,128)(2,1)} %shard_map.369.refs_0_), channel_id=1, source_target_pairs={{0,8},{8,16},{16,24},{24,28},{28,20},{20,12},{12,4},{4,0},{1,9},{9... | collective-permute-start | bytes 3538952 | tf_op jit(solution)/shard_map/ppermute | solution.py:736
  19.9 26.0 %collective-permute-start.1 = (bf16[1184,384]{1,0:T(8,128)(2,1)}, bf16[1184,384]{1,0:T(8,128)(2,1)}, u32[]{:S(2)}, u32[]{:S(2)}) collective-permute-start(bf16[1184,384]{1,0:T(8,128)(2,1)} %concatenate.32), channel_id=1, source_target_pairs={{0,2},{1,3},{2,0},{3,1},{4,6},{5,7},{6,4},{7,5},{8,10},{9,11},{10,... | collective-permute-start | bytes 2727944 | tf_op jit(solution)/shard_map/ppermute | solution.py:711
  46.4 28.1 %collective-permute-start.8 = (bf16[2,192,1536]{2,1,0:T(8,128)(2,1)S(1)}, bf16[2,192,1536]{2,1,0:T(8,128)(2,1)}, u32[]{:S(2)}, u32[]{:S(2)}) collective-permute-start(bf16[2,192,1536]{2,1,0:T(8,128)(2,1)S(1)} %collective-permute-done.5.refs_6_), channel_id=1, source_target_pairs={{0,8},{8,16},{16,24},{24,28},{28,20},{20,12},{12,4},{4,0},{1,9},{9... | collective-permute-start | bytes 3538952 | tf_op jit(solution)/shard_map/ppermute | solution.py:736
  46.4 28.1 %collective-permute-start.9 = (bf16[2,192,1536]{2,1,0:T(8,128)(2,1)S(1)}, bf16[2,192,1536]{2,1,0:T(8,128)(2,1)}, u32[]{:S(2)}, u32[]{:S(2)}) collective-permute-start(bf16[2,192,1536]{2,1,0:T(8,128)(2,1)S(1)} %collective-permute-done.6.refs_1_), channel_id=1, source_target_pairs={{8,0},{16,8},{24,16},{28,24},{20,28},{12,20},{4,12},{0,4},{9,1},{1... | collective-permute-start | bytes 3538952 | tf_op jit(solution)/shard_map/ppermute | solution.py:736
  74.6 27.4 %collective-permute-start.12 = (bf16[2,192,1536]{2,1,0:T(8,128)(2,1)}, bf16[2,192,1536]{2,1,0:T(8,128)(2,1)S(1)}, u32[]{:S(2)}, u32[]{:S(2)}) collective-permute-start(bf16[2,192,1536]{2,1,0:T(8,128)(2,1)} %collective-permute-done.8.refs_5_), channel_id=1, source_target_pairs={{0,8},{8,16},{16,24},{24,28},{28,20},{20,12},{12,4},{4,0},{1,9},{9... | collective-permute-start | bytes 3538952 | tf_op jit(solution)/shard_map/ppermute | solution.py:736
  75.2 27.3 %collective-permute-start.13 = (bf16[2,192,1536]{2,1,0:T(8,128)(2,1)}, bf16[2,192,1536]{2,1,0:T(8,128)(2,1)S(1)}, u32[]{:S(2)}, u32[]{:S(2)}) collective-permute-start(bf16[2,192,1536]{2,1,0:T(8,128)(2,1)} %collective-permute-done.9.refs_2_), channel_id=1, source_target_pairs={{8,0},{16,8},{24,16},{28,24},{20,28},{12,20},{4,12},{0,4},{9,1},{1... | collective-permute-start | bytes 3538952 | tf_op jit(solution)/shard_map/ppermute | solution.py:736
  76.8 27.9 %collective-permute-start.11 = (bf16[1184,384]{1,0:T(8,128)(2,1)}, bf16[1184,384]{1,0:T(8,128)(2,1)}, u32[]{:S(2)}, u32[]{:S(2)}) collective-permute-start(bf16[1184,384]{1,0:T(8,128)(2,1)} %concatenate.35), channel_id=1, source_target_pairs={{0,2},{1,3},{2,0},{3,1},{4,6},{5,7},{6,4},{7,5},{8,10},{9,11},{10,... | collective-permute-start | bytes 2727944 | tf_op jit(solution)/shard_map/ppermute | solution.py:711
  117.3 26.8 %collective-permute-start.18 = (bf16[2,192,1536]{2,1,0:T(8,128)(2,1)}, bf16[2,192,1536]{2,1,0:T(8,128)(2,1)}, u32[]{:S(2)}, u32[]{:S(2)}) collective-permute-start(bf16[2,192,1536]{2,1,0:T(8,128)(2,1)} %shard_map.370.refs_0_), channel_id=1, source_target_pairs={{8,0},{16,8},{24,16},{28,24},{20,28},{12,20},{4,12},{0,4},{9,1},{1... | collective-permute-start | bytes 3538952 | tf_op jit(solution)/shard_map/ppermute | solution.py:736
  118.4 25.7 %collective-permute-start.17 = (bf16[2,192,1536]{2,1,0:T(8,128)(2,1)}, bf16[2,192,1536]{2,1,0:T(8,128)(2,1)}, u32[]{:S(2)}, u32[]{:S(2)}) collective-permute-start(bf16[2,192,1536]{2,1,0:T(8,128)(2,1)} %shard_map.370.refs_0_), channel_id=1, source_target_pairs={{0,8},{8,16},{16,24},{24,28},{28,20},{20,12},{12,4},{4,0},{1,9},{9... | collective-permute-start | bytes 3538952 | tf_op jit(solution)/shard_map/ppermute | solution.py:736
  144.0 28.3 %collective-permute-start.19 = (bf16[2,192,1536]{2,1,0:T(8,128)(2,1)}, bf16[2,192,1536]{2,1,0:T(8,128)(2,1)S(1)}, u32[]{:S(2)}, u32[]{:S(2)}) collective-permute-start(bf16[2,192,1536]{2,1,0:T(8,128)(2,1)} %collective-permute-done.17.refs_6_), channel_id=1, source_target_pairs={{0,8},{8,16},{16,24},{24,28},{28,20},{20,12},{12,4},{4,0},{1,9},{9... | collective-permute-start | bytes 3538952 | tf_op jit(solution)/shard_map/ppermute | solution.py:736
  144.6 28.3 %collective-permute-start.20 = (bf16[2,192,1536]{2,1,0:T(8,128)(2,1)}, bf16[2,192,1536]{2,1,0:T(8,128)(2,1)S(1)}, u32[]{:S(2)}, u32[]{:S(2)}) collective-permute-start(bf16[2,192,1536]{2,1,0:T(8,128)(2,1)} %collective-permute-done.18.refs_1_), channel_id=1, source_target_pairs={{8,0},{16,8},{24,16},{28,24},{20,28},{12,20},{4,12},{0,4},{9,1},{1... | collective-permute-start | bytes 3538952 | tf_op jit(solution)/shard_map/ppermute | solution.py:736
  173.5 27.9 %collective-permute-start.24 = (bf16[2,192,1536]{2,1,0:T(8,128)(2,1)S(1)}, bf16[2,192,1536]{2,1,0:T(8,128)(2,1)S(1)}, u32[]{:S(2)}, u32[]{:S(2)}) collective-permute-start(bf16[2,192,1536]{2,1,0:T(8,128)(2,1)S(1)} %collective-permute-done.19.refs_5_), channel_id=1, source_target_pairs={{0,8},{8,16},{16,24},{24,28},{28,20},{20,12},{12,4},{4,0},{1,9},{9... | collective-permute-start | bytes 3538952 | tf_op jit(solution)/shard_map/ppermute | solution.py:736
  173.8 27.6 %collective-permute-start.25 = (bf16[2,192,1536]{2,1,0:T(8,128)(2,1)S(1)}, bf16[2,192,1536]{2,1,0:T(8,128)(2,1)S(1)}, u32[]{:S(2)}, u32[]{:S(2)}) collective-permute-start(bf16[2,192,1536]{2,1,0:T(8,128)(2,1)S(1)} %collective-permute-done.20.refs_2_), channel_id=1, source_target_pairs={{8,0},{16,8},{24,16},{28,24},{20,28},{12,20},{4,12},{0,4},{9,1},{1... | collective-permute-start | bytes 3538952 | tf_op jit(solution)/shard_map/ppermute | solution.py:736
  183.0 21.6 %collective-permute-start.23 = (bf16[1184,384]{1,0:T(8,128)(2,1)S(1)}, bf16[1184,384]{1,0:T(8,128)(2,1)S(1)}, u32[]{:S(2)}, u32[]{:S(2)}) collective-permute-start(bf16[1184,384]{1,0:T(8,128)(2,1)S(1)} %get-tuple-element.406), channel_id=1, source_target_pairs={{0,2},{1,3},{2,0},{3,1},{4,6},{5,7},{6,4},{7,5},{8,10},{9,11},{10,... | collective-permute-start | bytes 2727944 | tf_op jit(solution)/shard_map/ppermute | solution.py:711
  217.1 25.5 %collective-permute-start.34 = (bf16[2,192,1536]{2,1,0:T(8,128)(2,1)S(1)}, bf16[2,192,1536]{2,1,0:T(8,128)(2,1)S(1)}, u32[]{:S(2)}, u32[]{:S(2)}) collective-permute-start(bf16[2,192,1536]{2,1,0:T(8,128)(2,1)S(1)} %copy-done.10), channel_id=1, source_target_pairs={{8,0},{16,8},{24,16},{28,24},{20,28},{12,20},{4,12},{0,4},{9,1},{1... | collective-permute-start | bytes 3538952 | tf_op jit(solution)/shard_map/ppermute | solution.py:736
  218.5 25.2 %collective-permute-start.33 = (bf16[2,192,1536]{2,1,0:T(8,128)(2,1)S(1)}, bf16[2,192,1536]{2,1,0:T(8,128)(2,1)S(1)}, u32[]{:S(2)}, u32[]{:S(2)}) collective-permute-start(bf16[2,192,1536]{2,1,0:T(8,128)(2,1)S(1)} %copy-done.10), channel_id=1, source_target_pairs={{0,8},{8,16},{16,24},{24,28},{28,20},{20,12},{12,4},{4,0},{1,9},{9... | collective-permute-start | bytes 3538952 | tf_op jit(solution)/shard_map/ppermute | solution.py:736
  220.3 26.2 %collective-permute-start.32 = (bf16[1184,384]{1,0:T(8,128)(2,1)S(1)}, bf16[1184,384]{1,0:T(8,128)(2,1)S(1)}, u32[]{:S(2)}, u32[]{:S(2)}) collective-permute-start(bf16[1184,384]{1,0:T(8,128)(2,1)S(1)} %add_convert_fusion.18), channel_id=1, source_target_pairs={{0,2},{1,3},{2,0},{3,1},{4,6},{5,7},{6,4},{7,5},{8,10},{9,11},{10,... | collective-permute-start | bytes 2727944 | tf_op jit(solution)/shard_map/ppermute | solution.py:711
  247.1 28.1 %collective-permute-start.36 = (bf16[2,192,1536]{2,1,0:T(8,128)(2,1)S(1)}, bf16[2,192,1536]{2,1,0:T(8,128)(2,1)}, u32[]{:S(2)}, u32[]{:S(2)}) collective-permute-start(bf16[2,192,1536]{2,1,0:T(8,128)(2,1)S(1)} %collective-permute-done.33.refs_6_), channel_id=1, source_target_pairs={{0,8},{8,16},{16,24},{24,28},{28,20},{20,12},{12,4},{4,0},{1,9},{9... | collective-permute-start | bytes 3538952 | tf_op jit(solution)/shard_map/ppermute | solution.py:736
  247.7 28.0 %collective-permute-start.37 = (bf16[2,192,1536]{2,1,0:T(8,128)(2,1)S(1)}, bf16[2,192,1536]{2,1,0:T(8,128)(2,1)}, u32[]{:S(2)}, u32[]{:S(2)}) collective-permute-start(bf16[2,192,1536]{2,1,0:T(8,128)(2,1)S(1)} %collective-permute-done.34.refs_1_), channel_id=1, source_target_pairs={{8,0},{16,8},{24,16},{28,24},{20,28},{12,20},{4,12},{0,4},{9,1},{1... | collective-permute-start | bytes 3538952 | tf_op jit(solution)/shard_map/ppermute | solution.py:736
  275.7 27.1 %collective-permute-start.38 = (bf16[2,192,1536]{2,1,0:T(8,128)(2,1)}, bf16[2,192,1536]{2,1,0:T(8,128)(2,1)}, u32[]{:S(2)}, u32[]{:S(2)}) collective-permute-start(bf16[2,192,1536]{2,1,0:T(8,128)(2,1)} %collective-permute-done.36.refs_5_), channel_id=1, source_target_pairs={{0,8},{8,16},{16,24},{24,28},{28,20},{20,12},{12,4},{4,0},{1,9},{9... | collective-permute-start | bytes 3538952 | tf_op jit(solution)/shard_map/ppermute | solution.py:736
  276.5 26.8 %collective-permute-start.39 = (bf16[2,192,1536]{2,1,0:T(8,128)(2,1)}, bf16[2,192,1536]{2,1,0:T(8,128)(2,1)}, u32[]{:S(2)}, u32[]{:S(2)}) collective-permute-start(bf16[2,192,1536]{2,1,0:T(8,128)(2,1)} %collective-permute-done.37.refs_2_), channel_id=1, source_target_pairs={{8,0},{16,8},{24,16},{28,24},{20,28},{12,20},{4,12},{0,4},{9,1},{1... | collective-permute-start | bytes 3538952 | tf_op jit(solution)/shard_map/ppermute | solution.py:736
  320.1 26.9 %collective-permute-start.42 = (bf16[2,192,1536]{2,1,0:T(8,128)(2,1)}, bf16[2,192,1536]{2,1,0:T(8,128)(2,1)}, u32[]{:S(2)}, u32[]{:S(2)}) collective-permute-start(bf16[2,192,1536]{2,1,0:T(8,128)(2,1)} %get-tuple-element.456), channel_id=1, source_target_pairs={{0,8},{8,16},{16,24},{24,28},{28,20},{20,12},{12,4},{4,0},{1,9},{9... | collective-permute-start | bytes 3538952 | tf_op jit(solution)/shard_map/ppermute | solution.py:736
  320.9 26.2 %collective-permute-start.43 = (bf16[2,192,1536]{2,1,0:T(8,128)(2,1)}, bf16[2,192,1536]{2,1,0:T(8,128)(2,1)}, u32[]{:S(2)}, u32[]{:S(2)}) collective-permute-start(bf16[2,192,1536]{2,1,0:T(8,128)(2,1)} %get-tuple-element.457), channel_id=1, source_target_pairs={{8,0},{16,8},{24,16},{28,24},{20,28},{12,20},{4,12},{0,4},{9,1},{1... | collective-permute-start | bytes 3538952 | tf_op jit(solution)/shard_map/ppermute | solution.py:736
  353.9 28.1 %collective-permute-start.47 = (bf16[2,192,1536]{2,1,0:T(8,128)(2,1)}, bf16[2,192,1536]{2,1,0:T(8,128)(2,1)S(1)}, u32[]{:S(2)}, u32[]{:S(2)}) collective-permute-start(bf16[2,192,1536]{2,1,0:T(8,128)(2,1)} %get-tuple-element.476), channel_id=1, source_target_pairs={{0,8},{8,16},{16,24},{24,28},{28,20},{20,12},{12,4},{4,0},{1,9},{9... | collective-permute-start | bytes 3538952 | tf_op jit(solution)/shard_map/ppermute | solution.py:736
  354.7 28.1 %collective-permute-start.48 = (bf16[2,192,1536]{2,1,0:T(8,128)(2,1)}, bf16[2,192,1536]{2,1,0:T(8,128)(2,1)}, u32[]{:S(2)}, u32[]{:S(2)}) collective-permute-start(bf16[2,192,1536]{2,1,0:T(8,128)(2,1)} %get-tuple-element.477), channel_id=1, source_target_pairs={{8,0},{16,8},{24,16},{28,24},{20,28},{12,20},{4,12},{0,4},{9,1},{1... | collective-permute-start | bytes 3538952 | tf_op jit(solution)/shard_map/ppermute | solution.py:736
  368.2 21.8 %collective-permute-start.46 = (bf16[1184,384]{1,0:T(8,128)(2,1)}, bf16[1184,384]{1,0:T(8,128)(2,1)}, u32[]{:S(2)}, u32[]{:S(2)}) collective-permute-start(bf16[1184,384]{1,0:T(8,128)(2,1)} %add_convert_fusion.17), channel_id=1, source_target_pairs={{0,2},{1,3},{2,0},{3,1},{4,6},{5,7},{6,4},{7,5},{8,10},{9,11},{10,... | collective-permute-start | bytes 2727944 | tf_op jit(solution)/shard_map/ppermute | solution.py:711
  385.4 26.8 %collective-permute-start.50 = (bf16[2,192,1536]{2,1,0:T(8,128)(2,1)S(1)}, bf16[2,192,1536]{2,1,0:T(8,128)(2,1)S(1)}, u32[]{:S(2)}, u32[]{:S(2)}) collective-permute-start(bf16[2,192,1536]{2,1,0:T(8,128)(2,1)S(1)} %get-tuple-element.486), channel_id=1, source_target_pairs={{0,8},{8,16},{16,24},{24,28},{28,20},{20,12},{12,4},{4,0},{1,9},{9... | collective-permute-start | bytes 3538952 | tf_op jit(solution)/shard_map/ppermute | solution.py:736
  386.2 26.4 %collective-permute-start.51 = (bf16[2,192,1536]{2,1,0:T(8,128)(2,1)S(1)}, bf16[2,192,1536]{2,1,0:T(8,128)(2,1)S(1)}, u32[]{:S(2)}, u32[]{:S(2)}) collective-permute-start(bf16[2,192,1536]{2,1,0:T(8,128)(2,1)S(1)} %get-tuple-element.487), channel_id=1, source_target_pairs={{8,0},{16,8},{24,16},{28,24},{20,28},{12,20},{4,12},{0,4},{9,1},{1... | collective-permute-start | bytes 3538952 | tf_op jit(solution)/shard_map/ppermute | solution.py:736
  394.7 21.0 %collective-permute-start.53 = (f32[2,1184]{1,0:T(2,128)S(1)}, f32[2,1184]{1,0:T(2,128)S(1)}, u32[]{:S(2)}, u32[]{:S(2)}) collective-permute-start(f32[2,1184]{1,0:T(2,128)S(1)} %pad_maximum_fusion.7), channel_id=1, source_target_pairs={{0,3},{1,2},{2,1},{3,0},{4,7},{5,6},{6,5},{7,4},{8,11},{9,10},{10,... | collective-permute-start | bytes 28424 | tf_op jit(solution)/shard_map/ppermute | solution.py:711
  415.7 28.7 %collective-permute-start.57 = (bf16[2,192,1536]{2,1,0:T(8,128)(2,1)}, bf16[2,192,1536]{2,1,0:T(8,128)(2,1)}, u32[]{:S(2)}, u32[]{:S(2)}) collective-permute-start(bf16[2,192,1536]{2,1,0:T(8,128)(2,1)} %add_convert_fusion.10), channel_id=1, source_target_pairs={{0,8},{8,16},{16,24},{24,28},{28,20},{20,12},{12,4},{4,0},{1,9},{9... | collective-permute-start | bytes 3538952 | tf_op jit(solution)/shard_map/ppermute | solution.py:736
  416.7 27.7 %collective-permute-start.58 = (bf16[2,192,1536]{2,1,0:T(8,128)(2,1)S(1)}, bf16[2,192,1536]{2,1,0:T(8,128)(2,1)}, u32[]{:S(2)}, u32[]{:S(2)}) collective-permute-start(bf16[2,192,1536]{2,1,0:T(8,128)(2,1)S(1)} %get-tuple-element.502), channel_id=1, source_target_pairs={{8,0},{16,8},{24,16},{28,24},{20,28},{12,20},{4,12},{0,4},{9,1},{1... | collective-permute-start | bytes 3538952 | tf_op jit(solution)/shard_map/ppermute | solution.py:736
  424.1 22.3 %collective-permute-start.56 = (bf16[1184,384]{1,0:T(8,128)(2,1)S(1)}, bf16[1184,384]{1,0:T(8,128)(2,1)}, u32[]{:S(2)}, u32[]{:S(2)}) collective-permute-start(bf16[1184,384]{1,0:T(8,128)(2,1)S(1)} %get-tuple-element.500), channel_id=1, source_target_pairs={{0,2},{1,3},{2,0},{3,1},{4,6},{5,7},{6,4},{7,5},{8,10},{9,11},{10,... | collective-permute-start | bytes 2727944 | tf_op jit(solution)/shard_map/ppermute | solution.py:711
  447.0 29.2 %collective-permute-start.54 = (bf16[1184,384]{1,0:T(8,128)(2,1)}, bf16[1184,384]{1,0:T(8,128)(2,1)S(1)}, u32[]{:S(2)}, u32[]{:S(2)}) collective-permute-start(bf16[1184,384]{1,0:T(8,128)(2,1)} %get-tuple-element.499), channel_id=1, source_target_pairs={{0,1},{1,0},{2,3},{3,2},{4,5},{5,4},{6,7},{7,6},{8,9},{9,8},{10,11... | collective-permute-start | bytes 2727944 | tf_op jit(solution)/shard_map/ppermute | solution.py:711
  447.1 29.1 %collective-permute-start.60 = (bf16[1184,384]{1,0:T(8,128)(2,1)}, bf16[1184,384]{1,0:T(8,128)(2,1)}, u32[]{:S(2)}, u32[]{:S(2)}) collective-permute-start(bf16[1184,384]{1,0:T(8,128)(2,1)} %get-tuple-element.516), channel_id=1, source_target_pairs={{0,1},{1,0},{2,3},{3,2},{4,5},{5,4},{6,7},{7,6},{8,9},{9,8},{10,11... | collective-permute-start | bytes 2727944 | tf_op jit(solution)/shard_map/ppermute | solution.py:711
  447.5 33.1 %collective-permute-start.62 = (bf16[2,192,1536]{2,1,0:T(8,128)(2,1)S(1)}, bf16[2,192,1536]{2,1,0:T(8,128)(2,1)}, u32[]{:S(2)}, u32[]{:S(2)}) collective-permute-start(bf16[2,192,1536]{2,1,0:T(8,128)(2,1)S(1)} %get-tuple-element.523), channel_id=1, source_target_pairs={{0,8},{8,16},{16,24},{24,28},{28,20},{20,12},{12,4},{4,0},{1,9},{9... | collective-permute-start | bytes 3538952 | tf_op jit(solution)/shard_map/ppermute | solution.py:736
  449.7 30.9 %collective-permute-start.63 = (bf16[2,192,1536]{2,1,0:T(8,128)(2,1)S(1)}, bf16[2,192,1536]{2,1,0:T(8,128)(2,1)}, u32[]{:S(2)}, u32[]{:S(2)}) collective-permute-start(bf16[2,192,1536]{2,1,0:T(8,128)(2,1)S(1)} %add_convert_fusion.9), channel_id=1, source_target_pairs={{8,0},{16,8},{24,16},{28,24},{20,28},{12,20},{4,12},{0,4},{9,1},{1... | collective-permute-start | bytes 3538952 | tf_op jit(solution)/shard_map/ppermute | solution.py:736
  483.6 29.5 %collective-permute-start.64 = (bf16[2,192,1536]{2,1,0:T(8,128)(2,1)S(1)}, bf16[2,192,1536]{2,1,0:T(8,128)(2,1)S(1)}, u32[]{:S(2)}, u32[]{:S(2)}) collective-permute-start(bf16[2,192,1536]{2,1,0:T(8,128)(2,1)S(1)} %get-tuple-element.542), channel_id=1, source_target_pairs={{0,8},{8,16},{16,24},{24,28},{28,20},{20,12},{12,4},{4,0},{1,9},{9... | collective-permute-start | bytes 3538952 | tf_op jit(solution)/shard_map/ppermute | solution.py:736
  484.3 28.8 %collective-permute-start.65 = (bf16[2,192,1536]{2,1,0:T(8,128)(2,1)S(1)}, bf16[2,192,1536]{2,1,0:T(8,128)(2,1)}, u32[]{:S(2)}, u32[]{:S(2)}) collective-permute-start(bf16[2,192,1536]{2,1,0:T(8,128)(2,1)S(1)} %get-tuple-element.543), channel_id=1, source_target_pairs={{8,0},{16,8},{24,16},{28,24},{20,28},{12,20},{4,12},{0,4},{9,1},{1... | collective-permute-start | bytes 3538952 | tf_op jit(solution)/shard_map/ppermute | solution.py:736
  485.7 27.4 %collective-permute-start.61 = (bf16[1184,384]{1,0:T(8,128)(2,1)}, bf16[1184,384]{1,0:T(8,128)(2,1)S(1)}, u32[]{:S(2)}, u32[]{:S(2)}) collective-permute-start(bf16[1184,384]{1,0:T(8,128)(2,1)} %add_convert_fusion.16), channel_id=1, source_target_pairs={{0,2},{1,3},{2,0},{3,1},{4,6},{5,7},{6,4},{7,5},{8,10},{9,11},{10,... | collective-permute-start | bytes 2727944 | tf_op jit(solution)/shard_map/ppermute | solution.py:711
  517.5 32.0 %collective-permute-start.66 = (bf16[2,192,1536]{2,1,0:T(8,128)(2,1)}, bf16[2,192,1536]{2,1,0:T(8,128)(2,1)}, u32[]{:S(2)}, u32[]{:S(2)}) collective-permute-start(bf16[2,192,1536]{2,1,0:T(8,128)(2,1)} %get-tuple-element.552), channel_id=1, source_target_pairs={{0,8},{8,16},{16,24},{24,28},{28,20},{20,12},{12,4},{4,0},{1,9},{9... | collective-permute-start | bytes 3538952 | tf_op jit(solution)/shard_map/ppermute | solution.py:736
  518.4 31.1 %collective-permute-start.67 = (bf16[2,192,1536]{2,1,0:T(8,128)(2,1)}, bf16[2,192,1536]{2,1,0:T(8,128)(2,1)}, u32[]{:S(2)}, u32[]{:S(2)}) collective-permute-start(bf16[2,192,1536]{2,1,0:T(8,128)(2,1)} %get-tuple-element.553), channel_id=1, source_target_pairs={{8,0},{16,8},{24,16},{28,24},{20,28},{12,20},{4,12},{0,4},{9,1},{1... | collective-permute-start | bytes 3538952 | tf_op jit(solution)/shard_map/ppermute | solution.py:736
  572.1 26.4 %collective-permute-start.72 = (bf16[2,192,1536]{2,1,0:T(8,128)(2,1)}, bf16[2,192,1536]{2,1,0:T(8,128)(2,1)}, u32[]{:S(2)}, u32[]{:S(2)}) collective-permute-start(bf16[2,192,1536]{2,1,0:T(8,128)(2,1)} %pad_maximum_fusion.3), channel_id=1, source_target_pairs={{0,8},{8,16},{16,24},{24,28},{28,20},{20,12},{12,4},{4,0},{1,9},{9... | collective-permute-start | bytes 3538952 | tf_op jit(solution)/shard_map/ppermute | solution.py:736
  572.9 26.3 %collective-permute-start.73 = (bf16[2,192,1536]{2,1,0:T(8,128)(2,1)}, bf16[2,192,1536]{2,1,0:T(8,128)(2,1)}, u32[]{:S(2)}, u32[]{:S(2)}) collective-permute-start(bf16[2,192,1536]{2,1,0:T(8,128)(2,1)} %pad_maximum_fusion.4), channel_id=1, source_target_pairs={{8,0},{16,8},{24,16},{28,24},{20,28},{12,20},{4,12},{0,4},{9,1},{1... | collective-permute-start | bytes 3538952 | tf_op jit(solution)/shard_map/ppermute | solution.py:736
  610.5 30.9 %collective-permute-start.75 = (bf16[2,192,1536]{2,1,0:T(8,128)(2,1)}, bf16[2,192,1536]{2,1,0:T(8,128)(2,1)}, u32[]{:S(2)}, u32[]{:S(2)}) collective-permute-start(bf16[2,192,1536]{2,1,0:T(8,128)(2,1)} %get-tuple-element.589), channel_id=1, source_target_pairs={{0,8},{8,16},{16,24},{24,28},{28,20},{20,12},{12,4},{4,0},{1,9},{9... | collective-permute-start | bytes 3538952 | tf_op jit(solution)/shard_map/ppermute | solution.py:736
  612.6 28.9 %collective-permute-start.76 = (bf16[2,192,1536]{2,1,0:T(8,128)(2,1)}, bf16[2,192,1536]{2,1,0:T(8,128)(2,1)}, u32[]{:S(2)}, u32[]{:S(2)}) collective-permute-start(bf16[2,192,1536]{2,1,0:T(8,128)(2,1)} %get-tuple-element.590), channel_id=1, source_target_pairs={{8,0},{16,8},{24,16},{28,24},{20,28},{12,20},{4,12},{0,4},{9,1},{1... | collective-permute-start | bytes 3538952 | tf_op jit(solution)/shard_map/ppermute | solution.py:736
  646.0 28.5 %collective-permute-start.83 = (bf16[2,192,1536]{2,1,0:T(8,128)(2,1)}, bf16[2,192,1536]{2,1,0:T(8,128)(2,1)}, u32[]{:S(2)}, u32[]{:S(2)}) collective-permute-start(bf16[2,192,1536]{2,1,0:T(8,128)(2,1)} %get-tuple-element.617), channel_id=1, source_target_pairs={{0,8},{8,16},{16,24},{24,28},{28,20},{20,12},{12,4},{4,0},{1,9},{9... | collective-permute-start | bytes 3538952 | tf_op jit(solution)/shard_map/ppermute | solution.py:736
  647.2 27.7 %collective-permute-start.84 = (bf16[2,192,1536]{2,1,0:T(8,128)(2,1)}, bf16[2,192,1536]{2,1,0:T(8,128)(2,1)}, u32[]{:S(2)}, u32[]{:S(2)}) collective-permute-start(bf16[2,192,1536]{2,1,0:T(8,128)(2,1)} %get-tuple-element.618), channel_id=1, source_target_pairs={{8,0},{16,8},{24,16},{28,24},{20,28},{12,20},{4,12},{0,4},{9,1},{1... | collective-permute-start | bytes 3538952 | tf_op jit(solution)/shard_map/ppermute | solution.py:736
  (105 other events, 3020.2 us)
